TPU v7x, 32 devices: a whole 2x2x4 slice. The times are simulated.
32 devices in a mesh: grp: 2 (over y), seq: 16 (over z, x, core).
Axes of the slice: x: 2, y: 2, z: 4, core: 2. Of those that a mesh axis runs over, the one named last changes fastest.
Arguments:
- tokens: bfloat16 [32768, 512], P(('grp', 'seq')), parts along dimension 0, may hold values from -6 to 6
- cotangent: bfloat16 [32768, 512], P(('grp', 'seq')), parts along dimension 0, may hold values from -6 to 6
- factor_one: bfloat16 [16, 1024, 1024], P('seq'), may hold values from -0.1875 to 0.1875
- factor_two: bfloat16 [1024, 16, 16], P('seq'), may hold values from -1.5 to 1.5
- up_blocks: bfloat16 [4, 128, 512], replicated, may hold values from -0.5 to 0.5
- down_blocks: bfloat16 [4, 512, 128], replicated, may hold values from -0.25 to 0.25
Outputs:
- grad_tokens: bfloat16 [32768, 512], P(('grp', 'seq')), parts along dimension 0
- grad_one: float32 [32, 1024, 1024], P(('grp', 'seq')), parts along dimension 0
- grad_two: float32 [2048, 16, 16], P(('grp', 'seq')), parts along dimension 0
- grad_up: float32 [8, 128, 512], P('grp'), parts along dimension 0
- grad_down: float32 [8, 512, 128], P('grp'), parts along dimension 0
There are 2 independent parts, one for each index of `grp`. A program takes and returns all parts, laid end to end along the dimension named above; an argument that names none is the same for every part. Nothing has to cross between parts.
All inputs are finite; a program needn't handle non-finite values.
Results may differ from a plain program's by a relative error of at most 0.012.
Values may be sent and summed in bfloat16 or wider, within the bound.
No kernel may reach another device: no remote copies, remote signals or barrier semaphores. Data moves between devices by JAX's collectives and lax.ppermute only.
A program may use at most 128 MiB of HBM per device.

v0:
```python
import jax
import jax.numpy as jnp
from jax import lax
from jax.sharding import PartitionSpec as P


def silu_slope(values):
    logistic = jax.nn.sigmoid(values)
    return logistic * (1.0 + values * (1.0 - logistic))


def swap_groups(hidden, groups):
    leading = hidden.shape[0]
    inner = hidden.shape[2]
    return (
        hidden.reshape(leading, groups, groups, inner // groups)
        .transpose(0, 2, 1, 3)
        .reshape(leading, groups, inner)
    )


def middle_part(blocked, mixed, incoming, up_blocks, down_blocks):
    kept_shape = blocked.shape
    groups = up_blocks.shape[0]
    channel_part = up_blocks.shape[1]
    features = blocked.astype(jnp.float32)
    gate_value = jax.nn.silu(features)
    mixed_f = mixed.astype(jnp.float32)
    hidden_state = (features + mixed_f * gate_value).astype(jnp.bfloat16)
    row_count = hidden_state.size // (groups * channel_part)
    hidden_rows = hidden_state.reshape(row_count, groups, channel_part)
    grad_rows = incoming.reshape(row_count, groups, channel_part)
    before_act = jnp.einsum(
        "rbc,bcf->rbf", hidden_rows, up_blocks, preferred_element_type=jnp.float32
    )
    activated = jax.nn.silu(before_act).astype(jnp.bfloat16)
    permuted = swap_groups(activated, groups)
    down_part = jnp.einsum("rbf,rbc->bfc", permuted, grad_rows, preferred_element_type=jnp.float32)
    grad_perm = jnp.einsum(
        "rbc,bfc->rbf", grad_rows, down_blocks, preferred_element_type=jnp.float32
    )
    grad_act = swap_groups(grad_perm, groups)
    grad_before = (grad_act * silu_slope(before_act)).astype(jnp.bfloat16)
    up_part = jnp.einsum(
        "rbc,rbf->bcf", hidden_rows, grad_before, preferred_element_type=jnp.float32
    )
    back_hidden = jnp.einsum(
        "rbf,bcf->rbc", grad_before, up_blocks, preferred_element_type=jnp.float32
    )
    grad_hidden = (
        (grad_rows.astype(jnp.float32) + back_hidden).reshape(kept_shape).astype(jnp.bfloat16)
    )
    grad_hidden_f = grad_hidden.astype(jnp.float32)
    grad_mixed = (grad_hidden_f * gate_value).astype(jnp.bfloat16)
    gate_grad = (grad_hidden_f * (1.0 + mixed_f * silu_slope(features))).astype(jnp.bfloat16)
    return (grad_mixed, gate_grad, up_part, down_part)


def on_device(tokens, cotangent, factor_one, factor_two, up_blocks, down_blocks):
    seq_count = lax.axis_size("seq")
    channels = tokens.shape[1]
    block_size = factor_one.shape[1]
    blocks_here = tokens.shape[0] // block_size
    scale_all = float(seq_count * tokens.shape[0]) ** (-0.5)
    blocked = tokens.reshape(blocks_here, block_size, channels)
    grad_blocked = cotangent.reshape(blocks_here, block_size, channels)
    first_mix = jnp.einsum(
        "jki,jic->jkc", factor_one, blocked, preferred_element_type=jnp.float32
    ).astype(jnp.bfloat16)
    first_cols = lax.all_to_all(first_mix, "seq", split_axis=1, concat_axis=0, tiled=True)
    second_cols = jnp.einsum(
        "kmj,jkc->mkc", factor_two, first_cols, preferred_element_type=jnp.float32
    ).astype(jnp.bfloat16)
    second_mix = lax.all_to_all(second_cols, "seq", split_axis=0, concat_axis=1, tiled=True)
    grad_mixed, gate_grad, up_part, down_part = middle_part(
        blocked, second_mix, grad_blocked, up_blocks, down_blocks
    )
    grad_mixed_cols = lax.all_to_all(grad_mixed, "seq", split_axis=1, concat_axis=0, tiled=True)
    grad_first_cols = jnp.einsum(
        "kmj,mkc->jkc", factor_two, grad_mixed_cols, preferred_element_type=jnp.float32
    ).astype(jnp.bfloat16)
    grad_first = lax.all_to_all(grad_first_cols, "seq", split_axis=0, concat_axis=1, tiled=True)
    two_local = jnp.einsum(
        "mkc,jkc->kmj", grad_mixed_cols, first_cols, preferred_element_type=jnp.float32
    )
    one_local = jnp.einsum("jkc,jic->jki", grad_first, blocked, preferred_element_type=jnp.float32)
    back_one = jnp.einsum(
        "jki,jkc->jic", factor_one, grad_first, preferred_element_type=jnp.float32
    )
    grad_tokens = (
        (gate_grad.astype(jnp.float32) + back_one).astype(jnp.bfloat16).reshape(tokens.shape)
    )
    up_sum, down_sum = lax.psum((up_part, down_part), "seq")
    return (
        grad_tokens,
        one_local * scale_all,
        two_local * scale_all,
        up_sum * scale_all,
        down_sum * scale_all,
    )


def solution(mesh):
    return jax.shard_map(
        on_device,
        mesh=mesh,
        in_specs=(
            P(("grp", "seq"), None),
            P(("grp", "seq"), None),
            P("seq", None, None),
            P("seq", None, None),
            P(),
            P(),
        ),
        out_specs=(
            P(("grp", "seq"), None),
            P(("grp", "seq"), None, None),
            P(("grp", "seq"), None, None),
            P("grp", None, None),
            P("grp", None, None),
        ),
        check_vma=False,
    )
```

profile of v0, /device:TPU:0, one launch (start us, length us, event | category | flops | bytes accessed | tf_op | source)
XLA Modules:
  0.0 314.9 jit_solution(15890360697970657873)
XLA Ops:
  7.2 1.6 copy-done
  8.8 2.5 fusion.31
  11.2 2.9 copy.113
  14.2 0.5 broadcast.17
  14.7 8.0 %reduce = bf16[1024,512]{1,0:T(8,128)(2,1)S(1)} reduce(bf16[1024,1,512]{2,1,0:T(2,128)(2,1)} %bitcast.103, bf16[]{:T(256)} %broadcast.17), dimensions={1}, to_apply=%bitcast.96.reduce_sub_computation | reduce | bytes 2097154
  22.7 1.6 reshape.102
  24.3 7.4 %all-to-all-start = ((bf16[16,2,16384]{2,1,0:T(2,128)(2,1)}), bf16[16,2,16384]{2,1,0:T(2,128)(2,1)S(1)}, u32[]{:S(2)}, u32[]{:S(2)}) async-start(bf16[16,2,16384]{2,1,0:T(2,128)(2,1)} %reshape.102), calls=%async_computation | async-start | bytes 2097152 | tf_op jit(solution)/shard_map/all_to_all | solution.py:70
  32.0 22.7 %all-to-all-done = bf16[16,2,16384]{2,1,0:T(2,128)(2,1)S(1)} async-done(((bf16[16,2,16384]{2,1,0:T(2,128)(2,1)}), bf16[16,2,16384]{2,1,0:T(2,128)(2,1)S(1)}, u32[]{:S(2)}, u32[]{:S(2)}) %all-to-all-start) | async-done | bytes 1048608 | tf_op jit(solution)/shard_map/all_to_all | solution.py:70
  54.6 3.4 %reshape.103 = bf16[1024,1,512]{2,1,0:T(2,128)(2,1)} reshape(bf16[16,2,16384]{2,1,0:T(2,128)(2,1)S(1)} %all-to-all-done) | data formatting | bytes 2097152
  58.1 1.9 copy.102
  59.9 1.0 copy-done.4
  60.9 0.8 fusion.29
  61.7 1.5 copy.79
  63.2 6.9 %all-to-all-start.1 = ((bf16[16,64,512]{2,1,0:T(8,128)(2,1)}), bf16[16,64,512]{2,1,0:T(8,128)(2,1)}, u32[]{:S(2)}, u32[]{:S(2)}) async-start(bf16[16,64,512]{2,1,0:T(8,128)(2,1)} %copy.79), calls=%async_computation.1 | async-start | bytes 2097152 | tf_op jit(solution)/shard_map/all_to_all | solution.py:74
  70.2 1.3 copy.75
  71.5 1.5 copy.72
  73.0 2.3 fusion.38
  75.3 4.1 %copy.74 = f32[1024,4,4,128]{0,3,2,1:T(8,128)} copy(f32[1024,4,4,128]{0,3,1,2:T(8,128)S(1)} %bitcast.97) | data formatting | bytes 16777216 | tf_op jit(solution)/shard_map/transpose | solution.py:17
  79.4 13.8 %all-to-all-done.1 = bf16[16,64,512]{2,1,0:T(8,128)(2,1)} async-done(((bf16[16,64,512]{2,1,0:T(8,128)(2,1)}), bf16[16,64,512]{2,1,0:T(8,128)(2,1)}, u32[]{:S(2)}, u32[]{:S(2)}) %all-to-all-start.1) | async-done | bytes 1048608 | tf_op jit(solution)/shard_map/all_to_all | solution.py:74
  93.2 2.8 bitcast_convert_fusion
  96.0 3.0 copy.80
  98.9 2.6 fusion.13
  101.6 8.1 %fusion.7 = (bf16[1024,4,512]{0,2,1:T(8,128)(2,1)}, bf16[1024,4,512]{0,2,1:T(8,128)(2,1)S(1)}) fusion(f32[1024,4,4,128]{0,3,2,1:T(8,128)} %copy.74, bf16[1024,4,128]{0,2,1:T(8,128)(2,1)S(1)} %bitcast.112, bf16[4,128,512]{2,1,0:T(8,128)(2,1)S(1)} %copy-done.7), kind=kOutput, calls=%fused_computation.10 | convolution fusion | flops 559939584 | bytes 18350080 | tf_op jit(solution)/shard_map/rbc,bcf->rbf/dot_general | solution.py:33
  109.7 0.7 fusion.19
  110.4 1.4 copy-done.1
  111.8 1.0 copy-done.2
  113.0 2.7 fusion.9
  115.7 6.0 %copy.85 = bf16[1,1024,512]{2,0,1:T(2,128)(2,1)} copy(bf16[1,1024,512]{1,2,0:T(8,128)(2,1)} %bitcast.111) | data formatting | bytes 2097152 | tf_op jit(solution)/shard_map/convert_element_type | solution.py:54
  121.7 9.0 %reduce.1 = bf16[1024,512]{1,0:T(8,128)(2,1)} reduce(bf16[1024,1,512]{2,1,0:T(2,128)(2,1)} %bitcast.104, bf16[]{:T(256)} %broadcast.17), dimensions={1}, to_apply=%bitcast.77.reduce_sub_computation | reduce | bytes 2097154
  130.7 2.6 reshape.104
  133.3 6.9 %all-to-all-start.2 = ((bf16[16,2,16384]{2,1,0:T(2,128)(2,1)}), bf16[16,2,16384]{2,1,0:T(2,128)(2,1)}, u32[]{:S(2)}, u32[]{:S(2)}) async-start(bf16[16,2,16384]{2,1,0:T(2,128)(2,1)} %reshape.104), calls=%async_computation.2 | async-start | bytes 2097152 | tf_op jit(solution)/shard_map/all_to_all | solution.py:78
  140.2 2.6 copy.92
  142.9 2.3 fusion.40
  145.1 18.1 %all-to-all-done.2 = bf16[16,2,16384]{2,1,0:T(2,128)(2,1)} async-done(((bf16[16,2,16384]{2,1,0:T(2,128)(2,1)}), bf16[16,2,16384]{2,1,0:T(2,128)(2,1)}, u32[]{:S(2)}, u32[]{:S(2)}) %all-to-all-start.2) | async-done | bytes 1048608 | tf_op jit(solution)/shard_map/all_to_all | solution.py:78
  163.2 5.8 %reshape.105 = bf16[1024,1,512]{2,1,0:T(2,128)(2,1)} reshape(bf16[16,2,16384]{2,1,0:T(2,128)(2,1)} %all-to-all-done.2) | data formatting | bytes 2097152
  169.0 1.9 copy.103
  170.9 0.7 fusion.30
  171.6 1.5 copy.88
  173.2 6.9 %all-to-all-start.3 = ((bf16[16,64,512]{2,1,0:T(8,128)(2,1)}), bf16[16,64,512]{2,1,0:T(8,128)(2,1)}, u32[]{:S(2)}, u32[]{:S(2)}) async-start(bf16[16,64,512]{2,1,0:T(8,128)(2,1)} %copy.88), calls=%async_computation.3 | async-start | bytes 2097152 | tf_op jit(solution)/shard_map/all_to_all | solution.py:82
  180.4 5.0 %fusion.39 = f32[4,128,512]{2,1,0:T(8,128)} fusion(bf16[1024,4,128]{0,2,1:T(8,128)(2,1)} %bitcast.113, bf16[1024,4,512]{0,2,1:T(8,128)(2,1)} %copy-done.1), kind=kOutput, calls=%fused_computation.52 | convolution fusion | flops 536870912 | bytes 6291456 | tf_op jit(solution)/shard_map/rbc,rbf->bcf/dot_general | solution.py:44
  185.4 106.4 %all-reduce.3.cloned.1.call-done = (f32[4,128,512]{2,1,0:T(8,128)}, f32[4,512,128]{2,1,0:T(8,128)}) async-done(((f32[4,128,512]{2,1,0:T(8,128)}, f32[4,512,128]{2,1,0:T(8,128)}), (f32[4,128,512]{2,1,0:T(8,128)}, f32[4,512,128]{2,1,0:T(8,128)})) %all-reduce.3.cloned.1.call-update) | async-done | bytes 2097168 | tf_op jit(solution)/shard_map/psum | solution.py:93
  291.9 2.5 broadcast_multiply_fusion.1
  294.3 1.0 broadcast_multiply_fusion
  295.4 2.0 convolution_multiply_fusion
  297.4 1.9 copy.95
  299.3 4.9 %multiply_bitcast_fusion = f32[1,1024,1024]{2,1,0:T(8,128)} fusion(bf16[1024,512]{1,0:T(8,128)(2,1)} %bitcast.17, bf16[1024,512]{1,0:T(8,128)(2,1)} %param.6), kind=kOutput, calls=%fused_computation.11 | convolution fusion | flops 1074790400 | bytes 6291456 | tf_op jit(solution)/shard_map/jkc,jic->jki/dot_general | solution.py:86
  304.3 2.5 fusion.18
  306.8 1.3 copy.94
  (24 shorter events, 0.9 us)
Async XLA Ops:
  7.2 1.6 copy-start
  22.7 9.0 %copy-start.11 = (bf16[64,16,16]{0,2,1:T(8,128)(2,1)S(1)}, bf16[64,16,16]{0,2,1:T(8,128)(2,1)}, u32[]{:S(2)}) copy-start(bf16[64,16,16]{0,2,1:T(8,128)(2,1)} %param.9) | copy-start | bytes 98308
  24.3 30.3 %all-to-all-start = ((bf16[16,2,16384]{2,1,0:T(2,128)(2,1)}), bf16[16,2,16384]{2,1,0:T(2,128)(2,1)S(1)}, u32[]{:S(2)}, u32[]{:S(2)}) async-start(bf16[16,2,16384]{2,1,0:T(2,128)(2,1)} %reshape.102), calls=%async_computation | async-start | bytes 2097152 | tf_op jit(solution)/shard_map/all_to_all | solution.py:70
  59.9 1.0 copy-start.4
  61.7 8.5 %copy-start.8 = (bf16[1024,512]{1,0:T(8,128)(2,1)S(1)}, bf16[1024,512]{1,0:T(8,128)(2,1)}, u32[]{:S(2)}) copy-start(bf16[1024,512]{1,0:T(8,128)(2,1)} %param.6) | copy-start | bytes 3145732
  63.2 29.9 %all-to-all-start.1 = ((bf16[16,64,512]{2,1,0:T(8,128)(2,1)}), bf16[16,64,512]{2,1,0:T(8,128)(2,1)}, u32[]{:S(2)}, u32[]{:S(2)}) async-start(bf16[16,64,512]{2,1,0:T(8,128)(2,1)} %copy.79), calls=%async_computation.1 | async-start | bytes 2097152 | tf_op jit(solution)/shard_map/all_to_all | solution.py:74
  98.9 2.6 copy-start.7
  101.6 8.1 %copy-start.6 = (bf16[1024,512]{0,1:T(8,128)(2,1)}, bf16[1024,512]{0,1:T(8,128)(2,1)S(1)}, u32[]{:S(2)}) copy-start(bf16[1024,512]{0,1:T(8,128)(2,1)S(1)} %fusion.13) | copy-start | bytes 3145732
  109.7 2.1 copy-start.1
  109.7 3.1 copy-start.2
  109.7 3.4 %copy-start.3 = (bf16[1024,512]{0,1:T(8,128)(2,1)S(1)}, bf16[1024,512]{0,1:T(8,128)(2,1)}, u32[]{:S(2)}) copy-start(bf16[1024,512]{0,1:T(8,128)(2,1)} %copy.75) | copy-start | bytes 3145732
  133.3 29.9 %all-to-all-start.2 = ((bf16[16,2,16384]{2,1,0:T(2,128)(2,1)}), bf16[16,2,16384]{2,1,0:T(2,128)(2,1)}, u32[]{:S(2)}, u32[]{:S(2)}) async-start(bf16[16,2,16384]{2,1,0:T(2,128)(2,1)} %reshape.104), calls=%async_computation.2 | async-start | bytes 2097152 | tf_op jit(solution)/shard_map/all_to_all | solution.py:78
  173.2 126.2 %all-to-all-start.3 = ((bf16[16,64,512]{2,1,0:T(8,128)(2,1)}), bf16[16,64,512]{2,1,0:T(8,128)(2,1)}, u32[]{:S(2)}, u32[]{:S(2)}) async-start(bf16[16,64,512]{2,1,0:T(8,128)(2,1)} %copy.88), calls=%async_computation.3 | async-start | bytes 2097152 | tf_op jit(solution)/shard_map/all_to_all | solution.py:82
  180.1 111.8 %all-reduce.3.cloned.1.call-start = ((), (), s32[]{:S(2)}) async-start(), calls=%async_computation.4 | async-start | bytes 4194304 | tf_op jit(solution)/shard_map/psum | solution.py:93
  291.9 2.5 copy-start.9
  291.9 3.5 %copy-start.5 = (bf16[1,1024,512]{2,1,0:T(8,128)(2,1)S(1)}, bf16[1,1024,512]{2,1,0:T(8,128)(2,1)}, u32[]{:S(2)}) copy-start(bf16[1,1024,512]{2,1,0:T(8,128)(2,1)} %copy-done.4) | copy-start | bytes 3145732
  299.3 4.9 %copy-start.10 = (bf16[1024,512]{0,1:T(8,128)(2,1)S(1)}, bf16[1024,512]{0,1:T(8,128)(2,1)}, u32[]{:S(2)}) copy-start(bf16[1024,512]{0,1:T(8,128)(2,1)} %get-tuple-element.30) | copy-start | bytes 3145732
Sparse Core Ops, SparseCore 0:
  185.5 106.2 all-reduce.2
where the time goes:
time: 316 us; the launch traced here: 315 us
  waiting for transfers between devices  161 us (51%)
  local copies, waits for them, and re-layouts  50.8 us (16%)
  matrix products  31.8 us (10%)
  other arithmetic  28.7 us (9%)
  starting transfers between devices  28.4 us (9%)
  between operations  14.2 us (4%)
    psum x1, waiting for transfers between devices, on_device(): up_sum, down_sum = lax.psum((up_part, down_part), 'seq')  106 us
    unnamed x36, local copies, waits for them, and re-layouts  29.2 us
    all_to_all x1, waiting for transfers between devices, on_device(): lax.all_to_all(first_mix, 'seq', split_axis=1, concat_axis=0, tiled=True)  22.7 us
    all_to_all x1, waiting for transfers between devices, on_device(): lax.all_to_all(grad_mixed, 'seq', split_axis=1, concat_axis=0, tiled=True)  18.1 us
    unnamed x2, other arithmetic  17 us
    all_to_all x1, waiting for transfers between devices, on_device(): lax.all_to_all(second_cols, 'seq', split_axis=0, concat_axis=1, tiled=True)  13.8 us
    dot_general x1, matrix products, middle_part(): jnp.einsum('rbc,bcf->rbf', hidden_rows, up_blocks, preferred_element_type...  8.07 us
    all_to_all x1, starting transfers between devices, on_device(): lax.all_to_all(first_mix, 'seq', split_axis=1, concat_axis=0, tiled=True)  7.36 us
  transfers between devices with their start and end apart: 5, of which 4 were waited for; matrix products, arithmetic and copies ran while one was open for 9% of the time, Pallas kernels for 0%

commit v1 on v0

v1 whole, which is shorter than its diff:
```python
import jax
import jax.numpy as jnp
from jax import lax
from jax.experimental import pallas as pl
from jax.experimental.pallas import tpu as pltpu
from jax.sharding import PartitionSpec as P

BF = jnp.bfloat16
F32 = jnp.float32
PIECES = 1
VMEM_BYTES = 40 * 1024 * 1024


def sigmoid(z):
    return 0.5 + 0.5 * jnp.tanh(0.5 * z)


def dot(a, b, ca, cb, **kw):
    return lax.dot_general(a, b, (((ca,), (cb,)), ((), ())), preferred_element_type=F32, **kw)


def rows_of(ref):
    value = ref[...]
    return value.reshape(-1, value.shape[-1])


def params(steps=1):
    return pltpu.CompilerParams(
        dimension_semantics=("arbitrary",) * steps, vmem_limit_bytes=VMEM_BYTES
    )


def cost(flops, moved, trans=0):
    return pl.CostEstimate(flops=int(flops), bytes_accessed=int(moved), transcendentals=int(trans))


class Plan:
    def __init__(self, count, block, channels):
        self.count = count
        self.block = block
        self.channels = channels
        self.here = block // count
        self.pieces = PIECES if self.here % (16 * PIECES) == 0 else 1
        self.part = self.here // self.pieces
        self.rows = block // self.pieces
        self.grouped = self.part % 16 == 0

    def view(self, array):
        if self.pieces == 1:
            return array
        return array.reshape(self.count, self.pieces, self.part, array.shape[-1])

    def spec(self, rows, columns, piece, index=lambda i: (i, 0)):
        if self.pieces == 1:
            return pl.BlockSpec((rows, columns), index)

        def whole(i):
            at, col = index(i)
            return (at, piece, 0, col)

        return pl.BlockSpec((rows // self.part, 1, self.part, columns), whole)


def mix_first(plan, factor, blocked, piece):
    def body(factor_ref, x_ref, out_ref):
        out_ref[...] = dot(rows_of(factor_ref), x_ref[...], 1, 0).astype(BF)

    step = min(256, plan.rows)
    return pl.pallas_call(
        body,
        grid=(plan.rows // step,),
        in_specs=[
            plan.spec(step, plan.block, piece),
            pl.BlockSpec((plan.block, plan.channels), lambda i: (0, 0)),
        ],
        out_specs=pl.BlockSpec((step, plan.channels), lambda i: (i, 0)),
        out_shape=jax.ShapeDtypeStruct((plan.rows, plan.channels), BF),
        compiler_params=params(),
        cost_estimate=cost(
            2 * plan.rows * plan.block * plan.channels,
            2 * (plan.rows * plan.block + 2 * plan.block * plan.channels),
        ),
        name="mix_first",
    )(plan.view(factor), blocked)


def spread_factor(plan, factor_two):
    n = plan.count
    groups = plan.here // 16
    wide = n * 16
    turned = factor_two.reshape(groups, 16, n, n).transpose(0, 2, 1, 3).reshape(groups, wide, n)

    def body(in_ref, out_ref):
        col = lax.broadcasted_iota(jnp.int32, (n, wide), 1)
        row = lax.broadcasted_iota(jnp.int32, (n, wide), 0)
        pick = jnp.where(col // 16 == row, 1.0, 0.0).astype(BF)
        full = dot(in_ref[0], pick, 1, 0)
        r = lax.broadcasted_iota(jnp.int32, (wide, wide), 0)
        c = lax.broadcasted_iota(jnp.int32, (wide, wide), 1)
        out_ref[0] = jnp.where(r % 16 == c % 16, full, 0.0).astype(BF)

    return pl.pallas_call(
        body,
        grid=(groups,),
        in_specs=[pl.BlockSpec((1, wide, n), lambda g: (g, 0, 0))],
        out_specs=pl.BlockSpec((1, wide, wide), lambda g: (g, 0, 0)),
        out_shape=jax.ShapeDtypeStruct((groups, wide, wide), BF),
        compiler_params=params(),
        cost_estimate=cost(2 * groups * wide * wide * n, 2 * groups * wide * wide),
        name="spread_factor",
    )(turned)


def mix_second(plan, spread, cols, piece, back):
    n = plan.count
    wide = n * 16
    groups = plan.part // 16

    def body(m_ref, in_ref, out_ref):
        rows = in_ref[...].reshape(wide, plan.channels)
        got = dot(m_ref[0], rows, 0 if back else 1, 0).astype(BF)
        out_ref[...] = got.reshape(n, 16, plan.channels)

    out = pl.pallas_call(
        body,
        grid=(groups,),
        in_specs=[
            pl.BlockSpec((1, wide, wide), lambda g: (piece * groups + g, 0, 0)),
            pl.BlockSpec((n, 16, plan.channels), lambda g: (0, g, 0)),
        ],
        out_specs=pl.BlockSpec((n, 16, plan.channels), lambda g: (0, g, 0)),
        out_shape=jax.ShapeDtypeStruct((n, plan.part, plan.channels), BF),
        compiler_params=params(),
        cost_estimate=cost(
            2 * groups * wide * wide * plan.channels,
            4 * plan.rows * plan.channels + 2 * groups * wide * wide,
        ),
        name="mix_second_back" if back else "mix_second",
    )(spread, cols.reshape(n, plan.part, plan.channels))
    return out.reshape(plan.rows, plan.channels)


def grad_second(plan, grads, firsts, scale):
    n = plan.count
    wide = n * 16
    groups = plan.part // 16

    def body(g_ref, u_ref, out_ref):
        g = g_ref[...].reshape(wide, plan.channels)
        u = u_ref[...].reshape(wide, plan.channels)
        full = dot(g, u, 1, 1)
        r = lax.broadcasted_iota(jnp.int32, (wide, wide), 0)
        c = lax.broadcasted_iota(jnp.int32, (wide, wide), 1)
        kept = jnp.where(r % 16 == c % 16, full, 0.0)
        row = lax.broadcasted_iota(jnp.int32, (wide, n), 0)
        col = lax.broadcasted_iota(jnp.int32, (wide, n), 1)
        pick = jnp.where(row // 16 == col, 1.0, 0.0)
        out_ref[0] = dot(kept, pick, 1, 0, precision=lax.Precision.HIGHEST) * scale

    out = pl.pallas_call(
        body,
        grid=(groups,),
        in_specs=[pl.BlockSpec((n, 16, plan.channels), lambda g: (0, g, 0))] * 2,
        out_specs=pl.BlockSpec((1, wide, n), lambda g: (g, 0, 0)),
        out_shape=jax.ShapeDtypeStruct((groups, wide, n), F32),
        compiler_params=params(),
        cost_estimate=cost(
            2 * groups * wide * wide * plan.channels, 4 * plan.rows * plan.channels
        ),
        name="grad_second",
    )(
        grads.reshape(n, plan.part, plan.channels),
        firsts.reshape(n, plan.part, plan.channels),
    )
    return out.reshape(groups, n, 16, n).transpose(0, 2, 1, 3).reshape(plan.part, n, n)


def middle(plan, blocked, incoming, mixed, up_blocks, down_blocks, piece, before):
    groups, width, inner = up_blocks.shape
    sub = inner // groups
    step = min(256, plan.rows)

    def body(*refs):
        x_ref, g_ref, v_ref, up_ref, down_ref = refs[:5]
        dv_ref, r_ref, w_ref = refs[-3:]

        @pl.when(pl.program_id(0) == 0)
        def _():
            if before is None:
                w_ref[...] = jnp.zeros_like(w_ref)
            else:
                w_ref[...] = refs[5][...]

        x = rows_of(x_ref).astype(F32)
        g = rows_of(g_ref)
        v = v_ref[...].astype(F32)
        sx = sigmoid(x)
        gate = x * sx
        h = (x + v * gate).astype(BF)
        h_parts = [h[:, b * width : (b + 1) * width] for b in range(groups)]
        g_parts = [g[:, b * width : (b + 1) * width] for b in range(groups)]
        acts, slopes, back = [], [], []
        for b in range(groups):
            a = dot(h_parts[b], up_ref[b], 1, 0)
            s = sigmoid(a)
            q = a * s
            acts.append(q.astype(BF))
            slopes.append(s + q * (1.0 - s))
            back.append(dot(g_parts[b], down_ref[b], 1, 1))
        grads = []
        for b in range(groups):
            lanes = slice(b * sub, (b + 1) * sub)
            perm = jnp.concatenate([acts[p][:, lanes] for p in range(groups)], axis=1)
            w_ref[groups + b] += dot(g_parts[b], perm, 0, 0)
            dq = jnp.concatenate([back[p][:, lanes] for p in range(groups)], axis=1)
            da = (dq * slopes[b]).astype(BF)
            w_ref[b] += dot(h_parts[b], da, 0, 0)
            grads.append(dot(da, up_ref[b], 1, 1))
        dh = (g.astype(F32) + jnp.concatenate(grads, axis=1)).astype(BF).astype(F32)
        dv_ref[...] = (dh * gate).astype(BF)
        r_ref[...] = (dh * (1.0 + v * (sx + gate * (1.0 - sx)))).astype(BF)

    block = pl.BlockSpec((step, plan.channels), lambda i: (i, 0))
    full = pl.BlockSpec((2 * groups, width, inner), lambda i: (0, 0, 0))
    in_specs = [
        plan.spec(step, plan.channels, piece),
        plan.spec(step, plan.channels, piece),
        block,
        pl.BlockSpec(up_blocks.shape, lambda i: (0, 0, 0)),
        pl.BlockSpec(down_blocks.shape, lambda i: (0, 0, 0)),
    ]
    operands = [plan.view(blocked), plan.view(incoming), mixed, up_blocks, down_blocks]
    if before is not None:
        in_specs.append(full)
        operands.append(before)
    hidden = plan.rows * groups * inner
    return pl.pallas_call(
        body,
        grid=(plan.rows // step,),
        in_specs=in_specs,
        out_specs=[block, block, full],
        out_shape=[
            jax.ShapeDtypeStruct((plan.rows, plan.channels), BF),
            jax.ShapeDtypeStruct((plan.rows, plan.channels), BF),
            jax.ShapeDtypeStruct((2 * groups, width, inner), F32),
        ],
        compiler_params=params(),
        cost_estimate=cost(
            10 * hidden * width, 10 * plan.rows * plan.channels + 8 * groups * width * inner, hidden
        ),
        name="middle",
    )(*operands)


def finish(plan, factor, grad_firsts, blocked, gate_grads, piece, scale, rows_before, sum_before):
    last = piece == plan.pieces - 1
    step = min(256, plan.block)
    n_gates = plan.pieces if last else 0

    def body(*refs):
        factor_ref, d_ref, x_ref = refs[:3]
        one_ref, out_ref = refs[-2:]
        d = d_ref[...]
        one = dot(d, x_ref[...], 1, 1) * scale
        one_ref[...] = one.reshape(one_ref.shape)
        total = dot(rows_of(factor_ref), d, 0, 0)
        at = 3
        if piece > 0:
            total = total + refs[4][...]
            at = 5
        if last:
            if plan.pieces == 1:
                out_ref[...] = (total + refs[at][...].astype(F32)).astype(BF)
            else:
                total = total.reshape(step // plan.here, plan.pieces, plan.part, plan.channels)
                for q in range(plan.pieces):
                    got = (total[:, q] + refs[at + q][...].astype(F32)).astype(BF)
                    out_ref[:, q] = got
        else:
            out_ref[...] = total

    wide = pl.BlockSpec((step, plan.channels), lambda i: (i, 0))
    in_specs = [
        plan.spec(plan.rows, step, piece, lambda i: (0, i)),
        pl.BlockSpec((plan.rows, plan.channels), lambda i: (0, 0)),
        wide,
    ]
    operands = [plan.view(factor), grad_firsts, blocked]
    aliases = {}
    if piece > 0:
        in_specs += [pl.BlockSpec(memory_space=pl.ANY), wide]
        operands += [rows_before, sum_before]
        aliases = {3: 0}
    if last:
        if plan.pieces == 1:
            in_specs.append(wide)
            operands += gate_grads
            out_spec = wide
            out_shape = (plan.block, plan.channels)
        else:
            in_specs += [
                pl.BlockSpec((step // plan.here, plan.part, plan.channels), lambda i: (i, 0, 0))
            ] * n_gates
            operands += [r.reshape(plan.count, plan.part, plan.channels) for r in gate_grads]
            out_spec = pl.BlockSpec(
                (step // plan.here, plan.pieces, plan.part, plan.channels), lambda i: (i, 0, 0, 0)
            )
            out_shape = (plan.count, plan.pieces, plan.part, plan.channels)
    else:
        out_spec = wide
        out_shape = (plan.block, plan.channels)
    one_shape = (plan.block, plan.block)
    if plan.pieces > 1:
        one_shape = (plan.count, plan.pieces, plan.part, plan.block)
    return pl.pallas_call(
        body,
        grid=(plan.block // step,),
        in_specs=in_specs,
        out_specs=[plan.spec(plan.rows, step, piece, lambda i: (0, i)), out_spec],
        out_shape=[
            jax.ShapeDtypeStruct(one_shape, F32),
            jax.ShapeDtypeStruct(out_shape, BF if last else F32),
        ],
        input_output_aliases=aliases,
        compiler_params=params(),
        cost_estimate=cost(
            4 * plan.rows * plan.block * plan.channels,
            6 * plan.rows * plan.block + 8 * plan.block * plan.channels,
        ),
        name="finish",
    )(*operands)


def sum_over(values, count):
    if count & (count - 1) or values.shape[0] % count:
        return lax.psum(values, "seq")
    me = lax.axis_index("seq")
    total = values
    steps = [1 << s for s in range(count.bit_length() - 1)]
    for step in steps:
        halves = total.reshape(2, total.shape[0] // 2, total.shape[1])
        mine = (me // step) % 2
        keep = lax.dynamic_index_in_dim(halves, mine, 0, keepdims=False)
        send = lax.dynamic_index_in_dim(halves, 1 - mine, 0, keepdims=False).astype(BF)
        got = lax.ppermute(send, "seq", [(i, i ^ step) for i in range(count)])
        total = keep + got.astype(F32)
    total = total.astype(BF)
    for step in reversed(steps):
        mine = (me // step) % 2
        got = lax.ppermute(total, "seq", [(i, i ^ step) for i in range(count)])
        low = jnp.where(mine == 0, total, got)
        high = jnp.where(mine == 0, got, total)
        total = jnp.concatenate([low, high], axis=0)
    return total


def write_weights(total, up_shape, down_shape, scale):
    groups, width, inner = up_shape

    def body(up_in, down_in, up_ref, down_ref):
        up_ref[0] = up_in[...].astype(F32) * scale
        down_ref[0] = (down_in[...].astype(F32) * scale).T

    return pl.pallas_call(
        body,
        grid=(groups,),
        in_specs=[
            pl.BlockSpec((width, inner), lambda b: (b, 0)),
            pl.BlockSpec((width, inner), lambda b: (groups + b, 0)),
        ],
        out_specs=[
            pl.BlockSpec((1, width, inner), lambda b: (b, 0, 0)),
            pl.BlockSpec((1, inner, width), lambda b: (b, 0, 0)),
        ],
        out_shape=[
            jax.ShapeDtypeStruct(up_shape, F32),
            jax.ShapeDtypeStruct(down_shape, F32),
        ],
        compiler_params=params(),
        cost_estimate=cost(groups * width * inner, 12 * groups * width * inner),
        name="write_weights",
    )(total, total)


def on_device(tokens, cotangent, factor_one, factor_two, up_blocks, down_blocks):
    count = lax.axis_size("seq")
    block, channels = factor_one.shape[1], tokens.shape[1]
    plan = Plan(count, block, channels)
    scale = float(count * tokens.shape[0]) ** (-0.5)
    factor = factor_one.reshape(block, block)
    pieces = range(plan.pieces)

    def exchange(rows):
        cut = rows.reshape(count, plan.part, channels)
        got = lax.all_to_all(cut, "seq", split_axis=0, concat_axis=0, tiled=True)
        return got.reshape(plan.rows, channels)

    if plan.grouped:
        spread = spread_factor(plan, factor_two)

    def second(cols, piece, back):
        if plan.grouped:
            return mix_second(plan, spread, cols, piece, back)
        cut = cols.reshape(count, plan.part, channels)
        names = "kmj,mkc->jkc" if back else "kmj,jkc->mkc"
        got = jnp.einsum(names, factor_two, cut, preferred_element_type=F32).astype(BF)
        return got.reshape(plan.rows, channels)

    def second_grad(grads, firsts):
        if plan.grouped:
            return grad_second(plan, grads, firsts, scale)
        shape = (count, plan.part, channels)
        got = jnp.einsum(
            "mkc,jkc->kmj", grads.reshape(shape), firsts.reshape(shape), preferred_element_type=F32
        )
        return got * scale

    firsts = [exchange(mix_first(plan, factor, tokens, q)) for q in pieces]
    mixed = [exchange(second(firsts[q], q, False)) for q in pieces]
    weights = None
    grad_mixed, gate_grads = [], []
    for q in pieces:
        dv, r, weights = middle(
            plan, tokens, cotangent, mixed[q], up_blocks, down_blocks, q, weights
        )
        grad_mixed.append(exchange(dv))
        gate_grads.append(r)
    grad_firsts = [exchange(second(grad_mixed[q], q, True)) for q in pieces]
    two = [second_grad(grad_mixed[q], firsts[q]) for q in pieces]
    total = sum_over(weights.reshape(-1, weights.shape[-1]), count)
    grad_up, grad_down = write_weights(total, up_blocks.shape, down_blocks.shape, scale)
    one, tokens_sum = None, None
    for q in pieces:
        one, tokens_sum = finish(
            plan, factor, grad_firsts[q], tokens, gate_grads, q, scale, one, tokens_sum
        )
    return (
        tokens_sum.reshape(tokens.shape),
        one.reshape(1, block, block),
        jnp.concatenate(two, axis=0),
        grad_up,
        grad_down,
    )


def solution(mesh):
    return jax.shard_map(
        on_device,
        mesh=mesh,
        in_specs=(
            P(("grp", "seq"), None),
            P(("grp", "seq"), None),
            P("seq", None, None),
            P("seq", None, None),
            P(),
            P(),
        ),
        out_specs=(
            P(("grp", "seq"), None),
            P(("grp", "seq"), None, None),
            P(("grp", "seq"), None, None),
            P("grp", None, None),
            P("grp", None, None),
        ),
        check_vma=False,
    )
```

time: 316 us -> 174 us (0.55)
  waiting for transfers between devices: 161 us -> 86.8 us
  matrix products: 31.8 us -> 0 us
  local copies, waits for them, and re-layouts: 50.8 us -> 19.6 us
  other arithmetic: 28.7 us -> 3.97 us
  Pallas kernels: 0 us -> 23.4 us
  between operations: 14.2 us -> 0.93 us
  starting transfers between devices: 28.4 us -> 38.4 us
    psum x1 -> x0, waiting for transfers between devices: 106 us -> none  [on_device(): up_sum, down_sum = lax.psum((up_part, down_part), 'seq')]
    ppermute x0 -> x8, waiting for transfers between devices: none -> 42.1 us  [the longest x4 22.3 us: sum_over(): got = lax.ppermute(send, 'seq', [(i, i ^ step) for i in range(count)])]
    dot_general x11 -> x0, matrix products: 31.8 us -> none  [the longest x1 8.07 us: middle_part(): jnp.einsum('rbc,bcf->rbf', hidden_rows, up_blocks, preferred_element_type...]
    pallas_call x0 -> x8, Pallas kernels: none -> 23.4 us  [the longest x1 7.01 us: middle(): pl.pallas_call(body, grid=(plan.rows // step,), in_specs=in_specs, out_sp...]
    unnamed x2 -> x0, other arithmetic: 17 us -> none
    convert_element_type x5 -> x4, local copies, waits for them, and re-layouts: 15 us -> 0.14 us  [sum_over(): lax.dynamic_index_in_dim(halves, 1 - mine, 0, keepdims=False).astype(BF)]
    ppermute x0 -> x8, starting transfers between devices: none -> 13 us  [the longest x4 7.03 us: sum_over(): got = lax.ppermute(total, 'seq', [(i, i ^ step) for i in range(count)])]
    unnamed x36, local copies, waits for them, and re-layouts: 29.2 us -> 18 us
  transfers between devices with their start and end apart: 5 -> 12, of which waited for: 4 -> 8; matrix products, arithmetic and copies ran while one was open for 9% -> 3% of each run, Pallas kernels for 0% -> 4%
where the time goes in v1:
time: 174 us; the launch traced here: 173 us
  waiting for transfers between devices  86.8 us (50%)
  starting transfers between devices  38.4 us (22%)
  Pallas kernels  23.4 us (13%)
  local copies, waits for them, and re-layouts  19.6 us (11%)
  other arithmetic  3.97 us (2%)
    all_to_all x4, waiting for transfers between devices, exchange(): got = lax.all_to_all(cut, 'seq', split_axis=0, concat_axis=0, tiled=True)  44.8 us
    all_to_all x4, starting transfers between devices, exchange(): got = lax.all_to_all(cut, 'seq', split_axis=0, concat_axis=0, tiled=True)  25.3 us
    ppermute x4, waiting for transfers between devices, sum_over(): got = lax.ppermute(send, 'seq', [(i, i ^ step) for i in range(count)])  22.3 us
    ppermute x4, waiting for transfers between devices, sum_over(): got = lax.ppermute(total, 'seq', [(i, i ^ step) for i in range(count)])  19.7 us
    unnamed x36, local copies, waits for them, and re-layouts  18 us
    ppermute x4, starting transfers between devices, sum_over(): got = lax.ppermute(total, 'seq', [(i, i ^ step) for i in range(count)])  7.03 us
    pallas_call x1, Pallas kernels, middle(): pl.pallas_call(body, grid=(plan.rows // step,), in_specs=in_specs, out_sp...  7.01 us
    ppermute x4, starting transfers between devices, sum_over(): got = lax.ppermute(send, 'seq', [(i, i ^ step) for i in range(count)])  5.99 us
  transfers between devices with their start and end apart: 12, of which 8 were waited for; matrix products, arithmetic and copies ran while one was open for 3% of the time, Pallas kernels for 4%

profile of v1, /device:TPU:0, one launch (start us, length us, event | category | flops | bytes accessed | tf_op | source)
XLA Modules:
  0.0 173.1 jit_solution(14694011023976833258)
XLA Ops:
  0.6 1.6 copy-done.2
  2.2 1.2 copy-done.8
  3.5 1.8 %mix_first.1 = bf16[1024,512]{1,0:T(8,128)(2,1)S(1)} custom-call(bf16[1024,1024]{1,0:T(8,128)(2,1)S(1)} %bitcast.40, bf16[1024,512]{1,0:T(8,128)(2,1)S(1)} %copy-done.8), custom_call_target="tpu_custom_call" | custom-call | flops 1073741824 | bytes 4194304 | tf_op jit(solution)/shard_map/mix_first/pallas_call | solution.py:69
  5.2 1.0 copy-done.1
  6.2 7.5 %all-to-all-start = ((bf16[16,64,512]{2,1,0:T(8,128)(2,1)}), bf16[16,64,512]{2,1,0:T(8,128)(2,1)S(1)}, u32[]{:S(2)}, u32[]{:S(2)}) async-start(bf16[16,64,512]{2,1,0:T(8,128)(2,1)} %bitcast.38), calls=%async_computation | async-start | bytes 2097152 | tf_op jit(solution)/shard_map/all_to_all | solution.py:395
  14.1 0.7 spread_factor.1.m_ref
  14.8 21.8 %all-to-all-done.in_ref.u_ref = bf16[16,64,512]{2,1,0:T(8,128)(2,1)S(1)} async-done(((bf16[16,64,512]{2,1,0:T(8,128)(2,1)}), bf16[16,64,512]{2,1,0:T(8,128)(2,1)S(1)}, u32[]{:S(2)}, u32[]{:S(2)}) %all-to-all-start) | async-done | bytes 1048608 | tf_op jit(solution)/shard_map/all_to_all | solution.py:395
  36.6 2.2 %mix_second.1 = bf16[16,64,512]{2,1,0:T(8,128)(2,1)} custom-call(bf16[4,256,256]{2,1,0:T(8,128)(2,1)S(1)} %spread_factor.1.m_ref, bf16[16,64,512]{2,1,0:T(8,128)(2,1)S(1)} %all-to-all-done.in_ref.u_ref), custom_call_target="tpu_custom_call" | custom-call | flops 268435456 | bytes 2621440 | tf_op jit(solution)/shard_map/mix_second/pallas_call | solution.py:124
  38.8 6.9 %all-to-all-start.1 = ((bf16[16,64,512]{2,1,0:T(8,128)(2,1)}), bf16[16,64,512]{2,1,0:T(8,128)(2,1)S(1)}, u32[]{:S(2)}, u32[]{:S(2)}) async-start(bf16[16,64,512]{2,1,0:T(8,128)(2,1)} %mix_second.1), calls=%async_computation.1 | async-start | bytes 2097152 | tf_op jit(solution)/shard_map/all_to_all | solution.py:395
  45.7 22.9 %all-to-all-done.1 = bf16[16,64,512]{2,1,0:T(8,128)(2,1)S(1)} async-done(((bf16[16,64,512]{2,1,0:T(8,128)(2,1)}), bf16[16,64,512]{2,1,0:T(8,128)(2,1)S(1)}, u32[]{:S(2)}, u32[]{:S(2)}) %all-to-all-start.1) | async-done | bytes 1048608 | tf_op jit(solution)/shard_map/all_to_all | solution.py:395
  68.6 1.0 copy-done.6
  69.6 1.2 copy-done.7
  70.8 1.2 copy-done.9
  72.1 1.2 copy-done.11
  73.3 1.0 copy-done.13
  74.3 7.0 %middle.1 = (bf16[1024,512]{1,0:T(8,128)(2,1)S(1)}, bf16[1024,512]{1,0:T(8,128)(2,1)S(1)}, f32[8,128,512]{2,1,0:T(8,128)S(1)}) custom-call(bf16[1024,512]{1,0:T(8,128)(2,1)S(1)} %copy-done.9, bf16[1024,512]{1,0:T(8,128)(2,1)S(1)} %copy-done.11, bf16[1024,512]{1,0:T(8,128)(2,1)S(1)} %bitcast.46, bf16[4,128,512]{2,1,0:T(8,128)(2,1)S(1)} %copy-done.12, ...), custom_call_target="tpu_custom_call" | custom-call | flops 2684354560 | bytes 7340032 | tf_op jit(solution)/shard_map/middle/pallas_call | solution.py:237
  81.3 1.0 copy-done.14
  82.3 1.3 copy-done.4
  83.7 0.3 copy-done.5
  84.0 0.6 collective-permute-start
  84.6 6.6 %all-to-all-start.2 = ((bf16[16,64,512]{2,1,0:T(8,128)(2,1)}), bf16[16,64,512]{2,1,0:T(8,128)(2,1)S(1)}, u32[]{:S(2)}, u32[]{:S(2)}) async-start(bf16[16,64,512]{2,1,0:T(8,128)(2,1)} %bitcast.45), calls=%async_computation.2 | async-start | bytes 2097152 | tf_op jit(solution)/shard_map/all_to_all | solution.py:395
  91.2 1.6 bitcast_add_fusion
  92.7 1.0 copy-done.16
  93.7 2.0 %collective-permute-start.1 = (bf16[256,512]{1,0:T(8,128)(2,1)S(1)}, bf16[256,512]{1,0:T(8,128)(2,1)S(1)}, u32[]{:S(2)}, u32[]{:S(2)}) collective-permute-start(bf16[256,512]{1,0:T(8,128)(2,1)S(1)} %fusion.1), channel_id=1, source_target_pairs={{0,2},{1,3},{2,0},{3,1},{4,6},{5,7},{6,4},{7,5},{8,10},{9,11},{10,... | collective-permute-start | bytes 786440 | tf_op jit(solution)/shard_map/ppermute | solution.py:345
  95.7 12.8 %collective-permute-done.1 = bf16[256,512]{1,0:T(8,128)(2,1)S(1)} collective-permute-done((bf16[256,512]{1,0:T(8,128)(2,1)S(1)}, bf16[256,512]{1,0:T(8,128)(2,1)S(1)}, u32[]{:S(2)}, u32[]{:S(2)}) %collective-permute-start.1) | collective-permute-done | bytes 262176 | tf_op jit(solution)/shard_map/ppermute | solution.py:345
  108.5 1.1 bitcast_add_fusion.1
  109.7 0.8 collective-permute-start.2
  110.5 6.9 %collective-permute-done.2 = bf16[128,512]{1,0:T(8,128)(2,1)S(1)} collective-permute-done((bf16[128,512]{1,0:T(8,128)(2,1)S(1)}, bf16[128,512]{1,0:T(8,128)(2,1)S(1)}, u32[]{:S(2)}, u32[]{:S(2)}) %collective-permute-start.2) | collective-permute-done | bytes 131104 | tf_op jit(solution)/shard_map/ppermute | solution.py:345
  117.4 2.6 %collective-permute-start.3 = (bf16[64,512]{1,0:T(8,128)(2,1)S(1)}, bf16[64,512]{1,0:T(8,128)(2,1)S(1)}, u32[]{:S(2)}, u32[]{:S(2)}) collective-permute-start(bf16[64,512]{1,0:T(8,128)(2,1)S(1)} %fusion.4), channel_id=1, source_target_pairs={{0,8},{1,9},{2,10},{3,11},{4,12},{5,13},{6,14},{7,15},{8,0},{9,1},... | collective-permute-start | bytes 196616 | tf_op jit(solution)/shard_map/ppermute | solution.py:345
  120.0 2.6 %collective-permute-done.3 = bf16[64,512]{1,0:T(8,128)(2,1)S(1)} collective-permute-done((bf16[64,512]{1,0:T(8,128)(2,1)S(1)}, bf16[64,512]{1,0:T(8,128)(2,1)S(1)}, u32[]{:S(2)}, u32[]{:S(2)}) %collective-permute-start.3) | collective-permute-done | bytes 65568 | tf_op jit(solution)/shard_map/ppermute | solution.py:345
  122.7 2.7 %collective-permute-start.4 = (bf16[64,512]{1,0:T(8,128)(2,1)S(1)}, bf16[64,512]{1,0:T(8,128)(2,1)S(1)}, u32[]{:S(2)}, u32[]{:S(2)}) collective-permute-start(bf16[64,512]{1,0:T(8,128)(2,1)S(1)} %fusion.3), channel_id=1, source_target_pairs={{0,8},{1,9},{2,10},{3,11},{4,12},{5,13},{6,14},{7,15},{8,0},{9,1},... | collective-permute-start | bytes 196616 | tf_op jit(solution)/shard_map/ppermute | solution.py:350
  125.3 2.5 %collective-permute-done.4 = bf16[64,512]{1,0:T(8,128)(2,1)S(1)} collective-permute-done((bf16[64,512]{1,0:T(8,128)(2,1)S(1)}, bf16[64,512]{1,0:T(8,128)(2,1)S(1)}, u32[]{:S(2)}, u32[]{:S(2)}) %collective-permute-start.4) | collective-permute-done | bytes 65568 | tf_op jit(solution)/shard_map/ppermute | solution.py:350
  127.9 2.4 %collective-permute-start.5 = (bf16[128,512]{1,0:T(8,128)(2,1)S(1)}, bf16[128,512]{1,0:T(8,128)(2,1)S(1)}, u32[]{:S(2)}, u32[]{:S(2)}) collective-permute-start(bf16[128,512]{1,0:T(8,128)(2,1)S(1)} %pad_maximum_fusion.3), channel_id=1, source_target_pairs={{0,4},{1,5},{2,6},{3,7},{4,0},{5,1},{6,2},{7,3},{8,12},{9,13},{10,... | collective-permute-start | bytes 393224 | tf_op jit(solution)/shard_map/ppermute | solution.py:350
  130.3 1.2 mix_second_back.1
  131.5 1.0 copy-done
  132.5 4.4 %all-to-all-start.3 = ((bf16[16,64,512]{2,1,0:T(8,128)(2,1)}), bf16[16,64,512]{2,1,0:T(8,128)(2,1)}, u32[]{:S(2)}, u32[]{:S(2)}) async-start(bf16[16,64,512]{2,1,0:T(8,128)(2,1)} %copy-done), calls=%async_computation.3 | async-start | bytes 2097152 | tf_op jit(solution)/shard_map/all_to_all | solution.py:395
  137.0 1.9 %collective-permute-start.6 = (bf16[256,512]{1,0:T(8,128)(2,1)S(1)}, bf16[256,512]{1,0:T(8,128)(2,1)S(1)}, u32[]{:S(2)}, u32[]{:S(2)}) collective-permute-start(bf16[256,512]{1,0:T(8,128)(2,1)S(1)} %pad_maximum_fusion.2), channel_id=1, source_target_pairs={{0,2},{1,3},{2,0},{3,1},{4,6},{5,7},{6,4},{7,5},{8,10},{9,11},{10,... | collective-permute-start | bytes 786440 | tf_op jit(solution)/shard_map/ppermute | solution.py:350
  138.9 15.1 %collective-permute-done.6 = bf16[256,512]{1,0:T(8,128)(2,1)S(1)} collective-permute-done((bf16[256,512]{1,0:T(8,128)(2,1)S(1)}, bf16[256,512]{1,0:T(8,128)(2,1)S(1)}, u32[]{:S(2)}, u32[]{:S(2)}) %collective-permute-start.6) | collective-permute-done | bytes 262176 | tf_op jit(solution)/shard_map/ppermute | solution.py:350
  154.1 0.8 pad_maximum_fusion.1
  154.9 2.1 %collective-permute-done.7 = bf16[512,512]{1,0:T(8,128)(2,1)S(1)} collective-permute-done((bf16[512,512]{1,0:T(8,128)(2,1)}, bf16[512,512]{1,0:T(8,128)(2,1)S(1)}, u32[]{:S(2)}, u32[]{:S(2)}) %collective-permute-start.7) | collective-permute-done | bytes 524320 | tf_op jit(solution)/shard_map/ppermute | solution.py:350
  157.3 1.9 %write_weights.1 = (f32[4,128,512]{2,1,0:T(8,128)}, f32[4,512,128]{2,1,0:T(8,128)}) custom-call(bf16[1024,512]{1,0:T(8,128)(2,1)S(1)} %pad_maximum_fusion.up_in.down_in, bf16[1024,512]{1,0:T(8,128)(2,1)S(1)} %pad_maximum_fusion.up_in.down_in), custom_call_target="tpu_custom_call" | custom-call | flops 262144 | bytes 3145728 | tf_op jit(solution)/shard_map/write_weights/pallas_call | solution.py:364
  159.3 2.9 %grad_second.1 = f32[4,256,16]{2,1,0:T(8,128)S(1)} custom-call(bf16[16,64,512]{2,1,0:T(8,128)(2,1)S(1)} %all-to-all-done.2.in_ref.g_ref, bf16[16,64,512]{2,1,0:T(8,128)(2,1)S(1)} %all-to-all-done.in_ref.u_ref), custom_call_target="tpu_custom_call" | custom-call | flops 268435456 | bytes 2097152 | tf_op jit(solution)/shard_map/grad_second/pallas_call | solution.py:160
  162.2 0.2 copy.12
  162.4 0.9 reshape.62
  163.4 1.6 copy-done.3
  165.0 1.2 copy-done.10
  166.2 1.2 copy-done.15
  167.4 5.7 %finish.1 = (f32[1024,1024]{1,0:T(8,128)}, bf16[1024,512]{1,0:T(8,128)(2,1)}) custom-call(bf16[1024,1024]{1,0:T(8,128)(2,1)S(1)} %bitcast.41, bf16[1024,512]{1,0:T(8,128)(2,1)} %bitcast.6.refs_1_, bf16[1024,512]{1,0:T(8,128)(2,1)S(1)} %copy-done.10, bf16[1024,512]{1,0:T(8,128)(2,1)S(1)} %copy-done.15), custom_call_target="tpu_custom_call" | custom-call | flops 2147483648 | bytes 10485760 | tf_op jit(solution)/shard_map/finish/pallas_call | solution.py:315
  (40 shorter events, 1.1 us)
Async XLA Ops:
  0.6 1.6 copy-start.2
  2.2 1.2 copy-start.8
  5.2 1.0 copy-start.1
  6.2 7.5 %copy-start.17 = (bf16[64,16,16]{0,2,1:T(8,128)(2,1)S(1)}, bf16[64,16,16]{0,2,1:T(8,128)(2,1)}, u32[]{:S(2)}) copy-start(bf16[64,16,16]{0,2,1:T(8,128)(2,1)} %param.9) | copy-start | bytes 98308
  6.2 30.4 %all-to-all-start = ((bf16[16,64,512]{2,1,0:T(8,128)(2,1)}), bf16[16,64,512]{2,1,0:T(8,128)(2,1)S(1)}, u32[]{:S(2)}, u32[]{:S(2)}) async-start(bf16[16,64,512]{2,1,0:T(8,128)(2,1)} %bitcast.38), calls=%async_computation | async-start | bytes 2097152 | tf_op jit(solution)/shard_map/all_to_all | solution.py:395
  14.8 54.8 %copy-start.12 = (bf16[4,128,512]{2,1,0:T(8,128)(2,1)S(1)}, bf16[4,128,512]{2,1,0:T(8,128)(2,1)}, u32[]{:S(2)}) copy-start(bf16[4,128,512]{2,1,0:T(8,128)(2,1)} %refs_3_.1) | copy-start | bytes 1572868
  38.8 29.8 %all-to-all-start.1 = ((bf16[16,64,512]{2,1,0:T(8,128)(2,1)}), bf16[16,64,512]{2,1,0:T(8,128)(2,1)S(1)}, u32[]{:S(2)}, u32[]{:S(2)}) async-start(bf16[16,64,512]{2,1,0:T(8,128)(2,1)} %mix_second.1), calls=%async_computation.1 | async-start | bytes 2097152 | tf_op jit(solution)/shard_map/all_to_all | solution.py:395
  68.6 1.0 copy-start.6
  69.6 1.2 copy-start.7
  70.8 1.2 copy-start.9
  72.1 1.2 copy-start.11
  73.3 1.0 copy-start.13
  81.3 1.0 copy-start.14
  82.3 1.3 copy-start.4
  82.3 1.7 copy-start.5
  84.0 7.2 %collective-permute-start = (bf16[512,512]{1,0:T(8,128)(2,1)S(1)}, bf16[512,512]{1,0:T(8,128)(2,1)}, u32[]{:S(2)}, u32[]{:S(2)}) collective-permute-start(bf16[512,512]{1,0:T(8,128)(2,1)S(1)} %fusion), channel_id=1, source_target_pairs={{0,1},{1,0},{2,3},{3,2},{4,5},{5,4},{6,7},{7,6},{8,9},{9,8},{10,11... | collective-permute-start | bytes 1572872 | tf_op jit(solution)/shard_map/ppermute | solution.py:345
  84.6 45.7 %all-to-all-start.2 = ((bf16[16,64,512]{2,1,0:T(8,128)(2,1)}), bf16[16,64,512]{2,1,0:T(8,128)(2,1)S(1)}, u32[]{:S(2)}, u32[]{:S(2)}) async-start(bf16[16,64,512]{2,1,0:T(8,128)(2,1)} %bitcast.45), calls=%async_computation.2 | async-start | bytes 2097152 | tf_op jit(solution)/shard_map/all_to_all | solution.py:395
  92.7 1.0 copy-start.16
  93.7 14.8 %collective-permute-start.1 = (bf16[256,512]{1,0:T(8,128)(2,1)S(1)}, bf16[256,512]{1,0:T(8,128)(2,1)S(1)}, u32[]{:S(2)}, u32[]{:S(2)}) collective-permute-start(bf16[256,512]{1,0:T(8,128)(2,1)S(1)} %fusion.1), channel_id=1, source_target_pairs={{0,2},{1,3},{2,0},{3,1},{4,6},{5,7},{6,4},{7,5},{8,10},{9,11},{10,... | collective-permute-start | bytes 786440 | tf_op jit(solution)/shard_map/ppermute | solution.py:345
  109.7 7.6 %collective-permute-start.2 = (bf16[128,512]{1,0:T(8,128)(2,1)S(1)}, bf16[128,512]{1,0:T(8,128)(2,1)S(1)}, u32[]{:S(2)}, u32[]{:S(2)}) collective-permute-start(bf16[128,512]{1,0:T(8,128)(2,1)S(1)} %fusion.2), channel_id=1, source_target_pairs={{0,4},{1,5},{2,6},{3,7},{4,0},{5,1},{6,2},{7,3},{8,12},{9,13},{10,... | collective-permute-start | bytes 393224 | tf_op jit(solution)/shard_map/ppermute | solution.py:345
  117.4 5.2 %collective-permute-start.3 = (bf16[64,512]{1,0:T(8,128)(2,1)S(1)}, bf16[64,512]{1,0:T(8,128)(2,1)S(1)}, u32[]{:S(2)}, u32[]{:S(2)}) collective-permute-start(bf16[64,512]{1,0:T(8,128)(2,1)S(1)} %fusion.4), channel_id=1, source_target_pairs={{0,8},{1,9},{2,10},{3,11},{4,12},{5,13},{6,14},{7,15},{8,0},{9,1},... | collective-permute-start | bytes 196616 | tf_op jit(solution)/shard_map/ppermute | solution.py:345
  122.7 5.2 %collective-permute-start.4 = (bf16[64,512]{1,0:T(8,128)(2,1)S(1)}, bf16[64,512]{1,0:T(8,128)(2,1)S(1)}, u32[]{:S(2)}, u32[]{:S(2)}) collective-permute-start(bf16[64,512]{1,0:T(8,128)(2,1)S(1)} %fusion.3), channel_id=1, source_target_pairs={{0,8},{1,9},{2,10},{3,11},{4,12},{5,13},{6,14},{7,15},{8,0},{9,1},... | collective-permute-start | bytes 196616 | tf_op jit(solution)/shard_map/ppermute | solution.py:350
  127.9 9.0 %collective-permute-start.5 = (bf16[128,512]{1,0:T(8,128)(2,1)S(1)}, bf16[128,512]{1,0:T(8,128)(2,1)S(1)}, u32[]{:S(2)}, u32[]{:S(2)}) collective-permute-start(bf16[128,512]{1,0:T(8,128)(2,1)S(1)} %pad_maximum_fusion.3), channel_id=1, source_target_pairs={{0,4},{1,5},{2,6},{3,7},{4,0},{5,1},{6,2},{7,3},{8,12},{9,13},{10,... | collective-permute-start | bytes 393224 | tf_op jit(solution)/shard_map/ppermute | solution.py:350
  131.5 1.0 copy-start
  132.5 30.9 %all-to-all-start.3 = ((bf16[16,64,512]{2,1,0:T(8,128)(2,1)}), bf16[16,64,512]{2,1,0:T(8,128)(2,1)}, u32[]{:S(2)}, u32[]{:S(2)}) async-start(bf16[16,64,512]{2,1,0:T(8,128)(2,1)} %copy-done), calls=%async_computation.3 | async-start | bytes 2097152 | tf_op jit(solution)/shard_map/all_to_all | solution.py:395
  137.0 17.0 %collective-permute-start.6 = (bf16[256,512]{1,0:T(8,128)(2,1)S(1)}, bf16[256,512]{1,0:T(8,128)(2,1)S(1)}, u32[]{:S(2)}, u32[]{:S(2)}) collective-permute-start(bf16[256,512]{1,0:T(8,128)(2,1)S(1)} %pad_maximum_fusion.2), channel_id=1, source_target_pairs={{0,2},{1,3},{2,0},{3,1},{4,6},{5,7},{6,4},{7,5},{8,10},{9,11},{10,... | collective-permute-start | bytes 786440 | tf_op jit(solution)/shard_map/ppermute | solution.py:350
  154.9 2.1 %collective-permute-start.7 = (bf16[512,512]{1,0:T(8,128)(2,1)}, bf16[512,512]{1,0:T(8,128)(2,1)S(1)}, u32[]{:S(2)}, u32[]{:S(2)}) collective-permute-start(bf16[512,512]{1,0:T(8,128)(2,1)} %pad_maximum_fusion.1), channel_id=1, source_target_pairs={{0,1},{1,0},{2,3},{3,2},{4,5},{5,4},{6,7},{7,6},{8,9},{9,8},{10,11... | collective-permute-start | bytes 1572872 | tf_op jit(solution)/shard_map/ppermute | solution.py:350
  163.4 1.6 copy-start.3
  165.0 1.2 copy-start.10
  166.2 1.2 copy-start.15

commit v2 on v1

--- a/solution.py
+++ b/solution.py
@@ -7,8 +7,8 @@
 
 BF = jnp.bfloat16
 F32 = jnp.float32
-PIECES = 1
-VMEM_BYTES = 40 * 1024 * 1024
+PIECES = 2
+VMEM_BYTES = 60 * 1024 * 1024
 
 
 def sigmoid(z):

time: 174 us -> 195 us (1.12)
  Pallas kernels: 23.4 us -> 52.7 us
  local copies, waits for them, and re-layouts: 19.6 us -> 6.63 us
  starting transfers between devices: 38.4 us -> 47.4 us
  waiting for transfers between devices: 86.8 us -> 81.7 us
    unnamed x36 -> x18, local copies, waits for them, and re-layouts: 18 us -> 1.61 us
    all_to_all x4 -> x8, starting transfers between devices: 25.3 us -> 38.2 us  [exchange(): got = lax.all_to_all(cut, 'seq', split_axis=0, concat_axis=0, tiled=True)]
    pallas_call x1 -> x2, Pallas kernels: 7.01 us -> 13.7 us  [middle(): pl.pallas_call(body, grid=(plan.rows // step,), in_specs=in_specs, out_sp...]
    pallas_call x2 -> x4, Pallas kernels: 3.35 us -> 9.01 us  [mix_second(): pl.pallas_call(body, grid=(groups,), in_specs=[pl.BlockSpec((1, wide, wid...]
    all_to_all x4 -> x8, waiting for transfers between devices: 44.8 us -> 39.5 us  [exchange(): got = lax.all_to_all(cut, 'seq', split_axis=0, concat_axis=0, tiled=True)]
    pallas_call x1 -> x2, Pallas kernels: 5.71 us -> 10.8 us  [finish(): pl.pallas_call(body, grid=(plan.block // step,), in_specs=in_specs, out_s...]
    ppermute x4, starting transfers between devices: 7.03 us -> 2.2 us  [sum_over(): got = lax.ppermute(total, 'seq', [(i, i ^ step) for i in range(count)])]
    pallas_call x1 -> x2, Pallas kernels: 1.76 us -> 6.03 us  [mix_first(): pl.pallas_call(body, grid=(plan.rows // step,), in_specs=[plan.spec(step,...]
  transfers between devices with their start and end apart: 12 -> 16, of which waited for: 8 -> 8; matrix products, arithmetic and copies ran while one was open for 3% -> 4% of each run, Pallas kernels for 4% -> 19%
where the time goes in v2:
time: 195 us; the launch traced here: 193 us
  waiting for transfers between devices  81.7 us (42%)
  Pallas kernels  52.7 us (27%)
  starting transfers between devices  47.4 us (24%)
  local copies, waits for them, and re-layouts  6.63 us (3%)
  other arithmetic  3.71 us (2%)
    all_to_all x8, waiting for transfers between devices, exchange(): got = lax.all_to_all(cut, 'seq', split_axis=0, concat_axis=0, tiled=True)  39.5 us
    all_to_all x8, starting transfers between devices, exchange(): got = lax.all_to_all(cut, 'seq', split_axis=0, concat_axis=0, tiled=True)  38.2 us
    ppermute x4, waiting for transfers between devices, sum_over(): got = lax.ppermute(send, 'seq', [(i, i ^ step) for i in range(count)])  25.4 us
    ppermute x4, waiting for transfers between devices, sum_over(): got = lax.ppermute(total, 'seq', [(i, i ^ step) for i in range(count)])  16.8 us
    pallas_call x2, Pallas kernels, middle(): pl.pallas_call(body, grid=(plan.rows // step,), in_specs=in_specs, out_sp...  13.7 us
    pallas_call x2, Pallas kernels, finish(): pl.pallas_call(body, grid=(plan.block // step,), in_specs=in_specs, out_s...  10.8 us
    pallas_call x4, Pallas kernels, mix_second(): pl.pallas_call(body, grid=(groups,), in_specs=[pl.BlockSpec((1, wide, wid...  9.01 us
    ppermute x4, starting transfers between devices, sum_over(): got = lax.ppermute(send, 'seq', [(i, i ^ step) for i in range(count)])  6.94 us
  transfers between devices with their start and end apart: 16, of which 8 were waited for; matrix products, arithmetic and copies ran while one was open for 4% of the time, Pallas kernels for 19%

profile of v2, /device:TPU:0, one launch (start us, length us, event | category | flops | bytes accessed | tf_op | source)
XLA Modules:
  0.0 193.1 jit_solution(13888369291604931282)
XLA Ops:
  0.6 3.0 %mix_first.3 = bf16[512,512]{1,0:T(8,128)(2,1)} custom-call(bf16[16,2,32,1024]{3,2,1,0:T(8,128)(2,1)} %bitcast.52, bf16[1024,512]{1,0:T(8,128)(2,1)} %refs_2_.3), custom_call_target="tpu_custom_call" | custom-call | flops 536870912 | bytes 3145728 | tf_op jit(solution)/shard_map/mix_first/pallas_call | solution.py:69
  3.6 7.4 %all-to-all-start.2 = ((bf16[16,32,512]{2,1,0:T(8,128)(2,1)}), bf16[16,32,512]{2,1,0:T(8,128)(2,1)S(1)}, u32[]{:S(2)}, u32[]{:S(2)}) async-start(bf16[16,32,512]{2,1,0:T(8,128)(2,1)} %bitcast.62), calls=%async_computation.2 | async-start | bytes 1048576 | tf_op jit(solution)/shard_map/all_to_all | solution.py:395
  11.0 3.0 %mix_first.2 = bf16[512,512]{1,0:T(8,128)(2,1)} custom-call(bf16[16,2,32,1024]{3,2,1,0:T(8,128)(2,1)} %bitcast.53, bf16[1024,512]{1,0:T(8,128)(2,1)} %refs_2_.3), custom_call_target="tpu_custom_call" | custom-call | flops 536870912 | bytes 3145728 | tf_op jit(solution)/shard_map/mix_first/pallas_call | solution.py:69
  14.0 11.4 %all-to-all-done.2.in_ref.u_ref = bf16[16,32,512]{2,1,0:T(8,128)(2,1)S(1)} async-done(((bf16[16,32,512]{2,1,0:T(8,128)(2,1)}), bf16[16,32,512]{2,1,0:T(8,128)(2,1)S(1)}, u32[]{:S(2)}, u32[]{:S(2)}) %all-to-all-start.2) | async-done | bytes 524320 | tf_op jit(solution)/shard_map/all_to_all | solution.py:395
  25.5 4.1 %all-to-all-start = ((bf16[16,32,512]{2,1,0:T(8,128)(2,1)}), bf16[16,32,512]{2,1,0:T(8,128)(2,1)S(1)}, u32[]{:S(2)}, u32[]{:S(2)}) async-start(bf16[16,32,512]{2,1,0:T(8,128)(2,1)} %bitcast.61), calls=%async_computation | async-start | bytes 1048576 | tf_op jit(solution)/shard_map/all_to_all | solution.py:395
  29.6 0.2 reshape.85
  29.7 0.9 copy.12
  30.6 3.3 %spread_factor.1.m_ref = bf16[4,256,256]{2,1,0:T(8,128)(2,1)} custom-call(bf16[4,256,16]{2,1,0:T(8,128)(2,1)} %bitcast.71), custom_call_target="tpu_custom_call" | custom-call | flops 8388608 | bytes 524288 | tf_op jit(solution)/shard_map/spread_factor/pallas_call | solution.py:102
  34.0 2.2 %mix_second.3 = bf16[16,32,512]{2,1,0:T(8,128)(2,1)} custom-call(bf16[4,256,256]{2,1,0:T(8,128)(2,1)} %spread_factor.1.m_ref, bf16[16,32,512]{2,1,0:T(8,128)(2,1)} %copy-done), custom_call_target="tpu_custom_call" | custom-call | flops 134217728 | bytes 1310720 | tf_op jit(solution)/shard_map/mix_second/pallas_call | solution.py:124
  36.2 7.9 %all-to-all-done.in_ref.u_ref = bf16[16,32,512]{2,1,0:T(8,128)(2,1)S(1)} async-done(((bf16[16,32,512]{2,1,0:T(8,128)(2,1)}), bf16[16,32,512]{2,1,0:T(8,128)(2,1)S(1)}, u32[]{:S(2)}, u32[]{:S(2)}) %all-to-all-start) | async-done | bytes 524320 | tf_op jit(solution)/shard_map/all_to_all | solution.py:395
  44.0 4.1 %all-to-all-start.3 = ((bf16[16,32,512]{2,1,0:T(8,128)(2,1)}), bf16[16,32,512]{2,1,0:T(8,128)(2,1)S(1)}, u32[]{:S(2)}, u32[]{:S(2)}) async-start(bf16[16,32,512]{2,1,0:T(8,128)(2,1)} %mix_second.3), calls=%async_computation.3 | async-start | bytes 1048576 | tf_op jit(solution)/shard_map/all_to_all | solution.py:395
  48.2 2.2 %mix_second.2 = bf16[16,32,512]{2,1,0:T(8,128)(2,1)} custom-call(bf16[4,256,256]{2,1,0:T(8,128)(2,1)} %spread_factor.1.m_ref, bf16[16,32,512]{2,1,0:T(8,128)(2,1)} %copy-done.1), custom_call_target="tpu_custom_call" | custom-call | flops 134217728 | bytes 1310720 | tf_op jit(solution)/shard_map/mix_second/pallas_call | solution.py:124
  50.4 12.2 %all-to-all-done.3 = bf16[16,32,512]{2,1,0:T(8,128)(2,1)S(1)} async-done(((bf16[16,32,512]{2,1,0:T(8,128)(2,1)}), bf16[16,32,512]{2,1,0:T(8,128)(2,1)S(1)}, u32[]{:S(2)}, u32[]{:S(2)}) %all-to-all-start.3) | async-done | bytes 524320 | tf_op jit(solution)/shard_map/all_to_all | solution.py:395
  62.6 4.1 %all-to-all-start.1 = ((bf16[16,32,512]{2,1,0:T(8,128)(2,1)}), bf16[16,32,512]{2,1,0:T(8,128)(2,1)S(1)}, u32[]{:S(2)}, u32[]{:S(2)}) async-start(bf16[16,32,512]{2,1,0:T(8,128)(2,1)} %mix_second.2), calls=%async_computation.1 | async-start | bytes 1048576 | tf_op jit(solution)/shard_map/all_to_all | solution.py:395
  66.8 6.5 %middle.2 = (bf16[512,512]{1,0:T(8,128)(2,1)}, bf16[512,512]{1,0:T(8,128)(2,1)}, f32[8,128,512]{2,1,0:T(8,128)}) custom-call(bf16[16,2,32,512]{3,2,1,0:T(8,128)(2,1)} %bitcast.56, bf16[16,2,32,512]{3,2,1,0:T(8,128)(2,1)} %bitcast.72, bf16[512,512]{1,0:T(8,128)(2,1)} %bitcast.77, bf16[4,128,512]{2,1,0:T(8,128)(2,1)} %refs_3_.3, bf16[4,512,128]{2,1,0:T(8,128)(2,1)} %refs_4_.3), custom_call_target="tpu_custom_call" | custom-call | flops 1342177280 | bytes 4718592 | tf_op jit(solution)/shard_map/middle/pallas_call | solution.py:237
  73.2 7.9 %all-to-all-done.1 = bf16[16,32,512]{2,1,0:T(8,128)(2,1)S(1)} async-done(((bf16[16,32,512]{2,1,0:T(8,128)(2,1)}), bf16[16,32,512]{2,1,0:T(8,128)(2,1)S(1)}, u32[]{:S(2)}, u32[]{:S(2)}) %all-to-all-start.1) | async-done | bytes 524320 | tf_op jit(solution)/shard_map/all_to_all | solution.py:395
  81.2 0.8 copy-done.4
  82.0 7.2 %middle.3 = (bf16[512,512]{1,0:T(8,128)(2,1)}, bf16[512,512]{1,0:T(8,128)(2,1)}, f32[8,128,512]{2,1,0:T(8,128)}) custom-call(bf16[16,2,32,512]{3,2,1,0:T(8,128)(2,1)} %bitcast.57, bf16[16,2,32,512]{3,2,1,0:T(8,128)(2,1)} %bitcast.73, bf16[512,512]{1,0:T(8,128)(2,1)} %bitcast.63, bf16[4,128,512]{2,1,0:T(8,128)(2,1)} %refs_3_.3, bf16[4,512,128]{2,1,0:T(8,128)(2,1)} %refs_4_.3, ...), custom_call_target="tpu_custom_call" | custom-call | flops 1342177280 | bytes 4718592 | tf_op jit(solution)/shard_map/middle/pallas_call | solution.py:237
  89.2 1.3 fusion
  90.6 4.3 %all-to-all-start.6 = ((bf16[16,32,512]{2,1,0:T(8,128)(2,1)}), bf16[16,32,512]{2,1,0:T(8,128)(2,1)S(1)}, u32[]{:S(2)}, u32[]{:S(2)}) async-start(bf16[16,32,512]{2,1,0:T(8,128)(2,1)} %bitcast.11), calls=%async_computation.6 | async-start | bytes 1048576 | tf_op jit(solution)/shard_map/all_to_all | solution.py:395
  95.0 1.4 bitcast_add_fusion
  96.4 2.0 %collective-permute-start.1 = (bf16[256,512]{1,0:T(8,128)(2,1)S(1)}, bf16[256,512]{1,0:T(8,128)(2,1)S(1)}, u32[]{:S(2)}, u32[]{:S(2)}) collective-permute-start(bf16[256,512]{1,0:T(8,128)(2,1)S(1)} %fusion.1), channel_id=1, source_target_pairs={{0,2},{1,3},{2,0},{3,1},{4,6},{5,7},{6,4},{7,5},{8,10},{9,11},{10,... | collective-permute-start | bytes 786440 | tf_op jit(solution)/shard_map/ppermute | solution.py:345
  98.4 10.3 %collective-permute-done.1 = bf16[256,512]{1,0:T(8,128)(2,1)S(1)} collective-permute-done((bf16[256,512]{1,0:T(8,128)(2,1)S(1)}, bf16[256,512]{1,0:T(8,128)(2,1)S(1)}, u32[]{:S(2)}, u32[]{:S(2)}) %collective-permute-start.1) | collective-permute-done | bytes 262176 | tf_op jit(solution)/shard_map/ppermute | solution.py:345
  108.8 2.0 %collective-permute-start.2 = (bf16[128,512]{1,0:T(8,128)(2,1)S(1)}, bf16[128,512]{1,0:T(8,128)(2,1)S(1)}, u32[]{:S(2)}, u32[]{:S(2)}) collective-permute-start(bf16[128,512]{1,0:T(8,128)(2,1)S(1)} %fusion.2), channel_id=1, source_target_pairs={{0,4},{1,5},{2,6},{3,7},{4,0},{5,1},{6,2},{7,3},{8,12},{9,13},{10,... | collective-permute-start | bytes 393224 | tf_op jit(solution)/shard_map/ppermute | solution.py:345
  110.8 4.1 %all-to-all-start.4 = ((bf16[16,32,512]{2,1,0:T(8,128)(2,1)}), bf16[16,32,512]{2,1,0:T(8,128)(2,1)S(1)}, u32[]{:S(2)}, u32[]{:S(2)}) async-start(bf16[16,32,512]{2,1,0:T(8,128)(2,1)} %bitcast.9), calls=%async_computation.4 | async-start | bytes 1048576 | tf_op jit(solution)/shard_map/all_to_all | solution.py:395
  115.0 2.9 %collective-permute-start.3 = (bf16[64,512]{1,0:T(8,128)(2,1)S(1)}, bf16[64,512]{1,0:T(8,128)(2,1)S(1)}, u32[]{:S(2)}, u32[]{:S(2)}) collective-permute-start(bf16[64,512]{1,0:T(8,128)(2,1)S(1)} %fusion.4), channel_id=1, source_target_pairs={{0,8},{1,9},{2,10},{3,11},{4,12},{5,13},{6,14},{7,15},{8,0},{9,1},... | collective-permute-start | bytes 196616 | tf_op jit(solution)/shard_map/ppermute | solution.py:345
  117.9 15.1 %collective-permute-done.3 = bf16[64,512]{1,0:T(8,128)(2,1)S(1)} collective-permute-done((bf16[64,512]{1,0:T(8,128)(2,1)S(1)}, bf16[64,512]{1,0:T(8,128)(2,1)S(1)}, u32[]{:S(2)}, u32[]{:S(2)}) %collective-permute-start.3) | collective-permute-done | bytes 65568 | tf_op jit(solution)/shard_map/ppermute | solution.py:345
  133.1 5.1 %collective-permute-done.4 = bf16[64,512]{1,0:T(8,128)(2,1)S(1)} collective-permute-done((bf16[64,512]{1,0:T(8,128)(2,1)S(1)}, bf16[64,512]{1,0:T(8,128)(2,1)S(1)}, u32[]{:S(2)}, u32[]{:S(2)}) %collective-permute-start.4) | collective-permute-done | bytes 65568 | tf_op jit(solution)/shard_map/ppermute | solution.py:350
  138.4 2.3 %mix_second_back.3 = bf16[16,32,512]{2,1,0:T(8,128)(2,1)} custom-call(bf16[4,256,256]{2,1,0:T(8,128)(2,1)} %spread_factor.1.m_ref, bf16[16,32,512]{2,1,0:T(8,128)(2,1)} %copy-done.2), custom_call_target="tpu_custom_call" | custom-call | flops 134217728 | bytes 1310720 | tf_op jit(solution)/shard_map/mix_second_back/pallas_call | solution.py:124
  140.6 4.8 %all-to-all-start.7 = ((bf16[16,32,512]{2,1,0:T(8,128)(2,1)}), bf16[16,32,512]{2,1,0:T(8,128)(2,1)S(1)}, u32[]{:S(2)}, u32[]{:S(2)}) async-start(bf16[16,32,512]{2,1,0:T(8,128)(2,1)} %mix_second_back.3), calls=%async_computation.7 | async-start | bytes 1048576 | tf_op jit(solution)/shard_map/all_to_all | solution.py:395
  145.5 2.0 %collective-permute-start.6 = (bf16[256,512]{1,0:T(8,128)(2,1)S(1)}, bf16[256,512]{1,0:T(8,128)(2,1)S(1)}, u32[]{:S(2)}, u32[]{:S(2)}) collective-permute-start(bf16[256,512]{1,0:T(8,128)(2,1)S(1)} %pad_maximum_fusion.2), channel_id=1, source_target_pairs={{0,2},{1,3},{2,0},{3,1},{4,6},{5,7},{6,4},{7,5},{8,10},{9,11},{10,... | collective-permute-start | bytes 786440 | tf_op jit(solution)/shard_map/ppermute | solution.py:350
  147.5 11.7 %collective-permute-done.6 = bf16[256,512]{1,0:T(8,128)(2,1)S(1)} collective-permute-done((bf16[256,512]{1,0:T(8,128)(2,1)S(1)}, bf16[256,512]{1,0:T(8,128)(2,1)S(1)}, u32[]{:S(2)}, u32[]{:S(2)}) %collective-permute-start.6) | collective-permute-done | bytes 262176 | tf_op jit(solution)/shard_map/ppermute | solution.py:350
  159.2 0.1 broadcast_select_fusion.3
  159.4 2.3 %mix_second_back.2 = bf16[16,32,512]{2,1,0:T(8,128)(2,1)} custom-call(bf16[4,256,256]{2,1,0:T(8,128)(2,1)} %spread_factor.1.m_ref, bf16[16,32,512]{2,1,0:T(8,128)(2,1)} %copy-done.3), custom_call_target="tpu_custom_call" | custom-call | flops 134217728 | bytes 1310720 | tf_op jit(solution)/shard_map/mix_second_back/pallas_call | solution.py:124
  161.7 5.4 %all-to-all-start.5 = ((bf16[16,32,512]{2,1,0:T(8,128)(2,1)}), bf16[16,32,512]{2,1,0:T(8,128)(2,1)S(1)}, u32[]{:S(2)}, u32[]{:S(2)}) async-start(bf16[16,32,512]{2,1,0:T(8,128)(2,1)} %mix_second_back.2), calls=%async_computation.5 | async-start | bytes 1048576 | tf_op jit(solution)/shard_map/all_to_all | solution.py:395
  167.1 3.1 %grad_second.2 = f32[2,256,16]{2,1,0:T(8,128)} custom-call(bf16[16,32,512]{2,1,0:T(8,128)(2,1)} %copy-done.2, bf16[16,32,512]{2,1,0:T(8,128)(2,1)} %copy-done), custom_call_target="tpu_custom_call" | custom-call | flops 134217728 | bytes 1048576 | tf_op jit(solution)/shard_map/grad_second/pallas_call | solution.py:160
  170.2 1.1 copy.13
  171.3 0.2 reshape.102
  171.5 3.1 %grad_second.3 = f32[2,256,16]{2,1,0:T(8,128)} custom-call(bf16[16,32,512]{2,1,0:T(8,128)(2,1)} %copy-done.3, bf16[16,32,512]{2,1,0:T(8,128)(2,1)} %copy-done.1), custom_call_target="tpu_custom_call" | custom-call | flops 134217728 | bytes 1048576 | tf_op jit(solution)/shard_map/grad_second/pallas_call | solution.py:160
  174.5 1.1 copy.14
  175.7 0.2 reshape.104
  175.8 0.2 broadcast_select_fusion.1
  176.0 1.0 pad_maximum_fusion.up_in.down_in
  177.1 0.8 pad_maximum_fusion.3
  177.8 3.7 %write_weights.1 = (f32[4,128,512]{2,1,0:T(8,128)}, f32[4,512,128]{2,1,0:T(8,128)}) custom-call(bf16[1024,512]{1,0:T(8,128)(2,1)} %pad_maximum_fusion.up_in.down_in, bf16[1024,512]{1,0:T(8,128)(2,1)} %pad_maximum_fusion.up_in.down_in), custom_call_target="tpu_custom_call" | custom-call | flops 262144 | bytes 3145728 | tf_op jit(solution)/shard_map/write_weights/pallas_call | solution.py:364
  181.5 5.2 %finish.2 = (f32[16,2,32,1024]{3,2,1,0:T(8,128)}, f32[1024,512]{1,0:T(8,128)}) custom-call(bf16[16,2,32,1024]{3,2,1,0:T(8,128)(2,1)} %bitcast.54, bf16[512,512]{1,0:T(8,128)(2,1)} %bitcast.76, bf16[1024,512]{1,0:T(8,128)(2,1)} %refs_2_.3), custom_call_target="tpu_custom_call" | custom-call | flops 1073741824 | bytes 7340032 | tf_op jit(solution)/shard_map/finish/pallas_call | solution.py:315
  186.7 0.8 copy-done.5
  187.5 5.6 %finish.3 = (f32[16,2,32,1024]{3,2,1,0:T(8,128)}, bf16[16,2,32,512]{3,2,1,0:T(8,128)(2,1)}) custom-call(bf16[16,2,32,1024]{3,2,1,0:T(8,128)(2,1)} %bitcast.55, bf16[512,512]{1,0:T(8,128)(2,1)} %bitcast.64, bf16[1024,512]{1,0:T(8,128)(2,1)} %refs_2_.3, f32[16,2,32,1024]{3,2,1,0:T(8,128)} %get-tuple-element.20.refs_3_, ...), custom_call_target="tpu_custom_call", output_to_operand_aliasing={{0}: (3, {})} | custom-call | flops 1073741824 | bytes 7340032 | tf_op jit(solution)/shard_map/finish/pallas_call | solution.py:315
  (39 shorter events, 0.7 us)
Async XLA Ops:
  3.6 21.8 %all-to-all-start.2 = ((bf16[16,32,512]{2,1,0:T(8,128)(2,1)}), bf16[16,32,512]{2,1,0:T(8,128)(2,1)S(1)}, u32[]{:S(2)}, u32[]{:S(2)}) async-start(bf16[16,32,512]{2,1,0:T(8,128)(2,1)} %bitcast.62), calls=%async_computation.2 | async-start | bytes 1048576 | tf_op jit(solution)/shard_map/all_to_all | solution.py:395
  11.0 18.6 %copy-start.8 = (bf16[64,16,16]{0,2,1:T(8,128)(2,1)S(1)}, bf16[64,16,16]{0,2,1:T(8,128)(2,1)}, u32[]{:S(2)}) copy-start(bf16[64,16,16]{0,2,1:T(8,128)(2,1)} %param.9) | copy-start | bytes 98308
  25.5 8.5 %copy-start = (bf16[16,32,512]{2,1,0:T(8,128)(2,1)}, bf16[16,32,512]{2,1,0:T(8,128)(2,1)S(1)}, u32[]{:S(2)}) copy-start(bf16[16,32,512]{2,1,0:T(8,128)(2,1)S(1)} %all-to-all-done.2.in_ref.u_ref) | copy-start | bytes 1572868
  25.5 18.6 %all-to-all-start = ((bf16[16,32,512]{2,1,0:T(8,128)(2,1)}), bf16[16,32,512]{2,1,0:T(8,128)(2,1)S(1)}, u32[]{:S(2)}, u32[]{:S(2)}) async-start(bf16[16,32,512]{2,1,0:T(8,128)(2,1)} %bitcast.61), calls=%async_computation | async-start | bytes 1048576 | tf_op jit(solution)/shard_map/all_to_all | solution.py:395
  44.0 4.1 %copy-start.1 = (bf16[16,32,512]{2,1,0:T(8,128)(2,1)}, bf16[16,32,512]{2,1,0:T(8,128)(2,1)S(1)}, u32[]{:S(2)}) copy-start(bf16[16,32,512]{2,1,0:T(8,128)(2,1)S(1)} %all-to-all-done.in_ref.u_ref) | copy-start | bytes 1572868
  44.0 18.6 %all-to-all-start.3 = ((bf16[16,32,512]{2,1,0:T(8,128)(2,1)}), bf16[16,32,512]{2,1,0:T(8,128)(2,1)S(1)}, u32[]{:S(2)}, u32[]{:S(2)}) async-start(bf16[16,32,512]{2,1,0:T(8,128)(2,1)} %mix_second.3), calls=%async_computation.3 | async-start | bytes 1048576 | tf_op jit(solution)/shard_map/all_to_all | solution.py:395
  62.6 4.1 %copy-start.7 = (bf16[16,32,512]{2,1,0:T(8,128)(2,1)}, bf16[16,32,512]{2,1,0:T(8,128)(2,1)S(1)}, u32[]{:S(2)}) copy-start(bf16[16,32,512]{2,1,0:T(8,128)(2,1)S(1)} %all-to-all-done.3) | copy-start | bytes 1572868
  62.6 18.6 %all-to-all-start.1 = ((bf16[16,32,512]{2,1,0:T(8,128)(2,1)}), bf16[16,32,512]{2,1,0:T(8,128)(2,1)S(1)}, u32[]{:S(2)}, u32[]{:S(2)}) async-start(bf16[16,32,512]{2,1,0:T(8,128)(2,1)} %mix_second.2), calls=%async_computation.1 | async-start | bytes 1048576 | tf_op jit(solution)/shard_map/all_to_all | solution.py:395
  81.2 0.8 copy-start.4
  90.5 4.5 %collective-permute-start = (bf16[512,512]{1,0:T(8,128)(2,1)S(1)}, bf16[512,512]{1,0:T(8,128)(2,1)S(1)}, u32[]{:S(2)}, u32[]{:S(2)}) collective-permute-start(bf16[512,512]{1,0:T(8,128)(2,1)S(1)} %fusion), channel_id=1, source_target_pairs={{0,1},{1,0},{2,3},{3,2},{4,5},{5,4},{6,7},{7,6},{8,9},{9,8},{10,11... | collective-permute-start | bytes 1572872 | tf_op jit(solution)/shard_map/ppermute | solution.py:345
  90.6 20.2 %all-to-all-start.6 = ((bf16[16,32,512]{2,1,0:T(8,128)(2,1)}), bf16[16,32,512]{2,1,0:T(8,128)(2,1)S(1)}, u32[]{:S(2)}, u32[]{:S(2)}) async-start(bf16[16,32,512]{2,1,0:T(8,128)(2,1)} %bitcast.11), calls=%async_computation.6 | async-start | bytes 1048576 | tf_op jit(solution)/shard_map/all_to_all | solution.py:395
  96.4 12.3 %collective-permute-start.1 = (bf16[256,512]{1,0:T(8,128)(2,1)S(1)}, bf16[256,512]{1,0:T(8,128)(2,1)S(1)}, u32[]{:S(2)}, u32[]{:S(2)}) collective-permute-start(bf16[256,512]{1,0:T(8,128)(2,1)S(1)} %fusion.1), channel_id=1, source_target_pairs={{0,2},{1,3},{2,0},{3,1},{4,6},{5,7},{6,4},{7,5},{8,10},{9,11},{10,... | collective-permute-start | bytes 786440 | tf_op jit(solution)/shard_map/ppermute | solution.py:345
  108.8 6.1 %collective-permute-start.2 = (bf16[128,512]{1,0:T(8,128)(2,1)S(1)}, bf16[128,512]{1,0:T(8,128)(2,1)S(1)}, u32[]{:S(2)}, u32[]{:S(2)}) collective-permute-start(bf16[128,512]{1,0:T(8,128)(2,1)S(1)} %fusion.2), channel_id=1, source_target_pairs={{0,4},{1,5},{2,6},{3,7},{4,0},{5,1},{6,2},{7,3},{8,12},{9,13},{10,... | collective-permute-start | bytes 393224 | tf_op jit(solution)/shard_map/ppermute | solution.py:345
  110.8 27.6 %copy-start.2 = (bf16[16,32,512]{2,1,0:T(8,128)(2,1)}, bf16[16,32,512]{2,1,0:T(8,128)(2,1)S(1)}, u32[]{:S(2)}) copy-start(bf16[16,32,512]{2,1,0:T(8,128)(2,1)S(1)} %all-to-all-done.6.in_ref.g_ref) | copy-start | bytes 1572868
  110.8 29.8 %all-to-all-start.4 = ((bf16[16,32,512]{2,1,0:T(8,128)(2,1)}), bf16[16,32,512]{2,1,0:T(8,128)(2,1)S(1)}, u32[]{:S(2)}, u32[]{:S(2)}) async-start(bf16[16,32,512]{2,1,0:T(8,128)(2,1)} %bitcast.9), calls=%async_computation.4 | async-start | bytes 1048576 | tf_op jit(solution)/shard_map/all_to_all | solution.py:395
  115.0 18.0 %collective-permute-start.3 = (bf16[64,512]{1,0:T(8,128)(2,1)S(1)}, bf16[64,512]{1,0:T(8,128)(2,1)S(1)}, u32[]{:S(2)}, u32[]{:S(2)}) collective-permute-start(bf16[64,512]{1,0:T(8,128)(2,1)S(1)} %fusion.4), channel_id=1, source_target_pairs={{0,8},{1,9},{2,10},{3,11},{4,12},{5,13},{6,14},{7,15},{8,0},{9,1},... | collective-permute-start | bytes 196616 | tf_op jit(solution)/shard_map/ppermute | solution.py:345
  133.0 5.2 %collective-permute-start.4 = (bf16[64,512]{1,0:T(8,128)(2,1)S(1)}, bf16[64,512]{1,0:T(8,128)(2,1)S(1)}, u32[]{:S(2)}, u32[]{:S(2)}) collective-permute-start(bf16[64,512]{1,0:T(8,128)(2,1)S(1)} %fusion.3), channel_id=1, source_target_pairs={{0,8},{1,9},{2,10},{3,11},{4,12},{5,13},{6,14},{7,15},{8,0},{9,1},... | collective-permute-start | bytes 196616 | tf_op jit(solution)/shard_map/ppermute | solution.py:350
  138.3 7.1 %collective-permute-start.5 = (bf16[128,512]{1,0:T(8,128)(2,1)S(1)}, bf16[128,512]{1,0:T(8,128)(2,1)S(1)}, u32[]{:S(2)}, u32[]{:S(2)}) collective-permute-start(bf16[128,512]{1,0:T(8,128)(2,1)S(1)} %pad_maximum_fusion.4), channel_id=1, source_target_pairs={{0,4},{1,5},{2,6},{3,7},{4,0},{5,1},{6,2},{7,3},{8,12},{9,13},{10,... | collective-permute-start | bytes 393224 | tf_op jit(solution)/shard_map/ppermute | solution.py:350
  140.6 18.7 %copy-start.3 = (bf16[16,32,512]{2,1,0:T(8,128)(2,1)}, bf16[16,32,512]{2,1,0:T(8,128)(2,1)S(1)}, u32[]{:S(2)}) copy-start(bf16[16,32,512]{2,1,0:T(8,128)(2,1)S(1)} %all-to-all-done.4.in_ref.g_ref) | copy-start | bytes 1572868
  140.6 21.1 %all-to-all-start.7 = ((bf16[16,32,512]{2,1,0:T(8,128)(2,1)}), bf16[16,32,512]{2,1,0:T(8,128)(2,1)S(1)}, u32[]{:S(2)}, u32[]{:S(2)}) async-start(bf16[16,32,512]{2,1,0:T(8,128)(2,1)} %mix_second_back.3), calls=%async_computation.7 | async-start | bytes 1048576 | tf_op jit(solution)/shard_map/all_to_all | solution.py:395
  145.5 13.7 %collective-permute-start.6 = (bf16[256,512]{1,0:T(8,128)(2,1)S(1)}, bf16[256,512]{1,0:T(8,128)(2,1)S(1)}, u32[]{:S(2)}, u32[]{:S(2)}) collective-permute-start(bf16[256,512]{1,0:T(8,128)(2,1)S(1)} %pad_maximum_fusion.2), channel_id=1, source_target_pairs={{0,2},{1,3},{2,0},{3,1},{4,6},{5,7},{6,4},{7,5},{8,10},{9,11},{10,... | collective-permute-start | bytes 786440 | tf_op jit(solution)/shard_map/ppermute | solution.py:350
  159.3 16.5 %collective-permute-start.7 = (bf16[512,512]{1,0:T(8,128)(2,1)S(1)}, bf16[512,512]{1,0:T(8,128)(2,1)S(1)}, u32[]{:S(2)}, u32[]{:S(2)}) collective-permute-start(bf16[512,512]{1,0:T(8,128)(2,1)S(1)} %pad_maximum_fusion.1), channel_id=1, source_target_pairs={{0,1},{1,0},{2,3},{3,2},{4,5},{5,4},{6,7},{7,6},{8,9},{9,8},{10,11... | collective-permute-start | bytes 1572872 | tf_op jit(solution)/shard_map/ppermute | solution.py:350
  161.7 12.8 %copy-start.6 = (bf16[16,32,512]{2,1,0:T(8,128)(2,1)}, bf16[16,32,512]{2,1,0:T(8,128)(2,1)S(1)}, u32[]{:S(2)}) copy-start(bf16[16,32,512]{2,1,0:T(8,128)(2,1)S(1)} %all-to-all-done.7) | copy-start | bytes 1572868
  161.7 25.0 %all-to-all-start.5 = ((bf16[16,32,512]{2,1,0:T(8,128)(2,1)}), bf16[16,32,512]{2,1,0:T(8,128)(2,1)S(1)}, u32[]{:S(2)}, u32[]{:S(2)}) async-start(bf16[16,32,512]{2,1,0:T(8,128)(2,1)} %mix_second_back.2), calls=%async_computation.5 | async-start | bytes 1048576 | tf_op jit(solution)/shard_map/all_to_all | solution.py:395
  186.7 0.8 copy-start.5

commit v3 on v2

v3 whole, which is shorter than its diff:
```python
import jax
import jax.numpy as jnp
from jax import lax
from jax.experimental import pallas as pl
from jax.experimental.pallas import tpu as pltpu
from jax.sharding import PartitionSpec as P

BF = jnp.bfloat16
F32 = jnp.float32
PIECES = 1
VMEM_BYTES = 60 * 1024 * 1024
SCALAR = pl.BlockSpec(memory_space=pltpu.SMEM)


def sigmoid(z):
    return 0.5 + 0.5 * jnp.tanh(0.5 * z)


def dot(a, b, ca, cb, **kw):
    return lax.dot_general(a, b, (((ca,), (cb,)), ((), ())), preferred_element_type=F32, **kw)


def rows_of(ref):
    value = ref[...]
    return value.reshape(-1, value.shape[-1])


def params(steps=1):
    return pltpu.CompilerParams(
        dimension_semantics=("arbitrary",) * steps, vmem_limit_bytes=VMEM_BYTES
    )


def cost(flops, moved, trans=0):
    return pl.CostEstimate(flops=int(flops), bytes_accessed=int(moved), transcendentals=int(trans))


class Plan:
    def __init__(self, count, block, channels):
        self.count = count
        self.block = block
        self.channels = channels
        self.here = block // count
        self.pieces = PIECES if self.here % (16 * PIECES) == 0 else 1
        self.part = self.here // self.pieces
        self.rows = block // self.pieces
        self.grouped = self.part % 16 == 0
        self.direct = self.grouped and count <= 16
        self.arrays = count if self.direct else 1
        self.block_shape = (self.part, channels) if self.direct else (count, self.part, channels)

    def block_specs(self):
        return [
            pl.BlockSpec(self.block_shape, lambda i: (0,) * len(self.block_shape))
        ] * self.arrays

    def block_shapes(self):
        return [jax.ShapeDtypeStruct(self.block_shape, BF)] * self.arrays

    def whole(self):
        return pltpu.VMEM((self.count, self.part, self.channels), BF)

    def view(self, array):
        if self.pieces == 1:
            return array
        return array.reshape(self.count, self.pieces, self.part, array.shape[-1])

    def spec(self, rows, columns, piece, index=lambda i: (i, 0)):
        if self.pieces == 1:
            return pl.BlockSpec((rows, columns), index)

        def whole(i):
            at, col = index(i)
            return (at, piece, 0, col)

        return pl.BlockSpec((rows // self.part, 1, self.part, columns), whole)


def assemble(refs, whole, me):
    if len(refs) == 1:
        whole[...] = refs[0][...]
    else:
        for s, ref in enumerate(refs):
            whole[me ^ s] = ref[...]


def hand_out(whole, refs, me):
    if len(refs) == 1:
        refs[0][...] = whole[...]
    else:
        for s, ref in enumerate(refs):
            ref[...] = whole[me ^ s]


def mix_first(plan, me, factor, blocked, piece):
    step = min(256, plan.rows)
    last = plan.rows // step - 1

    def body(me_ref, factor_ref, x_ref, *rest):
        outs, whole = rest[:-1], rest[-1]
        i = pl.program_id(0)
        got = dot(rows_of(factor_ref), x_ref[...], 1, 0).astype(BF)
        whole[pl.ds(i * (step // plan.part), step // plan.part)] = got.reshape(
            step // plan.part, plan.part, plan.channels
        )

        @pl.when(i == last)
        def _():
            hand_out(whole, outs, me_ref[0])

    return pl.pallas_call(
        body,
        grid=(last + 1,),
        in_specs=[
            SCALAR,
            plan.spec(step, plan.block, piece),
            pl.BlockSpec((plan.block, plan.channels), lambda i: (0, 0)),
        ],
        out_specs=plan.block_specs(),
        out_shape=plan.block_shapes(),
        scratch_shapes=[plan.whole()],
        compiler_params=params(),
        cost_estimate=cost(
            2 * plan.rows * plan.block * plan.channels,
            2 * (plan.rows * plan.block + 2 * plan.block * plan.channels),
        ),
        name="mix_first",
    )(me, plan.view(factor), blocked)


def spread_factor(plan, factor_two):
    n = plan.count
    groups = plan.here // 16
    wide = n * 16
    turned = factor_two.reshape(groups, 16, n, n).transpose(0, 2, 1, 3).reshape(groups, wide, n)

    def body(in_ref, out_ref):
        col = lax.broadcasted_iota(jnp.int32, (n, wide), 1)
        row = lax.broadcasted_iota(jnp.int32, (n, wide), 0)
        pick = jnp.where(col // 16 == row, 1.0, 0.0).astype(BF)
        r = lax.broadcasted_iota(jnp.int32, (wide, wide), 0)
        c = lax.broadcasted_iota(jnp.int32, (wide, wide), 1)
        same = r % 16 == c % 16
        for g in range(groups):
            full = dot(in_ref[g], pick, 1, 0)
            out_ref[g] = jnp.where(same, full, 0.0).astype(BF)

    return pl.pallas_call(
        body,
        out_shape=jax.ShapeDtypeStruct((groups, wide, wide), BF),
        compiler_params=params(0),
        cost_estimate=cost(2 * groups * wide * wide * n, 2 * groups * wide * wide),
        name="spread_factor",
    )(turned)


def mix_second(plan, me, spread, cols, piece, back):
    n = plan.count
    wide = n * 16
    groups = plan.part // 16
    number = plan.arrays

    def body(me_ref, m_ref, *rest):
        ins, outs, (whole, made) = rest[:number], rest[number : 2 * number], rest[2 * number :]
        assemble(ins, whole, me_ref[0])
        for g in range(groups):
            at = slice(g * 16, (g + 1) * 16)
            rows = whole[:, at, :].reshape(wide, plan.channels)
            got = dot(m_ref[g], rows, 0 if back else 1, 0).astype(BF)
            made[:, at, :] = got.reshape(n, 16, plan.channels)
        hand_out(made, outs, me_ref[0])

    return pl.pallas_call(
        body,
        grid=(1,),
        in_specs=[SCALAR, pl.BlockSpec((groups, wide, wide), lambda i: (piece, 0, 0))]
        + plan.block_specs(),
        out_specs=plan.block_specs(),
        out_shape=plan.block_shapes(),
        scratch_shapes=[plan.whole(), plan.whole()],
        compiler_params=params(),
        cost_estimate=cost(
            2 * groups * wide * wide * plan.channels,
            4 * plan.rows * plan.channels + 2 * groups * wide * wide,
        ),
        name="mix_second_back" if back else "mix_second",
    )(me, spread, *cols)


def grad_second(plan, me, grads, firsts, scale):
    n = plan.count
    wide = n * 16
    groups = plan.part // 16
    number = plan.arrays

    def body(me_ref, *rest):
        out_ref, gs, us = rest[2 * number :]
        assemble(rest[:number], gs, me_ref[0])
        assemble(rest[number : 2 * number], us, me_ref[0])
        r = lax.broadcasted_iota(jnp.int32, (wide, wide), 0)
        c = lax.broadcasted_iota(jnp.int32, (wide, wide), 1)
        same = r % 16 == c % 16
        row = lax.broadcasted_iota(jnp.int32, (wide, n), 0)
        col = lax.broadcasted_iota(jnp.int32, (wide, n), 1)
        pick = jnp.where(row // 16 == col, 1.0, 0.0)
        for g in range(groups):
            at = slice(g * 16, (g + 1) * 16)
            full = dot(
                gs[:, at, :].reshape(wide, plan.channels),
                us[:, at, :].reshape(wide, plan.channels),
                1,
                1,
            )
            kept = jnp.where(same, full, 0.0)
            out_ref[g] = dot(kept, pick, 1, 0, precision=lax.Precision.HIGHEST) * scale

    out = pl.pallas_call(
        body,
        grid=(1,),
        in_specs=[SCALAR] + plan.block_specs() + plan.block_specs(),
        out_specs=pl.BlockSpec((groups, wide, n), lambda i: (0, 0, 0)),
        out_shape=jax.ShapeDtypeStruct((groups, wide, n), F32),
        scratch_shapes=[plan.whole(), plan.whole()],
        compiler_params=params(),
        cost_estimate=cost(
            2 * groups * wide * wide * plan.channels, 4 * plan.rows * plan.channels
        ),
        name="grad_second",
    )(me, *grads, *firsts)
    return out.reshape(groups, n, 16, n).transpose(0, 2, 1, 3).reshape(plan.part, n, n)


def middle(plan, me, blocked, incoming, mixed, up_blocks, down_blocks, piece, before):
    groups, width, inner = up_blocks.shape
    sub = inner // groups
    step = min(256, plan.rows)
    last = plan.rows // step - 1
    number = plan.arrays
    devices = step // plan.part

    def body(me_ref, x_ref, g_ref, up_ref, down_ref, *rest):
        mixed_refs, rest = rest[:number], rest[number:]
        if before is not None:
            before_ref, rest = rest[0], rest[1:]
        r_ref, w_ref = rest[:2]
        outs, (v_all, dv_all) = rest[2 : 2 + number], rest[2 + number :]
        i = pl.program_id(0)

        @pl.when(i == 0)
        def _():
            assemble(mixed_refs, v_all, me_ref[0])
            if before is None:
                w_ref[...] = jnp.zeros_like(w_ref)
            else:
                w_ref[...] = before_ref[...]

        here = pl.ds(i * devices, devices)
        x = rows_of(x_ref).astype(F32)
        g = rows_of(g_ref)
        v = v_all[here].reshape(step, plan.channels).astype(F32)
        sx = sigmoid(x)
        gate = x * sx
        h = (x + v * gate).astype(BF)
        h_parts = [h[:, b * width : (b + 1) * width] for b in range(groups)]
        g_parts = [g[:, b * width : (b + 1) * width] for b in range(groups)]
        acts, slopes, back = [], [], []
        for b in range(groups):
            a = dot(h_parts[b], up_ref[b], 1, 0)
            s = sigmoid(a)
            q = a * s
            acts.append(q.astype(BF))
            slopes.append(s + q * (1.0 - s))
            back.append(dot(g_parts[b], down_ref[b], 1, 1))
        grads = []
        for b in range(groups):
            lanes = slice(b * sub, (b + 1) * sub)
            perm = jnp.concatenate([acts[p][:, lanes] for p in range(groups)], axis=1)
            w_ref[groups + b] += dot(g_parts[b], perm, 0, 0)
            dq = jnp.concatenate([back[p][:, lanes] for p in range(groups)], axis=1)
            da = (dq * slopes[b]).astype(BF)
            w_ref[b] += dot(h_parts[b], da, 0, 0)
            grads.append(dot(da, up_ref[b], 1, 1))
        dh = (g.astype(F32) + jnp.concatenate(grads, axis=1)).astype(BF).astype(F32)
        dv_all[here] = (dh * gate).astype(BF).reshape(devices, plan.part, plan.channels)
        r_ref[...] = (dh * (1.0 + v * (sx + gate * (1.0 - sx)))).astype(BF)

        @pl.when(i == last)
        def _():
            hand_out(dv_all, outs, me_ref[0])

    block = pl.BlockSpec((step, plan.channels), lambda i: (i, 0))
    full = pl.BlockSpec((2 * groups, width, inner), lambda i: (0, 0, 0))
    in_specs = [
        SCALAR,
        plan.spec(step, plan.channels, piece),
        plan.spec(step, plan.channels, piece),
        pl.BlockSpec(up_blocks.shape, lambda i: (0, 0, 0)),
        pl.BlockSpec(down_blocks.shape, lambda i: (0, 0, 0)),
    ] + plan.block_specs()
    operands = [me, plan.view(blocked), plan.view(incoming), up_blocks, down_blocks, *mixed]
    if before is not None:
        in_specs.append(full)
        operands.append(before)
    hidden = plan.rows * groups * inner
    got = pl.pallas_call(
        body,
        grid=(last + 1,),
        in_specs=in_specs,
        out_specs=[block, full] + plan.block_specs(),
        out_shape=[
            jax.ShapeDtypeStruct((plan.rows, plan.channels), BF),
            jax.ShapeDtypeStruct((2 * groups, width, inner), F32),
        ]
        + plan.block_shapes(),
        scratch_shapes=[plan.whole(), plan.whole()],
        compiler_params=params(),
        cost_estimate=cost(
            10 * hidden * width, 10 * plan.rows * plan.channels + 8 * groups * width * inner, hidden
        ),
        name="middle",
    )(*operands)
    return got[2:], got[0], got[1]


def finish(plan, me, factor, grad_firsts, blocked, gate_grads, piece, scale, rows_before, sum_before):
    final = piece == plan.pieces - 1
    step = min(256, plan.block)
    n_gates = plan.pieces if final else 0
    number = plan.arrays

    def body(*refs):
        me_ref, factor_ref, x_ref = refs[:3]
        ins = refs[3 : 3 + number]
        others = refs[3 + number : -3]
        one_ref, out_ref, d_all = refs[-3:]

        @pl.when(pl.program_id(0) == 0)
        def _():
            assemble(ins, d_all, me_ref[0])

        d = d_all[...].reshape(plan.rows, plan.channels)
        one = dot(d, x_ref[...], 1, 1) * scale
        one_ref[...] = one.reshape(one_ref.shape)
        total = dot(rows_of(factor_ref), d, 0, 0)
        if piece > 0:
            total = total + others[1][...]
            others = others[2:]
        if final:
            if plan.pieces == 1:
                out_ref[...] = (total + others[0][...].astype(F32)).astype(BF)
            else:
                total = total.reshape(step // plan.here, plan.pieces, plan.part, plan.channels)
                for q in range(plan.pieces):
                    out_ref[:, q] = (total[:, q] + others[q][...].astype(F32)).astype(BF)
        else:
            out_ref[...] = total

    wide = pl.BlockSpec((step, plan.channels), lambda i: (i, 0))
    in_specs = [SCALAR, plan.spec(plan.rows, step, piece, lambda i: (0, i)), wide]
    in_specs += plan.block_specs()
    operands = [me, plan.view(factor), blocked, *grad_firsts]
    aliases = {}
    if piece > 0:
        aliases = {len(operands): 0}
        in_specs += [pl.BlockSpec(memory_space=pl.ANY), wide]
        operands += [rows_before, sum_before]
    out_spec, out_shape = wide, (plan.block, plan.channels)
    if final and plan.pieces == 1:
        in_specs.append(wide)
        operands += gate_grads
    elif final:
        in_specs += [
            pl.BlockSpec((step // plan.here, plan.part, plan.channels), lambda i: (i, 0, 0))
        ] * n_gates
        operands += [r.reshape(plan.count, plan.part, plan.channels) for r in gate_grads]
        out_spec = pl.BlockSpec(
            (step // plan.here, plan.pieces, plan.part, plan.channels), lambda i: (i, 0, 0, 0)
        )
        out_shape = (plan.count, plan.pieces, plan.part, plan.channels)
    one_shape = (plan.block, plan.block)
    if plan.pieces > 1:
        one_shape = (plan.count, plan.pieces, plan.part, plan.block)
    return pl.pallas_call(
        body,
        grid=(plan.block // step,),
        in_specs=in_specs,
        out_specs=[plan.spec(plan.rows, step, piece, lambda i: (0, i)), out_spec],
        out_shape=[
            jax.ShapeDtypeStruct(one_shape, F32),
            jax.ShapeDtypeStruct(out_shape, BF if final else F32),
        ],
        scratch_shapes=[plan.whole()],
        input_output_aliases=aliases,
        compiler_params=params(),
        cost_estimate=cost(
            4 * plan.rows * plan.block * plan.channels,
            6 * plan.rows * plan.block + 8 * plan.block * plan.channels,
        ),
        name="finish",
    )(*operands)


def sum_over(values, count):
    if count & (count - 1) or values.shape[0] % count:
        return lax.psum(values, "seq")
    me = lax.axis_index("seq")
    total = values
    steps = [1 << s for s in range(count.bit_length() - 1)]
    for step in steps:
        halves = total.reshape(2, total.shape[0] // 2, total.shape[1])
        mine = (me // step) % 2
        keep = lax.dynamic_index_in_dim(halves, mine, 0, keepdims=False)
        send = lax.dynamic_index_in_dim(halves, 1 - mine, 0, keepdims=False).astype(BF)
        got = lax.ppermute(send, "seq", [(i, i ^ step) for i in range(count)])
        total = keep + got.astype(F32)
    total = total.astype(BF)
    for step in reversed(steps):
        mine = (me // step) % 2
        got = lax.ppermute(total, "seq", [(i, i ^ step) for i in range(count)])
        low = jnp.where(mine == 0, total, got)
        high = jnp.where(mine == 0, got, total)
        total = jnp.concatenate([low, high], axis=0)
    return total


def write_weights(total, up_shape, down_shape, scale):
    groups, width, inner = up_shape

    def body(up_in, down_in, up_ref, down_ref):
        up_ref[0] = up_in[...].astype(F32) * scale
        down_ref[0] = (down_in[...].astype(F32) * scale).T

    return pl.pallas_call(
        body,
        grid=(groups,),
        in_specs=[
            pl.BlockSpec((width, inner), lambda b: (b, 0)),
            pl.BlockSpec((width, inner), lambda b: (groups + b, 0)),
        ],
        out_specs=[
            pl.BlockSpec((1, width, inner), lambda b: (b, 0, 0)),
            pl.BlockSpec((1, inner, width), lambda b: (b, 0, 0)),
        ],
        out_shape=[
            jax.ShapeDtypeStruct(up_shape, F32),
            jax.ShapeDtypeStruct(down_shape, F32),
        ],
        compiler_params=params(),
        cost_estimate=cost(groups * width * inner, 12 * groups * width * inner),
        name="write_weights",
    )(total, total)


def on_device(tokens, cotangent, factor_one, factor_two, up_blocks, down_blocks):
    count = lax.axis_size("seq")
    block, channels = factor_one.shape[1], tokens.shape[1]
    plan = Plan(count, block, channels)
    scale = float(count * tokens.shape[0]) ** (-0.5)
    factor = factor_one.reshape(block, block)
    pieces = range(plan.pieces)

    me = lax.axis_index("seq").astype(jnp.int32).reshape(1)

    def exchange(blocks):
        if not plan.direct:
            return [lax.all_to_all(blocks[0], "seq", split_axis=0, concat_axis=0, tiled=True)]
        return [blocks[0]] + [
            lax.ppermute(blocks[s], "seq", [(i, i ^ s) for i in range(count)])
            for s in range(1, count)
        ]

    if plan.grouped:
        spread = spread_factor(plan, factor_two)

    def second(cols, piece, back):
        if plan.grouped:
            return mix_second(plan, me, spread, cols, piece, back)
        names = "kmj,mkc->jkc" if back else "kmj,jkc->mkc"
        return [jnp.einsum(names, factor_two, cols[0], preferred_element_type=F32).astype(BF)]

    def second_grad(grads, firsts):
        if plan.grouped:
            return grad_second(plan, me, grads, firsts, scale)
        got = jnp.einsum("mkc,jkc->kmj", grads[0], firsts[0], preferred_element_type=F32)
        return got * scale

    firsts = [exchange(mix_first(plan, me, factor, tokens, q)) for q in pieces]
    mixed = [exchange(second(firsts[q], q, False)) for q in pieces]
    weights = None
    grad_mixed, gate_grads = [], []
    for q in pieces:
        dv, r, weights = middle(
            plan, me, tokens, cotangent, mixed[q], up_blocks, down_blocks, q, weights
        )
        grad_mixed.append(exchange(dv))
        gate_grads.append(r)
    grad_firsts = [exchange(second(grad_mixed[q], q, True)) for q in pieces]
    two = [second_grad(grad_mixed[q], firsts[q]) for q in pieces]
    total = sum_over(weights.reshape(-1, weights.shape[-1]), count)
    grad_up, grad_down = write_weights(total, up_blocks.shape, down_blocks.shape, scale)
    one, tokens_sum = None, None
    for q in pieces:
        one, tokens_sum = finish(
            plan, me, factor, grad_firsts[q], tokens, gate_grads, q, scale, one, tokens_sum
        )
    return (
        tokens_sum.reshape(tokens.shape),
        one.reshape(1, block, block),
        jnp.concatenate(two, axis=0),
        grad_up,
        grad_down,
    )


def solution(mesh):
    return jax.shard_map(
        on_device,
        mesh=mesh,
        in_specs=(
            P(("grp", "seq"), None),
            P(("grp", "seq"), None),
            P("seq", None, None),
            P("seq", None, None),
            P(),
            P(),
        ),
        out_specs=(
            P(("grp", "seq"), None),
            P(("grp", "seq"), None, None),
            P(("grp", "seq"), None, None),
            P("grp", None, None),
            P("grp", None, None),
        ),
        check_vma=False,
    )
```

time: 195 us -> 216 us (1.11)
  starting transfers between devices: 47.4 us -> 106 us
  waiting for transfers between devices: 81.7 us -> 59.5 us
  Pallas kernels: 52.7 us -> 38.2 us
    ppermute x0 -> x60, starting transfers between devices: none -> 91.5 us  [exchange(): lax.ppermute(blocks[s], 'seq', [(i, i ^ s) for i in range(count)])]
    all_to_all x8 -> x0, waiting for transfers between devices: 39.5 us -> none  [exchange(): got = lax.all_to_all(cut, 'seq', split_axis=0, concat_axis=0, tiled=True)]
    all_to_all x8 -> x0, starting transfers between devices: 38.2 us -> none  [exchange(): got = lax.all_to_all(cut, 'seq', split_axis=0, concat_axis=0, tiled=True)]
    ppermute x0 -> x60, waiting for transfers between devices: none -> 35.2 us  [exchange(): lax.ppermute(blocks[s], 'seq', [(i, i ^ s) for i in range(count)])]
    ppermute x4, waiting for transfers between devices: 25.4 us -> 13.9 us  [sum_over(): got = lax.ppermute(send, 'seq', [(i, i ^ step) for i in range(count)])]
    pallas_call x11 -> x6, Pallas kernels: 38.2 us -> 27.7 us  [the longest x1 10.9 us: middle(): pl.pallas_call(body, grid=(last + 1,), in_specs=in_specs, out_specs=[bloc...]
    ppermute x4, waiting for transfers between devices: 16.8 us -> 10.4 us  [sum_over(): got = lax.ppermute(total, 'seq', [(i, i ^ step) for i in range(count)])]
    ppermute x4, starting transfers between devices: 2.2 us -> 6.97 us  [sum_over(): got = lax.ppermute(total, 'seq', [(i, i ^ step) for i in range(count)])]
  transfers between devices with their start and end apart: 16 -> 68, of which waited for: 8 -> 23; matrix products, arithmetic and copies ran while one was open for 4% -> 2% of each run, Pallas kernels for 19% -> 4%
where the time goes in v3:
time: 216 us; the launch traced here: 215 us
  starting transfers between devices  106 us (49%)
  waiting for transfers between devices  59.5 us (28%)
  Pallas kernels  38.2 us (18%)
  local copies, waits for them, and re-layouts  7.04 us (3%)
  other arithmetic  2.95 us (1%)
    ppermute x60, starting transfers between devices, exchange(): lax.ppermute(blocks[s], 'seq', [(i, i ^ s) for i in range(count)])  91.5 us
    ppermute x60, waiting for transfers between devices, exchange(): lax.ppermute(blocks[s], 'seq', [(i, i ^ s) for i in range(count)])  35.2 us
    ppermute x4, waiting for transfers between devices, sum_over(): got = lax.ppermute(send, 'seq', [(i, i ^ step) for i in range(count)])  13.9 us
    pallas_call x1, Pallas kernels, middle(): pl.pallas_call(body, grid=(last + 1,), in_specs=in_specs, out_specs=[bloc...  10.9 us
    ppermute x4, waiting for transfers between devices, sum_over(): got = lax.ppermute(total, 'seq', [(i, i ^ step) for i in range(count)])  10.4 us
    ppermute x4, starting transfers between devices, sum_over(): got = lax.ppermute(send, 'seq', [(i, i ^ step) for i in range(count)])  7.46 us
    ppermute x4, starting transfers between devices, sum_over(): got = lax.ppermute(total, 'seq', [(i, i ^ step) for i in range(count)])  6.97 us
    pallas_call x1, Pallas kernels, finish(): pl.pallas_call(body, grid=(plan.block // step,), in_specs=in_specs, out_s...  6.79 us
  transfers between devices with their start and end apart: 68, of which 23 were waited for; matrix products, arithmetic and copies ran while one was open for 2% of the time, Pallas kernels for 4%

profile of v3, /device:TPU:0, one launch (start us, length us, event | category | flops | bytes accessed | tf_op | source)
XLA Modules:
  0.0 215.3 jit_solution(15548379622205176470)
XLA Ops:
  0.6 4.9 %mix_first.1 = (bf16[64,512]{1,0:T(8,128)(2,1)}, bf16[64,512]{1,0:T(8,128)(2,1)}, bf16[64,512]{1,0:T(8,128)(2,1)}, bf16[64,512]{1,0:T(8,128)(2,1)}, bf16[64,512]...) custom-call(s32[1]{0:T(128)} %bitcast.me_ref.refs_0_, ...), custom_call_target="tpu_custom_call" | custom-call | flops 1073741824 | bytes 4194304 | tf_op jit(solution)/shard_map/mix_first/pallas_call | solution.py:111
  6.1 2.6 %collective-permute-start.1 = (bf16[64,512]{1,0:T(8,128)(2,1)}, bf16[64,512]{1,0:T(8,128)(2,1)S(1)}, u32[]{:S(2)}, u32[]{:S(2)}) collective-permute-start(bf16[64,512]{1,0:T(8,128)(2,1)} %get-tuple-element.77), channel_id=1, source_target_pairs={{0,2},{1,3},{2,0},{3,1},{4,6},{5,7},{6,4},{7,5},{8,10},{9,11},{10,... | collective-permute-start | bytes 196616 | tf_op jit(solution)/shard_map/ppermute | solution.py:468
  10.5 2.6 %collective-permute-start.5 = (bf16[64,512]{1,0:T(8,128)(2,1)}, bf16[64,512]{1,0:T(8,128)(2,1)S(1)}, u32[]{:S(2)}, u32[]{:S(2)}) collective-permute-start(bf16[64,512]{1,0:T(8,128)(2,1)} %get-tuple-element.81), channel_id=1, source_target_pairs={{0,6},{1,7},{2,4},{3,5},{4,2},{5,3},{6,0},{7,1},{8,14},{9,15},{10,... | collective-permute-start | bytes 196616 | tf_op jit(solution)/shard_map/ppermute | solution.py:468
  13.6 2.6 %collective-permute-start.7 = (bf16[64,512]{1,0:T(8,128)(2,1)}, bf16[64,512]{1,0:T(8,128)(2,1)S(1)}, u32[]{:S(2)}, u32[]{:S(2)}) collective-permute-start(bf16[64,512]{1,0:T(8,128)(2,1)} %get-tuple-element.83), channel_id=1, source_target_pairs={{0,8},{1,9},{2,10},{3,11},{4,12},{5,13},{6,14},{7,15},{8,0},{9,1},... | collective-permute-start | bytes 196616 | tf_op jit(solution)/shard_map/ppermute | solution.py:468
  17.1 2.3 %collective-permute-start.9 = (bf16[64,512]{1,0:T(8,128)(2,1)}, bf16[64,512]{1,0:T(8,128)(2,1)S(1)}, u32[]{:S(2)}, u32[]{:S(2)}) collective-permute-start(bf16[64,512]{1,0:T(8,128)(2,1)} %get-tuple-element.85), channel_id=1, source_target_pairs={{0,10},{1,11},{2,8},{3,9},{4,14},{5,15},{6,12},{7,13},{8,2},{9,3},... | collective-permute-start | bytes 196616 | tf_op jit(solution)/shard_map/ppermute | solution.py:468
  20.4 2.7 %collective-permute-start.11 = (bf16[64,512]{1,0:T(8,128)(2,1)}, bf16[64,512]{1,0:T(8,128)(2,1)S(1)}, u32[]{:S(2)}, u32[]{:S(2)}) collective-permute-start(bf16[64,512]{1,0:T(8,128)(2,1)} %get-tuple-element.87), channel_id=1, source_target_pairs={{0,12},{1,13},{2,14},{3,15},{4,8},{5,9},{6,10},{7,11},{8,4},{9,5},... | collective-permute-start | bytes 196616 | tf_op jit(solution)/shard_map/ppermute | solution.py:468
  23.2 4.2 %collective-permute-start.12 = (bf16[64,512]{1,0:T(8,128)(2,1)}, bf16[64,512]{1,0:T(8,128)(2,1)S(1)}, u32[]{:S(2)}, u32[]{:S(2)}) collective-permute-start(bf16[64,512]{1,0:T(8,128)(2,1)} %get-tuple-element.88), channel_id=1, source_target_pairs={{0,13},{1,12},{2,15},{3,14},{4,9},{5,8},{6,11},{7,10},{8,5},{9,4},... | collective-permute-start | bytes 196616 | tf_op jit(solution)/shard_map/ppermute | solution.py:468
  28.3 3.2 %collective-permute-start.13 = (bf16[64,512]{1,0:T(8,128)(2,1)}, bf16[64,512]{1,0:T(8,128)(2,1)S(1)}, u32[]{:S(2)}, u32[]{:S(2)}) collective-permute-start(bf16[64,512]{1,0:T(8,128)(2,1)} %get-tuple-element.89), channel_id=1, source_target_pairs={{0,14},{1,15},{2,12},{3,13},{4,10},{5,11},{6,8},{7,9},{8,6},{9,7},... | collective-permute-start | bytes 196616 | tf_op jit(solution)/shard_map/ppermute | solution.py:468
  37.3 2.3 %collective-permute-done.14.rest_15_.rest_31_ = bf16[64,512]{1,0:T(8,128)(2,1)S(1)} collective-permute-done((bf16[64,512]{1,0:T(8,128)(2,1)}, bf16[64,512]{1,0:T(8,128)(2,1)S(1)}, u32[]{:S(2)}, u32[]{:S(2)}) %collective-permute-start.14) | collective-permute-done | bytes 65568 | tf_op jit(solution)/shard_map/ppermute | solution.py:468
  40.2 2.9 %mix_second.1 = (bf16[64,512]{1,0:T(8,128)(2,1)}, bf16[64,512]{1,0:T(8,128)(2,1)}, bf16[64,512]{1,0:T(8,128)(2,1)}, bf16[64,512]{1,0:T(8,128)(2,1)}, bf16[64,512...) custom-call(s32[1]{0:T(128)} %bitcast.me_ref.refs_0_, ...), custom_call_target="tpu_custom_call" | custom-call | flops 268435456 | bytes 2621440 | tf_op jit(solution)/shard_map/mix_second/pallas_call | solution.py:173
  45.0 2.8 %collective-permute-start.18 = (bf16[64,512]{1,0:T(8,128)(2,1)}, bf16[64,512]{1,0:T(8,128)(2,1)S(1)}, u32[]{:S(2)}, u32[]{:S(2)}) collective-permute-start(bf16[64,512]{1,0:T(8,128)(2,1)} %get-tuple-element.95), channel_id=1, source_target_pairs={{0,4},{1,5},{2,6},{3,7},{4,0},{5,1},{6,2},{7,3},{8,12},{9,13},{10,... | collective-permute-start | bytes 196616 | tf_op jit(solution)/shard_map/ppermute | solution.py:468
  50.2 2.9 %collective-permute-start.22 = (bf16[64,512]{1,0:T(8,128)(2,1)}, bf16[64,512]{1,0:T(8,128)(2,1)S(1)}, u32[]{:S(2)}, u32[]{:S(2)}) collective-permute-start(bf16[64,512]{1,0:T(8,128)(2,1)} %get-tuple-element.99), channel_id=1, source_target_pairs={{0,8},{1,9},{2,10},{3,11},{4,12},{5,13},{6,14},{7,15},{8,0},{9,1},... | collective-permute-start | bytes 196616 | tf_op jit(solution)/shard_map/ppermute | solution.py:468
  53.2 2.5 %collective-permute-start.24 = (bf16[64,512]{1,0:T(8,128)(2,1)}, bf16[64,512]{1,0:T(8,128)(2,1)S(1)}, u32[]{:S(2)}, u32[]{:S(2)}) collective-permute-start(bf16[64,512]{1,0:T(8,128)(2,1)} %get-tuple-element.101), channel_id=1, source_target_pairs={{0,10},{1,11},{2,8},{3,9},{4,14},{5,15},{6,12},{7,13},{8,2},{9,3},... | collective-permute-start | bytes 196616 | tf_op jit(solution)/shard_map/ppermute | solution.py:468
  60.7 5.7 %collective-permute-done.23.rest_9_ = bf16[64,512]{1,0:T(8,128)(2,1)S(1)} collective-permute-done((bf16[64,512]{1,0:T(8,128)(2,1)}, bf16[64,512]{1,0:T(8,128)(2,1)S(1)}, u32[]{:S(2)}, u32[]{:S(2)}) %collective-permute-start.23) | collective-permute-done | bytes 65568 | tf_op jit(solution)/shard_map/ppermute | solution.py:468
  66.4 2.3 %collective-permute-start.28 = (bf16[64,512]{1,0:T(8,128)(2,1)}, bf16[64,512]{1,0:T(8,128)(2,1)S(1)}, u32[]{:S(2)}, u32[]{:S(2)}) collective-permute-start(bf16[64,512]{1,0:T(8,128)(2,1)} %get-tuple-element.105), channel_id=1, source_target_pairs={{0,14},{1,15},{2,12},{3,13},{4,10},{5,11},{6,8},{7,9},{8,6},{9,7},... | collective-permute-start | bytes 196616 | tf_op jit(solution)/shard_map/ppermute | solution.py:468
  68.7 2.3 %collective-permute-start.29 = (bf16[64,512]{1,0:T(8,128)(2,1)}, bf16[64,512]{1,0:T(8,128)(2,1)S(1)}, u32[]{:S(2)}, u32[]{:S(2)}) collective-permute-start(bf16[64,512]{1,0:T(8,128)(2,1)} %get-tuple-element.106), channel_id=1, source_target_pairs={{0,15},{1,14},{2,13},{3,12},{4,11},{5,10},{6,9},{7,8},{8,7},{9,6},... | collective-permute-start | bytes 196616 | tf_op jit(solution)/shard_map/ppermute | solution.py:468
  71.1 2.9 %collective-permute-done.28.rest_14_ = bf16[64,512]{1,0:T(8,128)(2,1)S(1)} collective-permute-done((bf16[64,512]{1,0:T(8,128)(2,1)}, bf16[64,512]{1,0:T(8,128)(2,1)S(1)}, u32[]{:S(2)}, u32[]{:S(2)}) %collective-permute-start.28) | collective-permute-done | bytes 65568 | tf_op jit(solution)/shard_map/ppermute | solution.py:468
  76.2 10.9 %middle.1 = (bf16[1024,512]{1,0:T(8,128)(2,1)}, f32[8,128,512]{2,1,0:T(8,128)}, bf16[64,512]{1,0:T(8,128)(2,1)}, bf16[64,512]{1,0:T(8,128)(2,1)}, bf16[64,512]{1...) custom-call(s32[1]{0:T(128)} %bitcast.me_ref.refs_0_, ...), custom_call_target="tpu_custom_call" | custom-call | flops 2684354560 | bytes 7340032 | tf_op jit(solution)/shard_map/middle/pallas_call | solution.py:305
  93.4 6.8 %collective-permute-done.61 = bf16[256,512]{1,0:T(8,128)(2,1)S(1)} collective-permute-done((bf16[256,512]{1,0:T(8,128)(2,1)S(1)}, bf16[256,512]{1,0:T(8,128)(2,1)S(1)}, u32[]{:S(2)}, u32[]{:S(2)}) %collective-permute-start.61) | collective-permute-done | bytes 262176 | tf_op jit(solution)/shard_map/ppermute | solution.py:414
  100.4 2.9 %collective-permute-start.62 = (bf16[128,512]{1,0:T(8,128)(2,1)S(1)}, bf16[128,512]{1,0:T(8,128)(2,1)S(1)}, u32[]{:S(2)}, u32[]{:S(2)}) collective-permute-start(bf16[128,512]{1,0:T(8,128)(2,1)S(1)} %fusion.2), channel_id=1, source_target_pairs={{0,4},{1,5},{2,6},{3,7},{4,0},{5,1},{6,2},{7,3},{8,12},{9,13},{10,... | collective-permute-start | bytes 393224 | tf_op jit(solution)/shard_map/ppermute | solution.py:414
  103.2 3.0 %collective-permute-done.62 = bf16[128,512]{1,0:T(8,128)(2,1)S(1)} collective-permute-done((bf16[128,512]{1,0:T(8,128)(2,1)S(1)}, bf16[128,512]{1,0:T(8,128)(2,1)S(1)}, u32[]{:S(2)}, u32[]{:S(2)}) %collective-permute-start.62) | collective-permute-done | bytes 131104 | tf_op jit(solution)/shard_map/ppermute | solution.py:414
  106.4 2.9 %collective-permute-start.63 = (bf16[64,512]{1,0:T(8,128)(2,1)S(1)}, bf16[64,512]{1,0:T(8,128)(2,1)S(1)}, u32[]{:S(2)}, u32[]{:S(2)}) collective-permute-start(bf16[64,512]{1,0:T(8,128)(2,1)S(1)} %fusion.4), channel_id=1, source_target_pairs={{0,8},{1,9},{2,10},{3,11},{4,12},{5,13},{6,14},{7,15},{8,0},{9,1},... | collective-permute-start | bytes 196616 | tf_op jit(solution)/shard_map/ppermute | solution.py:414
  109.4 2.3 %collective-permute-done.63 = bf16[64,512]{1,0:T(8,128)(2,1)S(1)} collective-permute-done((bf16[64,512]{1,0:T(8,128)(2,1)S(1)}, bf16[64,512]{1,0:T(8,128)(2,1)S(1)}, u32[]{:S(2)}, u32[]{:S(2)}) %collective-permute-start.63) | collective-permute-done | bytes 65568 | tf_op jit(solution)/shard_map/ppermute | solution.py:414
  111.7 3.0 %collective-permute-start.64 = (bf16[64,512]{1,0:T(8,128)(2,1)S(1)}, bf16[64,512]{1,0:T(8,128)(2,1)S(1)}, u32[]{:S(2)}, u32[]{:S(2)}) collective-permute-start(bf16[64,512]{1,0:T(8,128)(2,1)S(1)} %fusion.3), channel_id=1, source_target_pairs={{0,8},{1,9},{2,10},{3,11},{4,12},{5,13},{6,14},{7,15},{8,0},{9,1},... | collective-permute-start | bytes 196616 | tf_op jit(solution)/shard_map/ppermute | solution.py:419
  114.7 2.4 %collective-permute-done.64 = bf16[64,512]{1,0:T(8,128)(2,1)S(1)} collective-permute-done((bf16[64,512]{1,0:T(8,128)(2,1)S(1)}, bf16[64,512]{1,0:T(8,128)(2,1)S(1)}, u32[]{:S(2)}, u32[]{:S(2)}) %collective-permute-start.64) | collective-permute-done | bytes 65568 | tf_op jit(solution)/shard_map/ppermute | solution.py:419
  117.2 2.4 %collective-permute-start.65 = (bf16[128,512]{1,0:T(8,128)(2,1)S(1)}, bf16[128,512]{1,0:T(8,128)(2,1)S(1)}, u32[]{:S(2)}, u32[]{:S(2)}) collective-permute-start(bf16[128,512]{1,0:T(8,128)(2,1)S(1)} %pad_maximum_fusion.3), channel_id=1, source_target_pairs={{0,4},{1,5},{2,6},{3,7},{4,0},{5,1},{6,2},{7,3},{8,12},{9,13},{10,... | collective-permute-start | bytes 393224 | tf_op jit(solution)/shard_map/ppermute | solution.py:419
  119.6 2.9 %collective-permute-done.65 = bf16[128,512]{1,0:T(8,128)(2,1)S(1)} collective-permute-done((bf16[128,512]{1,0:T(8,128)(2,1)S(1)}, bf16[128,512]{1,0:T(8,128)(2,1)S(1)}, u32[]{:S(2)}, u32[]{:S(2)}) %collective-permute-start.65) | collective-permute-done | bytes 131104 | tf_op jit(solution)/shard_map/ppermute | solution.py:419
  124.1 5.0 %collective-permute-done.66 = bf16[256,512]{1,0:T(8,128)(2,1)S(1)} collective-permute-done((bf16[256,512]{1,0:T(8,128)(2,1)S(1)}, bf16[256,512]{1,0:T(8,128)(2,1)S(1)}, u32[]{:S(2)}, u32[]{:S(2)}) %collective-permute-start.66) | collective-permute-done | bytes 262176 | tf_op jit(solution)/shard_map/ppermute | solution.py:419
  131.2 2.0 collective-permute-start.33
  134.0 3.5 %collective-permute-start.35 = (bf16[64,512]{1,0:T(8,128)(2,1)S(1)}, bf16[64,512]{1,0:T(8,128)(2,1)S(1)}, u32[]{:S(2)}, u32[]{:S(2)}) collective-permute-start(bf16[64,512]{1,0:T(8,128)(2,1)S(1)} %copy-done.40), channel_id=1, source_target_pairs={{0,6},{1,7},{2,4},{3,5},{4,2},{5,3},{6,0},{7,1},{8,14},{9,15},{10,... | collective-permute-start | bytes 196616 | tf_op jit(solution)/shard_map/ppermute | solution.py:468
  140.5 2.3 %collective-permute-start.39 = (bf16[64,512]{1,0:T(8,128)(2,1)S(1)}, bf16[64,512]{1,0:T(8,128)(2,1)S(1)}, u32[]{:S(2)}, u32[]{:S(2)}) collective-permute-start(bf16[64,512]{1,0:T(8,128)(2,1)S(1)} %copy-done.36), channel_id=1, source_target_pairs={{0,10},{1,11},{2,8},{3,9},{4,14},{5,15},{6,12},{7,13},{8,2},{9,3},... | collective-permute-start | bytes 196616 | tf_op jit(solution)/shard_map/ppermute | solution.py:468
  144.5 5.5 %collective-permute-done.37.rest_8_ = bf16[64,512]{1,0:T(8,128)(2,1)S(1)} collective-permute-done((bf16[64,512]{1,0:T(8,128)(2,1)S(1)}, bf16[64,512]{1,0:T(8,128)(2,1)S(1)}, u32[]{:S(2)}, u32[]{:S(2)}) %collective-permute-start.37) | collective-permute-done | bytes 65568 | tf_op jit(solution)/shard_map/ppermute | solution.py:468
  150.0 2.1 collective-permute-start.41
  153.0 2.7 %collective-permute-start.43 = (bf16[64,512]{1,0:T(8,128)(2,1)S(1)}, bf16[64,512]{1,0:T(8,128)(2,1)S(1)}, u32[]{:S(2)}, u32[]{:S(2)}) collective-permute-start(bf16[64,512]{1,0:T(8,128)(2,1)S(1)} %copy-done.32), channel_id=1, source_target_pairs={{0,14},{1,15},{2,12},{3,13},{4,10},{5,11},{6,8},{7,9},{8,6},{9,7},... | collective-permute-start | bytes 196616 | tf_op jit(solution)/shard_map/ppermute | solution.py:468
  155.8 2.4 %collective-permute-start.44 = (bf16[64,512]{1,0:T(8,128)(2,1)S(1)}, bf16[64,512]{1,0:T(8,128)(2,1)S(1)}, u32[]{:S(2)}, u32[]{:S(2)}) collective-permute-start(bf16[64,512]{1,0:T(8,128)(2,1)S(1)} %copy-done.31), channel_id=1, source_target_pairs={{0,15},{1,14},{2,13},{3,12},{4,11},{5,10},{6,9},{7,8},{8,7},{9,6},... | collective-permute-start | bytes 196616 | tf_op jit(solution)/shard_map/ppermute | solution.py:468
  158.2 2.5 %collective-permute-done.43.rest_14_ = bf16[64,512]{1,0:T(8,128)(2,1)S(1)} collective-permute-done((bf16[64,512]{1,0:T(8,128)(2,1)S(1)}, bf16[64,512]{1,0:T(8,128)(2,1)S(1)}, u32[]{:S(2)}, u32[]{:S(2)}) %collective-permute-start.43) | collective-permute-done | bytes 65568 | tf_op jit(solution)/shard_map/ppermute | solution.py:468
  162.9 3.0 %mix_second_back.1 = (bf16[64,512]{1,0:T(8,128)(2,1)}, bf16[64,512]{1,0:T(8,128)(2,1)}, bf16[64,512]{1,0:T(8,128)(2,1)}, bf16[64,512]{1,0:T(8,128)(2,1)}, bf16[6...) custom-call(s32[1]{0:T(128)} %bitcast.me_ref.refs_0_, ...), custom_call_target="tpu_custom_call" | custom-call | flops 268435456 | bytes 2621440 | tf_op jit(solution)/shard_map/mix_second_back/pallas_call | solution.py:173
  167.9 2.6 %collective-permute-start.48 = (bf16[64,512]{1,0:T(8,128)(2,1)}, bf16[64,512]{1,0:T(8,128)(2,1)S(1)}, u32[]{:S(2)}, u32[]{:S(2)}) collective-permute-start(bf16[64,512]{1,0:T(8,128)(2,1)} %get-tuple-element.127), channel_id=1, source_target_pairs={{0,4},{1,5},{2,6},{3,7},{4,0},{5,1},{6,2},{7,3},{8,12},{9,13},{10,... | collective-permute-start | bytes 196616 | tf_op jit(solution)/shard_map/ppermute | solution.py:468
  170.6 4.1 %grad_second.1 = f32[4,256,16]{2,1,0:T(8,128)} custom-call(s32[1]{0:T(128)} %bitcast.me_ref.refs_0_, bf16[64,512]{1,0:T(8,128)(2,1)} %get-tuple-element.107.rest_0_, bf16[64,512]{1,0:T(8,128)(2,1)} %copy-done.15, bf16[64,512]{1,0:T(8,128)(2,1)} %copy-done.16, bf16[64,512]{1,0:T(8,128)(2,1)} %copy-done.17, bf16[64,512]{1,0:T(8,128)(2,1)} %copy-done.18, ...), custom_call_target="tpu_custom_call" | custom-call | flops 268435456 | bytes 2097152 | tf_op jit(solution)/shard_map/grad_second/pallas_call | solution.py:217
  177.0 2.2 %collective-permute-start.50 = (bf16[64,512]{1,0:T(8,128)(2,1)S(1)}, bf16[64,512]{1,0:T(8,128)(2,1)S(1)}, u32[]{:S(2)}, u32[]{:S(2)}) collective-permute-start(bf16[64,512]{1,0:T(8,128)(2,1)S(1)} %copy-done.68), channel_id=1, source_target_pairs={{0,6},{1,7},{2,4},{3,5},{4,2},{5,3},{6,0},{7,1},{8,14},{9,15},{10,... | collective-permute-start | bytes 196616 | tf_op jit(solution)/shard_map/ppermute | solution.py:468
  179.5 2.1 collective-permute-start.52
  182.5 2.7 %collective-permute-start.54 = (bf16[64,512]{1,0:T(8,128)(2,1)S(1)}, bf16[64,512]{1,0:T(8,128)(2,1)S(1)}, u32[]{:S(2)}, u32[]{:S(2)}) collective-permute-start(bf16[64,512]{1,0:T(8,128)(2,1)S(1)} %copy-done.60), channel_id=1, source_target_pairs={{0,10},{1,11},{2,8},{3,9},{4,14},{5,15},{6,12},{7,13},{8,2},{9,3},... | collective-permute-start | bytes 196616 | tf_op jit(solution)/shard_map/ppermute | solution.py:468
  188.0 3.0 %collective-permute-done.52.refs_11_ = bf16[64,512]{1,0:T(8,128)(2,1)S(1)} collective-permute-done((bf16[64,512]{1,0:T(8,128)(2,1)S(1)}, bf16[64,512]{1,0:T(8,128)(2,1)S(1)}, u32[]{:S(2)}, u32[]{:S(2)}) %collective-permute-start.52) | collective-permute-done | bytes 65568 | tf_op jit(solution)/shard_map/ppermute | solution.py:468
  191.0 2.4 %collective-permute-done.53.refs_12_ = bf16[64,512]{1,0:T(8,128)(2,1)S(1)} collective-permute-done((bf16[64,512]{1,0:T(8,128)(2,1)S(1)}, bf16[64,512]{1,0:T(8,128)(2,1)S(1)}, u32[]{:S(2)}, u32[]{:S(2)}) %collective-permute-start.53) | collective-permute-done | bytes 65568 | tf_op jit(solution)/shard_map/ppermute | solution.py:468
  193.4 2.5 %collective-permute-start.58 = (bf16[64,512]{1,0:T(8,128)(2,1)S(1)}, bf16[64,512]{1,0:T(8,128)(2,1)S(1)}, u32[]{:S(2)}, u32[]{:S(2)}) collective-permute-start(bf16[64,512]{1,0:T(8,128)(2,1)S(1)} %copy-done.50), channel_id=1, source_target_pairs={{0,14},{1,15},{2,12},{3,13},{4,10},{5,11},{6,8},{7,9},{8,6},{9,7},... | collective-permute-start | bytes 196616 | tf_op jit(solution)/shard_map/ppermute | solution.py:468
  200.9 3.3 %collective-permute-done.59.refs_18_ = bf16[64,512]{1,0:T(8,128)(2,1)S(1)} collective-permute-done((bf16[64,512]{1,0:T(8,128)(2,1)S(1)}, bf16[64,512]{1,0:T(8,128)(2,1)S(1)}, u32[]{:S(2)}, u32[]{:S(2)}) %collective-permute-start.59) | collective-permute-done | bytes 65568 | tf_op jit(solution)/shard_map/ppermute | solution.py:468
  204.8 6.8 %finish.1 = (f32[1024,1024]{1,0:T(8,128)}, bf16[1024,512]{1,0:T(8,128)(2,1)}) custom-call(s32[1]{0:T(128)} %bitcast.me_ref.refs_0_, bf16[1024,1024]{1,0:T(8,128)(2,1)} %bitcast.46, bf16[1024,512]{1,0:T(8,128)(2,1)} %refs_2_.1, bf16[64,512]{1,0:T(8,128)(2,1)} %get-tuple-element.123.refs_3_, bf16[64,512]{1,0:T(8,128)(2,1)} %copy-done.46, ...), custom_call_target="tpu_custom_call" | custom-call | flops 2147483648 | bytes 10485760 | tf_op jit(solution)/shard_map/finish/pallas_call | solution.py:383
  211.6 3.7 %write_weights.1 = (f32[4,128,512]{2,1,0:T(8,128)}, f32[4,512,128]{2,1,0:T(8,128)}) custom-call(bf16[1024,512]{1,0:T(8,128)(2,1)} %pad_maximum_fusion.up_in.down_in, bf16[1024,512]{1,0:T(8,128)(2,1)} %pad_maximum_fusion.up_in.down_in), custom_call_target="tpu_custom_call" | custom-call | flops 262144 | bytes 3145728 | tf_op jit(solution)/shard_map/write_weights/pallas_call | solution.py:433
  (288 shorter events, 56.2 us)
Async XLA Ops:
  6.1 7.1 %collective-permute-start.1 = (bf16[64,512]{1,0:T(8,128)(2,1)}, bf16[64,512]{1,0:T(8,128)(2,1)S(1)}, u32[]{:S(2)}, u32[]{:S(2)}) collective-permute-start(bf16[64,512]{1,0:T(8,128)(2,1)} %get-tuple-element.77), channel_id=1, source_target_pairs={{0,2},{1,3},{2,0},{3,1},{4,6},{5,7},{6,4},{7,5},{8,10},{9,11},{10,... | collective-permute-start | bytes 196616 | tf_op jit(solution)/shard_map/ppermute | solution.py:468
  8.7 7.5 %collective-permute-start.3 = (bf16[64,512]{1,0:T(8,128)(2,1)}, bf16[64,512]{1,0:T(8,128)(2,1)S(1)}, u32[]{:S(2)}, u32[]{:S(2)}) collective-permute-start(bf16[64,512]{1,0:T(8,128)(2,1)} %get-tuple-element.79), channel_id=1, source_target_pairs={{0,4},{1,5},{2,6},{3,7},{4,0},{5,1},{6,2},{7,3},{8,12},{9,13},{10,... | collective-permute-start | bytes 196616 | tf_op jit(solution)/shard_map/ppermute | solution.py:468
  10.5 6.6 %collective-permute-start.4 = (bf16[64,512]{1,0:T(8,128)(2,1)}, bf16[64,512]{1,0:T(8,128)(2,1)S(1)}, u32[]{:S(2)}, u32[]{:S(2)}) collective-permute-start(bf16[64,512]{1,0:T(8,128)(2,1)} %get-tuple-element.80), channel_id=1, source_target_pairs={{0,5},{1,4},{2,7},{3,6},{4,1},{5,0},{6,3},{7,2},{8,13},{9,12},{10,... | collective-permute-start | bytes 196616 | tf_op jit(solution)/shard_map/ppermute | solution.py:468
  10.5 8.9 %collective-permute-start.5 = (bf16[64,512]{1,0:T(8,128)(2,1)}, bf16[64,512]{1,0:T(8,128)(2,1)S(1)}, u32[]{:S(2)}, u32[]{:S(2)}) collective-permute-start(bf16[64,512]{1,0:T(8,128)(2,1)} %get-tuple-element.81), channel_id=1, source_target_pairs={{0,6},{1,7},{2,4},{3,5},{4,2},{5,3},{6,0},{7,1},{8,14},{9,15},{10,... | collective-permute-start | bytes 196616 | tf_op jit(solution)/shard_map/ppermute | solution.py:468
  13.1 7.3 %collective-permute-start.6 = (bf16[64,512]{1,0:T(8,128)(2,1)}, bf16[64,512]{1,0:T(8,128)(2,1)S(1)}, u32[]{:S(2)}, u32[]{:S(2)}) collective-permute-start(bf16[64,512]{1,0:T(8,128)(2,1)} %get-tuple-element.82), channel_id=1, source_target_pairs={{0,7},{1,6},{2,5},{3,4},{4,3},{5,2},{6,1},{7,0},{8,15},{9,14},{10,... | collective-permute-start | bytes 196616 | tf_op jit(solution)/shard_map/ppermute | solution.py:468
  13.6 9.6 %collective-permute-start.7 = (bf16[64,512]{1,0:T(8,128)(2,1)}, bf16[64,512]{1,0:T(8,128)(2,1)S(1)}, u32[]{:S(2)}, u32[]{:S(2)}) collective-permute-start(bf16[64,512]{1,0:T(8,128)(2,1)} %get-tuple-element.83), channel_id=1, source_target_pairs={{0,8},{1,9},{2,10},{3,11},{4,12},{5,13},{6,14},{7,15},{8,0},{9,1},... | collective-permute-start | bytes 196616 | tf_op jit(solution)/shard_map/ppermute | solution.py:468
  16.2 12.1 %collective-permute-start.8 = (bf16[64,512]{1,0:T(8,128)(2,1)}, bf16[64,512]{1,0:T(8,128)(2,1)S(1)}, u32[]{:S(2)}, u32[]{:S(2)}) collective-permute-start(bf16[64,512]{1,0:T(8,128)(2,1)} %get-tuple-element.84), channel_id=1, source_target_pairs={{0,9},{1,8},{2,11},{3,10},{4,13},{5,12},{6,15},{7,14},{8,1},{9,0},... | collective-permute-start | bytes 196616 | tf_op jit(solution)/shard_map/ppermute | solution.py:468
  17.1 15.0 %collective-permute-start.9 = (bf16[64,512]{1,0:T(8,128)(2,1)}, bf16[64,512]{1,0:T(8,128)(2,1)S(1)}, u32[]{:S(2)}, u32[]{:S(2)}) collective-permute-start(bf16[64,512]{1,0:T(8,128)(2,1)} %get-tuple-element.85), channel_id=1, source_target_pairs={{0,10},{1,11},{2,8},{3,9},{4,14},{5,15},{6,12},{7,13},{8,2},{9,3},... | collective-permute-start | bytes 196616 | tf_op jit(solution)/shard_map/ppermute | solution.py:468
  19.5 17.8 %collective-permute-start.10 = (bf16[64,512]{1,0:T(8,128)(2,1)}, bf16[64,512]{1,0:T(8,128)(2,1)S(1)}, u32[]{:S(2)}, u32[]{:S(2)}) collective-permute-start(bf16[64,512]{1,0:T(8,128)(2,1)} %get-tuple-element.86), channel_id=1, source_target_pairs={{0,11},{1,10},{2,9},{3,8},{4,15},{5,14},{6,13},{7,12},{8,3},{9,2},... | collective-permute-start | bytes 196616 | tf_op jit(solution)/shard_map/ppermute | solution.py:468
  20.4 16.8 %collective-permute-start.11 = (bf16[64,512]{1,0:T(8,128)(2,1)}, bf16[64,512]{1,0:T(8,128)(2,1)S(1)}, u32[]{:S(2)}, u32[]{:S(2)}) collective-permute-start(bf16[64,512]{1,0:T(8,128)(2,1)} %get-tuple-element.87), channel_id=1, source_target_pairs={{0,12},{1,13},{2,14},{3,15},{4,8},{5,9},{6,10},{7,11},{8,4},{9,5},... | collective-permute-start | bytes 196616 | tf_op jit(solution)/shard_map/ppermute | solution.py:468
  23.2 14.1 %collective-permute-start.12 = (bf16[64,512]{1,0:T(8,128)(2,1)}, bf16[64,512]{1,0:T(8,128)(2,1)S(1)}, u32[]{:S(2)}, u32[]{:S(2)}) collective-permute-start(bf16[64,512]{1,0:T(8,128)(2,1)} %get-tuple-element.88), channel_id=1, source_target_pairs={{0,13},{1,12},{2,15},{3,14},{4,9},{5,8},{6,11},{7,10},{8,5},{9,4},... | collective-permute-start | bytes 196616 | tf_op jit(solution)/shard_map/ppermute | solution.py:468
  28.3 9.0 %collective-permute-start.13 = (bf16[64,512]{1,0:T(8,128)(2,1)}, bf16[64,512]{1,0:T(8,128)(2,1)S(1)}, u32[]{:S(2)}, u32[]{:S(2)}) collective-permute-start(bf16[64,512]{1,0:T(8,128)(2,1)} %get-tuple-element.89), channel_id=1, source_target_pairs={{0,14},{1,15},{2,12},{3,13},{4,10},{5,11},{6,8},{7,9},{8,6},{9,7},... | collective-permute-start | bytes 196616 | tf_op jit(solution)/shard_map/ppermute | solution.py:468
  32.2 7.4 %collective-permute-start.14 = (bf16[64,512]{1,0:T(8,128)(2,1)}, bf16[64,512]{1,0:T(8,128)(2,1)S(1)}, u32[]{:S(2)}, u32[]{:S(2)}) collective-permute-start(bf16[64,512]{1,0:T(8,128)(2,1)} %get-tuple-element.90), channel_id=1, source_target_pairs={{0,15},{1,14},{2,13},{3,12},{4,11},{5,10},{6,9},{7,8},{8,7},{9,6},... | collective-permute-start | bytes 196616 | tf_op jit(solution)/shard_map/ppermute | solution.py:468
  43.2 7.0 %collective-permute-start.17 = (bf16[64,512]{1,0:T(8,128)(2,1)}, bf16[64,512]{1,0:T(8,128)(2,1)S(1)}, u32[]{:S(2)}, u32[]{:S(2)}) collective-permute-start(bf16[64,512]{1,0:T(8,128)(2,1)} %get-tuple-element.94), channel_id=1, source_target_pairs={{0,3},{1,2},{2,1},{3,0},{4,7},{5,6},{6,5},{7,4},{8,11},{9,10},{10,... | collective-permute-start | bytes 196616 | tf_op jit(solution)/shard_map/ppermute | solution.py:468
  45.0 8.1 %collective-permute-start.18 = (bf16[64,512]{1,0:T(8,128)(2,1)}, bf16[64,512]{1,0:T(8,128)(2,1)S(1)}, u32[]{:S(2)}, u32[]{:S(2)}) collective-permute-start(bf16[64,512]{1,0:T(8,128)(2,1)} %get-tuple-element.95), channel_id=1, source_target_pairs={{0,4},{1,5},{2,6},{3,7},{4,0},{5,1},{6,2},{7,3},{8,12},{9,13},{10,... | collective-permute-start | bytes 196616 | tf_op jit(solution)/shard_map/ppermute | solution.py:468
  47.8 7.9 %collective-permute-start.20 = (bf16[64,512]{1,0:T(8,128)(2,1)}, bf16[64,512]{1,0:T(8,128)(2,1)S(1)}, u32[]{:S(2)}, u32[]{:S(2)}) collective-permute-start(bf16[64,512]{1,0:T(8,128)(2,1)} %get-tuple-element.97), channel_id=1, source_target_pairs={{0,6},{1,7},{2,4},{3,5},{4,2},{5,3},{6,0},{7,1},{8,14},{9,15},{10,... | collective-permute-start | bytes 196616 | tf_op jit(solution)/shard_map/ppermute | solution.py:468
  49.5 7.5 %collective-permute-start.21 = (bf16[64,512]{1,0:T(8,128)(2,1)}, bf16[64,512]{1,0:T(8,128)(2,1)S(1)}, u32[]{:S(2)}, u32[]{:S(2)}) collective-permute-start(bf16[64,512]{1,0:T(8,128)(2,1)} %get-tuple-element.98), channel_id=1, source_target_pairs={{0,7},{1,6},{2,5},{3,4},{4,3},{5,2},{6,1},{7,0},{8,15},{9,14},{10,... | collective-permute-start | bytes 196616 | tf_op jit(solution)/shard_map/ppermute | solution.py:468
  50.2 8.6 %collective-permute-start.22 = (bf16[64,512]{1,0:T(8,128)(2,1)}, bf16[64,512]{1,0:T(8,128)(2,1)S(1)}, u32[]{:S(2)}, u32[]{:S(2)}) collective-permute-start(bf16[64,512]{1,0:T(8,128)(2,1)} %get-tuple-element.99), channel_id=1, source_target_pairs={{0,8},{1,9},{2,10},{3,11},{4,12},{5,13},{6,14},{7,15},{8,0},{9,1},... | collective-permute-start | bytes 196616 | tf_op jit(solution)/shard_map/ppermute | solution.py:468
  53.1 13.4 %collective-permute-start.23 = (bf16[64,512]{1,0:T(8,128)(2,1)}, bf16[64,512]{1,0:T(8,128)(2,1)S(1)}, u32[]{:S(2)}, u32[]{:S(2)}) collective-permute-start(bf16[64,512]{1,0:T(8,128)(2,1)} %get-tuple-element.100), channel_id=1, source_target_pairs={{0,9},{1,8},{2,11},{3,10},{4,13},{5,12},{6,15},{7,14},{8,1},{9,0},... | collective-permute-start | bytes 196616 | tf_op jit(solution)/shard_map/ppermute | solution.py:468
  53.2 15.5 %collective-permute-start.24 = (bf16[64,512]{1,0:T(8,128)(2,1)}, bf16[64,512]{1,0:T(8,128)(2,1)S(1)}, u32[]{:S(2)}, u32[]{:S(2)}) collective-permute-start(bf16[64,512]{1,0:T(8,128)(2,1)} %get-tuple-element.101), channel_id=1, source_target_pairs={{0,10},{1,11},{2,8},{3,9},{4,14},{5,15},{6,12},{7,13},{8,2},{9,3},... | collective-permute-start | bytes 196616 | tf_op jit(solution)/shard_map/ppermute | solution.py:468
  55.7 15.3 %collective-permute-start.25 = (bf16[64,512]{1,0:T(8,128)(2,1)}, bf16[64,512]{1,0:T(8,128)(2,1)S(1)}, u32[]{:S(2)}, u32[]{:S(2)}) collective-permute-start(bf16[64,512]{1,0:T(8,128)(2,1)} %get-tuple-element.102), channel_id=1, source_target_pairs={{0,11},{1,10},{2,9},{3,8},{4,15},{5,14},{6,13},{7,12},{8,3},{9,2},... | collective-permute-start | bytes 196616 | tf_op jit(solution)/shard_map/ppermute | solution.py:468
  57.0 14.0 %collective-permute-start.26 = (bf16[64,512]{1,0:T(8,128)(2,1)}, bf16[64,512]{1,0:T(8,128)(2,1)S(1)}, u32[]{:S(2)}, u32[]{:S(2)}) collective-permute-start(bf16[64,512]{1,0:T(8,128)(2,1)} %get-tuple-element.103), channel_id=1, source_target_pairs={{0,12},{1,13},{2,14},{3,15},{4,8},{5,9},{6,10},{7,11},{8,4},{9,5},... | collective-permute-start | bytes 196616 | tf_op jit(solution)/shard_map/ppermute | solution.py:468
  58.8 12.2 %collective-permute-start.27 = (bf16[64,512]{1,0:T(8,128)(2,1)}, bf16[64,512]{1,0:T(8,128)(2,1)S(1)}, u32[]{:S(2)}, u32[]{:S(2)}) collective-permute-start(bf16[64,512]{1,0:T(8,128)(2,1)} %get-tuple-element.104), channel_id=1, source_target_pairs={{0,13},{1,12},{2,15},{3,14},{4,9},{5,8},{6,11},{7,10},{8,5},{9,4},... | collective-permute-start | bytes 196616 | tf_op jit(solution)/shard_map/ppermute | solution.py:468
  66.4 7.6 %collective-permute-start.28 = (bf16[64,512]{1,0:T(8,128)(2,1)}, bf16[64,512]{1,0:T(8,128)(2,1)S(1)}, u32[]{:S(2)}, u32[]{:S(2)}) collective-permute-start(bf16[64,512]{1,0:T(8,128)(2,1)} %get-tuple-element.105), channel_id=1, source_target_pairs={{0,14},{1,15},{2,12},{3,13},{4,10},{5,11},{6,8},{7,9},{8,6},{9,7},... | collective-permute-start | bytes 196616 | tf_op jit(solution)/shard_map/ppermute | solution.py:468
  68.7 6.9 %collective-permute-start.29 = (bf16[64,512]{1,0:T(8,128)(2,1)}, bf16[64,512]{1,0:T(8,128)(2,1)S(1)}, u32[]{:S(2)}, u32[]{:S(2)}) collective-permute-start(bf16[64,512]{1,0:T(8,128)(2,1)} %get-tuple-element.106), channel_id=1, source_target_pairs={{0,15},{1,14},{2,13},{3,12},{4,11},{5,10},{6,9},{7,8},{8,7},{9,6},... | collective-permute-start | bytes 196616 | tf_op jit(solution)/shard_map/ppermute | solution.py:468
  91.9 8.4 %collective-permute-start.61 = (bf16[256,512]{1,0:T(8,128)(2,1)S(1)}, bf16[256,512]{1,0:T(8,128)(2,1)S(1)}, u32[]{:S(2)}, u32[]{:S(2)}) collective-permute-start(bf16[256,512]{1,0:T(8,128)(2,1)S(1)} %fusion.1), channel_id=1, source_target_pairs={{0,2},{1,3},{2,0},{3,1},{4,6},{5,7},{6,4},{7,5},{8,10},{9,11},{10,... | collective-permute-start | bytes 786440 | tf_op jit(solution)/shard_map/ppermute | solution.py:414
  129.2 53.4 %collective-permute-start.67 = (bf16[512,512]{1,0:T(8,128)(2,1)S(1)}, bf16[512,512]{1,0:T(8,128)(2,1)S(1)}, u32[]{:S(2)}, u32[]{:S(2)}) collective-permute-start(bf16[512,512]{1,0:T(8,128)(2,1)S(1)} %pad_maximum_fusion.1), channel_id=1, source_target_pairs={{0,1},{1,0},{2,3},{3,2},{4,5},{5,4},{6,7},{7,6},{8,9},{9,8},{10,11... | collective-permute-start | bytes 1572872 | tf_op jit(solution)/shard_map/ppermute | solution.py:419
  131.2 6.8 %collective-permute-start.33 = (bf16[64,512]{1,0:T(8,128)(2,1)S(1)}, bf16[64,512]{1,0:T(8,128)(2,1)S(1)}, u32[]{:S(2)}, u32[]{:S(2)}) collective-permute-start(bf16[64,512]{1,0:T(8,128)(2,1)S(1)} %copy-done.42), channel_id=1, source_target_pairs={{0,4},{1,5},{2,6},{3,7},{4,0},{5,1},{6,2},{7,3},{8,12},{9,13},{10,... | collective-permute-start | bytes 196616 | tf_op jit(solution)/shard_map/ppermute | solution.py:468
  138.0 12.0 %collective-permute-start.37 = (bf16[64,512]{1,0:T(8,128)(2,1)S(1)}, bf16[64,512]{1,0:T(8,128)(2,1)S(1)}, u32[]{:S(2)}, u32[]{:S(2)}) collective-permute-start(bf16[64,512]{1,0:T(8,128)(2,1)S(1)} %copy-done.38), channel_id=1, source_target_pairs={{0,8},{1,9},{2,10},{3,11},{4,12},{5,13},{6,14},{7,15},{8,0},{9,1},... | collective-permute-start | bytes 196616 | tf_op jit(solution)/shard_map/ppermute | solution.py:468
  139.2 12.8 %collective-permute-start.38 = (bf16[64,512]{1,0:T(8,128)(2,1)S(1)}, bf16[64,512]{1,0:T(8,128)(2,1)S(1)}, u32[]{:S(2)}, u32[]{:S(2)}) collective-permute-start(bf16[64,512]{1,0:T(8,128)(2,1)S(1)} %copy-done.37), channel_id=1, source_target_pairs={{0,9},{1,8},{2,11},{3,10},{4,13},{5,12},{6,15},{7,14},{8,1},{9,0},... | collective-permute-start | bytes 196616 | tf_op jit(solution)/shard_map/ppermute | solution.py:468
  140.5 12.5 %collective-permute-start.39 = (bf16[64,512]{1,0:T(8,128)(2,1)S(1)}, bf16[64,512]{1,0:T(8,128)(2,1)S(1)}, u32[]{:S(2)}, u32[]{:S(2)}) collective-permute-start(bf16[64,512]{1,0:T(8,128)(2,1)S(1)} %copy-done.36), channel_id=1, source_target_pairs={{0,10},{1,11},{2,8},{3,9},{4,14},{5,15},{6,12},{7,13},{8,2},{9,3},... | collective-permute-start | bytes 196616 | tf_op jit(solution)/shard_map/ppermute | solution.py:468
  142.8 12.9 %collective-permute-start.40 = (bf16[64,512]{1,0:T(8,128)(2,1)S(1)}, bf16[64,512]{1,0:T(8,128)(2,1)S(1)}, u32[]{:S(2)}, u32[]{:S(2)}) collective-permute-start(bf16[64,512]{1,0:T(8,128)(2,1)S(1)} %copy-done.35), channel_id=1, source_target_pairs={{0,11},{1,10},{2,9},{3,8},{4,15},{5,14},{6,13},{7,12},{8,3},{9,2},... | collective-permute-start | bytes 196616 | tf_op jit(solution)/shard_map/ppermute | solution.py:468
  150.0 8.2 %collective-permute-start.41 = (bf16[64,512]{1,0:T(8,128)(2,1)S(1)}, bf16[64,512]{1,0:T(8,128)(2,1)S(1)}, u32[]{:S(2)}, u32[]{:S(2)}) collective-permute-start(bf16[64,512]{1,0:T(8,128)(2,1)S(1)} %copy-done.34), channel_id=1, source_target_pairs={{0,12},{1,13},{2,14},{3,15},{4,8},{5,9},{6,10},{7,11},{8,4},{9,5},... | collective-permute-start | bytes 196616 | tf_op jit(solution)/shard_map/ppermute | solution.py:468
  153.0 7.7 %collective-permute-start.43 = (bf16[64,512]{1,0:T(8,128)(2,1)S(1)}, bf16[64,512]{1,0:T(8,128)(2,1)S(1)}, u32[]{:S(2)}, u32[]{:S(2)}) collective-permute-start(bf16[64,512]{1,0:T(8,128)(2,1)S(1)} %copy-done.32), channel_id=1, source_target_pairs={{0,14},{1,15},{2,12},{3,13},{4,10},{5,11},{6,8},{7,9},{8,6},{9,7},... | collective-permute-start | bytes 196616 | tf_op jit(solution)/shard_map/ppermute | solution.py:468
  166.5 10.5 %collective-permute-start.46 = (bf16[64,512]{1,0:T(8,128)(2,1)}, bf16[64,512]{1,0:T(8,128)(2,1)S(1)}, u32[]{:S(2)}, u32[]{:S(2)}) collective-permute-start(bf16[64,512]{1,0:T(8,128)(2,1)} %get-tuple-element.125), channel_id=1, source_target_pairs={{0,2},{1,3},{2,0},{3,1},{4,6},{5,7},{6,4},{7,5},{8,10},{9,11},{10,... | collective-permute-start | bytes 196616 | tf_op jit(solution)/shard_map/ppermute | solution.py:468
  167.5 11.7 %collective-permute-start.47 = (bf16[64,512]{1,0:T(8,128)(2,1)}, bf16[64,512]{1,0:T(8,128)(2,1)S(1)}, u32[]{:S(2)}, u32[]{:S(2)}) collective-permute-start(bf16[64,512]{1,0:T(8,128)(2,1)} %get-tuple-element.126), channel_id=1, source_target_pairs={{0,3},{1,2},{2,1},{3,0},{4,7},{5,6},{6,5},{7,4},{8,11},{9,10},{10,... | collective-permute-start | bytes 196616 | tf_op jit(solution)/shard_map/ppermute | solution.py:468
  167.9 11.6 %collective-permute-start.48 = (bf16[64,512]{1,0:T(8,128)(2,1)}, bf16[64,512]{1,0:T(8,128)(2,1)S(1)}, u32[]{:S(2)}, u32[]{:S(2)}) collective-permute-start(bf16[64,512]{1,0:T(8,128)(2,1)} %get-tuple-element.127), channel_id=1, source_target_pairs={{0,4},{1,5},{2,6},{3,7},{4,0},{5,1},{6,2},{7,3},{8,12},{9,13},{10,... | collective-permute-start | bytes 196616 | tf_op jit(solution)/shard_map/ppermute | solution.py:468
  170.5 11.0 %collective-permute-start.49 = (bf16[64,512]{1,0:T(8,128)(2,1)}, bf16[64,512]{1,0:T(8,128)(2,1)S(1)}, u32[]{:S(2)}, u32[]{:S(2)}) collective-permute-start(bf16[64,512]{1,0:T(8,128)(2,1)} %get-tuple-element.128), channel_id=1, source_target_pairs={{0,5},{1,4},{2,7},{3,6},{4,1},{5,0},{6,3},{7,2},{8,13},{9,12},{10,... | collective-permute-start | bytes 196616 | tf_op jit(solution)/shard_map/ppermute | solution.py:468
  177.0 8.4 %collective-permute-start.50 = (bf16[64,512]{1,0:T(8,128)(2,1)S(1)}, bf16[64,512]{1,0:T(8,128)(2,1)S(1)}, u32[]{:S(2)}, u32[]{:S(2)}) collective-permute-start(bf16[64,512]{1,0:T(8,128)(2,1)S(1)} %copy-done.68), channel_id=1, source_target_pairs={{0,6},{1,7},{2,4},{3,5},{4,2},{5,3},{6,0},{7,1},{8,14},{9,15},{10,... | collective-permute-start | bytes 196616 | tf_op jit(solution)/shard_map/ppermute | solution.py:468
  179.2 7.0 %collective-permute-start.51 = (bf16[64,512]{1,0:T(8,128)(2,1)S(1)}, bf16[64,512]{1,0:T(8,128)(2,1)S(1)}, u32[]{:S(2)}, u32[]{:S(2)}) collective-permute-start(bf16[64,512]{1,0:T(8,128)(2,1)S(1)} %copy-done.66), channel_id=1, source_target_pairs={{0,7},{1,6},{2,5},{3,4},{4,3},{5,2},{6,1},{7,0},{8,15},{9,14},{10,... | collective-permute-start | bytes 196616 | tf_op jit(solution)/shard_map/ppermute | solution.py:468
  179.5 11.5 %collective-permute-start.52 = (bf16[64,512]{1,0:T(8,128)(2,1)S(1)}, bf16[64,512]{1,0:T(8,128)(2,1)S(1)}, u32[]{:S(2)}, u32[]{:S(2)}) collective-permute-start(bf16[64,512]{1,0:T(8,128)(2,1)S(1)} %copy-done.64), channel_id=1, source_target_pairs={{0,8},{1,9},{2,10},{3,11},{4,12},{5,13},{6,14},{7,15},{8,0},{9,1},... | collective-permute-start | bytes 196616 | tf_op jit(solution)/shard_map/ppermute | solution.py:468
  181.6 11.8 %collective-permute-start.53 = (bf16[64,512]{1,0:T(8,128)(2,1)S(1)}, bf16[64,512]{1,0:T(8,128)(2,1)S(1)}, u32[]{:S(2)}, u32[]{:S(2)}) collective-permute-start(bf16[64,512]{1,0:T(8,128)(2,1)S(1)} %copy-done.62), channel_id=1, source_target_pairs={{0,9},{1,8},{2,11},{3,10},{4,13},{5,12},{6,15},{7,14},{8,1},{9,0},... | collective-permute-start | bytes 196616 | tf_op jit(solution)/shard_map/ppermute | solution.py:468
  182.5 14.5 %collective-permute-start.54 = (bf16[64,512]{1,0:T(8,128)(2,1)S(1)}, bf16[64,512]{1,0:T(8,128)(2,1)S(1)}, u32[]{:S(2)}, u32[]{:S(2)}) collective-permute-start(bf16[64,512]{1,0:T(8,128)(2,1)S(1)} %copy-done.60), channel_id=1, source_target_pairs={{0,10},{1,11},{2,8},{3,9},{4,14},{5,15},{6,12},{7,13},{8,2},{9,3},... | collective-permute-start | bytes 196616 | tf_op jit(solution)/shard_map/ppermute | solution.py:468
  185.4 14.4 %collective-permute-start.55 = (bf16[64,512]{1,0:T(8,128)(2,1)S(1)}, bf16[64,512]{1,0:T(8,128)(2,1)S(1)}, u32[]{:S(2)}, u32[]{:S(2)}) collective-permute-start(bf16[64,512]{1,0:T(8,128)(2,1)S(1)} %copy-done.56), channel_id=1, source_target_pairs={{0,11},{1,10},{2,9},{3,8},{4,15},{5,14},{6,13},{7,12},{8,3},{9,2},... | collective-permute-start | bytes 196616 | tf_op jit(solution)/shard_map/ppermute | solution.py:468
  186.1 13.7 %collective-permute-start.56 = (bf16[64,512]{1,0:T(8,128)(2,1)S(1)}, bf16[64,512]{1,0:T(8,128)(2,1)S(1)}, u32[]{:S(2)}, u32[]{:S(2)}) collective-permute-start(bf16[64,512]{1,0:T(8,128)(2,1)S(1)} %copy-done.53), channel_id=1, source_target_pairs={{0,12},{1,13},{2,14},{3,15},{4,8},{5,9},{6,10},{7,11},{8,4},{9,5},... | collective-permute-start | bytes 196616 | tf_op jit(solution)/shard_map/ppermute | solution.py:468
  191.0 8.9 %collective-permute-start.57 = (bf16[64,512]{1,0:T(8,128)(2,1)S(1)}, bf16[64,512]{1,0:T(8,128)(2,1)S(1)}, u32[]{:S(2)}, u32[]{:S(2)}) collective-permute-start(bf16[64,512]{1,0:T(8,128)(2,1)S(1)} %copy-done.52), channel_id=1, source_target_pairs={{0,13},{1,12},{2,15},{3,14},{4,9},{5,8},{6,11},{7,10},{8,5},{9,4},... | collective-permute-start | bytes 196616 | tf_op jit(solution)/shard_map/ppermute | solution.py:468
  193.4 7.5 %collective-permute-start.58 = (bf16[64,512]{1,0:T(8,128)(2,1)S(1)}, bf16[64,512]{1,0:T(8,128)(2,1)S(1)}, u32[]{:S(2)}, u32[]{:S(2)}) collective-permute-start(bf16[64,512]{1,0:T(8,128)(2,1)S(1)} %copy-done.50), channel_id=1, source_target_pairs={{0,14},{1,15},{2,12},{3,13},{4,10},{5,11},{6,8},{7,9},{8,6},{9,7},... | collective-permute-start | bytes 196616 | tf_op jit(solution)/shard_map/ppermute | solution.py:468
  197.0 7.2 %collective-permute-start.59 = (bf16[64,512]{1,0:T(8,128)(2,1)S(1)}, bf16[64,512]{1,0:T(8,128)(2,1)S(1)}, u32[]{:S(2)}, u32[]{:S(2)}) collective-permute-start(bf16[64,512]{1,0:T(8,128)(2,1)S(1)} %copy-done.48), channel_id=1, source_target_pairs={{0,15},{1,14},{2,13},{3,12},{4,11},{5,10},{6,9},{7,8},{8,7},{9,6},... | collective-permute-start | bytes 196616 | tf_op jit(solution)/shard_map/ppermute | solution.py:468
  (106 other events, 1587.7 us)

commit v4 on v1

--- a/solution.py
+++ b/solution.py
@@ -331,27 +331,40 @@
     )(*operands)
 
 
-def sum_over(values, count):
-    if count & (count - 1) or values.shape[0] % count:
-        return lax.psum(values, "seq")
-    me = lax.axis_index("seq")
-    total = values
-    steps = [1 << s for s in range(count.bit_length() - 1)]
-    for step in steps:
-        halves = total.reshape(2, total.shape[0] // 2, total.shape[1])
-        mine = (me // step) % 2
-        keep = lax.dynamic_index_in_dim(halves, mine, 0, keepdims=False)
-        send = lax.dynamic_index_in_dim(halves, 1 - mine, 0, keepdims=False).astype(BF)
-        got = lax.ppermute(send, "seq", [(i, i ^ step) for i in range(count)])
-        total = keep + got.astype(F32)
-    total = total.astype(BF)
-    for step in reversed(steps):
-        mine = (me // step) % 2
-        got = lax.ppermute(total, "seq", [(i, i ^ step) for i in range(count)])
-        low = jnp.where(mine == 0, total, got)
-        high = jnp.where(mine == 0, got, total)
-        total = jnp.concatenate([low, high], axis=0)
-    return total
+def radices(count):
+    steps, stride = [], 1
+    while stride < count:
+        radix = 4 if stride >= 4 and count // stride == 4 else 2
+        steps.append((stride, radix))
+        stride *= radix
+    return steps
+
+
+def swap(values, count, stride, s):
+    return lax.ppermute(values, "seq", [(i, i ^ (stride * s)) for i in range(count)])
+
+
+def scatter_step(total, count, stride, radix):
+    digit = (lax.axis_index("seq") // stride) % radix
+    cut = total.reshape(radix, total.shape[0] // radix, total.shape[1])
+    kept = lax.dynamic_index_in_dim(cut, digit, 0, keepdims=False)
+    for s in range(1, radix):
+        send = lax.dynamic_index_in_dim(cut, digit ^ s, 0, keepdims=False).astype(BF)
+        kept = kept + swap(send, count, stride, s).astype(F32)
+    return kept
+
+
+def gather_step(share, count, stride, radix):
+    digit = (lax.axis_index("seq") // stride) % radix
+    got = [share] + [swap(share, count, stride, s) for s in range(1, radix)]
+    if radix == 2:
+        low = jnp.where(digit == 0, got[0], got[1])
+        high = jnp.where(digit == 0, got[1], got[0])
+        return jnp.concatenate([low, high], axis=0)
+    whole = jnp.zeros((radix,) + share.shape, share.dtype)
+    for s in range(radix):
+        whole = lax.dynamic_update_index_in_dim(whole, got[s], digit ^ s, 0)
+    return whole.reshape(radix * share.shape[0], share.shape[1])
 
 
 def write_weights(total, up_shape, down_shape, scale):
@@ -389,6 +402,10 @@
     scale = float(count * tokens.shape[0]) ** (-0.5)
     factor = factor_one.reshape(block, block)
     pieces = range(plan.pieces)
+    tokens, cotangent, factor, up_blocks, down_blocks = (
+        pltpu.with_memory_space_constraint(a, pltpu.HBM)
+        for a in (tokens, cotangent, factor, up_blocks, down_blocks)
+    )
 
     def exchange(rows):
         cut = rows.reshape(count, plan.part, channels)
@@ -425,9 +442,17 @@
         )
         grad_mixed.append(exchange(dv))
         gate_grads.append(r)
-    grad_firsts = [exchange(second(grad_mixed[q], q, True)) for q in pieces]
+    total = weights.reshape(-1, weights.shape[-1])
+    steps = radices(count)
+    for step in steps:
+        total = scatter_step(total, count, *step)
+    total = total.astype(BF)
+    back = [second(grad_mixed[q], q, True) for q in pieces]
+    back, total = lax.optimization_barrier((back, total))
+    for step in reversed(steps):
+        total = gather_step(total, count, *step)
+    grad_firsts = [exchange(b) for b in back]
     two = [second_grad(grad_mixed[q], firsts[q]) for q in pieces]
-    total = sum_over(weights.reshape(-1, weights.shape[-1]), count)
     grad_up, grad_down = write_weights(total, up_blocks.shape, down_blocks.shape, scale)
     one, tokens_sum = None, None
     for q in pieces:

time: 174 us -> 163 us (0.937)
  blocking collectives: 0 us -> 31.5 us
  waiting for transfers between devices: 86.8 us -> 56.7 us
  local copies, waits for them, and re-layouts: 19.6 us -> 9.39 us
  starting transfers between devices: 38.4 us -> 30.4 us
  Pallas kernels: 23.4 us -> 27.5 us
    all_to_all x0 -> x1, blocking collectives: none -> 31.5 us  [exchange(): got = lax.all_to_all(cut, 'seq', split_axis=0, concat_axis=0, tiled=True)]
    all_to_all x4 -> x3, waiting for transfers between devices: 44.8 us -> 21.9 us  [exchange(): got = lax.all_to_all(cut, 'seq', split_axis=0, concat_axis=0, tiled=True)]
    unnamed x36 -> x14, local copies, waits for them, and re-layouts: 18 us -> 6.45 us
    all_to_all x4 -> x3, starting transfers between devices: 25.3 us -> 16.8 us  [exchange(): got = lax.all_to_all(cut, 'seq', split_axis=0, concat_axis=0, tiled=True)]
    ppermute x8 -> x10, waiting for transfers between devices: 42.1 us -> 34.8 us  [swap(): lax.ppermute(values, 'seq', [(i, i ^ stride * s) for i in range(count)])]
    pallas_call x1, Pallas kernels: 1.76 us -> 4.76 us  [mix_first(): pl.pallas_call(body, grid=(plan.rows // step,), in_specs=[plan.spec(step,...]
    ppermute x8 -> x10, starting transfers between devices: 13 us -> 13.5 us  [swap(): lax.ppermute(values, 'seq', [(i, i ^ stride * s) for i in range(count)])]
  transfers between devices with their start and end apart: 12 -> 13, of which waited for: 8 -> 6; matrix products, arithmetic and copies ran while one was open for 3% -> 5% of each run, Pallas kernels for 4% -> 3%
where the time goes in v4:
time: 163 us; the launch traced here: 161 us
  waiting for transfers between devices  56.7 us (35%)
  blocking collectives  31.5 us (19%)
  starting transfers between devices  30.4 us (19%)
  Pallas kernels  27.5 us (17%)
  local copies, waits for them, and re-layouts  9.39 us (6%)
  other arithmetic  4.87 us (3%)
    ppermute x10, waiting for transfers between devices, swap(): lax.ppermute(values, 'seq', [(i, i ^ stride * s) for i in range(count)])  34.8 us
    all_to_all x1, blocking collectives, exchange(): got = lax.all_to_all(cut, 'seq', split_axis=0, concat_axis=0, tiled=True)  31.5 us
    all_to_all x3, waiting for transfers between devices, exchange(): got = lax.all_to_all(cut, 'seq', split_axis=0, concat_axis=0, tiled=True)  21.9 us
    all_to_all x3, starting transfers between devices, exchange(): got = lax.all_to_all(cut, 'seq', split_axis=0, concat_axis=0, tiled=True)  16.8 us
    ppermute x10, starting transfers between devices, swap(): lax.ppermute(values, 'seq', [(i, i ^ stride * s) for i in range(count)])  13.5 us
    pallas_call x1, Pallas kernels, middle(): pl.pallas_call(body, grid=(plan.rows // step,), in_specs=in_specs, out_sp...  8.45 us
    pallas_call x1, Pallas kernels, finish(): pl.pallas_call(body, grid=(plan.block // step,), in_specs=in_specs, out_s...  6.56 us
    unnamed x14, local copies, waits for them, and re-layouts  6.45 us
  transfers between devices with their start and end apart: 13, of which 6 were waited for; matrix products, arithmetic and copies ran while one was open for 5% of the time, Pallas kernels for 3%

profile of v4, /device:TPU:0, one launch (start us, length us, event | category | flops | bytes accessed | tf_op | source)
XLA Modules:
  0.0 161.3 jit_solution(16560070112072433896)
XLA Ops:
  0.6 4.8 %mix_first.1 = bf16[1024,512]{1,0:T(8,128)(2,1)} custom-call(bf16[1024,1024]{1,0:T(8,128)(2,1)} %bitcast.62, bf16[1024,512]{1,0:T(8,128)(2,1)} %refs_2_.1), custom_call_target="tpu_custom_call" | custom-call | flops 1073741824 | bytes 4194304 | tf_op jit(solution)/shard_map/mix_first/pallas_call | solution.py:69
  5.4 7.5 %all-to-all-start = ((bf16[16,64,512]{2,1,0:T(8,128)(2,1)}), bf16[16,64,512]{2,1,0:T(8,128)(2,1)S(1)}, u32[]{:S(2)}, u32[]{:S(2)}) async-start(bf16[16,64,512]{2,1,0:T(8,128)(2,1)} %bitcast.3), calls=%async_computation | async-start | bytes 2097152 | tf_op jit(solution)/shard_map/all_to_all | solution.py:412
  12.9 0.2 reshape.61
  13.1 0.2 copy.11
  13.3 0.7 spread_factor.1.m_ref
  14.0 21.9 %all-to-all-done.in_ref.u_ref = bf16[16,64,512]{2,1,0:T(8,128)(2,1)S(1)} async-done(((bf16[16,64,512]{2,1,0:T(8,128)(2,1)}), bf16[16,64,512]{2,1,0:T(8,128)(2,1)S(1)}, u32[]{:S(2)}, u32[]{:S(2)}) %all-to-all-start) | async-done | bytes 1048608 | tf_op jit(solution)/shard_map/all_to_all | solution.py:412
  35.8 1.1 mix_second.1
  36.9 31.5 %all_to_all.20 = bf16[16,64,512]{2,1,0:T(8,128)(2,1)S(1)} all-to-all(bf16[16,64,512]{2,1,0:T(8,128)(2,1)S(1)} %mix_second.1), channel_id=1, replica_groups=mesh['grp'=2,'seq'=16] {'seq'}, dimensions={0} | all-to-all | bytes 2097152 | tf_op jit(solution)/shard_map/all_to_all | solution.py:412
  68.4 8.4 %middle.1 = (bf16[1024,512]{1,0:T(8,128)(2,1)S(1)}, bf16[1024,512]{1,0:T(8,128)(2,1)S(1)}, f32[8,128,512]{2,1,0:T(8,128)S(1)}) custom-call(bf16[1024,512]{1,0:T(8,128)(2,1)} %refs_2_.1, bf16[1024,512]{1,0:T(8,128)(2,1)} %refs_1_.1, bf16[1024,512]{1,0:T(8,128)(2,1)S(1)} %bitcast.59, bf16[4,128,512]{2,1,0:T(8,128)(2,1)} %refs_3_.1, bf16[4,512,128]{2,1,0:T(8,128)(2,1)} %refs_4_.1), custom_call_target="tpu_custom_call" | custom-call | flops 2684354560 | bytes 7340032 | tf_op jit(solution)/shard_map/middle/pallas_call | solution.py:237
  76.9 0.0 copy-start.1
  76.9 1.3 copy-done.1
  78.2 1.0 copy-done.2
  79.2 1.0 copy-done.3
  80.2 5.0 %all-to-all-start.2 = ((bf16[16,64,512]{2,1,0:T(8,128)(2,1)}), bf16[16,64,512]{2,1,0:T(8,128)(2,1)S(1)}, u32[]{:S(2)}, u32[]{:S(2)}) async-start(bf16[16,64,512]{2,1,0:T(8,128)(2,1)} %bitcast.58), calls=%async_computation.2 | async-start | bytes 2097152 | tf_op jit(solution)/shard_map/all_to_all | solution.py:412
  85.2 1.3 fusion
  86.5 0.5 collective-permute-start
  86.9 1.7 %collective-permute-done = bf16[512,512]{1,0:T(8,128)(2,1)} collective-permute-done((bf16[512,512]{1,0:T(8,128)(2,1)S(1)}, bf16[512,512]{1,0:T(8,128)(2,1)}, u32[]{:S(2)}, u32[]{:S(2)}) %collective-permute-start) | collective-permute-done | bytes 524320 | tf_op jit(solution)/shard_map/ppermute | solution.py:344
  88.6 1.5 bitcast_add_fusion
  90.2 0.0 copy-start.5
  90.2 1.0 copy-done.5
  91.2 2.0 %collective-permute-start.1 = (bf16[256,512]{1,0:T(8,128)(2,1)S(1)}, bf16[256,512]{1,0:T(8,128)(2,1)S(1)}, u32[]{:S(2)}, u32[]{:S(2)}) collective-permute-start(bf16[256,512]{1,0:T(8,128)(2,1)S(1)} %fusion.1), channel_id=1, source_target_pairs={{0,2},{1,3},{2,0},{3,1},{4,6},{5,7},{6,4},{7,5},{8,10},{9,11},{10,... | collective-permute-start | bytes 786440 | tf_op jit(solution)/shard_map/ppermute | solution.py:344
  93.1 10.6 %collective-permute-done.1 = bf16[256,512]{1,0:T(8,128)(2,1)S(1)} collective-permute-done((bf16[256,512]{1,0:T(8,128)(2,1)S(1)}, bf16[256,512]{1,0:T(8,128)(2,1)S(1)}, u32[]{:S(2)}, u32[]{:S(2)}) %collective-permute-start.1) | collective-permute-done | bytes 262176 | tf_op jit(solution)/shard_map/ppermute | solution.py:344
  103.7 1.1 bitcast_add_fusion.1
  104.9 3.5 %collective-permute-start.4 = (bf16[64,512]{1,0:T(8,128)(2,1)S(1)}, bf16[64,512]{1,0:T(8,128)(2,1)S(1)}, u32[]{:S(2)}, u32[]{:S(2)}) collective-permute-start(bf16[64,512]{1,0:T(8,128)(2,1)S(1)} %get-tuple-element.28), channel_id=1, source_target_pairs={{0,12},{1,13},{2,14},{3,15},{4,8},{5,9},{6,10},{7,11},{8,4},{9,5},... | collective-permute-start | bytes 196616 | tf_op jit(solution)/shard_map/ppermute | solution.py:344
  108.3 1.5 collective-permute-start.3
  109.8 0.0 collective-permute-start.2
  109.8 1.6 collective-permute-done.4
  111.4 6.0 %collective-permute-done.3 = bf16[64,512]{1,0:T(8,128)(2,1)S(1)} collective-permute-done((bf16[64,512]{1,0:T(8,128)(2,1)S(1)}, bf16[64,512]{1,0:T(8,128)(2,1)S(1)}, u32[]{:S(2)}, u32[]{:S(2)}) %collective-permute-start.3) | collective-permute-done | bytes 65568 | tf_op jit(solution)/shard_map/ppermute | solution.py:344
  117.4 0.0 all-to-all-done.2.in_ref.g_ref
  117.4 1.2 mix_second_back.1
  118.6 0.0 copy-start
  118.6 1.0 copy-done
  119.6 0.0 collective-permute-start.5
  119.6 2.0 %collective-permute-start.6 = (bf16[64,512]{1,0:T(8,128)(2,1)S(1)}, bf16[64,512]{1,0:T(8,128)(2,1)S(1)}, u32[]{:S(2)}, u32[]{:S(2)}) collective-permute-start(bf16[64,512]{1,0:T(8,128)(2,1)S(1)} %fusion.4), channel_id=1, source_target_pairs={{0,8},{1,9},{2,10},{3,11},{4,12},{5,13},{6,14},{7,15},{8,0},{9,1},... | collective-permute-start | bytes 196616 | tf_op jit(solution)/shard_map/ppermute | solution.py:344
  121.6 2.4 %collective-permute-start.7 = (bf16[64,512]{1,0:T(8,128)(2,1)S(1)}, bf16[64,512]{1,0:T(8,128)(2,1)S(1)}, u32[]{:S(2)}, u32[]{:S(2)}) collective-permute-start(bf16[64,512]{1,0:T(8,128)(2,1)S(1)} %fusion.4), channel_id=1, source_target_pairs={{0,12},{1,13},{2,14},{3,15},{4,8},{5,9},{6,10},{7,11},{8,4},{9,5},... | collective-permute-start | bytes 196616 | tf_op jit(solution)/shard_map/ppermute | solution.py:344
  123.9 4.3 %all-to-all-start.3 = ((bf16[16,64,512]{2,1,0:T(8,128)(2,1)}), bf16[16,64,512]{2,1,0:T(8,128)(2,1)}, u32[]{:S(2)}, u32[]{:S(2)}) async-start(bf16[16,64,512]{2,1,0:T(8,128)(2,1)} %copy-done), calls=%async_computation.3 | async-start | bytes 2097152 | tf_op jit(solution)/shard_map/all_to_all | solution.py:412
  128.4 1.8 %collective-permute-start.8 = (bf16[256,512]{1,0:T(8,128)(2,1)S(1)}, bf16[256,512]{1,0:T(8,128)(2,1)S(1)}, u32[]{:S(2)}, u32[]{:S(2)}) collective-permute-start(bf16[256,512]{1,0:T(8,128)(2,1)S(1)} %bitcast.66), channel_id=1, source_target_pairs={{0,2},{1,3},{2,0},{3,1},{4,6},{5,7},{6,4},{7,5},{8,10},{9,11},{10,... | collective-permute-start | bytes 786440 | tf_op jit(solution)/shard_map/ppermute | solution.py:344
  130.2 15.0 %collective-permute-done.8 = bf16[256,512]{1,0:T(8,128)(2,1)S(1)} collective-permute-done((bf16[256,512]{1,0:T(8,128)(2,1)S(1)}, bf16[256,512]{1,0:T(8,128)(2,1)S(1)}, u32[]{:S(2)}, u32[]{:S(2)}) %collective-permute-start.8) | collective-permute-done | bytes 262176 | tf_op jit(solution)/shard_map/ppermute | solution.py:344
  145.3 0.1 broadcast_select_fusion.3
  145.3 0.8 pad_maximum_fusion.1
  146.2 2.9 %grad_second.1 = f32[4,256,16]{2,1,0:T(8,128)S(1)} custom-call(bf16[16,64,512]{2,1,0:T(8,128)(2,1)S(1)} %all-to-all-done.2.in_ref.g_ref, bf16[16,64,512]{2,1,0:T(8,128)(2,1)S(1)} %all-to-all-done.in_ref.u_ref), custom_call_target="tpu_custom_call" | custom-call | flops 268435456 | bytes 2097152 | tf_op jit(solution)/shard_map/grad_second/pallas_call | solution.py:160
  149.1 0.2 copy.12
  149.4 1.2 broadcast_select_fusion.1
  150.6 0.1 pad_maximum_fusion.up_in.down_in
  150.7 0.9 reshape.73
  151.6 1.9 %write_weights.1 = (f32[4,128,512]{2,1,0:T(8,128)}, f32[4,512,128]{2,1,0:T(8,128)}) custom-call(bf16[1024,512]{1,0:T(8,128)(2,1)S(1)} %pad_maximum_fusion.up_in.down_in, bf16[1024,512]{1,0:T(8,128)(2,1)S(1)} %pad_maximum_fusion.up_in.down_in), custom_call_target="tpu_custom_call" | custom-call | flops 262144 | bytes 3145728 | tf_op jit(solution)/shard_map/write_weights/pallas_call | solution.py:377
  153.5 1.2 copy-done.4
  154.7 6.6 %finish.1 = (f32[1024,1024]{1,0:T(8,128)}, bf16[1024,512]{1,0:T(8,128)(2,1)}) custom-call(bf16[1024,1024]{1,0:T(8,128)(2,1)} %bitcast.63, bf16[1024,512]{1,0:T(8,128)(2,1)} %bitcast.19.refs_1_, bf16[1024,512]{1,0:T(8,128)(2,1)} %refs_2_.1, bf16[1024,512]{1,0:T(8,128)(2,1)S(1)} %copy-done.4), custom_call_target="tpu_custom_call" | custom-call | flops 2147483648 | bytes 10485760 | tf_op jit(solution)/shard_map/finish/pallas_call | solution.py:315
  (20 shorter events, 0.2 us)
Async XLA Ops:
  5.4 7.5 %copy-start.6 = (bf16[64,16,16]{0,2,1:T(8,128)(2,1)S(1)}, bf16[64,16,16]{0,2,1:T(8,128)(2,1)}, u32[]{:S(2)}) copy-start(bf16[64,16,16]{0,2,1:T(8,128)(2,1)} %param.9) | copy-start | bytes 98308
  5.4 30.4 %all-to-all-start = ((bf16[16,64,512]{2,1,0:T(8,128)(2,1)}), bf16[16,64,512]{2,1,0:T(8,128)(2,1)S(1)}, u32[]{:S(2)}, u32[]{:S(2)}) async-start(bf16[16,64,512]{2,1,0:T(8,128)(2,1)} %bitcast.3), calls=%async_computation | async-start | bytes 2097152 | tf_op jit(solution)/shard_map/all_to_all | solution.py:412
  76.9 1.3 copy-start.1
  78.2 1.0 copy-start.2
  79.2 1.0 copy-start.3
  80.2 37.2 %all-to-all-start.2 = ((bf16[16,64,512]{2,1,0:T(8,128)(2,1)}), bf16[16,64,512]{2,1,0:T(8,128)(2,1)S(1)}, u32[]{:S(2)}, u32[]{:S(2)}) async-start(bf16[16,64,512]{2,1,0:T(8,128)(2,1)} %bitcast.58), calls=%async_computation.2 | async-start | bytes 2097152 | tf_op jit(solution)/shard_map/all_to_all | solution.py:412
  86.5 2.1 %collective-permute-start = (bf16[512,512]{1,0:T(8,128)(2,1)S(1)}, bf16[512,512]{1,0:T(8,128)(2,1)}, u32[]{:S(2)}, u32[]{:S(2)}) collective-permute-start(bf16[512,512]{1,0:T(8,128)(2,1)S(1)} %fusion), channel_id=1, source_target_pairs={{0,1},{1,0},{2,3},{3,2},{4,5},{5,4},{6,7},{7,6},{8,9},{9,8},{10,11... | collective-permute-start | bytes 1572872 | tf_op jit(solution)/shard_map/ppermute | solution.py:344
  90.2 1.0 copy-start.5
  91.2 12.5 %collective-permute-start.1 = (bf16[256,512]{1,0:T(8,128)(2,1)S(1)}, bf16[256,512]{1,0:T(8,128)(2,1)S(1)}, u32[]{:S(2)}, u32[]{:S(2)}) collective-permute-start(bf16[256,512]{1,0:T(8,128)(2,1)S(1)} %fusion.1), channel_id=1, source_target_pairs={{0,2},{1,3},{2,0},{3,1},{4,6},{5,7},{6,4},{7,5},{8,10},{9,11},{10,... | collective-permute-start | bytes 786440 | tf_op jit(solution)/shard_map/ppermute | solution.py:344
  104.9 6.5 %collective-permute-start.4 = (bf16[64,512]{1,0:T(8,128)(2,1)S(1)}, bf16[64,512]{1,0:T(8,128)(2,1)S(1)}, u32[]{:S(2)}, u32[]{:S(2)}) collective-permute-start(bf16[64,512]{1,0:T(8,128)(2,1)S(1)} %get-tuple-element.28), channel_id=1, source_target_pairs={{0,12},{1,13},{2,14},{3,15},{4,8},{5,9},{6,10},{7,11},{8,4},{9,5},... | collective-permute-start | bytes 196616 | tf_op jit(solution)/shard_map/ppermute | solution.py:344
  108.3 9.0 %collective-permute-start.3 = (bf16[64,512]{1,0:T(8,128)(2,1)S(1)}, bf16[64,512]{1,0:T(8,128)(2,1)S(1)}, u32[]{:S(2)}, u32[]{:S(2)}) collective-permute-start(bf16[64,512]{1,0:T(8,128)(2,1)S(1)} %get-tuple-element.29), channel_id=1, source_target_pairs={{0,8},{1,9},{2,10},{3,11},{4,12},{5,13},{6,14},{7,15},{8,0},{9,1},... | collective-permute-start | bytes 196616 | tf_op jit(solution)/shard_map/ppermute | solution.py:344
  109.8 7.5 %collective-permute-start.2 = (bf16[64,512]{1,0:T(8,128)(2,1)S(1)}, bf16[64,512]{1,0:T(8,128)(2,1)S(1)}, u32[]{:S(2)}, u32[]{:S(2)}) collective-permute-start(bf16[64,512]{1,0:T(8,128)(2,1)S(1)} %get-tuple-element.27), channel_id=1, source_target_pairs={{0,4},{1,5},{2,6},{3,7},{4,0},{5,1},{6,2},{7,3},{8,12},{9,13},{10,... | collective-permute-start | bytes 196616 | tf_op jit(solution)/shard_map/ppermute | solution.py:344
  118.6 1.0 copy-start
  119.6 8.8 %collective-permute-start.5 = (bf16[64,512]{1,0:T(8,128)(2,1)S(1)}, bf16[64,512]{1,0:T(8,128)(2,1)S(1)}, u32[]{:S(2)}, u32[]{:S(2)}) collective-permute-start(bf16[64,512]{1,0:T(8,128)(2,1)S(1)} %fusion.4), channel_id=1, source_target_pairs={{0,4},{1,5},{2,6},{3,7},{4,0},{5,1},{6,2},{7,3},{8,12},{9,13},{10,... | collective-permute-start | bytes 196616 | tf_op jit(solution)/shard_map/ppermute | solution.py:344
  119.6 8.8 %collective-permute-start.6 = (bf16[64,512]{1,0:T(8,128)(2,1)S(1)}, bf16[64,512]{1,0:T(8,128)(2,1)S(1)}, u32[]{:S(2)}, u32[]{:S(2)}) collective-permute-start(bf16[64,512]{1,0:T(8,128)(2,1)S(1)} %fusion.4), channel_id=1, source_target_pairs={{0,8},{1,9},{2,10},{3,11},{4,12},{5,13},{6,14},{7,15},{8,0},{9,1},... | collective-permute-start | bytes 196616 | tf_op jit(solution)/shard_map/ppermute | solution.py:344
  121.6 6.8 %collective-permute-start.7 = (bf16[64,512]{1,0:T(8,128)(2,1)S(1)}, bf16[64,512]{1,0:T(8,128)(2,1)S(1)}, u32[]{:S(2)}, u32[]{:S(2)}) collective-permute-start(bf16[64,512]{1,0:T(8,128)(2,1)S(1)} %fusion.4), channel_id=1, source_target_pairs={{0,12},{1,13},{2,14},{3,15},{4,8},{5,9},{6,10},{7,11},{8,4},{9,5},... | collective-permute-start | bytes 196616 | tf_op jit(solution)/shard_map/ppermute | solution.py:344
  123.9 29.6 %all-to-all-start.3 = ((bf16[16,64,512]{2,1,0:T(8,128)(2,1)}), bf16[16,64,512]{2,1,0:T(8,128)(2,1)}, u32[]{:S(2)}, u32[]{:S(2)}) async-start(bf16[16,64,512]{2,1,0:T(8,128)(2,1)} %copy-done), calls=%async_computation.3 | async-start | bytes 2097152 | tf_op jit(solution)/shard_map/all_to_all | solution.py:412
  128.4 16.9 %collective-permute-start.8 = (bf16[256,512]{1,0:T(8,128)(2,1)S(1)}, bf16[256,512]{1,0:T(8,128)(2,1)S(1)}, u32[]{:S(2)}, u32[]{:S(2)}) collective-permute-start(bf16[256,512]{1,0:T(8,128)(2,1)S(1)} %bitcast.66), channel_id=1, source_target_pairs={{0,2},{1,3},{2,0},{3,1},{4,6},{5,7},{6,4},{7,5},{8,10},{9,11},{10,... | collective-permute-start | bytes 786440 | tf_op jit(solution)/shard_map/ppermute | solution.py:344
  146.2 3.2 %collective-permute-start.9 = (bf16[512,512]{1,0:T(8,128)(2,1)}, bf16[512,512]{1,0:T(8,128)(2,1)}, u32[]{:S(2)}, u32[]{:S(2)}) collective-permute-start(bf16[512,512]{1,0:T(8,128)(2,1)} %pad_maximum_fusion.1), channel_id=1, source_target_pairs={{0,1},{1,0},{2,3},{3,2},{4,5},{5,4},{6,7},{7,6},{8,9},{9,8},{10,11... | collective-permute-start | bytes 1572872 | tf_op jit(solution)/shard_map/ppermute | solution.py:344
  153.5 1.2 copy-start.4

commit v5 on v4

--- a/solution.py
+++ b/solution.py
@@ -7,8 +7,14 @@
 
 BF = jnp.bfloat16
 F32 = jnp.float32
-PIECES = 1
+PIECES = 2
+INNER = 4
 VMEM_BYTES = 40 * 1024 * 1024
+SCALAR = pl.BlockSpec(memory_space=pltpu.SMEM)
+
+
+def in_hbm(array):
+    return pltpu.with_memory_space_constraint(array, pltpu.HBM)
 
 
 def sigmoid(z):
@@ -46,9 +52,9 @@
         self.grouped = self.part % 16 == 0
 
     def view(self, array):
-        if self.pieces == 1:
-            return array
-        return array.reshape(self.count, self.pieces, self.part, array.shape[-1])
+        if self.pieces > 1:
+            array = array.reshape(self.count, self.pieces, self.part, array.shape[-1])
+        return in_hbm(array)
 
     def spec(self, rows, columns, piece, index=lambda i: (i, 0)):
         if self.pieces == 1:
@@ -81,98 +87,117 @@
             2 * (plan.rows * plan.block + 2 * plan.block * plan.channels),
         ),
         name="mix_first",
-    )(plan.view(factor), blocked)
-
-
-def spread_factor(plan, factor_two):
-    n = plan.count
+    )(plan.view(factor), in_hbm(blocked))
+
+
+def spread_factor(plan, inner, factor_plane):
+    n, outer = plan.count * INNER, plan.count
     groups = plan.here // 16
+    tall, wide = outer * 16, n * 16
+    cut = factor_plane.reshape(groups, 16, n, n)
+    rows = cut.reshape(groups, 16, outer, INNER, n)
+    fwd = lax.dynamic_index_in_dim(rows, inner, 3, keepdims=False).transpose(0, 2, 1, 3)
+    cols = cut.reshape(groups, 16, n, outer, INNER)
+    bwd = lax.dynamic_index_in_dim(cols, inner, 4, keepdims=False).transpose(0, 3, 1, 2)
+    both = jnp.stack([fwd, bwd]).reshape(2 * groups, tall, n)
+
+    def body(inner_ref, in_ref, out_ref):
+        pick = picker(n, outer, inner_ref[0], False).astype(BF)
+        same = same_position(tall, wide)
+        for g in range(in_ref.shape[0]):
+            full = dot(in_ref[g], pick, 1, 0)
+            out_ref[g] = jnp.where(same, full, 0.0).astype(BF)
+
+    half = groups
+    return pl.pallas_call(
+        body,
+        grid=(2,),
+        in_specs=[SCALAR, pl.BlockSpec((half, tall, n), lambda i: (i, 0, 0))],
+        out_specs=pl.BlockSpec((half, tall, wide), lambda i: (i, 0, 0)),
+        out_shape=jax.ShapeDtypeStruct((2 * groups, tall, wide), BF),
+        compiler_params=params(),
+        cost_estimate=cost(4 * groups * tall * wide * n, 4 * groups * tall * wide),
+        name="spread_factor",
+    )(inner.reshape(1), both)
+
+
+def picker(n, outer, inner, turned):
     wide = n * 16
-    turned = factor_two.reshape(groups, 16, n, n).transpose(0, 2, 1, 3).reshape(groups, wide, n)
-
-    def body(in_ref, out_ref):
-        col = lax.broadcasted_iota(jnp.int32, (n, wide), 1)
-        row = lax.broadcasted_iota(jnp.int32, (n, wide), 0)
-        pick = jnp.where(col // 16 == row, 1.0, 0.0).astype(BF)
-        full = dot(in_ref[0], pick, 1, 0)
-        r = lax.broadcasted_iota(jnp.int32, (wide, wide), 0)
-        c = lax.broadcasted_iota(jnp.int32, (wide, wide), 1)
-        out_ref[0] = jnp.where(r % 16 == c % 16, full, 0.0).astype(BF)
-
+    shape = (wide, n) if turned else (n, wide)
+    col = lax.broadcasted_iota(jnp.int32, shape, 0 if turned else 1) // 16
+    block = lax.broadcasted_iota(jnp.int32, shape, 1 if turned else 0)
+    return jnp.where((col % outer) * INNER + ((col // outer) ^ inner) == block, 1.0, 0.0)
+
+
+def same_position(tall, wide):
+    r = lax.broadcasted_iota(jnp.int32, (tall, wide), 0)
+    c = lax.broadcasted_iota(jnp.int32, (tall, wide), 1)
+    return r % 16 == c % 16
+
+
+def group_rows(refs, g):
+    at = slice(g * 16, (g + 1) * 16)
+    parts = [r[:, at, :].reshape(-1, r.shape[-1]) for r in refs]
+    return parts[0] if len(parts) == 1 else jnp.concatenate(parts, axis=0)
+
+
+def mix_second(plan, spread, cols, piece, back):
+    outer = plan.count
+    groups = plan.part // 16
+    tall, wide = outer * 16, outer * INNER * 16
+    shape = (outer, plan.part, plan.channels)
+    base = (plan.pieces if back else 0) + piece
+
+    def body(m_ref, *rest):
+        ins, out_ref = rest[:-1], rest[-1]
+        for g in range(groups):
+            got = dot(m_ref[g], group_rows(ins, g), 1, 0).astype(BF)
+            out_ref[:, g * 16 : (g + 1) * 16, :] = got.reshape(outer, 16, plan.channels)
+
+    full = pl.BlockSpec(shape, lambda i: (0, 0, 0))
     return pl.pallas_call(
         body,
-        grid=(groups,),
-        in_specs=[pl.BlockSpec((1, wide, n), lambda g: (g, 0, 0))],
-        out_specs=pl.BlockSpec((1, wide, wide), lambda g: (g, 0, 0)),
-        out_shape=jax.ShapeDtypeStruct((groups, wide, wide), BF),
-        compiler_params=params(),
-        cost_estimate=cost(2 * groups * wide * wide * n, 2 * groups * wide * wide),
-        name="spread_factor",
-    )(turned)
-
-
-def mix_second(plan, spread, cols, piece, back):
-    n = plan.count
-    wide = n * 16
+        grid=(1,),
+        in_specs=[pl.BlockSpec((groups, tall, wide), lambda i: (base, 0, 0))] + [full] * INNER,
+        out_specs=full,
+        out_shape=jax.ShapeDtypeStruct(shape, BF),
+        compiler_params=params(),
+        cost_estimate=cost(
+            2 * groups * tall * wide * plan.channels,
+            2 * (INNER + 1) * plan.rows * plan.channels + 2 * groups * tall * wide,
+        ),
+        name="mix_second_back" if back else "mix_second",
+    )(spread, *cols)
+
+
+def grad_second(plan, inner, grads, firsts, scale):
+    outer, n = plan.count, plan.count * INNER
     groups = plan.part // 16
-
-    def body(m_ref, in_ref, out_ref):
-        rows = in_ref[...].reshape(wide, plan.channels)
-        got = dot(m_ref[0], rows, 0 if back else 1, 0).astype(BF)
-        out_ref[...] = got.reshape(n, 16, plan.channels)
-
+    tall, wide = outer * 16, n * 16
+
+    def body(inner_ref, g_ref, *rest):
+        us, out_ref = rest[:-1], rest[-1]
+        same = same_position(tall, wide)
+        pick = picker(n, outer, inner_ref[0], True)
+        for g in range(groups):
+            full = dot(group_rows([g_ref], g), group_rows(us, g), 1, 1)
+            kept = jnp.where(same, full, 0.0)
+            out_ref[g] = dot(kept, pick, 1, 0, precision=lax.Precision.HIGHEST) * scale
+
+    full = pl.BlockSpec((outer, plan.part, plan.channels), lambda i: (0, 0, 0))
     out = pl.pallas_call(
         body,
-        grid=(groups,),
-        in_specs=[
-            pl.BlockSpec((1, wide, wide), lambda g: (piece * groups + g, 0, 0)),
-            pl.BlockSpec((n, 16, plan.channels), lambda g: (0, g, 0)),
-        ],
-        out_specs=pl.BlockSpec((n, 16, plan.channels), lambda g: (0, g, 0)),
-        out_shape=jax.ShapeDtypeStruct((n, plan.part, plan.channels), BF),
+        grid=(1,),
+        in_specs=[SCALAR] + [full] * (INNER + 1),
+        out_specs=pl.BlockSpec((groups, tall, n), lambda i: (0, 0, 0)),
+        out_shape=jax.ShapeDtypeStruct((groups, tall, n), F32),
         compiler_params=params(),
         cost_estimate=cost(
-            2 * groups * wide * wide * plan.channels,
-            4 * plan.rows * plan.channels + 2 * groups * wide * wide,
-        ),
-        name="mix_second_back" if back else "mix_second",
-    )(spread, cols.reshape(n, plan.part, plan.channels))
-    return out.reshape(plan.rows, plan.channels)
-
-
-def grad_second(plan, grads, firsts, scale):
-    n = plan.count
-    wide = n * 16
-    groups = plan.part // 16
-
-    def body(g_ref, u_ref, out_ref):
-        g = g_ref[...].reshape(wide, plan.channels)
-        u = u_ref[...].reshape(wide, plan.channels)
-        full = dot(g, u, 1, 1)
-        r = lax.broadcasted_iota(jnp.int32, (wide, wide), 0)
-        c = lax.broadcasted_iota(jnp.int32, (wide, wide), 1)
-        kept = jnp.where(r % 16 == c % 16, full, 0.0)
-        row = lax.broadcasted_iota(jnp.int32, (wide, n), 0)
-        col = lax.broadcasted_iota(jnp.int32, (wide, n), 1)
-        pick = jnp.where(row // 16 == col, 1.0, 0.0)
-        out_ref[0] = dot(kept, pick, 1, 0, precision=lax.Precision.HIGHEST) * scale
-
-    out = pl.pallas_call(
-        body,
-        grid=(groups,),
-        in_specs=[pl.BlockSpec((n, 16, plan.channels), lambda g: (0, g, 0))] * 2,
-        out_specs=pl.BlockSpec((1, wide, n), lambda g: (g, 0, 0)),
-        out_shape=jax.ShapeDtypeStruct((groups, wide, n), F32),
-        compiler_params=params(),
-        cost_estimate=cost(
-            2 * groups * wide * wide * plan.channels, 4 * plan.rows * plan.channels
+            2 * groups * tall * wide * plan.channels, 2 * (INNER + 1) * plan.rows * plan.channels
         ),
         name="grad_second",
-    )(
-        grads.reshape(n, plan.part, plan.channels),
-        firsts.reshape(n, plan.part, plan.channels),
-    )
-    return out.reshape(groups, n, 16, n).transpose(0, 2, 1, 3).reshape(plan.part, n, n)
+    )(inner.reshape(1), grads, *firsts)
+    return out.reshape(groups, outer, 16, n).transpose(0, 2, 1, 3).reshape(plan.part, outer, n)
 
 
 def middle(plan, blocked, incoming, mixed, up_blocks, down_blocks, piece, before):
@@ -229,7 +254,7 @@
         pl.BlockSpec(up_blocks.shape, lambda i: (0, 0, 0)),
         pl.BlockSpec(down_blocks.shape, lambda i: (0, 0, 0)),
     ]
-    operands = [plan.view(blocked), plan.view(incoming), mixed, up_blocks, down_blocks]
+    operands = [plan.view(blocked), plan.view(incoming), mixed, in_hbm(up_blocks), in_hbm(down_blocks)]
     if before is not None:
         in_specs.append(full)
         operands.append(before)
@@ -285,7 +310,7 @@
         pl.BlockSpec((plan.rows, plan.channels), lambda i: (0, 0)),
         wide,
     ]
-    operands = [plan.view(factor), grad_firsts, blocked]
+    operands = [plan.view(factor), grad_firsts, in_hbm(blocked)]
     aliases = {}
     if piece > 0:
         in_specs += [pl.BlockSpec(memory_space=pl.ANY), wide]
@@ -397,72 +422,73 @@
 
 def on_device(tokens, cotangent, factor_one, factor_two, up_blocks, down_blocks):
     count = lax.axis_size("seq")
+    outer = count // INNER
     block, channels = factor_one.shape[1], tokens.shape[1]
-    plan = Plan(count, block, channels)
+    plan = Plan(outer, block, channels)
     scale = float(count * tokens.shape[0]) ** (-0.5)
     factor = factor_one.reshape(block, block)
     pieces = range(plan.pieces)
-    tokens, cotangent, factor, up_blocks, down_blocks = (
-        pltpu.with_memory_space_constraint(a, pltpu.HBM)
-        for a in (tokens, cotangent, factor, up_blocks, down_blocks)
-    )
-
-    def exchange(rows):
-        cut = rows.reshape(count, plan.part, channels)
-        got = lax.all_to_all(cut, "seq", split_axis=0, concat_axis=0, tiled=True)
-        return got.reshape(plan.rows, channels)
-
-    if plan.grouped:
-        spread = spread_factor(plan, factor_two)
-
-    def second(cols, piece, back):
-        if plan.grouped:
-            return mix_second(plan, spread, cols, piece, back)
-        cut = cols.reshape(count, plan.part, channels)
-        names = "kmj,mkc->jkc" if back else "kmj,jkc->mkc"
-        got = jnp.einsum(names, factor_two, cut, preferred_element_type=F32).astype(BF)
-        return got.reshape(plan.rows, channels)
-
-    def second_grad(grads, firsts):
-        if plan.grouped:
-            return grad_second(plan, grads, firsts, scale)
-        shape = (count, plan.part, channels)
-        got = jnp.einsum(
-            "mkc,jkc->kmj", grads.reshape(shape), firsts.reshape(shape), preferred_element_type=F32
+    inner = lax.axis_index("seq").astype(jnp.int32) % INNER
+    planes = [[z * INNER + i for z in range(outer)] for i in range(INNER)]
+
+    def across(rows):
+        cut = rows.reshape(outer, plan.part, channels)
+        return lax.all_to_all(
+            cut, "seq", split_axis=0, concat_axis=0, tiled=True, axis_index_groups=planes
         )
-        return got * scale
-
-    firsts = [exchange(mix_first(plan, factor, tokens, q)) for q in pieces]
-    mixed = [exchange(second(firsts[q], q, False)) for q in pieces]
+
+    def within(mine):
+        far = swap(mine, count, 2, 1)
+        return [mine, swap(mine, count, 1, 1), far, swap(far, count, 1, 1)]
+
+    flat = factor_two.reshape(factor_two.shape[0], -1)
+    plane_two = gather_step(gather_step(flat, count, 1, 2), count, 2, 2)
+    spread = spread_factor(plan, inner, plane_two)
+
+    def rows(value):
+        return value.reshape(plan.rows, channels)
+
+    firsts = [within(across(mix_first(plan, factor, tokens, q))) for q in pieces]
+    mixed = [across(mix_second(plan, spread, firsts[q], q, False)) for q in pieces]
     weights = None
-    grad_mixed, gate_grads = [], []
+    own_grads, gate_grads = [], []
     for q in pieces:
         dv, r, weights = middle(
-            plan, tokens, cotangent, mixed[q], up_blocks, down_blocks, q, weights
+            plan, tokens, cotangent, rows(mixed[q]), up_blocks, down_blocks, q, weights
         )
-        grad_mixed.append(exchange(dv))
+        own_grads.append(across(dv))
         gate_grads.append(r)
     total = weights.reshape(-1, weights.shape[-1])
     steps = radices(count)
     for step in steps:
         total = scatter_step(total, count, *step)
     total = total.astype(BF)
-    back = [second(grad_mixed[q], q, True) for q in pieces]
-    back, total = lax.optimization_barrier((back, total))
     for step in reversed(steps):
         total = gather_step(total, count, *step)
-    grad_firsts = [exchange(b) for b in back]
-    two = [second_grad(grad_mixed[q], firsts[q]) for q in pieces]
+    grad_firsts = [
+        across(mix_second(plan, spread, within(own_grads[q]), q, True)) for q in pieces
+    ]
+    two = jnp.concatenate(
+        [grad_second(plan, inner, own_grads[q], firsts[q], scale) for q in pieces], axis=0
+    )
+    here = factor_two.shape[0]
+    two = two.reshape(INNER, here, outer, count)
+    held = jnp.zeros_like(two)
+    for s in range(INNER):
+        part = lax.dynamic_index_in_dim(two, inner ^ s, 0, keepdims=False)
+        got = part if s == 0 else swap(part, count, 1, s)
+        held = lax.dynamic_update_index_in_dim(held, got, inner ^ s, 0)
+    two = held.transpose(1, 2, 0, 3).reshape(here, count, count)
     grad_up, grad_down = write_weights(total, up_blocks.shape, down_blocks.shape, scale)
     one, tokens_sum = None, None
     for q in pieces:
         one, tokens_sum = finish(
-            plan, factor, grad_firsts[q], tokens, gate_grads, q, scale, one, tokens_sum
+            plan, factor, rows(grad_firsts[q]), tokens, gate_grads, q, scale, one, tokens_sum
         )
     return (
         tokens_sum.reshape(tokens.shape),
         one.reshape(1, block, block),
-        jnp.concatenate(two, axis=0),
+        two,
         grad_up,
         grad_down,
     )

time: 163 us -> 214 us (1.31)
  Pallas kernels: 27.5 us -> 46 us
  local copies, waits for them, and re-layouts: 9.39 us -> 27.3 us
  starting transfers between devices: 30.4 us -> 43.9 us
  blocking collectives: 31.5 us -> 20.6 us
  waiting for transfers between devices: 56.7 us -> 62.9 us
  other arithmetic: 4.87 us -> 9.83 us
    all_to_all x3 -> x7, waiting for transfers between devices: 21.9 us -> 35.4 us  [across(): lax.all_to_all(cut, 'seq', split_axis=0, concat_axis=0, tiled=True, axis_...]
    pallas_call x4 -> x7, Pallas kernels: 5.85 us -> 18.2 us  [the longest x4 9.75 us: mix_second(): pl.pallas_call(body, grid=(1,), in_specs=[pl.BlockSpec((groups, tall, wid...]
    all_to_all x1, blocking collectives: 31.5 us -> 20.6 us  [across(): lax.all_to_all(cut, 'seq', split_axis=0, concat_axis=0, tiled=True, axis_...]
    unnamed x14 -> x46, local copies, waits for them, and re-layouts: 6.45 us -> 17.2 us
    all_to_all x3 -> x7, starting transfers between devices: 16.8 us -> 24.5 us  [across(): lax.all_to_all(cut, 'seq', split_axis=0, concat_axis=0, tiled=True, axis_...]
    ppermute x10 -> x27, waiting for transfers between devices: 34.8 us -> 27.5 us  [swap(): lax.ppermute(values, 'seq', [(i, i ^ stride * s) for i in range(count)])]
    ppermute x10 -> x27, starting transfers between devices: 13.5 us -> 19.4 us  [swap(): lax.ppermute(values, 'seq', [(i, i ^ stride * s) for i in range(count)])]
    pallas_call x1 -> x2, Pallas kernels: 6.56 us -> 9.39 us  [finish(): pl.pallas_call(body, grid=(plan.block // step,), in_specs=in_specs, out_s...]
  transfers between devices with their start and end apart: 13 -> 34, of which waited for: 6 -> 16; matrix products, arithmetic and copies ran while one was open for 5% -> 9% of each run, Pallas kernels for 3% -> 15%
where the time goes in v5:
time: 214 us; the launch traced here: 212 us
  waiting for transfers between devices  62.9 us (29%)
  Pallas kernels  46 us (21%)
  starting transfers between devices  43.9 us (21%)
  local copies, waits for them, and re-layouts  27.3 us (13%)
  blocking collectives  20.6 us (10%)
  other arithmetic  9.83 us (5%)
    all_to_all x7, waiting for transfers between devices, across(): lax.all_to_all(cut, 'seq', split_axis=0, concat_axis=0, tiled=True, axis_...  35.4 us
    ppermute x27, waiting for transfers between devices, swap(): lax.ppermute(values, 'seq', [(i, i ^ stride * s) for i in range(count)])  27.5 us
    all_to_all x7, starting transfers between devices, across(): lax.all_to_all(cut, 'seq', split_axis=0, concat_axis=0, tiled=True, axis_...  24.5 us
    all_to_all x1, blocking collectives, across(): lax.all_to_all(cut, 'seq', split_axis=0, concat_axis=0, tiled=True, axis_...  20.6 us
    ppermute x27, starting transfers between devices, swap(): lax.ppermute(values, 'seq', [(i, i ^ stride * s) for i in range(count)])  19.4 us
    unnamed x46, local copies, waits for them, and re-layouts  17.2 us
    pallas_call x2, Pallas kernels, middle(): pl.pallas_call(body, grid=(plan.rows // step,), in_specs=in_specs, out_sp...  11.2 us
    pallas_call x4, Pallas kernels, mix_second(): pl.pallas_call(body, grid=(1,), in_specs=[pl.BlockSpec((groups, tall, wid...  9.75 us
  transfers between devices with their start and end apart: 34, of which 16 were waited for; matrix products, arithmetic and copies ran while one was open for 9% of the time, Pallas kernels for 15%

profile of v5, /device:TPU:0, one launch (start us, length us, event | category | flops | bytes accessed | tf_op | source)
XLA Modules:
  0.0 211.7 jit_solution(14618867956434476090)
XLA Ops:
  0.6 2.3 %mix_first.3 = bf16[512,512]{1,0:T(8,128)(2,1)S(1)} custom-call(bf16[4,2,128,1024]{3,2,1,0:T(8,128)(2,1)} %bitcast.110, bf16[1024,512]{1,0:T(8,128)(2,1)} %refs_2_.3), custom_call_target="tpu_custom_call" | custom-call | flops 536870912 | bytes 3145728 | tf_op jit(solution)/shard_map/mix_first/pallas_call | solution.py:75
  3.0 20.6 %all_to_all.40.rest_0_ = bf16[4,128,512]{2,1,0:T(8,128)(2,1)S(1)} all-to-all(bf16[4,128,512]{2,1,0:T(8,128)(2,1)S(1)} %bitcast.98), channel_id=1, replica_groups={{0,4,8,12},{1,5,9,13},{2,6,10,14},{3,7,11,15},{16,20,24,28},{17,21,25,2..., dimensions={0} | all-to-all | bytes 1048576 | tf_op jit(solution)/shard_map/all_to_all | solution.py:436
  23.6 1.5 collective-permute-start.6
  25.1 3.0 %mix_first.2 = bf16[512,512]{1,0:T(8,128)(2,1)} custom-call(bf16[4,2,128,1024]{3,2,1,0:T(8,128)(2,1)} %bitcast.111, bf16[1024,512]{1,0:T(8,128)(2,1)} %refs_2_.3), custom_call_target="tpu_custom_call" | custom-call | flops 536870912 | bytes 3145728 | tf_op jit(solution)/shard_map/mix_first/pallas_call | solution.py:75
  28.1 3.5 %all-to-all-start = ((bf16[4,128,512]{2,1,0:T(8,128)(2,1)}), bf16[4,128,512]{2,1,0:T(8,128)(2,1)S(1)}, u32[]{:S(2)}, u32[]{:S(2)}) async-start(bf16[4,128,512]{2,1,0:T(8,128)(2,1)} %bitcast.12), calls=%async_computation | async-start | bytes 1048576 | tf_op jit(solution)/shard_map/all_to_all | solution.py:436
  32.5 4.3 %collective-permute-done.6.rest_2_ = bf16[4,128,512]{2,1,0:T(8,128)(2,1)S(1)} collective-permute-done((bf16[4,128,512]{2,1,0:T(8,128)(2,1)S(1)}, bf16[4,128,512]{2,1,0:T(8,128)(2,1)S(1)}, u32[]{:S(2)}, u32[]{:S(2)}) %collective-permute-start.6) | collective-permute-done | bytes 524320 | tf_op jit(solution)/shard_map/ppermute | solution.py:369
  38.4 8.6 %all-to-all-done.rest_0_ = bf16[4,128,512]{2,1,0:T(8,128)(2,1)S(1)} async-done(((bf16[4,128,512]{2,1,0:T(8,128)(2,1)}), bf16[4,128,512]{2,1,0:T(8,128)(2,1)S(1)}, u32[]{:S(2)}, u32[]{:S(2)}) %all-to-all-start) | async-done | bytes 524320 | tf_op jit(solution)/shard_map/all_to_all | solution.py:436
  51.3 2.5 %mix_second.3 = bf16[4,128,512]{2,1,0:T(8,128)(2,1)} custom-call(bf16[32,64,256]{2,1,0:T(8,128)(2,1)S(1)} %spread_factor.1.m_ref, bf16[4,128,512]{2,1,0:T(8,128)(2,1)S(1)} %all_to_all.40.rest_0_, bf16[4,128,512]{2,1,0:T(8,128)(2,1)S(1)} %collective-permute-done.5.rest_1_, bf16[4,128,512]{2,1,0:T(8,128)(2,1)S(1)} %collective-permute-done.6.rest_2_, ...), custom_call_target="tpu_custom_call" | custom-call | flops 134217728 | bytes 2883584 | tf_op jit(solution)/shard_map/mix_second/pallas_call | solution.py:158
  53.8 3.5 %all-to-all-start.3 = ((bf16[4,128,512]{2,1,0:T(8,128)(2,1)}), bf16[4,128,512]{2,1,0:T(8,128)(2,1)S(1)}, u32[]{:S(2)}, u32[]{:S(2)}) async-start(bf16[4,128,512]{2,1,0:T(8,128)(2,1)} %mix_second.3), calls=%async_computation.3 | async-start | bytes 1048576 | tf_op jit(solution)/shard_map/all_to_all | solution.py:436
  57.4 3.2 %collective-permute-done.3.rest_2_ = bf16[4,128,512]{2,1,0:T(8,128)(2,1)} collective-permute-done((bf16[4,128,512]{2,1,0:T(8,128)(2,1)S(1)}, bf16[4,128,512]{2,1,0:T(8,128)(2,1)}, u32[]{:S(2)}, u32[]{:S(2)}) %collective-permute-start.3) | collective-permute-done | bytes 524320 | tf_op jit(solution)/shard_map/ppermute | solution.py:369
  60.6 2.1 collective-permute-done.4.rest_3_
  62.7 2.3 %mix_second.2 = bf16[4,128,512]{2,1,0:T(8,128)(2,1)} custom-call(bf16[32,64,256]{2,1,0:T(8,128)(2,1)S(1)} %spread_factor.1.m_ref, bf16[4,128,512]{2,1,0:T(8,128)(2,1)S(1)} %all-to-all-done.rest_0_, bf16[4,128,512]{2,1,0:T(8,128)(2,1)S(1)} %collective-permute-done.2.rest_1_, bf16[4,128,512]{2,1,0:T(8,128)(2,1)} %collective-permute-done.3.rest_2_, ...), custom_call_target="tpu_custom_call" | custom-call | flops 134217728 | bytes 2883584 | tf_op jit(solution)/shard_map/mix_second/pallas_call | solution.py:158
  66.6 5.0 %all-to-all-done.3 = bf16[4,128,512]{2,1,0:T(8,128)(2,1)S(1)} async-done(((bf16[4,128,512]{2,1,0:T(8,128)(2,1)}), bf16[4,128,512]{2,1,0:T(8,128)(2,1)S(1)}, u32[]{:S(2)}, u32[]{:S(2)}) %all-to-all-start.3) | async-done | bytes 524320 | tf_op jit(solution)/shard_map/all_to_all | solution.py:436
  72.4 3.5 %all-to-all-start.1 = ((bf16[4,128,512]{2,1,0:T(8,128)(2,1)}), bf16[4,128,512]{2,1,0:T(8,128)(2,1)S(1)}, u32[]{:S(2)}, u32[]{:S(2)}) async-start(bf16[4,128,512]{2,1,0:T(8,128)(2,1)} %mix_second.2), calls=%async_computation.1 | async-start | bytes 1048576 | tf_op jit(solution)/shard_map/all_to_all | solution.py:436
  77.0 5.0 %middle.2 = (bf16[512,512]{1,0:T(8,128)(2,1)S(1)}, bf16[512,512]{1,0:T(8,128)(2,1)S(1)}, f32[8,128,512]{2,1,0:T(8,128)S(1)}) custom-call(bf16[4,2,128,512]{3,2,1,0:T(8,128)(2,1)} %bitcast.114, bf16[4,2,128,512]{3,2,1,0:T(8,128)(2,1)} %bitcast.123, bf16[512,512]{1,0:T(8,128)(2,1)S(1)} %bitcast.107, bf16[4,128,512]{2,1,0:T(8,128)(2,1)} %refs_3_.3, ...), custom_call_target="tpu_custom_call" | custom-call | flops 1342177280 | bytes 4718592 | tf_op jit(solution)/shard_map/middle/pallas_call | solution.py:262
  82.0 1.3 copy-done.8
  84.9 5.0 %all-to-all-done.1 = bf16[4,128,512]{2,1,0:T(8,128)(2,1)S(1)} async-done(((bf16[4,128,512]{2,1,0:T(8,128)(2,1)}), bf16[4,128,512]{2,1,0:T(8,128)(2,1)S(1)}, u32[]{:S(2)}, u32[]{:S(2)}) %all-to-all-start.1) | async-done | bytes 524320 | tf_op jit(solution)/shard_map/all_to_all | solution.py:436
  89.9 1.6 copy-done.9
  91.5 6.2 %middle.3 = (bf16[512,512]{1,0:T(8,128)(2,1)S(1)}, bf16[512,512]{1,0:T(8,128)(2,1)S(1)}, f32[8,128,512]{2,1,0:T(8,128)}) custom-call(bf16[4,2,128,512]{3,2,1,0:T(8,128)(2,1)} %bitcast.115, bf16[4,2,128,512]{3,2,1,0:T(8,128)(2,1)} %bitcast.124, bf16[512,512]{1,0:T(8,128)(2,1)S(1)} %bitcast.100, bf16[4,128,512]{2,1,0:T(8,128)(2,1)} %refs_3_.3, ...), custom_call_target="tpu_custom_call" | custom-call | flops 1342177280 | bytes 4718592 | tf_op jit(solution)/shard_map/middle/pallas_call | solution.py:262
  100.6 3.5 %all-to-all-start.6 = ((bf16[4,128,512]{2,1,0:T(8,128)(2,1)}), bf16[4,128,512]{2,1,0:T(8,128)(2,1)S(1)}, u32[]{:S(2)}, u32[]{:S(2)}) async-start(bf16[4,128,512]{2,1,0:T(8,128)(2,1)} %bitcast.106), calls=%async_computation.6 | async-start | bytes 1048576 | tf_op jit(solution)/shard_map/all_to_all | solution.py:436
  104.1 2.5 %bitcast_add_fusion = f32[512,512]{1,0:T(8,128)} fusion(bf16[512,512]{1,0:T(8,128)(2,1)} %collective-permute-done.17, f32[2,512,512]{2,1,0:T(8,128)} %bitcast.37, s32[]{:T(128)S(6)} %select_n.160), kind=kLoop, calls=%fused_computation.1 | loop fusion | flops 524288 | bytes 2621444 | tf_op jit(solution)/shard_map/add | solution.py:378
  106.7 1.8 fusion.1
  108.4 1.5 collective-permute-start.18
  109.9 9.6 %all-to-all-done.6.rest_0_.g_ref = bf16[4,128,512]{2,1,0:T(8,128)(2,1)S(1)} async-done(((bf16[4,128,512]{2,1,0:T(8,128)(2,1)}), bf16[4,128,512]{2,1,0:T(8,128)(2,1)S(1)}, u32[]{:S(2)}, u32[]{:S(2)}) %all-to-all-start.6) | async-done | bytes 524320 | tf_op jit(solution)/shard_map/all_to_all | solution.py:436
  119.5 3.7 %all-to-all-start.4 = ((bf16[4,128,512]{2,1,0:T(8,128)(2,1)}), bf16[4,128,512]{2,1,0:T(8,128)(2,1)S(1)}, u32[]{:S(2)}, u32[]{:S(2)}) async-start(bf16[4,128,512]{2,1,0:T(8,128)(2,1)} %bitcast.104), calls=%async_computation.4 | async-start | bytes 1048576 | tf_op jit(solution)/shard_map/all_to_all | solution.py:436
  124.4 1.8 collective-permute-start.19
  126.2 2.4 %collective-permute-start.21 = (bf16[64,512]{1,0:T(8,128)(2,1)S(1)}, bf16[64,512]{1,0:T(8,128)(2,1)S(1)}, u32[]{:S(2)}, u32[]{:S(2)}) collective-permute-start(bf16[64,512]{1,0:T(8,128)(2,1)S(1)} %get-tuple-element.36), channel_id=1, source_target_pairs={{0,12},{1,13},{2,14},{3,15},{4,8},{5,9},{6,10},{7,11},{8,4},{9,5},... | collective-permute-start | bytes 196616 | tf_op jit(solution)/shard_map/ppermute | solution.py:369
  128.6 1.5 collective-permute-start.12
  130.1 4.2 %collective-permute-done.19 = bf16[64,512]{1,0:T(8,128)(2,1)S(1)} collective-permute-done((bf16[64,512]{1,0:T(8,128)(2,1)S(1)}, bf16[64,512]{1,0:T(8,128)(2,1)S(1)}, u32[]{:S(2)}, u32[]{:S(2)}) %collective-permute-start.19) | collective-permute-done | bytes 65568 | tf_op jit(solution)/shard_map/ppermute | solution.py:369
  134.3 4.9 %collective-permute-done.21 = bf16[64,512]{1,0:T(8,128)(2,1)S(1)} collective-permute-done((bf16[64,512]{1,0:T(8,128)(2,1)S(1)}, bf16[64,512]{1,0:T(8,128)(2,1)S(1)}, u32[]{:S(2)}, u32[]{:S(2)}) %collective-permute-start.21) | collective-permute-done | bytes 65568 | tf_op jit(solution)/shard_map/ppermute | solution.py:369
  139.2 4.0 %collective-permute-done.20 = bf16[64,512]{1,0:T(8,128)(2,1)S(1)} collective-permute-done((bf16[64,512]{1,0:T(8,128)(2,1)S(1)}, bf16[64,512]{1,0:T(8,128)(2,1)S(1)}, u32[]{:S(2)}, u32[]{:S(2)}) %collective-permute-start.20) | collective-permute-done | bytes 65568 | tf_op jit(solution)/shard_map/ppermute | solution.py:369
  143.9 1.6 bitcast_dynamic-update-slice_fusion.3
  145.5 1.6 collective-permute-start.9
  147.0 2.0 collective-permute-start.23
  149.7 1.6 collective-permute-start.24
  152.0 2.9 %collective-permute-done.23 = bf16[64,512]{1,0:T(8,128)(2,1)S(1)} collective-permute-done((bf16[64,512]{1,0:T(8,128)(2,1)S(1)}, bf16[64,512]{1,0:T(8,128)(2,1)S(1)}, u32[]{:S(2)}, u32[]{:S(2)}) %collective-permute-start.23) | collective-permute-done | bytes 65568 | tf_op jit(solution)/shard_map/ppermute | solution.py:369
  156.5 1.4 collective-permute-start.25
  160.0 3.9 %grad_second.2 = f32[8,64,16]{2,1,0:T(8,128)S(1)} custom-call(s32[1]{0:T(128)} %bitcast.1.inner_ref, bf16[4,128,512]{2,1,0:T(8,128)(2,1)S(1)} %all-to-all-done.6.rest_0_.g_ref, bf16[4,128,512]{2,1,0:T(8,128)(2,1)S(1)} %all_to_all.40.rest_0_, bf16[4,128,512]{2,1,0:T(8,128)(2,1)S(1)} %copy-done.3, bf16[4,128,512]{2,1,0:T(8,128)(2,1)S(1)} %copy-done.1, ...), custom_call_target="tpu_custom_call" | custom-call | flops 134217728 | bytes 2621440 | tf_op jit(solution)/shard_map/grad_second/pallas_call | solution.py:188
  166.3 3.9 %grad_second.3 = f32[8,64,16]{2,1,0:T(8,128)S(1)} custom-call(s32[1]{0:T(128)} %bitcast.1.inner_ref, bf16[4,128,512]{2,1,0:T(8,128)(2,1)S(1)} %all-to-all-done.4.rest_0_.g_ref, bf16[4,128,512]{2,1,0:T(8,128)(2,1)S(1)} %all-to-all-done.rest_0_, bf16[4,128,512]{2,1,0:T(8,128)(2,1)S(1)} %copy-done.5, bf16[4,128,512]{2,1,0:T(8,128)(2,1)} %collective-permute-done.3.rest_2_, ...), custom_call_target="tpu_custom_call" | custom-call | flops 134217728 | bytes 2621440 | tf_op jit(solution)/shard_map/grad_second/pallas_call | solution.py:188
  170.7 2.6 %mix_second_back.3 = bf16[4,128,512]{2,1,0:T(8,128)(2,1)} custom-call(bf16[32,64,256]{2,1,0:T(8,128)(2,1)S(1)} %spread_factor.1.m_ref, bf16[4,128,512]{2,1,0:T(8,128)(2,1)S(1)} %all-to-all-done.6.rest_0_.g_ref, bf16[4,128,512]{2,1,0:T(8,128)(2,1)} %collective-permute-done.11.rest_1_, bf16[4,128,512]{2,1,0:T(8,128)(2,1)} %collective-permute-done.12.rest_2_, ...), custom_call_target="tpu_custom_call" | custom-call | flops 134217728 | bytes 2883584 | tf_op jit(solution)/shard_map/mix_second_back/pallas_call | solution.py:158
  173.4 3.5 %all-to-all-start.7 = ((bf16[4,128,512]{2,1,0:T(8,128)(2,1)}), bf16[4,128,512]{2,1,0:T(8,128)(2,1)S(1)}, u32[]{:S(2)}, u32[]{:S(2)}) async-start(bf16[4,128,512]{2,1,0:T(8,128)(2,1)} %mix_second_back.3), calls=%async_computation.7 | async-start | bytes 1048576 | tf_op jit(solution)/shard_map/all_to_all | solution.py:436
  182.3 2.3 %mix_second_back.2 = bf16[4,128,512]{2,1,0:T(8,128)(2,1)} custom-call(bf16[32,64,256]{2,1,0:T(8,128)(2,1)S(1)} %spread_factor.1.m_ref, bf16[4,128,512]{2,1,0:T(8,128)(2,1)S(1)} %all-to-all-done.4.rest_0_.g_ref, bf16[4,128,512]{2,1,0:T(8,128)(2,1)S(1)} %collective-permute-done.8.rest_1_, bf16[4,128,512]{2,1,0:T(8,128)(2,1)} %collective-permute-done.9.rest_2_, ...), custom_call_target="tpu_custom_call" | custom-call | flops 134217728 | bytes 2883584 | tf_op jit(solution)/shard_map/mix_second_back/pallas_call | solution.py:158
  184.7 4.2 %all-to-all-done.7 = bf16[4,128,512]{2,1,0:T(8,128)(2,1)S(1)} async-done(((bf16[4,128,512]{2,1,0:T(8,128)(2,1)}), bf16[4,128,512]{2,1,0:T(8,128)(2,1)S(1)}, u32[]{:S(2)}, u32[]{:S(2)}) %all-to-all-start.7) | async-done | bytes 524320 | tf_op jit(solution)/shard_map/all_to_all | solution.py:436
  188.9 3.5 %all-to-all-start.5 = ((bf16[4,128,512]{2,1,0:T(8,128)(2,1)}), bf16[4,128,512]{2,1,0:T(8,128)(2,1)S(1)}, u32[]{:S(2)}, u32[]{:S(2)}) async-start(bf16[4,128,512]{2,1,0:T(8,128)(2,1)} %mix_second_back.2), calls=%async_computation.5 | async-start | bytes 1048576 | tf_op jit(solution)/shard_map/all_to_all | solution.py:436
  195.3 1.9 write_weights.1
  197.2 4.6 %finish.2 = (f32[4,2,128,1024]{3,2,1,0:T(8,128)}, f32[1024,512]{1,0:T(8,128)S(1)}) custom-call(bf16[4,2,128,1024]{3,2,1,0:T(8,128)(2,1)} %bitcast.112, bf16[512,512]{1,0:T(8,128)(2,1)S(1)} %bitcast.105, bf16[1024,512]{1,0:T(8,128)(2,1)} %refs_2_.3), custom_call_target="tpu_custom_call" | custom-call | flops 1073741824 | bytes 7340032 | tf_op jit(solution)/shard_map/finish/pallas_call | solution.py:340
  201.9 3.0 %all-to-all-done.5 = bf16[4,128,512]{2,1,0:T(8,128)(2,1)S(1)} async-done(((bf16[4,128,512]{2,1,0:T(8,128)(2,1)}), bf16[4,128,512]{2,1,0:T(8,128)(2,1)S(1)}, u32[]{:S(2)}, u32[]{:S(2)}) %all-to-all-start.5) | async-done | bytes 524320 | tf_op jit(solution)/shard_map/all_to_all | solution.py:436
  207.0 4.8 %finish.3 = (f32[4,2,128,1024]{3,2,1,0:T(8,128)}, bf16[4,2,128,512]{3,2,1,0:T(8,128)(2,1)}) custom-call(bf16[4,2,128,1024]{3,2,1,0:T(8,128)(2,1)} %bitcast.113, bf16[512,512]{1,0:T(8,128)(2,1)S(1)} %bitcast.101, bf16[1024,512]{1,0:T(8,128)(2,1)} %refs_2_.3, f32[4,2,128,1024]{3,2,1,0:T(8,128)} %get-tuple-element.20.refs_3_, ...), custom_call_target="tpu_custom_call", output_to_operand_aliasing={{0}: (3, {})} | custom-call | flops 1073741824 | bytes 7340032 | tf_op jit(solution)/shard_map/finish/pallas_call | solution.py:340
  (116 shorter events, 35.1 us)
Async XLA Ops:
  0.6 24.5 %copy-start.21 = (bf16[64,16,16]{0,2,1:T(8,128)(2,1)S(1)}, bf16[64,16,16]{0,2,1:T(8,128)(2,1)}, u32[]{:S(2)}) copy-start(bf16[64,16,16]{0,2,1:T(8,128)(2,1)} %param.9) | copy-start | bytes 98308
  23.6 13.2 %collective-permute-start.6 = (bf16[4,128,512]{2,1,0:T(8,128)(2,1)S(1)}, bf16[4,128,512]{2,1,0:T(8,128)(2,1)S(1)}, u32[]{:S(2)}, u32[]{:S(2)}) collective-permute-start(bf16[4,128,512]{2,1,0:T(8,128)(2,1)S(1)} %all_to_all.40.rest_0_), channel_id=1, source_target_pairs={{0,2},{1,3},{2,0},{3,1},{4,6},{5,7},{6,4},{7,5},{8,10},{9,11},{10,... | collective-permute-start | bytes 1572872 | tf_op jit(solution)/shard_map/ppermute | solution.py:369
  25.1 6.5 %collective-permute-start = (bf16[64,256]{0,1:T(8,128)(2,1)S(1)}, bf16[64,256]{0,1:T(8,128)(2,1)S(1)}, u32[]{:S(2)}, u32[]{:S(2)}) collective-permute-start(bf16[64,256]{0,1:T(8,128)(2,1)S(1)} %bitcast.127), channel_id=1, source_target_pairs={{0,1},{1,0},{2,3},{3,2},{4,5},{5,4},{6,7},{7,6},{8,9},{9,8},{10,11... | collective-permute-start | bytes 98312 | tf_op jit(solution)/shard_map/ppermute | solution.py:369
  28.1 18.9 %all-to-all-start = ((bf16[4,128,512]{2,1,0:T(8,128)(2,1)}), bf16[4,128,512]{2,1,0:T(8,128)(2,1)S(1)}, u32[]{:S(2)}, u32[]{:S(2)}) async-start(bf16[4,128,512]{2,1,0:T(8,128)(2,1)} %bitcast.12), calls=%async_computation | async-start | bytes 1048576 | tf_op jit(solution)/shard_map/all_to_all | solution.py:436
  31.7 5.8 %collective-permute-start.1 = (bf16[128,256]{0,1:T(8,128)(2,1)S(1)}, bf16[128,256]{0,1:T(8,128)(2,1)S(1)}, u32[]{:S(2)}, u32[]{:S(2)}) collective-permute-start(bf16[128,256]{0,1:T(8,128)(2,1)S(1)} %pad_maximum_fusion.4), channel_id=1, source_target_pairs={{0,2},{1,3},{2,0},{3,1},{4,6},{5,7},{6,4},{7,5},{8,10},{9,11},{10,... | collective-permute-start | bytes 196616 | tf_op jit(solution)/shard_map/ppermute | solution.py:369
  32.3 19.0 %collective-permute-start.5 = (bf16[4,128,512]{2,1,0:T(8,128)(2,1)S(1)}, bf16[4,128,512]{2,1,0:T(8,128)(2,1)S(1)}, u32[]{:S(2)}, u32[]{:S(2)}) collective-permute-start(bf16[4,128,512]{2,1,0:T(8,128)(2,1)S(1)} %all_to_all.40.rest_0_), channel_id=1, source_target_pairs={{0,1},{1,0},{2,3},{3,2},{4,5},{5,4},{6,7},{7,6},{8,9},{9,8},{10,11... | collective-permute-start | bytes 1572872 | tf_op jit(solution)/shard_map/ppermute | solution.py:369
  36.8 14.5 %copy-start = (bf16[4,128,512]{2,1,0:T(8,128)(2,1)}, bf16[4,128,512]{2,1,0:T(8,128)(2,1)S(1)}, u32[]{:S(2)}) copy-start(bf16[4,128,512]{2,1,0:T(8,128)(2,1)S(1)} %collective-permute-done.6.rest_2_) | copy-start | bytes 1572868
  36.8 14.5 %collective-permute-start.7 = (bf16[4,128,512]{2,1,0:T(8,128)(2,1)S(1)}, bf16[4,128,512]{2,1,0:T(8,128)(2,1)}, u32[]{:S(2)}, u32[]{:S(2)}) collective-permute-start(bf16[4,128,512]{2,1,0:T(8,128)(2,1)S(1)} %collective-permute-done.6.rest_2_), channel_id=1, source_target_pairs={{0,1},{1,0},{2,3},{3,2},{4,5},{5,4},{6,7},{7,6},{8,9},{9,8},{10,11... | collective-permute-start | bytes 1572872 | tf_op jit(solution)/shard_map/ppermute | solution.py:369
  47.0 13.6 %collective-permute-start.3 = (bf16[4,128,512]{2,1,0:T(8,128)(2,1)S(1)}, bf16[4,128,512]{2,1,0:T(8,128)(2,1)}, u32[]{:S(2)}, u32[]{:S(2)}) collective-permute-start(bf16[4,128,512]{2,1,0:T(8,128)(2,1)S(1)} %all-to-all-done.rest_0_), channel_id=1, source_target_pairs={{0,2},{1,3},{2,0},{3,1},{4,6},{5,7},{6,4},{7,5},{8,10},{9,11},{10,... | collective-permute-start | bytes 1572872 | tf_op jit(solution)/shard_map/ppermute | solution.py:369
  51.3 2.5 %copy-start.2 = (bf16[4,128,512]{2,1,0:T(8,128)(2,1)}, bf16[4,128,512]{2,1,0:T(8,128)(2,1)S(1)}, u32[]{:S(2)}) copy-start(bf16[4,128,512]{2,1,0:T(8,128)(2,1)S(1)} %collective-permute-done.5.rest_1_) | copy-start | bytes 1572868
  53.8 17.8 %all-to-all-start.3 = ((bf16[4,128,512]{2,1,0:T(8,128)(2,1)}), bf16[4,128,512]{2,1,0:T(8,128)(2,1)S(1)}, u32[]{:S(2)}, u32[]{:S(2)}) async-start(bf16[4,128,512]{2,1,0:T(8,128)(2,1)} %mix_second.3), calls=%async_computation.3 | async-start | bytes 1048576 | tf_op jit(solution)/shard_map/all_to_all | solution.py:436
  57.3 3.3 %collective-permute-start.2 = (bf16[4,128,512]{2,1,0:T(8,128)(2,1)S(1)}, bf16[4,128,512]{2,1,0:T(8,128)(2,1)S(1)}, u32[]{:S(2)}, u32[]{:S(2)}) collective-permute-start(bf16[4,128,512]{2,1,0:T(8,128)(2,1)S(1)} %all-to-all-done.rest_0_), channel_id=1, source_target_pairs={{0,1},{1,0},{2,3},{3,2},{4,5},{5,4},{6,7},{7,6},{8,9},{9,8},{10,11... | collective-permute-start | bytes 1572872 | tf_op jit(solution)/shard_map/ppermute | solution.py:369
  60.6 2.1 %collective-permute-start.4 = (bf16[4,128,512]{2,1,0:T(8,128)(2,1)}, bf16[4,128,512]{2,1,0:T(8,128)(2,1)S(1)}, u32[]{:S(2)}, u32[]{:S(2)}) collective-permute-start(bf16[4,128,512]{2,1,0:T(8,128)(2,1)} %collective-permute-done.3.rest_2_), channel_id=1, source_target_pairs={{0,1},{1,0},{2,3},{3,2},{4,5},{5,4},{6,7},{7,6},{8,9},{9,8},{10,11... | collective-permute-start | bytes 1572872 | tf_op jit(solution)/shard_map/ppermute | solution.py:369
  72.4 17.4 %all-to-all-start.1 = ((bf16[4,128,512]{2,1,0:T(8,128)(2,1)}), bf16[4,128,512]{2,1,0:T(8,128)(2,1)S(1)}, u32[]{:S(2)}, u32[]{:S(2)}) async-start(bf16[4,128,512]{2,1,0:T(8,128)(2,1)} %mix_second.2), calls=%async_computation.1 | async-start | bytes 1048576 | tf_op jit(solution)/shard_map/all_to_all | solution.py:436
  75.9 1.0 copy-start.13
  81.9 1.3 copy-start.8
  89.9 1.6 copy-start.9
  100.5 3.6 %collective-permute-start.17 = (bf16[512,512]{1,0:T(8,128)(2,1)S(1)}, bf16[512,512]{1,0:T(8,128)(2,1)}, u32[]{:S(2)}, u32[]{:S(2)}) collective-permute-start(bf16[512,512]{1,0:T(8,128)(2,1)S(1)} %fusion), channel_id=1, source_target_pairs={{0,1},{1,0},{2,3},{3,2},{4,5},{5,4},{6,7},{7,6},{8,9},{9,8},{10,11... | collective-permute-start | bytes 1572872 | tf_op jit(solution)/shard_map/ppermute | solution.py:369
  100.6 18.9 %all-to-all-start.6 = ((bf16[4,128,512]{2,1,0:T(8,128)(2,1)}), bf16[4,128,512]{2,1,0:T(8,128)(2,1)S(1)}, u32[]{:S(2)}, u32[]{:S(2)}) async-start(bf16[4,128,512]{2,1,0:T(8,128)(2,1)} %bitcast.106), calls=%async_computation.6 | async-start | bytes 1048576 | tf_op jit(solution)/shard_map/all_to_all | solution.py:436
  108.4 14.8 %collective-permute-start.18 = (bf16[256,512]{1,0:T(8,128)(2,1)}, bf16[256,512]{1,0:T(8,128)(2,1)S(1)}, u32[]{:S(2)}, u32[]{:S(2)}) collective-permute-start(bf16[256,512]{1,0:T(8,128)(2,1)} %fusion.1), channel_id=1, source_target_pairs={{0,2},{1,3},{2,0},{3,1},{4,6},{5,7},{6,4},{7,5},{8,10},{9,11},{10,... | collective-permute-start | bytes 786440 | tf_op jit(solution)/shard_map/ppermute | solution.py:369
  119.5 26.0 %all-to-all-start.4 = ((bf16[4,128,512]{2,1,0:T(8,128)(2,1)}), bf16[4,128,512]{2,1,0:T(8,128)(2,1)S(1)}, u32[]{:S(2)}, u32[]{:S(2)}) async-start(bf16[4,128,512]{2,1,0:T(8,128)(2,1)} %bitcast.104), calls=%async_computation.4 | async-start | bytes 1048576 | tf_op jit(solution)/shard_map/all_to_all | solution.py:436
  124.3 4.2 %copy-start.19 = (f32[256,512]{1,0:T(8,128)}, f32[256,512]{1,0:T(8,128)S(1)}, u32[]{:S(2)}) copy-start(f32[256,512]{1,0:T(8,128)S(1)} %bitcast_add_fusion.1) | copy-start | bytes 1572868
  124.4 9.9 %collective-permute-start.19 = (bf16[64,512]{1,0:T(8,128)(2,1)S(1)}, bf16[64,512]{1,0:T(8,128)(2,1)S(1)}, u32[]{:S(2)}, u32[]{:S(2)}) collective-permute-start(bf16[64,512]{1,0:T(8,128)(2,1)S(1)} %get-tuple-element.35), channel_id=1, source_target_pairs={{0,4},{1,5},{2,6},{3,7},{4,0},{5,1},{6,2},{7,3},{8,12},{9,13},{10,... | collective-permute-start | bytes 196616 | tf_op jit(solution)/shard_map/ppermute | solution.py:369
  126.2 13.0 %collective-permute-start.21 = (bf16[64,512]{1,0:T(8,128)(2,1)S(1)}, bf16[64,512]{1,0:T(8,128)(2,1)S(1)}, u32[]{:S(2)}, u32[]{:S(2)}) collective-permute-start(bf16[64,512]{1,0:T(8,128)(2,1)S(1)} %get-tuple-element.36), channel_id=1, source_target_pairs={{0,12},{1,13},{2,14},{3,15},{4,8},{5,9},{6,10},{7,11},{8,4},{9,5},... | collective-permute-start | bytes 196616 | tf_op jit(solution)/shard_map/ppermute | solution.py:369
  128.6 14.6 %collective-permute-start.20 = (bf16[64,512]{1,0:T(8,128)(2,1)S(1)}, bf16[64,512]{1,0:T(8,128)(2,1)S(1)}, u32[]{:S(2)}, u32[]{:S(2)}) collective-permute-start(bf16[64,512]{1,0:T(8,128)(2,1)S(1)} %get-tuple-element.37), channel_id=1, source_target_pairs={{0,8},{1,9},{2,10},{3,11},{4,12},{5,13},{6,14},{7,15},{8,0},{9,1},... | collective-permute-start | bytes 196616 | tf_op jit(solution)/shard_map/ppermute | solution.py:369
  128.6 23.4 %collective-permute-start.12 = (bf16[4,128,512]{2,1,0:T(8,128)(2,1)S(1)}, bf16[4,128,512]{2,1,0:T(8,128)(2,1)}, u32[]{:S(2)}, u32[]{:S(2)}) collective-permute-start(bf16[4,128,512]{2,1,0:T(8,128)(2,1)S(1)} %all-to-all-done.6.rest_0_.g_ref), channel_id=1, source_target_pairs={{0,2},{1,3},{2,0},{3,1},{4,6},{5,7},{6,4},{7,5},{8,10},{9,11},{10,... | collective-permute-start | bytes 1572872 | tf_op jit(solution)/shard_map/ppermute | solution.py:369
  145.5 4.3 %collective-permute-start.22 = (bf16[64,512]{1,0:T(8,128)(2,1)S(1)}, bf16[64,512]{1,0:T(8,128)(2,1)S(1)}, u32[]{:S(2)}, u32[]{:S(2)}) collective-permute-start(bf16[64,512]{1,0:T(8,128)(2,1)S(1)} %get-tuple-element.30), channel_id=1, source_target_pairs={{0,4},{1,5},{2,6},{3,7},{4,0},{5,1},{6,2},{7,3},{8,12},{9,13},{10,... | collective-permute-start | bytes 196616 | tf_op jit(solution)/shard_map/ppermute | solution.py:369
  145.5 25.2 %collective-permute-start.11 = (bf16[4,128,512]{2,1,0:T(8,128)(2,1)S(1)}, bf16[4,128,512]{2,1,0:T(8,128)(2,1)}, u32[]{:S(2)}, u32[]{:S(2)}) collective-permute-start(bf16[4,128,512]{2,1,0:T(8,128)(2,1)S(1)} %all-to-all-done.6.rest_0_.g_ref), channel_id=1, source_target_pairs={{0,1},{1,0},{2,3},{3,2},{4,5},{5,4},{6,7},{7,6},{8,9},{9,8},{10,11... | collective-permute-start | bytes 1572872 | tf_op jit(solution)/shard_map/ppermute | solution.py:369
  145.5 33.3 %collective-permute-start.9 = (bf16[4,128,512]{2,1,0:T(8,128)(2,1)S(1)}, bf16[4,128,512]{2,1,0:T(8,128)(2,1)}, u32[]{:S(2)}, u32[]{:S(2)}) collective-permute-start(bf16[4,128,512]{2,1,0:T(8,128)(2,1)S(1)} %all-to-all-done.4.rest_0_.g_ref), channel_id=1, source_target_pairs={{0,2},{1,3},{2,0},{3,1},{4,6},{5,7},{6,4},{7,5},{8,10},{9,11},{10,... | collective-permute-start | bytes 1572872 | tf_op jit(solution)/shard_map/ppermute | solution.py:369
  147.0 7.9 %collective-permute-start.23 = (bf16[64,512]{1,0:T(8,128)(2,1)S(1)}, bf16[64,512]{1,0:T(8,128)(2,1)S(1)}, u32[]{:S(2)}, u32[]{:S(2)}) collective-permute-start(bf16[64,512]{1,0:T(8,128)(2,1)S(1)} %get-tuple-element.30), channel_id=1, source_target_pairs={{0,8},{1,9},{2,10},{3,11},{4,12},{5,13},{6,14},{7,15},{8,0},{9,1},... | collective-permute-start | bytes 196616 | tf_op jit(solution)/shard_map/ppermute | solution.py:369
  149.7 6.2 %collective-permute-start.24 = (bf16[64,512]{1,0:T(8,128)(2,1)S(1)}, bf16[64,512]{1,0:T(8,128)(2,1)S(1)}, u32[]{:S(2)}, u32[]{:S(2)}) collective-permute-start(bf16[64,512]{1,0:T(8,128)(2,1)S(1)} %get-tuple-element.30), channel_id=1, source_target_pairs={{0,12},{1,13},{2,14},{3,15},{4,8},{5,9},{6,10},{7,11},{8,4},{9,5},... | collective-permute-start | bytes 196616 | tf_op jit(solution)/shard_map/ppermute | solution.py:369
  152.0 18.7 %collective-permute-start.13 = (bf16[4,128,512]{2,1,0:T(8,128)(2,1)}, bf16[4,128,512]{2,1,0:T(8,128)(2,1)}, u32[]{:S(2)}, u32[]{:S(2)}) collective-permute-start(bf16[4,128,512]{2,1,0:T(8,128)(2,1)} %collective-permute-done.12.rest_2_), channel_id=1, source_target_pairs={{0,1},{1,0},{2,3},{3,2},{4,5},{5,4},{6,7},{7,6},{8,9},{9,8},{10,11... | collective-permute-start | bytes 1572872 | tf_op jit(solution)/shard_map/ppermute | solution.py:369
  156.5 22.2 %collective-permute-start.25 = (bf16[256,512]{1,0:T(8,128)(2,1)}, bf16[256,512]{1,0:T(8,128)(2,1)}, u32[]{:S(2)}, u32[]{:S(2)}) collective-permute-start(bf16[256,512]{1,0:T(8,128)(2,1)} %bitcast.52), channel_id=1, source_target_pairs={{0,2},{1,3},{2,0},{3,1},{4,6},{5,7},{6,4},{7,5},{8,10},{9,11},{10,... | collective-permute-start | bytes 786440 | tf_op jit(solution)/shard_map/ppermute | solution.py:369
  157.9 1.0 copy-start.1
  159.0 1.0 copy-start.3
  164.3 1.0 copy-start.5
  165.3 1.0 copy-start.7
  173.4 15.5 %all-to-all-start.7 = ((bf16[4,128,512]{2,1,0:T(8,128)(2,1)}), bf16[4,128,512]{2,1,0:T(8,128)(2,1)S(1)}, u32[]{:S(2)}, u32[]{:S(2)}) async-start(bf16[4,128,512]{2,1,0:T(8,128)(2,1)} %mix_second_back.3), calls=%async_computation.7 | async-start | bytes 1048576 | tf_op jit(solution)/shard_map/all_to_all | solution.py:436
  177.6 14.8 %collective-permute-start.15 = (f32[64,4,16]{0,2,1:T(8,128)}, f32[64,4,16]{0,2,1:T(8,128)}, u32[]{:S(2)}, u32[]{:S(2)}) collective-permute-start(f32[64,4,16]{0,2,1:T(8,128)} %bitcast.31), channel_id=1, source_target_pairs={{0,2},{1,3},{2,0},{3,1},{4,6},{5,7},{6,4},{7,5},{8,10},{9,11},{10,... | collective-permute-start | bytes 49160 | tf_op jit(solution)/shard_map/ppermute | solution.py:369
  178.2 3.0 %collective-permute-start.14 = (f32[64,4,16]{0,2,1:T(8,128)S(1)}, f32[64,4,16]{0,2,1:T(8,128)S(1)}, u32[]{:S(2)}, u32[]{:S(2)}) collective-permute-start(f32[64,4,16]{0,2,1:T(8,128)S(1)} %bitcast.128), channel_id=1, source_target_pairs={{0,1},{1,0},{2,3},{3,2},{4,5},{5,4},{6,7},{7,6},{8,9},{9,8},{10,11... | collective-permute-start | bytes 49160 | tf_op jit(solution)/shard_map/ppermute | solution.py:369
  178.2 4.1 %collective-permute-start.8 = (bf16[4,128,512]{2,1,0:T(8,128)(2,1)S(1)}, bf16[4,128,512]{2,1,0:T(8,128)(2,1)S(1)}, u32[]{:S(2)}, u32[]{:S(2)}) collective-permute-start(bf16[4,128,512]{2,1,0:T(8,128)(2,1)S(1)} %all-to-all-done.4.rest_0_.g_ref), channel_id=1, source_target_pairs={{0,1},{1,0},{2,3},{3,2},{4,5},{5,4},{6,7},{7,6},{8,9},{9,8},{10,11... | collective-permute-start | bytes 1572872 | tf_op jit(solution)/shard_map/ppermute | solution.py:369
  178.8 3.6 %collective-permute-start.10 = (bf16[4,128,512]{2,1,0:T(8,128)(2,1)}, bf16[4,128,512]{2,1,0:T(8,128)(2,1)S(1)}, u32[]{:S(2)}, u32[]{:S(2)}) collective-permute-start(bf16[4,128,512]{2,1,0:T(8,128)(2,1)} %collective-permute-done.9.rest_2_), channel_id=1, source_target_pairs={{0,1},{1,0},{2,3},{3,2},{4,5},{5,4},{6,7},{7,6},{8,9},{9,8},{10,11... | collective-permute-start | bytes 1572872 | tf_op jit(solution)/shard_map/ppermute | solution.py:369
  179.8 2.5 %copy-start.18 = (bf16[256,512]{1,0:T(8,128)(2,1)}, bf16[256,512]{1,0:T(8,128)(2,1)S(1)}, u32[]{:S(2)}) copy-start(bf16[256,512]{1,0:T(8,128)(2,1)S(1)} %get-tuple-element.34) | copy-start | bytes 786436
  180.7 12.4 %collective-permute-start.26 = (bf16[512,512]{1,0:T(8,128)(2,1)}, bf16[512,512]{1,0:T(8,128)(2,1)}, u32[]{:S(2)}, u32[]{:S(2)}) collective-permute-start(bf16[512,512]{1,0:T(8,128)(2,1)} %pad_maximum_fusion.2), channel_id=1, source_target_pairs={{0,1},{1,0},{2,3},{3,2},{4,5},{5,4},{6,7},{7,6},{8,9},{9,8},{10,11... | collective-permute-start | bytes 1572872 | tf_op jit(solution)/shard_map/ppermute | solution.py:369
  181.3 13.3 %collective-permute-start.16 = (f32[64,4,16]{0,2,1:T(8,128)}, f32[64,4,16]{0,2,1:T(8,128)}, u32[]{:S(2)}, u32[]{:S(2)}) collective-permute-start(f32[64,4,16]{0,2,1:T(8,128)} %bitcast.33), channel_id=1, source_target_pairs={{0,3},{1,2},{2,1},{3,0},{4,7},{5,6},{6,5},{7,4},{8,11},{9,10},{10,... | collective-permute-start | bytes 49160 | tf_op jit(solution)/shard_map/ppermute | solution.py:369
  188.9 16.0 %all-to-all-start.5 = ((bf16[4,128,512]{2,1,0:T(8,128)(2,1)}), bf16[4,128,512]{2,1,0:T(8,128)(2,1)S(1)}, u32[]{:S(2)}, u32[]{:S(2)}) async-start(bf16[4,128,512]{2,1,0:T(8,128)(2,1)} %mix_second_back.2), calls=%async_computation.5 | async-start | bytes 1048576 | tf_op jit(solution)/shard_map/all_to_all | solution.py:436
  195.3 6.5 %copy-start.20 = (f32[4,64,4,16]{1,3,0,2:T(8,128)}, f32[4,64,4,16]{1,3,0,2:T(8,128)S(1)}, u32[]{:S(2)}) copy-start(f32[4,64,4,16]{1,3,0,2:T(8,128)S(1)} %bitcast_dynamic-update-slice_fusion.4) | copy-start | bytes 196612
  204.9 1.0 copy-start.15
  (8 other events, 6.7 us)

commit v6 on v4

v6 whole, which is shorter than its diff:
```python
import jax
import jax.numpy as jnp
from jax import lax
from jax.experimental import pallas as pl
from jax.experimental.pallas import tpu as pltpu
from jax.sharding import PartitionSpec as P

BF = jnp.bfloat16
F32 = jnp.float32
VMEM_BYTES = 40 * 1024 * 1024
ANY = pl.BlockSpec(memory_space=pl.ANY)
SCALAR = pl.BlockSpec(memory_space=pltpu.SMEM)


def in_hbm(array):
    return pltpu.with_memory_space_constraint(array, pltpu.HBM)


def sigmoid(z):
    return 0.5 + 0.5 * jnp.tanh(0.5 * z)


def dot(a, b, ca, cb, **kw):
    return lax.dot_general(a, b, (((ca,), (cb,)), ((), ())), preferred_element_type=F32, **kw)


def params(steps=1):
    return pltpu.CompilerParams(
        dimension_semantics=("arbitrary",) * steps, vmem_limit_bytes=VMEM_BYTES
    )


def cost(flops, moved, trans=0):
    return pl.CostEstimate(flops=int(flops), bytes_accessed=int(moved), transcendentals=int(trans))


def row_copies(src, dst, sems, first, parts):
    rows = src.shape[0] // parts
    return [
        pltpu.make_async_copy(
            src.at[pl.ds(i * rows, rows)], dst.at[pl.ds(i * rows, rows)], sems.at[first + i]
        )
        for i in range(parts)
    ]


def mix_first(factor, blocked):
    block, channels = factor.shape[0], blocked.shape[1]
    tiles = 4
    step = block // tiles

    def body(f_hbm, x_hbm, u_hbm, f_all, x_all, u_all, sems):
        xs = row_copies(x_hbm, x_all, sems, 0, tiles)
        fs = row_copies(f_hbm, f_all, sems, tiles, tiles)
        us = row_copies(u_all, u_hbm, sems, 2 * tiles, tiles)
        for c in xs + fs:
            c.start()
        for c in xs:
            c.wait()
        for t in range(tiles):
            fs[t].wait()
            at = slice(t * step, (t + 1) * step)
            u_all[at, :] = dot(f_all[at, :], x_all[...], 1, 0).astype(BF)
            us[t].start()
        for c in us:
            c.wait()

    return pl.pallas_call(
        body,
        in_specs=[ANY, ANY],
        out_specs=ANY,
        out_shape=pltpu.HBM((block, channels), BF),
        scratch_shapes=[
            pltpu.VMEM((block, block), BF),
            pltpu.VMEM((block, channels), BF),
            pltpu.VMEM((block, channels), BF),
            pltpu.SemaphoreType.DMA((3 * tiles,)),
        ],
        compiler_params=params(0),
        cost_estimate=cost(2 * block * block * channels, 2 * block * (block + 2 * channels)),
        name="mix_first",
    )(in_hbm(factor), in_hbm(blocked))


def spread_factor(factor_two):
    here, n, _ = factor_two.shape
    groups = here // 16
    wide = n * 16
    turned = factor_two.reshape(groups, 16, n, n).transpose(0, 2, 1, 3).reshape(groups, wide, n)

    def body(in_ref, out_ref):
        col = lax.broadcasted_iota(jnp.int32, (n, wide), 1)
        row = lax.broadcasted_iota(jnp.int32, (n, wide), 0)
        pick = jnp.where(col // 16 == row, 1.0, 0.0).astype(BF)
        r = lax.broadcasted_iota(jnp.int32, (wide, wide), 0)
        c = lax.broadcasted_iota(jnp.int32, (wide, wide), 1)
        same = r % 16 == c % 16
        full = dot(in_ref[0], pick, 1, 0)
        out_ref[0] = jnp.where(same, full, 0.0).astype(BF)

    return pl.pallas_call(
        body,
        grid=(groups,),
        in_specs=[pl.BlockSpec((1, wide, n), lambda g: (g, 0, 0))],
        out_specs=pl.BlockSpec((1, wide, wide), lambda g: (g, 0, 0)),
        out_shape=jax.ShapeDtypeStruct((groups, wide, wide), BF),
        compiler_params=params(),
        cost_estimate=cost(2 * groups * wide * wide * n, 2 * groups * wide * wide),
        name="spread_factor",
    )(turned)


def mix_second(spread, cols, back):
    n, here, channels = cols.shape
    wide = n * 16
    groups = here // 16

    def body(m_ref, in_ref, out_ref):
        rows = in_ref[...].reshape(wide, channels)
        got = dot(m_ref[0], rows, 0 if back else 1, 0).astype(BF)
        out_ref[...] = got.reshape(n, 16, channels)

    blocks = pl.BlockSpec((n, 16, channels), lambda g: (0, g, 0))
    return pl.pallas_call(
        body,
        grid=(groups,),
        in_specs=[pl.BlockSpec((1, wide, wide), lambda g: (g, 0, 0)), blocks],
        out_specs=blocks,
        out_shape=pltpu.HBM(cols.shape, BF) if back else jax.ShapeDtypeStruct(cols.shape, BF),
        compiler_params=params(),
        cost_estimate=cost(
            2 * groups * wide * wide * channels, 4 * cols.size + 2 * groups * wide * wide
        ),
        name="mix_second_back" if back else "mix_second",
    )(spread, cols)


def grad_second(grads, firsts, scale):
    n, here, channels = grads.shape
    wide = n * 16
    groups = here // 16

    def body(g_ref, u_ref, out_ref):
        g = g_ref[...].reshape(wide, channels)
        u = u_ref[...].reshape(wide, channels)
        full = dot(g, u, 1, 1)
        r = lax.broadcasted_iota(jnp.int32, (wide, wide), 0)
        c = lax.broadcasted_iota(jnp.int32, (wide, wide), 1)
        kept = jnp.where(r % 16 == c % 16, full, 0.0)
        row = lax.broadcasted_iota(jnp.int32, (wide, n), 0)
        col = lax.broadcasted_iota(jnp.int32, (wide, n), 1)
        pick = jnp.where(row // 16 == col, 1.0, 0.0)
        out_ref[0] = dot(kept, pick, 1, 0, precision=lax.Precision.HIGHEST) * scale

    out = pl.pallas_call(
        body,
        grid=(groups,),
        in_specs=[pl.BlockSpec((n, 16, channels), lambda g: (0, g, 0))] * 2,
        out_specs=pl.BlockSpec((1, wide, n), lambda g: (g, 0, 0)),
        out_shape=jax.ShapeDtypeStruct((groups, wide, n), F32),
        compiler_params=params(),
        cost_estimate=cost(2 * groups * wide * wide * channels, 4 * grads.size),
        name="grad_second",
    )(grads, firsts)
    return out.reshape(groups, n, 16, n).transpose(0, 2, 1, 3).reshape(here, n, n)


def middle(half, blocked, incoming, mixed, up_blocks, down_blocks):
    groups, width, inner = up_blocks.shape
    sub = inner // groups
    rows, channels = blocked.shape
    step = min(256, rows)
    last = rows // step - 1

    def body(half_ref, x_ref, g_ref, v_ref, up_ref, down_ref, dv_ref, r_ref, kept_ref, sent_ref, w):
        i = pl.program_id(0)

        @pl.when(i == 0)
        def _():
            w[...] = jnp.zeros_like(w)

        x = x_ref[...].astype(F32)
        g = g_ref[...]
        v = v_ref[...].astype(F32)
        sx = sigmoid(x)
        gate = x * sx
        h = (x + v * gate).astype(BF)
        h_parts = [h[:, b * width : (b + 1) * width] for b in range(groups)]
        g_parts = [g[:, b * width : (b + 1) * width] for b in range(groups)]
        acts, slopes, back = [], [], []
        for b in range(groups):
            a = dot(h_parts[b], up_ref[b], 1, 0)
            s = sigmoid(a)
            q = a * s
            acts.append(q.astype(BF))
            slopes.append(s + q * (1.0 - s))
            back.append(dot(g_parts[b], down_ref[b], 1, 1))
        grads = []
        for b in range(groups):
            lanes = slice(b * sub, (b + 1) * sub)
            perm = jnp.concatenate([acts[p][:, lanes] for p in range(groups)], axis=1)
            w[1, b] += dot(g_parts[b], perm, 0, 0)
            dq = jnp.concatenate([back[p][:, lanes] for p in range(groups)], axis=1)
            da = (dq * slopes[b]).astype(BF)
            w[0, b] += dot(h_parts[b], da, 0, 0)
            grads.append(dot(da, up_ref[b], 1, 1))
        dh = (g.astype(F32) + jnp.concatenate(grads, axis=1)).astype(BF).astype(F32)
        dv_ref[...] = (dh * gate).astype(BF)
        r_ref[...] = (dh * (1.0 + v * (sx + gate * (1.0 - sx)))).astype(BF)

        @pl.when(i == last)
        def _():
            kept_ref[...] = w[half_ref[0]].astype(BF)
            sent_ref[...] = w[1 - half_ref[0]].astype(BF)

    block = pl.BlockSpec((step, channels), lambda i: (i, 0))
    full = pl.BlockSpec(up_blocks.shape, lambda i: (0, 0, 0))
    hidden = rows * groups * inner
    return pl.pallas_call(
        body,
        grid=(last + 1,),
        in_specs=[
            SCALAR,
            block,
            block,
            block,
            full,
            pl.BlockSpec(down_blocks.shape, lambda i: (0, 0, 0)),
        ],
        out_specs=[block, block, full, full],
        out_shape=[
            pltpu.HBM((rows, channels), BF),
            pltpu.HBM((rows, channels), BF),
            pltpu.HBM(up_blocks.shape, BF),
            pltpu.HBM(up_blocks.shape, BF),
        ],
        scratch_shapes=[pltpu.VMEM((2, groups, width, inner), F32)],
        compiler_params=params(),
        cost_estimate=cost(
            10 * hidden * width, 10 * rows * channels + 8 * groups * width * inner, hidden
        ),
        name="middle",
    )(half, in_hbm(blocked), in_hbm(incoming), mixed, in_hbm(up_blocks), in_hbm(down_blocks))


def finish(factor, grad_first, blocked, gate_grad, scale):
    block, channels = blocked.shape
    tiles = 4
    step = block // tiles

    def body(f_hbm, d_hbm, x_hbm, r_hbm, one_hbm, out_hbm, f, d, x, r, one, out, sems):
        ds = row_copies(d_hbm, d, sems, 0, tiles)
        xs = row_copies(x_hbm, x, sems, tiles, tiles)
        fs = row_copies(f_hbm, f, sems, 2 * tiles, tiles)
        rs = row_copies(r_hbm, r, sems, 3 * tiles, tiles)
        ones = row_copies(one, one_hbm, sems, 4 * tiles, tiles)
        outs = row_copies(out, out_hbm, sems, 5 * tiles, tiles)
        for c in ds + xs + fs + rs:
            c.start()
        for c in xs:
            c.wait()
        for t in range(tiles):
            at = slice(t * step, (t + 1) * step)
            ds[t].wait()
            one[at, :] = dot(d[at, :], x[...], 1, 1) * scale
            ones[t].start()
        for c in fs + rs:
            c.wait()
        for t in range(tiles):
            at = slice(t * step, (t + 1) * step)
            total = dot(f[:, at], d[...], 0, 0) + r[at, :].astype(F32)
            out[at, :] = total.astype(BF)
            outs[t].start()
        for c in ones + outs:
            c.wait()

    return pl.pallas_call(
        body,
        in_specs=[ANY] * 4,
        out_specs=[ANY] * 2,
        out_shape=[pltpu.HBM((block, block), F32), pltpu.HBM((block, channels), BF)],
        scratch_shapes=[
            pltpu.VMEM((block, block), BF),
            pltpu.VMEM((block, channels), BF),
            pltpu.VMEM((block, channels), BF),
            pltpu.VMEM((block, channels), BF),
            pltpu.VMEM((block, block), F32),
            pltpu.VMEM((block, channels), BF),
            pltpu.SemaphoreType.DMA((6 * tiles,)),
        ],
        compiler_params=params(0),
        cost_estimate=cost(4 * block * block * channels, 6 * block * block + 8 * block * channels),
        name="finish",
    )(in_hbm(factor), grad_first, in_hbm(blocked), in_hbm(gate_grad))


def radices(count):
    steps, stride = [], 1
    while stride < count:
        radix = 4 if stride >= 4 and count // stride == 4 else 2
        steps.append((stride, radix))
        stride *= radix
    return steps


def swap(values, count, stride, s):
    return lax.ppermute(values, "seq", [(i, i ^ (stride * s)) for i in range(count)])


def scatter_step(total, count, stride, radix, after=None):
    digit = (lax.axis_index("seq") // stride) % radix
    cut = total.reshape(radix, total.shape[0] // radix, total.shape[1])
    kept = lax.dynamic_index_in_dim(cut, digit, 0, keepdims=False)
    got = []
    for s in range(1, radix):
        send = lax.dynamic_index_in_dim(cut, digit ^ s, 0, keepdims=False).astype(BF)
        got.append(swap(send, count, stride, s))
    if after is not None:
        got, after = lax.optimization_barrier((got, after))
    for g in got:
        kept = kept + g.astype(F32)
    return kept


def gather_step(share, count, stride, radix):
    digit = (lax.axis_index("seq") // stride) % radix
    got = [share] + [swap(share, count, stride, s) for s in range(1, radix)]
    if radix == 2:
        low = jnp.where(digit == 0, got[0], got[1])
        high = jnp.where(digit == 0, got[1], got[0])
        return jnp.concatenate([low, high], axis=0)
    whole = jnp.zeros((radix,) + share.shape, share.dtype)
    for s in range(radix):
        whole = lax.dynamic_update_index_in_dim(whole, got[s], digit ^ s, 0)
    return whole.reshape(radix * share.shape[0], share.shape[1])


def write_weights(total, up_shape, down_shape, scale):
    groups, width, inner = up_shape

    def body(up_in, down_in, up_ref, down_ref):
        up_ref[0] = up_in[...].astype(F32) * scale
        down_ref[0] = (down_in[...].astype(F32) * scale).T

    return pl.pallas_call(
        body,
        grid=(groups,),
        in_specs=[
            pl.BlockSpec((width, inner), lambda b: (b, 0)),
            pl.BlockSpec((width, inner), lambda b: (groups + b, 0)),
        ],
        out_specs=[
            pl.BlockSpec((1, width, inner), lambda b: (b, 0, 0)),
            pl.BlockSpec((1, inner, width), lambda b: (b, 0, 0)),
        ],
        out_shape=[
            jax.ShapeDtypeStruct(up_shape, F32),
            jax.ShapeDtypeStruct(down_shape, F32),
        ],
        compiler_params=params(),
        cost_estimate=cost(groups * width * inner, 12 * groups * width * inner),
        name="write_weights",
    )(total, total)


def on_device(tokens, cotangent, factor_one, factor_two, up_blocks, down_blocks):
    count = lax.axis_size("seq")
    block, channels = factor_one.shape[1], tokens.shape[1]
    here = block // count
    scale = float(count * tokens.shape[0]) ** (-0.5)
    factor = factor_one.reshape(block, block)
    grouped = here % 16 == 0

    def exchange(values):
        cut = values.reshape(count, here, channels)
        return lax.all_to_all(cut, "seq", split_axis=0, concat_axis=0, tiled=True)

    if grouped:
        spread = spread_factor(factor_two)

    def second(cols, back):
        if grouped:
            return mix_second(spread, cols, back)
        names = "kmj,mkc->jkc" if back else "kmj,jkc->mkc"
        return jnp.einsum(names, factor_two, cols, preferred_element_type=F32).astype(BF)

    def second_grad(grads, firsts):
        if grouped:
            return grad_second(grads, firsts, scale)
        return jnp.einsum("mkc,jkc->kmj", grads, firsts, preferred_element_type=F32) * scale

    half = (lax.axis_index("seq") % 2).astype(jnp.int32).reshape(1)
    firsts = exchange(mix_first(factor, tokens))
    mixed = exchange(second(firsts, False)).reshape(block, channels)
    dv, gate_grad, kept, sent = middle(half, tokens, cotangent, mixed, up_blocks, down_blocks)
    grad_mixed = exchange(dv)
    back = second(grad_mixed, True)
    grad_first = exchange(back).reshape(block, channels)
    inner = kept.shape[-1]
    total = kept.astype(F32) + swap(sent, count, 1, 1).astype(F32)
    total = total.reshape(-1, inner)
    steps = radices(count)
    for step in steps[1:-1]:
        total = scatter_step(total, count, *step)
    total = scatter_step(total, count, *steps[-1], after=back).astype(BF)
    for step in reversed(steps):
        total = gather_step(total, count, *step)
    grad_up, grad_down = write_weights(total, up_blocks.shape, down_blocks.shape, scale)
    two = second_grad(grad_mixed, firsts)
    one, grad_tokens = finish(factor, grad_first, tokens, gate_grad, scale)
    return (grad_tokens, one.reshape(1, block, block), two, grad_up, grad_down)


def solution(mesh):
    return jax.shard_map(
        on_device,
        mesh=mesh,
        in_specs=(
            P(("grp", "seq"), None),
            P(("grp", "seq"), None),
            P("seq", None, None),
            P("seq", None, None),
            P(),
            P(),
        ),
        out_specs=(
            P(("grp", "seq"), None),
            P(("grp", "seq"), None, None),
            P(("grp", "seq"), None, None),
            P("grp", None, None),
            P("grp", None, None),
        ),
        check_vma=False,
    )
```

time: 163 us -> 175 us (1.074)
  waiting for transfers between devices: 56.7 us -> 97.3 us
  blocking collectives: 31.5 us -> 0 us
  starting transfers between devices: 30.4 us -> 38.4 us
  local copies, waits for them, and re-layouts: 9.39 us -> 2.6 us
    all_to_all x1 -> x0, blocking collectives: 31.5 us -> none  [exchange(): got = lax.all_to_all(cut, 'seq', split_axis=0, concat_axis=0, tiled=True)]
    all_to_all x3 -> x4, waiting for transfers between devices: 21.9 us -> 44.8 us  [exchange(): return lax.all_to_all(cut, 'seq', split_axis=0, concat_axis=0, tiled=True)]
    ppermute x10, waiting for transfers between devices: 34.8 us -> 52.5 us  [swap(): lax.ppermute(values, 'seq', [(i, i ^ stride * s) for i in range(count)])]
    all_to_all x3 -> x4, starting transfers between devices: 16.8 us -> 25.7 us  [exchange(): return lax.all_to_all(cut, 'seq', split_axis=0, concat_axis=0, tiled=True)]
    unnamed x14 -> x6, local copies, waits for them, and re-layouts: 6.45 us -> 0.98 us
    pallas_call x2, Pallas kernels: 2.24 us -> 4.44 us  [mix_second(): pl.pallas_call(body, grid=(groups,), in_specs=[pl.BlockSpec((1, wide, wid...]
  transfers between devices with their start and end apart: 13 -> 14, of which waited for: 6 -> 7; matrix products, arithmetic and copies ran while one was open for 5% -> 3% of each run, Pallas kernels for 3% -> 4%
where the time goes in v6:
time: 175 us; the launch traced here: 174 us
  waiting for transfers between devices  97.3 us (56%)
  starting transfers between devices  38.4 us (22%)
  Pallas kernels  29.2 us (17%)
  other arithmetic  5.35 us (3%)
  local copies, waits for them, and re-layouts  2.6 us (1%)
    ppermute x10, waiting for transfers between devices, swap(): lax.ppermute(values, 'seq', [(i, i ^ stride * s) for i in range(count)])  52.5 us
    all_to_all x4, waiting for transfers between devices, exchange(): return lax.all_to_all(cut, 'seq', split_axis=0, concat_axis=0, tiled=True)  44.8 us
    all_to_all x4, starting transfers between devices, exchange(): return lax.all_to_all(cut, 'seq', split_axis=0, concat_axis=0, tiled=True)  25.7 us
    ppermute x10, starting transfers between devices, swap(): lax.ppermute(values, 'seq', [(i, i ^ stride * s) for i in range(count)])  12.7 us
    pallas_call x1, Pallas kernels, middle(): pl.pallas_call(body, grid=(last + 1,), in_specs=[SCALAR, block, block, bl...  9.75 us
    pallas_call x1, Pallas kernels, finish(): pl.pallas_call(body, in_specs=[ANY] * 4, out_specs=[ANY] * 2, out_shape=[...  5.6 us
    pallas_call x2, Pallas kernels, mix_second(): pl.pallas_call(body, grid=(groups,), in_specs=[pl.BlockSpec((1, wide, wid...  4.44 us
    pallas_call x1, Pallas kernels, mix_first(): pl.pallas_call(body, in_specs=[ANY, ANY], out_specs=ANY, out_shape=pltpu....  3.92 us
  transfers between devices with their start and end apart: 14, of which 7 were waited for; matrix products, arithmetic and copies ran while one was open for 3% of the time, Pallas kernels for 4%

profile of v6, /device:TPU:0, one launch (start us, length us, event | category | flops | bytes accessed | tf_op | source)
XLA Modules:
  0.0 173.8 jit_solution(15815424676694433031)
XLA Ops:
  0.6 3.9 %mix_first.1 = bf16[1024,512]{1,0:T(8,128)(2,1)} custom-call(bf16[1024,1024]{1,0:T(8,128)(2,1)} %bitcast.55, bf16[1024,512]{1,0:T(8,128)(2,1)} %x_hbm.3), custom_call_target="tpu_custom_call" | custom-call | flops 1073741824 | bytes 4194304 | tf_op jit(solution)/shard_map/mix_first/pallas_call | solution.py:68
  4.6 0.0 copy-start.2
  4.6 7.5 %all-to-all-start = ((bf16[16,64,512]{2,1,0:T(8,128)(2,1)}), bf16[16,64,512]{2,1,0:T(8,128)(2,1)S(1)}, u32[]{:S(2)}, u32[]{:S(2)}) async-start(bf16[16,64,512]{2,1,0:T(8,128)(2,1)} %bitcast.52), calls=%async_computation | async-start | bytes 2097152 | tf_op jit(solution)/shard_map/all_to_all | solution.py:376
  12.1 0.2 reshape.54
  12.3 0.2 copy.11
  12.5 0.7 spread_factor.1.m_ref
  13.2 21.9 %all-to-all-done.in_ref.u_ref = bf16[16,64,512]{2,1,0:T(8,128)(2,1)S(1)} async-done(((bf16[16,64,512]{2,1,0:T(8,128)(2,1)}), bf16[16,64,512]{2,1,0:T(8,128)(2,1)S(1)}, u32[]{:S(2)}, u32[]{:S(2)}) %all-to-all-start) | async-done | bytes 1048608 | tf_op jit(solution)/shard_map/all_to_all | solution.py:376
  35.0 2.2 %mix_second.1 = bf16[16,64,512]{2,1,0:T(8,128)(2,1)} custom-call(bf16[4,256,256]{2,1,0:T(8,128)(2,1)S(1)} %spread_factor.1.m_ref, bf16[16,64,512]{2,1,0:T(8,128)(2,1)S(1)} %all-to-all-done.in_ref.u_ref), custom_call_target="tpu_custom_call" | custom-call | flops 268435456 | bytes 2621440 | tf_op jit(solution)/shard_map/mix_second/pallas_call | solution.py:124
  37.2 6.8 %all-to-all-start.1 = ((bf16[16,64,512]{2,1,0:T(8,128)(2,1)}), bf16[16,64,512]{2,1,0:T(8,128)(2,1)S(1)}, u32[]{:S(2)}, u32[]{:S(2)}) async-start(bf16[16,64,512]{2,1,0:T(8,128)(2,1)} %mix_second.1), calls=%async_computation.1 | async-start | bytes 2097152 | tf_op jit(solution)/shard_map/all_to_all | solution.py:376
  44.1 22.9 %all-to-all-done.1 = bf16[16,64,512]{2,1,0:T(8,128)(2,1)S(1)} async-done(((bf16[16,64,512]{2,1,0:T(8,128)(2,1)}), bf16[16,64,512]{2,1,0:T(8,128)(2,1)S(1)}, u32[]{:S(2)}, u32[]{:S(2)}) %all-to-all-start.1) | async-done | bytes 1048608 | tf_op jit(solution)/shard_map/all_to_all | solution.py:376
  67.0 9.7 %middle.1 = (bf16[1024,512]{1,0:T(8,128)(2,1)}, bf16[1024,512]{1,0:T(8,128)(2,1)}, bf16[4,128,512]{2,1,0:T(8,128)(2,1)}, bf16[4,128,512]{2,1,0:T(8,128)(2,1)}) custom-call(s32[1]{0:T(128)} %bitcast.3.half_ref, bf16[1024,512]{1,0:T(8,128)(2,1)} %x_hbm.3, bf16[1024,512]{1,0:T(8,128)(2,1)} %g_ref.1, bf16[1024,512]{1,0:T(8,128)(2,1)S(1)} %bitcast.51, ...), custom_call_target="tpu_custom_call" | custom-call | flops 2684354560 | bytes 7340032 | tf_op jit(solution)/shard_map/middle/pallas_call | solution.py:219
  76.8 0.0 copy-start.1
  76.8 7.0 %all-to-all-start.2 = ((bf16[16,64,512]{2,1,0:T(8,128)(2,1)}), bf16[16,64,512]{2,1,0:T(8,128)(2,1)S(1)}, u32[]{:S(2)}, u32[]{:S(2)}) async-start(bf16[16,64,512]{2,1,0:T(8,128)(2,1)} %bitcast.59), calls=%async_computation.2 | async-start | bytes 2097152 | tf_op jit(solution)/shard_map/all_to_all | solution.py:376
  83.8 0.4 collective-permute-start
  84.2 1.9 %collective-permute-done = bf16[4,128,512]{2,1,0:T(8,128)(2,1)} collective-permute-done((bf16[4,128,512]{2,1,0:T(8,128)(2,1)}, bf16[4,128,512]{2,1,0:T(8,128)(2,1)}, u32[]{:S(2)}, u32[]{:S(2)}) %collective-permute-start) | collective-permute-done | bytes 524320 | tf_op jit(solution)/shard_map/ppermute | solution.py:307
  86.1 1.2 convert_add_fusion
  87.3 0.0 copy-start
  87.3 1.0 copy-done
  88.3 1.9 %collective-permute-start.1 = (bf16[256,512]{1,0:T(8,128)(2,1)S(1)}, bf16[256,512]{1,0:T(8,128)(2,1)S(1)}, u32[]{:S(2)}, u32[]{:S(2)}) collective-permute-start(bf16[256,512]{1,0:T(8,128)(2,1)S(1)} %fusion), channel_id=1, source_target_pairs={{0,2},{1,3},{2,0},{3,1},{4,6},{5,7},{6,4},{7,5},{8,10},{9,11},{10,... | collective-permute-start | bytes 786440 | tf_op jit(solution)/shard_map/ppermute | solution.py:307
  90.2 11.7 %collective-permute-done.1 = bf16[256,512]{1,0:T(8,128)(2,1)S(1)} collective-permute-done((bf16[256,512]{1,0:T(8,128)(2,1)S(1)}, bf16[256,512]{1,0:T(8,128)(2,1)S(1)}, u32[]{:S(2)}, u32[]{:S(2)}) %collective-permute-start.1) | collective-permute-done | bytes 262176 | tf_op jit(solution)/shard_map/ppermute | solution.py:307
  101.9 1.1 bitcast_add_fusion
  103.1 3.8 %collective-permute-start.4 = (bf16[64,512]{1,0:T(8,128)(2,1)S(1)}, bf16[64,512]{1,0:T(8,128)(2,1)S(1)}, u32[]{:S(2)}, u32[]{:S(2)}) collective-permute-start(bf16[64,512]{1,0:T(8,128)(2,1)S(1)} %get-tuple-element.33), channel_id=1, source_target_pairs={{0,12},{1,13},{2,14},{3,15},{4,8},{5,9},{6,10},{7,11},{8,4},{9,5},... | collective-permute-start | bytes 196616 | tf_op jit(solution)/shard_map/ppermute | solution.py:307
  106.9 0.0 collective-permute-start.3
  106.9 0.7 collective-permute-start.2
  107.5 2.3 %mix_second_back.1 = bf16[16,64,512]{2,1,0:T(8,128)(2,1)} custom-call(bf16[4,256,256]{2,1,0:T(8,128)(2,1)S(1)} %spread_factor.1.m_ref, bf16[16,64,512]{2,1,0:T(8,128)(2,1)S(1)} %all-to-all-done.2.in_ref.g_ref), custom_call_target="tpu_custom_call" | custom-call | flops 268435456 | bytes 2621440 | tf_op jit(solution)/shard_map/mix_second_back/pallas_call | solution.py:124
  109.8 0.0 collective-permute-done.4
  109.8 6.1 %collective-permute-done.3 = bf16[64,512]{1,0:T(8,128)(2,1)S(1)} collective-permute-done((bf16[64,512]{1,0:T(8,128)(2,1)S(1)}, bf16[64,512]{1,0:T(8,128)(2,1)S(1)}, u32[]{:S(2)}, u32[]{:S(2)}) %collective-permute-start.3) | collective-permute-done | bytes 65568 | tf_op jit(solution)/shard_map/ppermute | solution.py:307
  115.9 0.0 collective-permute-done.2
  116.0 0.9 bitcast_dynamic-update-slice_fusion.3
  116.9 0.1 collective-permute-start.5
  116.9 4.4 %all-to-all-start.3 = ((bf16[16,64,512]{2,1,0:T(8,128)(2,1)}), bf16[16,64,512]{2,1,0:T(8,128)(2,1)}, u32[]{:S(2)}, u32[]{:S(2)}) async-start(bf16[16,64,512]{2,1,0:T(8,128)(2,1)} %mix_second_back.1), calls=%async_computation.3 | async-start | bytes 2097152 | tf_op jit(solution)/shard_map/all_to_all | solution.py:376
  121.3 2.8 %collective-permute-start.6 = (bf16[64,512]{1,0:T(8,128)(2,1)S(1)}, bf16[64,512]{1,0:T(8,128)(2,1)S(1)}, u32[]{:S(2)}, u32[]{:S(2)}) collective-permute-start(bf16[64,512]{1,0:T(8,128)(2,1)S(1)} %get-tuple-element.28), channel_id=1, source_target_pairs={{0,8},{1,9},{2,10},{3,11},{4,12},{5,13},{6,14},{7,15},{8,0},{9,1},... | collective-permute-start | bytes 196616 | tf_op jit(solution)/shard_map/ppermute | solution.py:307
  124.1 1.5 collective-permute-start.7
  125.6 0.0 collective-permute-done.5
  125.6 26.9 %collective-permute-done.6 = bf16[64,512]{1,0:T(8,128)(2,1)S(1)} collective-permute-done((bf16[64,512]{1,0:T(8,128)(2,1)S(1)}, bf16[64,512]{1,0:T(8,128)(2,1)S(1)}, u32[]{:S(2)}, u32[]{:S(2)}) %collective-permute-start.6) | collective-permute-done | bytes 65568 | tf_op jit(solution)/shard_map/ppermute | solution.py:307
  152.5 1.5 collective-permute-start.8
  154.1 5.9 %collective-permute-done.8 = bf16[256,512]{1,0:T(8,128)(2,1)S(1)} collective-permute-done((bf16[256,512]{1,0:T(8,128)(2,1)S(1)}, bf16[256,512]{1,0:T(8,128)(2,1)S(1)}, u32[]{:S(2)}, u32[]{:S(2)}) %collective-permute-start.8) | collective-permute-done | bytes 262176 | tf_op jit(solution)/shard_map/ppermute | solution.py:307
  160.0 0.1 broadcast_select_fusion.3
  160.0 0.8 pad_maximum_fusion.1
  160.9 0.0 collective-permute-start.9
  160.9 2.9 %grad_second.1 = f32[4,256,16]{2,1,0:T(8,128)S(1)} custom-call(bf16[16,64,512]{2,1,0:T(8,128)(2,1)S(1)} %all-to-all-done.2.in_ref.g_ref, bf16[16,64,512]{2,1,0:T(8,128)(2,1)S(1)} %all-to-all-done.in_ref.u_ref), custom_call_target="tpu_custom_call" | custom-call | flops 268435456 | bytes 2097152 | tf_op jit(solution)/shard_map/grad_second/pallas_call | solution.py:155
  163.8 0.2 copy.12
  164.0 1.2 broadcast_select_fusion.1
  165.3 0.1 pad_maximum_fusion.up_in.down_in
  165.4 0.9 reshape.63
  166.3 1.9 %write_weights.1 = (f32[4,128,512]{2,1,0:T(8,128)}, f32[4,512,128]{2,1,0:T(8,128)}) custom-call(bf16[1024,512]{1,0:T(8,128)(2,1)S(1)} %pad_maximum_fusion.up_in.down_in, bf16[1024,512]{1,0:T(8,128)(2,1)S(1)} %pad_maximum_fusion.up_in.down_in), custom_call_target="tpu_custom_call" | custom-call | flops 262144 | bytes 3145728 | tf_op jit(solution)/shard_map/write_weights/pallas_call | solution.py:345
  168.2 0.0 all-to-all-done.3
  168.2 5.6 %finish.1 = (f32[1024,1024]{1,0:T(8,128)}, bf16[1024,512]{1,0:T(8,128)(2,1)}) custom-call(bf16[1024,1024]{1,0:T(8,128)(2,1)} %bitcast.56, bf16[1024,512]{1,0:T(8,128)(2,1)} %bitcast.7.d_hbm, bf16[1024,512]{1,0:T(8,128)(2,1)} %x_hbm.3, bf16[1024,512]{1,0:T(8,128)(2,1)} %get-tuple-element.17.r_hbm), custom_call_target="tpu_custom_call" | custom-call | flops 2147483648 | bytes 10485760 | tf_op jit(solution)/shard_map/finish/pallas_call | solution.py:277
  (11 shorter events, 0.1 us)
Async XLA Ops:
  4.6 7.5 %copy-start.2 = (bf16[64,16,16]{0,2,1:T(8,128)(2,1)S(1)}, bf16[64,16,16]{0,2,1:T(8,128)(2,1)}, u32[]{:S(2)}) copy-start(bf16[64,16,16]{0,2,1:T(8,128)(2,1)} %param.9) | copy-start | bytes 98308
  4.6 30.5 %all-to-all-start = ((bf16[16,64,512]{2,1,0:T(8,128)(2,1)}), bf16[16,64,512]{2,1,0:T(8,128)(2,1)S(1)}, u32[]{:S(2)}, u32[]{:S(2)}) async-start(bf16[16,64,512]{2,1,0:T(8,128)(2,1)} %bitcast.52), calls=%async_computation | async-start | bytes 2097152 | tf_op jit(solution)/shard_map/all_to_all | solution.py:376
  37.2 29.8 %all-to-all-start.1 = ((bf16[16,64,512]{2,1,0:T(8,128)(2,1)}), bf16[16,64,512]{2,1,0:T(8,128)(2,1)S(1)}, u32[]{:S(2)}, u32[]{:S(2)}) async-start(bf16[16,64,512]{2,1,0:T(8,128)(2,1)} %mix_second.1), calls=%async_computation.1 | async-start | bytes 2097152 | tf_op jit(solution)/shard_map/all_to_all | solution.py:376
  76.8 9.3 %copy-start.1 = (bf16[4,128,512]{2,1,0:T(8,128)(2,1)S(1)}, bf16[4,128,512]{2,1,0:T(8,128)(2,1)}, u32[]{:S(2)}) copy-start(bf16[4,128,512]{2,1,0:T(8,128)(2,1)} %get-tuple-element.20) | copy-start | bytes 1572868
  76.8 30.8 %all-to-all-start.2 = ((bf16[16,64,512]{2,1,0:T(8,128)(2,1)}), bf16[16,64,512]{2,1,0:T(8,128)(2,1)S(1)}, u32[]{:S(2)}, u32[]{:S(2)}) async-start(bf16[16,64,512]{2,1,0:T(8,128)(2,1)} %bitcast.59), calls=%async_computation.2 | async-start | bytes 2097152 | tf_op jit(solution)/shard_map/all_to_all | solution.py:376
  83.8 2.3 %collective-permute-start = (bf16[4,128,512]{2,1,0:T(8,128)(2,1)}, bf16[4,128,512]{2,1,0:T(8,128)(2,1)}, u32[]{:S(2)}, u32[]{:S(2)}) collective-permute-start(bf16[4,128,512]{2,1,0:T(8,128)(2,1)} %get-tuple-element.21), channel_id=1, source_target_pairs={{0,1},{1,0},{2,3},{3,2},{4,5},{5,4},{6,7},{7,6},{8,9},{9,8},{10,11... | collective-permute-start | bytes 1572872 | tf_op jit(solution)/shard_map/ppermute | solution.py:307
  87.3 1.0 copy-start
  88.3 13.6 %collective-permute-start.1 = (bf16[256,512]{1,0:T(8,128)(2,1)S(1)}, bf16[256,512]{1,0:T(8,128)(2,1)S(1)}, u32[]{:S(2)}, u32[]{:S(2)}) collective-permute-start(bf16[256,512]{1,0:T(8,128)(2,1)S(1)} %fusion), channel_id=1, source_target_pairs={{0,2},{1,3},{2,0},{3,1},{4,6},{5,7},{6,4},{7,5},{8,10},{9,11},{10,... | collective-permute-start | bytes 786440 | tf_op jit(solution)/shard_map/ppermute | solution.py:307
  103.1 6.7 %collective-permute-start.4 = (bf16[64,512]{1,0:T(8,128)(2,1)S(1)}, bf16[64,512]{1,0:T(8,128)(2,1)S(1)}, u32[]{:S(2)}, u32[]{:S(2)}) collective-permute-start(bf16[64,512]{1,0:T(8,128)(2,1)S(1)} %get-tuple-element.33), channel_id=1, source_target_pairs={{0,12},{1,13},{2,14},{3,15},{4,8},{5,9},{6,10},{7,11},{8,4},{9,5},... | collective-permute-start | bytes 196616 | tf_op jit(solution)/shard_map/ppermute | solution.py:307
  106.9 9.1 %collective-permute-start.3 = (bf16[64,512]{1,0:T(8,128)(2,1)S(1)}, bf16[64,512]{1,0:T(8,128)(2,1)S(1)}, u32[]{:S(2)}, u32[]{:S(2)}) collective-permute-start(bf16[64,512]{1,0:T(8,128)(2,1)S(1)} %get-tuple-element.34), channel_id=1, source_target_pairs={{0,8},{1,9},{2,10},{3,11},{4,12},{5,13},{6,14},{7,15},{8,0},{9,1},... | collective-permute-start | bytes 196616 | tf_op jit(solution)/shard_map/ppermute | solution.py:307
  106.9 9.1 %collective-permute-start.2 = (bf16[64,512]{1,0:T(8,128)(2,1)S(1)}, bf16[64,512]{1,0:T(8,128)(2,1)}, u32[]{:S(2)}, u32[]{:S(2)}) collective-permute-start(bf16[64,512]{1,0:T(8,128)(2,1)S(1)} %get-tuple-element.35), channel_id=1, source_target_pairs={{0,4},{1,5},{2,6},{3,7},{4,0},{5,1},{6,2},{7,3},{8,12},{9,13},{10,... | collective-permute-start | bytes 196616 | tf_op jit(solution)/shard_map/ppermute | solution.py:307
  116.9 8.8 %collective-permute-start.5 = (bf16[64,512]{1,0:T(8,128)(2,1)S(1)}, bf16[64,512]{1,0:T(8,128)(2,1)S(1)}, u32[]{:S(2)}, u32[]{:S(2)}) collective-permute-start(bf16[64,512]{1,0:T(8,128)(2,1)S(1)} %get-tuple-element.28), channel_id=1, source_target_pairs={{0,4},{1,5},{2,6},{3,7},{4,0},{5,1},{6,2},{7,3},{8,12},{9,13},{10,... | collective-permute-start | bytes 196616 | tf_op jit(solution)/shard_map/ppermute | solution.py:307
  116.9 51.3 %all-to-all-start.3 = ((bf16[16,64,512]{2,1,0:T(8,128)(2,1)}), bf16[16,64,512]{2,1,0:T(8,128)(2,1)}, u32[]{:S(2)}, u32[]{:S(2)}) async-start(bf16[16,64,512]{2,1,0:T(8,128)(2,1)} %mix_second_back.1), calls=%async_computation.3 | async-start | bytes 2097152 | tf_op jit(solution)/shard_map/all_to_all | solution.py:376
  121.3 31.2 %collective-permute-start.6 = (bf16[64,512]{1,0:T(8,128)(2,1)S(1)}, bf16[64,512]{1,0:T(8,128)(2,1)S(1)}, u32[]{:S(2)}, u32[]{:S(2)}) collective-permute-start(bf16[64,512]{1,0:T(8,128)(2,1)S(1)} %get-tuple-element.28), channel_id=1, source_target_pairs={{0,8},{1,9},{2,10},{3,11},{4,12},{5,13},{6,14},{7,15},{8,0},{9,1},... | collective-permute-start | bytes 196616 | tf_op jit(solution)/shard_map/ppermute | solution.py:307
  124.1 28.4 %collective-permute-start.7 = (bf16[64,512]{1,0:T(8,128)(2,1)S(1)}, bf16[64,512]{1,0:T(8,128)(2,1)S(1)}, u32[]{:S(2)}, u32[]{:S(2)}) collective-permute-start(bf16[64,512]{1,0:T(8,128)(2,1)S(1)} %get-tuple-element.28), channel_id=1, source_target_pairs={{0,12},{1,13},{2,14},{3,15},{4,8},{5,9},{6,10},{7,11},{8,4},{9,5},... | collective-permute-start | bytes 196616 | tf_op jit(solution)/shard_map/ppermute | solution.py:307
  152.5 7.4 %collective-permute-start.8 = (bf16[256,512]{1,0:T(8,128)(2,1)S(1)}, bf16[256,512]{1,0:T(8,128)(2,1)S(1)}, u32[]{:S(2)}, u32[]{:S(2)}) collective-permute-start(bf16[256,512]{1,0:T(8,128)(2,1)S(1)} %bitcast.60), channel_id=1, source_target_pairs={{0,2},{1,3},{2,0},{3,1},{4,6},{5,7},{6,4},{7,5},{8,10},{9,11},{10,... | collective-permute-start | bytes 786440 | tf_op jit(solution)/shard_map/ppermute | solution.py:307
  160.9 3.2 %collective-permute-start.9 = (bf16[512,512]{1,0:T(8,128)(2,1)}, bf16[512,512]{1,0:T(8,128)(2,1)}, u32[]{:S(2)}, u32[]{:S(2)}) collective-permute-start(bf16[512,512]{1,0:T(8,128)(2,1)} %pad_maximum_fusion.1), channel_id=1, source_target_pairs={{0,1},{1,0},{2,3},{3,2},{4,5},{5,4},{6,7},{7,6},{8,9},{9,8},{10,11... | collective-permute-start | bytes 1572872 | tf_op jit(solution)/shard_map/ppermute | solution.py:307

commit v7 on v6

--- a/solution.py
+++ b/solution.py
@@ -243,29 +243,47 @@
     )(half, in_hbm(blocked), in_hbm(incoming), mixed, in_hbm(up_blocks), in_hbm(down_blocks))
 
 
+def bring(arrays, name):
+    number = len(arrays)
+
+    def body(*refs):
+        sems = refs[-1]
+        copies = [
+            pltpu.make_async_copy(refs[i], refs[number + i], sems.at[i]) for i in range(number)
+        ]
+        for c in copies:
+            c.start()
+        for c in copies:
+            c.wait()
+
+    return pl.pallas_call(
+        body,
+        in_specs=[ANY] * number,
+        out_specs=[pl.BlockSpec(memory_space=pltpu.VMEM)] * number,
+        out_shape=[pltpu.VMEM(a.shape, a.dtype) for a in arrays],
+        scratch_shapes=[pltpu.SemaphoreType.DMA((number,))],
+        compiler_params=pltpu.CompilerParams(vmem_limit_bytes=16 * 1024 * 1024),
+        cost_estimate=cost(0, sum(2 * a.size * a.dtype.itemsize for a in arrays)),
+        name=name,
+    )(*[in_hbm(a) for a in arrays])
+
+
 def finish(factor, grad_first, blocked, gate_grad, scale):
     block, channels = blocked.shape
     tiles = 4
     step = block // tiles
 
-    def body(f_hbm, d_hbm, x_hbm, r_hbm, one_hbm, out_hbm, f, d, x, r, one, out, sems):
+    def body(f, x, r, d_hbm, one_hbm, out_hbm, d, one, out, sems):
         ds = row_copies(d_hbm, d, sems, 0, tiles)
-        xs = row_copies(x_hbm, x, sems, tiles, tiles)
-        fs = row_copies(f_hbm, f, sems, 2 * tiles, tiles)
-        rs = row_copies(r_hbm, r, sems, 3 * tiles, tiles)
-        ones = row_copies(one, one_hbm, sems, 4 * tiles, tiles)
-        outs = row_copies(out, out_hbm, sems, 5 * tiles, tiles)
-        for c in ds + xs + fs + rs:
+        ones = row_copies(one, one_hbm, sems, tiles, tiles)
+        outs = row_copies(out, out_hbm, sems, 2 * tiles, tiles)
+        for c in ds:
             c.start()
-        for c in xs:
-            c.wait()
         for t in range(tiles):
             at = slice(t * step, (t + 1) * step)
             ds[t].wait()
             one[at, :] = dot(d[at, :], x[...], 1, 1) * scale
             ones[t].start()
-        for c in fs + rs:
-            c.wait()
         for t in range(tiles):
             at = slice(t * step, (t + 1) * step)
             total = dot(f[:, at], d[...], 0, 0) + r[at, :].astype(F32)
@@ -274,24 +292,25 @@
         for c in ones + outs:
             c.wait()
 
-    return pl.pallas_call(
-        body,
-        in_specs=[ANY] * 4,
+    vmem = pl.BlockSpec(memory_space=pltpu.VMEM)
+    return pl.pallas_call(
+        body,
+        in_specs=[vmem, vmem, vmem, ANY],
         out_specs=[ANY] * 2,
         out_shape=[pltpu.HBM((block, block), F32), pltpu.HBM((block, channels), BF)],
         scratch_shapes=[
-            pltpu.VMEM((block, block), BF),
-            pltpu.VMEM((block, channels), BF),
-            pltpu.VMEM((block, channels), BF),
             pltpu.VMEM((block, channels), BF),
             pltpu.VMEM((block, block), F32),
             pltpu.VMEM((block, channels), BF),
-            pltpu.SemaphoreType.DMA((6 * tiles,)),
+            pltpu.SemaphoreType.DMA((3 * tiles,)),
         ],
         compiler_params=params(0),
         cost_estimate=cost(4 * block * block * channels, 6 * block * block + 8 * block * channels),
         name="finish",
-    )(in_hbm(factor), grad_first, in_hbm(blocked), in_hbm(gate_grad))
+    )(
+        *[pltpu.with_memory_space_constraint(a, pltpu.VMEM) for a in (factor, blocked, gate_grad)],
+        grad_first,
+    )
 
 
 def radices(count):
@@ -395,7 +414,6 @@
     dv, gate_grad, kept, sent = middle(half, tokens, cotangent, mixed, up_blocks, down_blocks)
     grad_mixed = exchange(dv)
     back = second(grad_mixed, True)
-    grad_first = exchange(back).reshape(block, channels)
     inner = kept.shape[-1]
     total = kept.astype(F32) + swap(sent, count, 1, 1).astype(F32)
     total = total.reshape(-1, inner)
@@ -403,11 +421,16 @@
     for step in steps[1:-1]:
         total = scatter_step(total, count, *step)
     total = scatter_step(total, count, *steps[-1], after=back).astype(BF)
+    back, total, factor_late, tokens_late, gate_late = lax.optimization_barrier(
+        (back, total, factor, tokens, gate_grad)
+    )
     for step in reversed(steps):
         total = gather_step(total, count, *step)
+    grad_first = exchange(back).reshape(block, channels)
     grad_up, grad_down = write_weights(total, up_blocks.shape, down_blocks.shape, scale)
     two = second_grad(grad_mixed, firsts)
-    one, grad_tokens = finish(factor, grad_first, tokens, gate_grad, scale)
+    held = bring([factor_late, tokens_late, gate_late], "bring_last")
+    one, grad_tokens = finish(held[0], grad_first, held[1], held[2], scale)
     return (grad_tokens, one.reshape(1, block, block), two, grad_up, grad_down)
 
 

time: 175 us -> 159 us (0.909)
  waiting for transfers between devices: 97.3 us -> 77.8 us
  local copies, waits for them, and re-layouts: 2.6 us -> 4.89 us
    ppermute x10, waiting for transfers between devices: 52.5 us -> 33 us  [swap(): lax.ppermute(values, 'seq', [(i, i ^ stride * s) for i in range(count)])]
    pallas_call x1 -> x2, Pallas kernels: 5.6 us -> 6.93 us  [the longest x1 4.73 us: finish(): pl.pallas_call(body, in_specs=[vmem, vmem, vmem, ANY], out_specs=[ANY] *...]
  transfers between devices with their start and end apart: 14 -> 14, of which waited for: 7 -> 7; matrix products, arithmetic and copies ran while one was open for 3% -> 5% of each run, Pallas kernels for 4% -> 6%
where the time goes in v7:
time: 159 us; the launch traced here: 158 us
  waiting for transfers between devices  77.8 us (49%)
  starting transfers between devices  38.6 us (24%)
  Pallas kernels  30.6 us (19%)
  other arithmetic  5.48 us (3%)
  local copies, waits for them, and re-layouts  4.89 us (3%)
    all_to_all x4, waiting for transfers between devices, exchange(): return lax.all_to_all(cut, 'seq', split_axis=0, concat_axis=0, tiled=True)  44.8 us
    ppermute x10, waiting for transfers between devices, swap(): lax.ppermute(values, 'seq', [(i, i ^ stride * s) for i in range(count)])  33 us
    all_to_all x4, starting transfers between devices, exchange(): return lax.all_to_all(cut, 'seq', split_axis=0, concat_axis=0, tiled=True)  25.7 us
    ppermute x10, starting transfers between devices, swap(): lax.ppermute(values, 'seq', [(i, i ^ stride * s) for i in range(count)])  12.9 us
    pallas_call x1, Pallas kernels, middle(): pl.pallas_call(body, grid=(last + 1,), in_specs=[SCALAR, block, block, bl...  9.75 us
    pallas_call x1, Pallas kernels, finish(): pl.pallas_call(body, in_specs=[vmem, vmem, vmem, ANY], out_specs=[ANY] *...  4.73 us
    pallas_call x2, Pallas kernels, mix_second(): pl.pallas_call(body, grid=(groups,), in_specs=[pl.BlockSpec((1, wide, wid...  4.45 us
    pallas_call x1, Pallas kernels, mix_first(): pl.pallas_call(body, in_specs=[ANY, ANY], out_specs=ANY, out_shape=pltpu....  3.92 us
  transfers between devices with their start and end apart: 14, of which 7 were waited for; matrix products, arithmetic and copies ran while one was open for 5% of the time, Pallas kernels for 6%

profile of v7, /device:TPU:0, one launch (start us, length us, event | category | flops | bytes accessed | tf_op | source)
XLA Modules:
  0.0 158.2 jit_solution(17003340350274327315)
XLA Ops:
  0.6 3.9 %mix_first.1 = bf16[1024,512]{1,0:T(8,128)(2,1)} custom-call(bf16[1024,1024]{1,0:T(8,128)(2,1)} %bitcast.51, bf16[1024,512]{1,0:T(8,128)(2,1)} %refs_1_), custom_call_target="tpu_custom_call" | custom-call | flops 1073741824 | bytes 4194304 | tf_op jit(solution)/shard_map/mix_first/pallas_call | solution.py:68
  4.6 0.0 copy-start.3
  4.6 7.5 %all-to-all-start = ((bf16[16,64,512]{2,1,0:T(8,128)(2,1)}), bf16[16,64,512]{2,1,0:T(8,128)(2,1)S(1)}, u32[]{:S(2)}, u32[]{:S(2)}) async-start(bf16[16,64,512]{2,1,0:T(8,128)(2,1)} %bitcast.53), calls=%async_computation | async-start | bytes 2097152 | tf_op jit(solution)/shard_map/all_to_all | solution.py:395
  12.1 0.2 reshape.53
  12.3 0.2 copy.11
  12.5 0.7 spread_factor.1.m_ref
  13.2 21.9 %all-to-all-done.in_ref.u_ref = bf16[16,64,512]{2,1,0:T(8,128)(2,1)S(1)} async-done(((bf16[16,64,512]{2,1,0:T(8,128)(2,1)}), bf16[16,64,512]{2,1,0:T(8,128)(2,1)S(1)}, u32[]{:S(2)}, u32[]{:S(2)}) %all-to-all-start) | async-done | bytes 1048608 | tf_op jit(solution)/shard_map/all_to_all | solution.py:395
  35.0 2.2 %mix_second.1 = bf16[16,64,512]{2,1,0:T(8,128)(2,1)} custom-call(bf16[4,256,256]{2,1,0:T(8,128)(2,1)S(1)} %spread_factor.1.m_ref, bf16[16,64,512]{2,1,0:T(8,128)(2,1)S(1)} %all-to-all-done.in_ref.u_ref), custom_call_target="tpu_custom_call" | custom-call | flops 268435456 | bytes 2621440 | tf_op jit(solution)/shard_map/mix_second/pallas_call | solution.py:124
  37.2 6.8 %all-to-all-start.1 = ((bf16[16,64,512]{2,1,0:T(8,128)(2,1)}), bf16[16,64,512]{2,1,0:T(8,128)(2,1)S(1)}, u32[]{:S(2)}, u32[]{:S(2)}) async-start(bf16[16,64,512]{2,1,0:T(8,128)(2,1)} %mix_second.1), calls=%async_computation.1 | async-start | bytes 2097152 | tf_op jit(solution)/shard_map/all_to_all | solution.py:395
  44.1 22.9 %all-to-all-done.1 = bf16[16,64,512]{2,1,0:T(8,128)(2,1)S(1)} async-done(((bf16[16,64,512]{2,1,0:T(8,128)(2,1)}), bf16[16,64,512]{2,1,0:T(8,128)(2,1)S(1)}, u32[]{:S(2)}, u32[]{:S(2)}) %all-to-all-start.1) | async-done | bytes 1048608 | tf_op jit(solution)/shard_map/all_to_all | solution.py:395
  67.0 9.7 %middle.1 = (bf16[1024,512]{1,0:T(8,128)(2,1)}, bf16[1024,512]{1,0:T(8,128)(2,1)}, bf16[4,128,512]{2,1,0:T(8,128)(2,1)}, bf16[4,128,512]{2,1,0:T(8,128)(2,1)}) custom-call(s32[1]{0:T(128)} %bitcast.2.half_ref, bf16[1024,512]{1,0:T(8,128)(2,1)} %refs_1_, bf16[1024,512]{1,0:T(8,128)(2,1)} %g_ref.1, bf16[1024,512]{1,0:T(8,128)(2,1)S(1)} %bitcast.50, ...), custom_call_target="tpu_custom_call" | custom-call | flops 2684354560 | bytes 7340032 | tf_op jit(solution)/shard_map/middle/pallas_call | solution.py:219
  76.8 0.0 copy-start.2
  76.8 7.0 %all-to-all-start.2 = ((bf16[16,64,512]{2,1,0:T(8,128)(2,1)}), bf16[16,64,512]{2,1,0:T(8,128)(2,1)S(1)}, u32[]{:S(2)}, u32[]{:S(2)}) async-start(bf16[16,64,512]{2,1,0:T(8,128)(2,1)} %bitcast.56), calls=%async_computation.2 | async-start | bytes 2097152 | tf_op jit(solution)/shard_map/all_to_all | solution.py:395
  83.8 0.4 collective-permute-start
  84.2 1.9 %collective-permute-done = bf16[4,128,512]{2,1,0:T(8,128)(2,1)} collective-permute-done((bf16[4,128,512]{2,1,0:T(8,128)(2,1)}, bf16[4,128,512]{2,1,0:T(8,128)(2,1)}, u32[]{:S(2)}, u32[]{:S(2)}) %collective-permute-start) | collective-permute-done | bytes 524320 | tf_op jit(solution)/shard_map/ppermute | solution.py:326
  86.1 2.2 %convert_add_fusion = f32[4,128,512]{2,1,0:T(8,128)} fusion(bf16[4,128,512]{2,1,0:T(8,128)(2,1)} %collective-permute-done, bf16[4,128,512]{2,1,0:T(8,128)(2,1)S(1)} %copy-done.2), kind=kLoop, calls=%fused_computation.1 | loop fusion | flops 786432 | bytes 2097152 | tf_op jit(solution)/shard_map/add | solution.py:418
  88.3 1.1 fusion
  89.3 1.9 %collective-permute-start.1 = (bf16[256,512]{1,0:T(8,128)(2,1)S(1)}, bf16[256,512]{1,0:T(8,128)(2,1)S(1)}, u32[]{:S(2)}, u32[]{:S(2)}) collective-permute-start(bf16[256,512]{1,0:T(8,128)(2,1)S(1)} %fusion), channel_id=1, source_target_pairs={{0,2},{1,3},{2,0},{3,1},{4,6},{5,7},{6,4},{7,5},{8,10},{9,11},{10,... | collective-permute-start | bytes 786440 | tf_op jit(solution)/shard_map/ppermute | solution.py:326
  91.3 11.0 %collective-permute-done.1 = bf16[256,512]{1,0:T(8,128)(2,1)S(1)} collective-permute-done((bf16[256,512]{1,0:T(8,128)(2,1)S(1)}, bf16[256,512]{1,0:T(8,128)(2,1)S(1)}, u32[]{:S(2)}, u32[]{:S(2)}) %collective-permute-start.1) | collective-permute-done | bytes 262176 | tf_op jit(solution)/shard_map/ppermute | solution.py:326
  102.3 1.1 bitcast_add_fusion
  103.4 2.0 %collective-permute-start.2 = (bf16[64,512]{1,0:T(8,128)(2,1)S(1)}, bf16[64,512]{1,0:T(8,128)(2,1)S(1)}, u32[]{:S(2)}, u32[]{:S(2)}) collective-permute-start(bf16[64,512]{1,0:T(8,128)(2,1)S(1)} %get-tuple-element.49), channel_id=1, source_target_pairs={{0,4},{1,5},{2,6},{3,7},{4,0},{5,1},{6,2},{7,3},{8,12},{9,13},{10,... | collective-permute-start | bytes 196616 | tf_op jit(solution)/shard_map/ppermute | solution.py:326
  105.5 2.0 %collective-permute-start.3 = (bf16[64,512]{1,0:T(8,128)(2,1)S(1)}, bf16[64,512]{1,0:T(8,128)(2,1)S(1)}, u32[]{:S(2)}, u32[]{:S(2)}) collective-permute-start(bf16[64,512]{1,0:T(8,128)(2,1)S(1)} %get-tuple-element.48), channel_id=1, source_target_pairs={{0,8},{1,9},{2,10},{3,11},{4,12},{5,13},{6,14},{7,15},{8,0},{9,1},... | collective-permute-start | bytes 196616 | tf_op jit(solution)/shard_map/ppermute | solution.py:326
  107.4 0.5 collective-permute-start.4
  107.9 0.0 all-to-all-done.2.in_ref.g_ref
  107.9 2.3 %mix_second_back.1 = bf16[16,64,512]{2,1,0:T(8,128)(2,1)} custom-call(bf16[4,256,256]{2,1,0:T(8,128)(2,1)S(1)} %spread_factor.1.m_ref, bf16[16,64,512]{2,1,0:T(8,128)(2,1)S(1)} %all-to-all-done.2.in_ref.g_ref), custom_call_target="tpu_custom_call" | custom-call | flops 268435456 | bytes 2621440 | tf_op jit(solution)/shard_map/mix_second_back/pallas_call | solution.py:124
  110.2 0.0 collective-permute-done.2
  110.2 4.8 %collective-permute-done.3 = bf16[64,512]{1,0:T(8,128)(2,1)S(1)} collective-permute-done((bf16[64,512]{1,0:T(8,128)(2,1)S(1)}, bf16[64,512]{1,0:T(8,128)(2,1)S(1)}, u32[]{:S(2)}, u32[]{:S(2)}) %collective-permute-start.3) | collective-permute-done | bytes 65568 | tf_op jit(solution)/shard_map/ppermute | solution.py:326
  115.1 1.6 collective-permute-start.5
  116.6 1.0 collective-permute-start.6
  117.6 1.9 %collective-permute-start.7 = (bf16[64,512]{1,0:T(8,128)(2,1)S(1)}, bf16[64,512]{1,0:T(8,128)(2,1)S(1)}, u32[]{:S(2)}, u32[]{:S(2)}) collective-permute-start(bf16[64,512]{1,0:T(8,128)(2,1)S(1)} %fusion.3), channel_id=1, source_target_pairs={{0,12},{1,13},{2,14},{3,15},{4,8},{5,9},{6,10},{7,11},{8,4},{9,5},... | collective-permute-start | bytes 196616 | tf_op jit(solution)/shard_map/ppermute | solution.py:326
  119.5 4.3 %all-to-all-start.3 = ((bf16[16,64,512]{2,1,0:T(8,128)(2,1)}), bf16[16,64,512]{2,1,0:T(8,128)(2,1)}, u32[]{:S(2)}, u32[]{:S(2)}) async-start(bf16[16,64,512]{2,1,0:T(8,128)(2,1)} %mix_second_back.1), calls=%async_computation.3 | async-start | bytes 2097152 | tf_op jit(solution)/shard_map/all_to_all | solution.py:395
  123.9 0.2 collective-permute-done.6
  124.2 1.7 %collective-permute-start.8 = (bf16[256,512]{1,0:T(8,128)(2,1)S(1)}, bf16[256,512]{1,0:T(8,128)(2,1)S(1)}, u32[]{:S(2)}, u32[]{:S(2)}) collective-permute-start(bf16[256,512]{1,0:T(8,128)(2,1)S(1)} %bitcast.57), channel_id=1, source_target_pairs={{0,2},{1,3},{2,0},{3,1},{4,6},{5,7},{6,4},{7,5},{8,10},{9,11},{10,... | collective-permute-start | bytes 786440 | tf_op jit(solution)/shard_map/ppermute | solution.py:326
  125.9 15.0 %collective-permute-done.8 = bf16[256,512]{1,0:T(8,128)(2,1)S(1)} collective-permute-done((bf16[256,512]{1,0:T(8,128)(2,1)S(1)}, bf16[256,512]{1,0:T(8,128)(2,1)S(1)}, u32[]{:S(2)}, u32[]{:S(2)}) %collective-permute-start.8) | collective-permute-done | bytes 262176 | tf_op jit(solution)/shard_map/ppermute | solution.py:326
  140.9 0.1 broadcast_select_fusion.3
  140.9 0.8 pad_maximum_fusion.1
  141.7 2.9 %grad_second.1 = f32[4,256,16]{2,1,0:T(8,128)S(1)} custom-call(bf16[16,64,512]{2,1,0:T(8,128)(2,1)S(1)} %all-to-all-done.2.in_ref.g_ref, bf16[16,64,512]{2,1,0:T(8,128)(2,1)S(1)} %all-to-all-done.in_ref.u_ref), custom_call_target="tpu_custom_call" | custom-call | flops 268435456 | bytes 2097152 | tf_op jit(solution)/shard_map/grad_second/pallas_call | solution.py:155
  144.7 0.2 copy.12
  144.9 0.9 reshape.64
  145.8 1.2 broadcast_select_fusion.1
  147.1 0.1 pad_maximum_fusion.up_in.down_in
  147.1 2.2 %bring_last.1 = (bf16[1024,1024]{1,0:T(8,128)(2,1)S(1)}, bf16[1024,512]{1,0:T(8,128)(2,1)S(1)}, bf16[1024,512]{1,0:T(8,128)(2,1)S(1)}) custom-call(bf16[1024,1024]{1,0:T(8,128)(2,1)} %bitcast.52, bf16[1024,512]{1,0:T(8,128)(2,1)} %refs_1_, bf16[1024,512]{1,0:T(8,128)(2,1)} %get-tuple-element.33.refs_2_), custom_call_target="tpu_custom_call" | custom-call | bytes 8388608 | tf_op jit(solution)/shard_map/bring_last/pallas_call | solution.py:259
  149.4 0.0 copy-start
  149.4 1.0 copy-done
  150.3 1.9 %write_weights.1 = (f32[4,128,512]{2,1,0:T(8,128)}, f32[4,512,128]{2,1,0:T(8,128)}) custom-call(bf16[1024,512]{1,0:T(8,128)(2,1)S(1)} %pad_maximum_fusion.up_in.down_in, bf16[1024,512]{1,0:T(8,128)(2,1)S(1)} %pad_maximum_fusion.up_in.down_in), custom_call_target="tpu_custom_call" | custom-call | flops 262144 | bytes 3145728 | tf_op jit(solution)/shard_map/write_weights/pallas_call | solution.py:364
  152.2 0.0 all-to-all-done.3
  152.3 1.2 copy-done.1
  153.5 4.7 %finish.1 = (f32[1024,1024]{1,0:T(8,128)}, bf16[1024,512]{1,0:T(8,128)(2,1)}) custom-call(bf16[1024,1024]{1,0:T(8,128)(2,1)S(1)} %get-tuple-element.34.f, bf16[1024,512]{1,0:T(8,128)(2,1)S(1)} %get-tuple-element.35.x, bf16[1024,512]{1,0:T(8,128)(2,1)S(1)} %copy-done.1, bf16[1024,512]{1,0:T(8,128)(2,1)} %bitcast.15.d_hbm), custom_call_target="tpu_custom_call" | custom-call | flops 2147483648 | bytes 10485760 | tf_op jit(solution)/shard_map/finish/pallas_call | solution.py:296
  (15 shorter events, 0.2 us)
Async XLA Ops:
  4.6 7.5 %copy-start.3 = (bf16[64,16,16]{0,2,1:T(8,128)(2,1)S(1)}, bf16[64,16,16]{0,2,1:T(8,128)(2,1)}, u32[]{:S(2)}) copy-start(bf16[64,16,16]{0,2,1:T(8,128)(2,1)} %param.9) | copy-start | bytes 98308
  4.6 30.5 %all-to-all-start = ((bf16[16,64,512]{2,1,0:T(8,128)(2,1)}), bf16[16,64,512]{2,1,0:T(8,128)(2,1)S(1)}, u32[]{:S(2)}, u32[]{:S(2)}) async-start(bf16[16,64,512]{2,1,0:T(8,128)(2,1)} %bitcast.53), calls=%async_computation | async-start | bytes 2097152 | tf_op jit(solution)/shard_map/all_to_all | solution.py:395
  37.2 29.8 %all-to-all-start.1 = ((bf16[16,64,512]{2,1,0:T(8,128)(2,1)}), bf16[16,64,512]{2,1,0:T(8,128)(2,1)S(1)}, u32[]{:S(2)}, u32[]{:S(2)}) async-start(bf16[16,64,512]{2,1,0:T(8,128)(2,1)} %mix_second.1), calls=%async_computation.1 | async-start | bytes 2097152 | tf_op jit(solution)/shard_map/all_to_all | solution.py:395
  76.8 9.3 %copy-start.2 = (bf16[4,128,512]{2,1,0:T(8,128)(2,1)S(1)}, bf16[4,128,512]{2,1,0:T(8,128)(2,1)}, u32[]{:S(2)}) copy-start(bf16[4,128,512]{2,1,0:T(8,128)(2,1)} %get-tuple-element.25) | copy-start | bytes 1572868
  76.8 31.1 %all-to-all-start.2 = ((bf16[16,64,512]{2,1,0:T(8,128)(2,1)}), bf16[16,64,512]{2,1,0:T(8,128)(2,1)S(1)}, u32[]{:S(2)}, u32[]{:S(2)}) async-start(bf16[16,64,512]{2,1,0:T(8,128)(2,1)} %bitcast.56), calls=%async_computation.2 | async-start | bytes 2097152 | tf_op jit(solution)/shard_map/all_to_all | solution.py:395
  83.8 2.3 %collective-permute-start = (bf16[4,128,512]{2,1,0:T(8,128)(2,1)}, bf16[4,128,512]{2,1,0:T(8,128)(2,1)}, u32[]{:S(2)}, u32[]{:S(2)}) collective-permute-start(bf16[4,128,512]{2,1,0:T(8,128)(2,1)} %get-tuple-element.26), channel_id=1, source_target_pairs={{0,1},{1,0},{2,3},{3,2},{4,5},{5,4},{6,7},{7,6},{8,9},{9,8},{10,11... | collective-permute-start | bytes 1572872 | tf_op jit(solution)/shard_map/ppermute | solution.py:326
  89.3 12.9 %collective-permute-start.1 = (bf16[256,512]{1,0:T(8,128)(2,1)S(1)}, bf16[256,512]{1,0:T(8,128)(2,1)S(1)}, u32[]{:S(2)}, u32[]{:S(2)}) collective-permute-start(bf16[256,512]{1,0:T(8,128)(2,1)S(1)} %fusion), channel_id=1, source_target_pairs={{0,2},{1,3},{2,0},{3,1},{4,6},{5,7},{6,4},{7,5},{8,10},{9,11},{10,... | collective-permute-start | bytes 786440 | tf_op jit(solution)/shard_map/ppermute | solution.py:326
  103.4 6.7 %collective-permute-start.2 = (bf16[64,512]{1,0:T(8,128)(2,1)S(1)}, bf16[64,512]{1,0:T(8,128)(2,1)S(1)}, u32[]{:S(2)}, u32[]{:S(2)}) collective-permute-start(bf16[64,512]{1,0:T(8,128)(2,1)S(1)} %get-tuple-element.49), channel_id=1, source_target_pairs={{0,4},{1,5},{2,6},{3,7},{4,0},{5,1},{6,2},{7,3},{8,12},{9,13},{10,... | collective-permute-start | bytes 196616 | tf_op jit(solution)/shard_map/ppermute | solution.py:326
  105.5 9.6 %collective-permute-start.3 = (bf16[64,512]{1,0:T(8,128)(2,1)S(1)}, bf16[64,512]{1,0:T(8,128)(2,1)S(1)}, u32[]{:S(2)}, u32[]{:S(2)}) collective-permute-start(bf16[64,512]{1,0:T(8,128)(2,1)S(1)} %get-tuple-element.48), channel_id=1, source_target_pairs={{0,8},{1,9},{2,10},{3,11},{4,12},{5,13},{6,14},{7,15},{8,0},{9,1},... | collective-permute-start | bytes 196616 | tf_op jit(solution)/shard_map/ppermute | solution.py:326
  107.4 7.6 %collective-permute-start.4 = (bf16[64,512]{1,0:T(8,128)(2,1)S(1)}, bf16[64,512]{1,0:T(8,128)(2,1)S(1)}, u32[]{:S(2)}, u32[]{:S(2)}) collective-permute-start(bf16[64,512]{1,0:T(8,128)(2,1)S(1)} %get-tuple-element.47), channel_id=1, source_target_pairs={{0,12},{1,13},{2,14},{3,15},{4,8},{5,9},{6,10},{7,11},{8,4},{9,5},... | collective-permute-start | bytes 196616 | tf_op jit(solution)/shard_map/ppermute | solution.py:326
  115.1 8.9 %collective-permute-start.5 = (bf16[64,512]{1,0:T(8,128)(2,1)S(1)}, bf16[64,512]{1,0:T(8,128)(2,1)S(1)}, u32[]{:S(2)}, u32[]{:S(2)}) collective-permute-start(bf16[64,512]{1,0:T(8,128)(2,1)S(1)} %fusion.3), channel_id=1, source_target_pairs={{0,4},{1,5},{2,6},{3,7},{4,0},{5,1},{6,2},{7,3},{8,12},{9,13},{10,... | collective-permute-start | bytes 196616 | tf_op jit(solution)/shard_map/ppermute | solution.py:326
  116.6 7.6 %collective-permute-start.6 = (bf16[64,512]{1,0:T(8,128)(2,1)S(1)}, bf16[64,512]{1,0:T(8,128)(2,1)S(1)}, u32[]{:S(2)}, u32[]{:S(2)}) collective-permute-start(bf16[64,512]{1,0:T(8,128)(2,1)S(1)} %fusion.3), channel_id=1, source_target_pairs={{0,8},{1,9},{2,10},{3,11},{4,12},{5,13},{6,14},{7,15},{8,0},{9,1},... | collective-permute-start | bytes 196616 | tf_op jit(solution)/shard_map/ppermute | solution.py:326
  117.6 6.6 %collective-permute-start.7 = (bf16[64,512]{1,0:T(8,128)(2,1)S(1)}, bf16[64,512]{1,0:T(8,128)(2,1)S(1)}, u32[]{:S(2)}, u32[]{:S(2)}) collective-permute-start(bf16[64,512]{1,0:T(8,128)(2,1)S(1)} %fusion.3), channel_id=1, source_target_pairs={{0,12},{1,13},{2,14},{3,15},{4,8},{5,9},{6,10},{7,11},{8,4},{9,5},... | collective-permute-start | bytes 196616 | tf_op jit(solution)/shard_map/ppermute | solution.py:326
  119.5 32.7 %all-to-all-start.3 = ((bf16[16,64,512]{2,1,0:T(8,128)(2,1)}), bf16[16,64,512]{2,1,0:T(8,128)(2,1)}, u32[]{:S(2)}, u32[]{:S(2)}) async-start(bf16[16,64,512]{2,1,0:T(8,128)(2,1)} %mix_second_back.1), calls=%async_computation.3 | async-start | bytes 2097152 | tf_op jit(solution)/shard_map/all_to_all | solution.py:395
  124.2 16.6 %collective-permute-start.8 = (bf16[256,512]{1,0:T(8,128)(2,1)S(1)}, bf16[256,512]{1,0:T(8,128)(2,1)S(1)}, u32[]{:S(2)}, u32[]{:S(2)}) collective-permute-start(bf16[256,512]{1,0:T(8,128)(2,1)S(1)} %bitcast.57), channel_id=1, source_target_pairs={{0,2},{1,3},{2,0},{3,1},{4,6},{5,7},{6,4},{7,5},{8,10},{9,11},{10,... | collective-permute-start | bytes 786440 | tf_op jit(solution)/shard_map/ppermute | solution.py:326
  141.7 4.1 %collective-permute-start.9 = (bf16[512,512]{1,0:T(8,128)(2,1)}, bf16[512,512]{1,0:T(8,128)(2,1)}, u32[]{:S(2)}, u32[]{:S(2)}) collective-permute-start(bf16[512,512]{1,0:T(8,128)(2,1)} %pad_maximum_fusion.1), channel_id=1, source_target_pairs={{0,1},{1,0},{2,3},{3,2},{4,5},{5,4},{6,7},{7,6},{8,9},{9,8},{10,11... | collective-permute-start | bytes 1572872 | tf_op jit(solution)/shard_map/ppermute | solution.py:326
  149.4 1.0 copy-start
  152.2 1.2 copy-start.1

commit v8 on v7

--- a/solution.py
+++ b/solution.py
@@ -9,11 +9,16 @@
 F32 = jnp.float32
 VMEM_BYTES = 40 * 1024 * 1024
 ANY = pl.BlockSpec(memory_space=pl.ANY)
+VMEM = pl.BlockSpec(memory_space=pltpu.VMEM)
 SCALAR = pl.BlockSpec(memory_space=pltpu.SMEM)
 
 
 def in_hbm(array):
     return pltpu.with_memory_space_constraint(array, pltpu.HBM)
+
+
+def in_vmem(array):
+    return pltpu.with_memory_space_constraint(array, pltpu.VMEM)
 
 
 def sigmoid(z):
@@ -115,24 +120,32 @@
     wide = n * 16
     groups = here // 16
 
-    def body(m_ref, in_ref, out_ref):
-        rows = in_ref[...].reshape(wide, channels)
-        got = dot(m_ref[0], rows, 0 if back else 1, 0).astype(BF)
-        out_ref[...] = got.reshape(n, 16, channels)
-
-    blocks = pl.BlockSpec((n, 16, channels), lambda g: (0, g, 0))
-    return pl.pallas_call(
-        body,
-        grid=(groups,),
-        in_specs=[pl.BlockSpec((1, wide, wide), lambda g: (g, 0, 0)), blocks],
-        out_specs=blocks,
-        out_shape=pltpu.HBM(cols.shape, BF) if back else jax.ShapeDtypeStruct(cols.shape, BF),
-        compiler_params=params(),
+    def body(m_ref, in_ref, out_hbm, out, sems):
+        copies = []
+        for g in range(groups):
+            at = pl.ds(g * 16, 16)
+            rows = in_ref[:, at, :].reshape(wide, channels)
+            got = dot(m_ref[g], rows, 0 if back else 1, 0).astype(BF)
+            out[:, at, :] = got.reshape(n, 16, channels)
+            copies.append(
+                pltpu.make_async_copy(out.at[:, at, :], out_hbm.at[:, at, :], sems.at[g])
+            )
+            copies[-1].start()
+        for c in copies:
+            c.wait()
+
+    return pl.pallas_call(
+        body,
+        in_specs=[VMEM, VMEM],
+        out_specs=ANY,
+        out_shape=pltpu.HBM(cols.shape, BF),
+        scratch_shapes=[pltpu.VMEM(cols.shape, BF), pltpu.SemaphoreType.DMA((groups,))],
+        compiler_params=params(0),
         cost_estimate=cost(
             2 * groups * wide * wide * channels, 4 * cols.size + 2 * groups * wide * wide
         ),
         name="mix_second_back" if back else "mix_second",
-    )(spread, cols)
+    )(in_vmem(spread), in_vmem(cols))
 
 
 def grad_second(grads, firsts, scale):
@@ -141,27 +154,28 @@
     groups = here // 16
 
     def body(g_ref, u_ref, out_ref):
-        g = g_ref[...].reshape(wide, channels)
-        u = u_ref[...].reshape(wide, channels)
-        full = dot(g, u, 1, 1)
         r = lax.broadcasted_iota(jnp.int32, (wide, wide), 0)
         c = lax.broadcasted_iota(jnp.int32, (wide, wide), 1)
-        kept = jnp.where(r % 16 == c % 16, full, 0.0)
+        same = r % 16 == c % 16
         row = lax.broadcasted_iota(jnp.int32, (wide, n), 0)
         col = lax.broadcasted_iota(jnp.int32, (wide, n), 1)
         pick = jnp.where(row // 16 == col, 1.0, 0.0)
-        out_ref[0] = dot(kept, pick, 1, 0, precision=lax.Precision.HIGHEST) * scale
+        for k in range(groups):
+            at = pl.ds(k * 16, 16)
+            g = g_ref[:, at, :].reshape(wide, channels)
+            u = u_ref[:, at, :].reshape(wide, channels)
+            kept = jnp.where(same, dot(g, u, 1, 1), 0.0)
+            out_ref[k] = dot(kept, pick, 1, 0, precision=lax.Precision.HIGHEST) * scale
 
     out = pl.pallas_call(
         body,
-        grid=(groups,),
-        in_specs=[pl.BlockSpec((n, 16, channels), lambda g: (0, g, 0))] * 2,
-        out_specs=pl.BlockSpec((1, wide, n), lambda g: (g, 0, 0)),
+        in_specs=[VMEM, VMEM],
+        out_specs=VMEM,
         out_shape=jax.ShapeDtypeStruct((groups, wide, n), F32),
-        compiler_params=params(),
+        compiler_params=params(0),
         cost_estimate=cost(2 * groups * wide * wide * channels, 4 * grads.size),
         name="grad_second",
-    )(grads, firsts)
+    )(in_vmem(grads), in_vmem(firsts))
     return out.reshape(groups, n, 16, n).transpose(0, 2, 1, 3).reshape(here, n, n)
 
 
@@ -170,77 +184,77 @@
     sub = inner // groups
     rows, channels = blocked.shape
     step = min(256, rows)
-    last = rows // step - 1
-
-    def body(half_ref, x_ref, g_ref, v_ref, up_ref, down_ref, dv_ref, r_ref, kept_ref, sent_ref, w):
-        i = pl.program_id(0)
-
-        @pl.when(i == 0)
-        def _():
-            w[...] = jnp.zeros_like(w)
-
-        x = x_ref[...].astype(F32)
-        g = g_ref[...]
-        v = v_ref[...].astype(F32)
-        sx = sigmoid(x)
-        gate = x * sx
-        h = (x + v * gate).astype(BF)
-        h_parts = [h[:, b * width : (b + 1) * width] for b in range(groups)]
-        g_parts = [g[:, b * width : (b + 1) * width] for b in range(groups)]
-        acts, slopes, back = [], [], []
-        for b in range(groups):
-            a = dot(h_parts[b], up_ref[b], 1, 0)
-            s = sigmoid(a)
-            q = a * s
-            acts.append(q.astype(BF))
-            slopes.append(s + q * (1.0 - s))
-            back.append(dot(g_parts[b], down_ref[b], 1, 1))
-        grads = []
-        for b in range(groups):
-            lanes = slice(b * sub, (b + 1) * sub)
-            perm = jnp.concatenate([acts[p][:, lanes] for p in range(groups)], axis=1)
-            w[1, b] += dot(g_parts[b], perm, 0, 0)
-            dq = jnp.concatenate([back[p][:, lanes] for p in range(groups)], axis=1)
-            da = (dq * slopes[b]).astype(BF)
-            w[0, b] += dot(h_parts[b], da, 0, 0)
-            grads.append(dot(da, up_ref[b], 1, 1))
-        dh = (g.astype(F32) + jnp.concatenate(grads, axis=1)).astype(BF).astype(F32)
-        dv_ref[...] = (dh * gate).astype(BF)
-        r_ref[...] = (dh * (1.0 + v * (sx + gate * (1.0 - sx)))).astype(BF)
-
-        @pl.when(i == last)
-        def _():
-            kept_ref[...] = w[half_ref[0]].astype(BF)
-            sent_ref[...] = w[1 - half_ref[0]].astype(BF)
-
-    block = pl.BlockSpec((step, channels), lambda i: (i, 0))
-    full = pl.BlockSpec(up_blocks.shape, lambda i: (0, 0, 0))
+    tiles = rows // step
+
+    def body(half_ref, x_ref, g_ref, v_ref, up_ref, down_ref, dv_hbm, r_ref, kept_ref, sent_ref, *tmp):
+        dv, w, sems = tmp
+        w[...] = jnp.zeros_like(w)
+
+        def send(t):
+            at = pl.ds(t * step, step)
+            return pltpu.make_async_copy(dv.at[at], dv_hbm.at[at], sems.at[t])
+
+        def tile(t, carry):
+            at = pl.ds(pl.multiple_of(t * step, step), step)
+            x = x_ref[at, :].astype(F32)
+            g = g_ref[at, :]
+            v = v_ref[at, :].astype(F32)
+            sx = sigmoid(x)
+            gate = x * sx
+            h = (x + v * gate).astype(BF)
+            h_parts = [h[:, b * width : (b + 1) * width] for b in range(groups)]
+            g_parts = [g[:, b * width : (b + 1) * width] for b in range(groups)]
+            acts, slopes, back = [], [], []
+            for b in range(groups):
+                a = dot(h_parts[b], up_ref[b], 1, 0)
+                s = sigmoid(a)
+                q = a * s
+                acts.append(q.astype(BF))
+                slopes.append(s + q * (1.0 - s))
+                back.append(dot(g_parts[b], down_ref[b], 1, 1))
+            grads = []
+            for b in range(groups):
+                lanes = slice(b * sub, (b + 1) * sub)
+                perm = jnp.concatenate([acts[p][:, lanes] for p in range(groups)], axis=1)
+                w[1, b] += dot(g_parts[b], perm, 0, 0)
+                dq = jnp.concatenate([back[p][:, lanes] for p in range(groups)], axis=1)
+                da = (dq * slopes[b]).astype(BF)
+                w[0, b] += dot(h_parts[b], da, 0, 0)
+                grads.append(dot(da, up_ref[b], 1, 1))
+            dh = (g.astype(F32) + jnp.concatenate(grads, axis=1)).astype(BF).astype(F32)
+            dv[at, :] = (dh * gate).astype(BF)
+            send(t).start()
+            r_ref[at, :] = (dh * (1.0 + v * (sx + gate * (1.0 - sx)))).astype(BF)
+            return carry
+
+        lax.fori_loop(0, tiles, tile, 0)
+        kept_ref[...] = w[half_ref[0]].astype(BF)
+        sent_ref[...] = w[1 - half_ref[0]].astype(BF)
+        for t in range(tiles):
+            send(t).wait()
+
     hidden = rows * groups * inner
     return pl.pallas_call(
         body,
-        grid=(last + 1,),
-        in_specs=[
-            SCALAR,
-            block,
-            block,
-            block,
-            full,
-            pl.BlockSpec(down_blocks.shape, lambda i: (0, 0, 0)),
-        ],
-        out_specs=[block, block, full, full],
+        in_specs=[SCALAR] + [VMEM] * 5,
+        out_specs=[ANY, VMEM, VMEM, VMEM],
         out_shape=[
             pltpu.HBM((rows, channels), BF),
-            pltpu.HBM((rows, channels), BF),
-            pltpu.HBM(up_blocks.shape, BF),
-            pltpu.HBM(up_blocks.shape, BF),
-        ],
-        scratch_shapes=[pltpu.VMEM((2, groups, width, inner), F32)],
-        compiler_params=params(),
+            pltpu.VMEM((rows, channels), BF),
+            pltpu.VMEM(up_blocks.shape, BF),
+            pltpu.VMEM(up_blocks.shape, BF),
+        ],
+        scratch_shapes=[
+            pltpu.VMEM((rows, channels), BF),
+            pltpu.VMEM((2, groups, width, inner), F32),
+            pltpu.SemaphoreType.DMA((tiles,)),
+        ],
+        compiler_params=params(0),
         cost_estimate=cost(
             10 * hidden * width, 10 * rows * channels + 8 * groups * width * inner, hidden
         ),
         name="middle",
-    )(half, in_hbm(blocked), in_hbm(incoming), mixed, in_hbm(up_blocks), in_hbm(down_blocks))
+    )(half, *[in_vmem(a) for a in (blocked, incoming, mixed, up_blocks, down_blocks)])
 
 
 def bring(arrays, name):
@@ -273,15 +287,11 @@
     tiles = 4
     step = block // tiles
 
-    def body(f, x, r, d_hbm, one_hbm, out_hbm, d, one, out, sems):
-        ds = row_copies(d_hbm, d, sems, 0, tiles)
-        ones = row_copies(one, one_hbm, sems, tiles, tiles)
-        outs = row_copies(out, out_hbm, sems, 2 * tiles, tiles)
-        for c in ds:
-            c.start()
+    def body(f, x, r, d, one_hbm, out_hbm, one, out, sems):
+        ones = row_copies(one, one_hbm, sems, 0, tiles)
+        outs = row_copies(out, out_hbm, sems, tiles, tiles)
         for t in range(tiles):
             at = slice(t * step, (t + 1) * step)
-            ds[t].wait()
             one[at, :] = dot(d[at, :], x[...], 1, 1) * scale
             ones[t].start()
         for t in range(tiles):
@@ -292,25 +302,20 @@
         for c in ones + outs:
             c.wait()
 
-    vmem = pl.BlockSpec(memory_space=pltpu.VMEM)
-    return pl.pallas_call(
-        body,
-        in_specs=[vmem, vmem, vmem, ANY],
+    return pl.pallas_call(
+        body,
+        in_specs=[VMEM] * 4,
         out_specs=[ANY] * 2,
         out_shape=[pltpu.HBM((block, block), F32), pltpu.HBM((block, channels), BF)],
         scratch_shapes=[
-            pltpu.VMEM((block, channels), BF),
             pltpu.VMEM((block, block), F32),
             pltpu.VMEM((block, channels), BF),
-            pltpu.SemaphoreType.DMA((3 * tiles,)),
+            pltpu.SemaphoreType.DMA((2 * tiles,)),
         ],
         compiler_params=params(0),
         cost_estimate=cost(4 * block * block * channels, 6 * block * block + 8 * block * channels),
         name="finish",
-    )(
-        *[pltpu.with_memory_space_constraint(a, pltpu.VMEM) for a in (factor, blocked, gate_grad)],
-        grad_first,
-    )
+    )(*[in_vmem(a) for a in (factor, blocked, gate_grad, grad_first)])
 
 
 def radices(count):
@@ -326,24 +331,46 @@
     return lax.ppermute(values, "seq", [(i, i ^ (stride * s)) for i in range(count)])
 
 
-def scatter_step(total, count, stride, radix, after=None):
-    digit = (lax.axis_index("seq") // stride) % radix
-    cut = total.reshape(radix, total.shape[0] // radix, total.shape[1])
-    kept = lax.dynamic_index_in_dim(cut, digit, 0, keepdims=False)
-    got = []
-    for s in range(1, radix):
-        send = lax.dynamic_index_in_dim(cut, digit ^ s, 0, keepdims=False).astype(BF)
-        got.append(swap(send, count, stride, s))
-    if after is not None:
-        got, after = lax.optimization_barrier((got, after))
-    for g in got:
-        kept = kept + g.astype(F32)
-    return kept
-
-
-def gather_step(share, count, stride, radix):
+def add_and_cut(terms, digit, radix):
+    rows, columns = terms[0].shape
+    share = rows // radix
+
+    def body(digit_ref, *refs):
+        ins, kept_ref, outs = refs[: len(terms)], refs[len(terms)], refs[len(terms) + 1 :]
+
+        def part(s):
+            at = pl.ds(pl.multiple_of((digit_ref[0] ^ s) * share, share), share)
+            total = ins[0][at, :].astype(F32)
+            for ref in ins[1:]:
+                total = total + ref[at, :].astype(F32)
+            return total
+
+        kept_ref[...] = part(0)
+        for s, ref in enumerate(outs):
+            ref[...] = part(s + 1).astype(BF)
+
+    return pl.pallas_call(
+        body,
+        in_specs=[SCALAR] + [VMEM] * len(terms),
+        out_specs=[VMEM] * radix,
+        out_shape=[jax.ShapeDtypeStruct((share, columns), F32)]
+        + [jax.ShapeDtypeStruct((share, columns), BF)] * (radix - 1),
+        compiler_params=pltpu.CompilerParams(vmem_limit_bytes=16 * 1024 * 1024),
+        cost_estimate=cost(rows * columns, 8 * rows * columns),
+        name="add_and_cut",
+    )(digit.reshape(1), *terms)
+
+
+def scatter_step(terms, count, stride, radix):
+    digit = (lax.axis_index("seq").astype(jnp.int32) // stride) % radix
+    kept, *send = add_and_cut(terms, digit, radix)
+    return [kept] + [swap(a, count, stride, s + 1) for s, a in enumerate(send)]
+
+
+def gather_step(share, count, stride, radix, after=()):
     digit = (lax.axis_index("seq") // stride) % radix
     got = [share] + [swap(share, count, stride, s) for s in range(1, radix)]
+    got, after = lax.optimization_barrier((got, after))
     if radix == 2:
         low = jnp.where(digit == 0, got[0], got[1])
         high = jnp.where(digit == 0, got[1], got[0])
@@ -410,27 +437,27 @@
 
     half = (lax.axis_index("seq") % 2).astype(jnp.int32).reshape(1)
     firsts = exchange(mix_first(factor, tokens))
+    late = (tokens, cotangent, factor, up_blocks, down_blocks)
+    firsts, late = lax.optimization_barrier((firsts, late))
+    tokens_v, cotangent_v, factor_v, up_v, down_v = bring(late, "bring")
     mixed = exchange(second(firsts, False)).reshape(block, channels)
-    dv, gate_grad, kept, sent = middle(half, tokens, cotangent, mixed, up_blocks, down_blocks)
+    dv, gate_grad, kept, sent = middle(half, tokens_v, cotangent_v, mixed, up_v, down_v)
     grad_mixed = exchange(dv)
     back = second(grad_mixed, True)
-    inner = kept.shape[-1]
-    total = kept.astype(F32) + swap(sent, count, 1, 1).astype(F32)
-    total = total.reshape(-1, inner)
+    terms = [kept, swap(sent, count, 1, 1)]
+    terms = [t.reshape(-1, t.shape[-1]) for t in terms]
     steps = radices(count)
-    for step in steps[1:-1]:
-        total = scatter_step(total, count, *step)
-    total = scatter_step(total, count, *steps[-1], after=back).astype(BF)
-    back, total, factor_late, tokens_late, gate_late = lax.optimization_barrier(
-        (back, total, factor, tokens, gate_grad)
-    )
+    for step in steps[1:]:
+        terms = scatter_step(terms, count, *step)
+    terms, back = lax.optimization_barrier((terms, back))
+    total = sum(t.astype(F32) for t in terms).astype(BF)
+    back, total = lax.optimization_barrier((back, total))
+    grad_first = exchange(back).reshape(block, channels)
+    two = second_grad(grad_mixed, firsts)
     for step in reversed(steps):
-        total = gather_step(total, count, *step)
-    grad_first = exchange(back).reshape(block, channels)
+        total = gather_step(total, count, *step, after=two if step == steps[1] else ())
     grad_up, grad_down = write_weights(total, up_blocks.shape, down_blocks.shape, scale)
-    two = second_grad(grad_mixed, firsts)
-    held = bring([factor_late, tokens_late, gate_late], "bring_last")
-    one, grad_tokens = finish(held[0], grad_first, held[1], held[2], scale)
+    one, grad_tokens = finish(factor_v, grad_first, tokens_v, gate_grad, scale)
     return (grad_tokens, one.reshape(1, block, block), two, grad_up, grad_down)
 
 

time: 159 us -> 157 us (0.987)
  local copies, waits for them, and re-layouts: 4.89 us -> 15.8 us
  waiting for transfers between devices: 77.8 us -> 71.9 us
  other arithmetic: 5.48 us -> 0.25 us
  Pallas kernels: 30.6 us -> 26.6 us
    unnamed x8 -> x34, local copies, waits for them, and re-layouts: 2.2 us -> 14.2 us
    all_to_all x4, waiting for transfers between devices: 44.8 us -> 40 us  [exchange(): return lax.all_to_all(cut, 'seq', split_axis=0, concat_axis=0, tiled=True)]
    pallas_call x5 -> x7, Pallas kernels: 21.8 us -> 17.6 us  [the longest x1 7.71 us: middle(): pl.pallas_call(body, in_specs=[SCALAR] + [VMEM] * 5, out_specs=[ANY, VMEM...]
    add x2 -> x0, other arithmetic: 3.26 us -> none  [the longest x1 2.16 us: on_device(): total = kept.astype(F32) + swap(sent, count, 1, 1).astype(F32)]
  transfers between devices with their start and end apart: 14 -> 14, of which waited for: 7 -> 8; matrix products, arithmetic and copies ran while one was open for 5% -> 1% of each run, Pallas kernels for 6% -> 6%
where the time goes in v8:
time: 157 us; the launch traced here: 155 us
  waiting for transfers between devices  71.9 us (46%)
  starting transfers between devices  39.8 us (25%)
  Pallas kernels  26.6 us (17%)
  local copies, waits for them, and re-layouts  15.8 us (10%)
    all_to_all x4, waiting for transfers between devices, exchange(): return lax.all_to_all(cut, 'seq', split_axis=0, concat_axis=0, tiled=True)  40 us
    ppermute x10, waiting for transfers between devices, swap(): lax.ppermute(values, 'seq', [(i, i ^ stride * s) for i in range(count)])  32 us
    all_to_all x4, starting transfers between devices, exchange(): return lax.all_to_all(cut, 'seq', split_axis=0, concat_axis=0, tiled=True)  25.6 us
    ppermute x10, starting transfers between devices, swap(): lax.ppermute(values, 'seq', [(i, i ^ stride * s) for i in range(count)])  14.2 us
    unnamed x34, local copies, waits for them, and re-layouts  14.2 us
    pallas_call x1, Pallas kernels, middle(): pl.pallas_call(body, in_specs=[SCALAR] + [VMEM] * 5, out_specs=[ANY, VMEM...  7.71 us
    pallas_call x1, Pallas kernels, finish(): pl.pallas_call(body, in_specs=[VMEM] * 4, out_specs=[ANY] * 2, out_shape=...  4.37 us
    pallas_call x1, Pallas kernels, mix_first(): pl.pallas_call(body, in_specs=[ANY, ANY], out_specs=ANY, out_shape=pltpu....  3.92 us
  transfers between devices with their start and end apart: 14, of which 8 were waited for; matrix products, arithmetic and copies ran while one was open for 1% of the time, Pallas kernels for 6%

profile of v8, /device:TPU:0, one launch (start us, length us, event | category | flops | bytes accessed | tf_op | source)
XLA Modules:
  0.0 155.4 jit_solution(17923573917894485256)
XLA Ops:
  0.6 3.9 %mix_first.1 = bf16[1024,512]{1,0:T(8,128)(2,1)} custom-call(bf16[1024,1024]{1,0:T(8,128)(2,1)} %bitcast.35, bf16[1024,512]{1,0:T(8,128)(2,1)} %refs_0_), custom_call_target="tpu_custom_call" | custom-call | flops 1073741824 | bytes 4194304 | tf_op jit(solution)/shard_map/mix_first/pallas_call | solution.py:73
  4.6 7.5 %all-to-all-start = ((bf16[16,64,512]{2,1,0:T(8,128)(2,1)}), bf16[16,64,512]{2,1,0:T(8,128)(2,1)S(1)}, u32[]{:S(2)}, u32[]{:S(2)}) async-start(bf16[16,64,512]{2,1,0:T(8,128)(2,1)} %bitcast.37), calls=%async_computation | async-start | bytes 2097152 | tf_op jit(solution)/shard_map/all_to_all | solution.py:422
  12.5 0.7 spread_factor.1.m_ref
  13.2 21.9 %all-to-all-done.in_ref.u_ref = bf16[16,64,512]{2,1,0:T(8,128)(2,1)S(1)} async-done(((bf16[16,64,512]{2,1,0:T(8,128)(2,1)}), bf16[16,64,512]{2,1,0:T(8,128)(2,1)S(1)}, u32[]{:S(2)}, u32[]{:S(2)}) %all-to-all-start) | async-done | bytes 1048608 | tf_op jit(solution)/shard_map/all_to_all | solution.py:422
  35.0 1.2 mix_second.1
  36.3 6.9 %all-to-all-start.1 = ((bf16[16,64,512]{2,1,0:T(8,128)(2,1)}), bf16[16,64,512]{2,1,0:T(8,128)(2,1)S(1)}, u32[]{:S(2)}, u32[]{:S(2)}) async-start(bf16[16,64,512]{2,1,0:T(8,128)(2,1)} %mix_second.1), calls=%async_computation.1 | async-start | bytes 2097152 | tf_op jit(solution)/shard_map/all_to_all | solution.py:422
  43.2 2.5 %bring.1 = (bf16[1024,512]{1,0:T(8,128)(2,1)S(1)}, bf16[1024,512]{1,0:T(8,128)(2,1)S(1)}, bf16[1024,1024]{1,0:T(8,128)(2,1)S(1)}, bf16[4,128,512]{2,1,0:T(8,128)(2,1)S(1)}, bf16[4,512,128]{2,1,0:T(8,128)(2,1)S(1)}) custom-call(bf16[1024,512]{1,0:T(8,128)(2,1)} %refs_0_, bf16[1024,512]{1,0:T(8,128)(2,1)} %refs_1_, bf16[1024,1024]{1,0:T(8,128)(2,1)} %bitcast.36, ...), custom_call_target="tpu_custom_call" | custom-call | bytes 10485760 | tf_op jit(solution)/shard_map/bring/pallas_call | solution.py:273
  45.7 1.3 copy-done.4
  47.0 1.0 copy-done.6
  48.0 1.0 copy-done.9
  48.9 0.8 copy-done.12
  49.7 16.4 %all-to-all-done.1 = bf16[16,64,512]{2,1,0:T(8,128)(2,1)S(1)} async-done(((bf16[16,64,512]{2,1,0:T(8,128)(2,1)}), bf16[16,64,512]{2,1,0:T(8,128)(2,1)S(1)}, u32[]{:S(2)}, u32[]{:S(2)}) %all-to-all-start.1) | async-done | bytes 1048608 | tf_op jit(solution)/shard_map/all_to_all | solution.py:422
  66.1 1.2 copy-done.7
  67.3 1.2 copy-done.10
  68.5 1.0 copy-done.13
  69.6 7.7 %middle.1 = (bf16[1024,512]{1,0:T(8,128)(2,1)}, bf16[1024,512]{1,0:T(8,128)(2,1)S(1)}, bf16[4,128,512]{2,1,0:T(8,128)(2,1)S(1)}, bf16[4,128,512]{2,1,0:T(8,128)(2,1)S(1)}) custom-call(s32[1]{0:T(128)} %bitcast.2.half_ref, bf16[1024,512]{1,0:T(8,128)(2,1)S(1)} %copy-done.7, bf16[1024,512]{1,0:T(8,128)(2,1)S(1)} %copy-done.10, bf16[1024,512]{1,0:T(8,128)(2,1)S(1)} %bitcast.32, ...), custom_call_target="tpu_custom_call" | custom-call | flops 2684354560 | bytes 7340032 | tf_op jit(solution)/shard_map/middle/pallas_call | solution.py:237
  77.3 0.8 copy-done
  78.1 0.8 copy-done.11
  78.9 1.0 copy-done.14
  79.9 6.8 %all-to-all-start.2 = ((bf16[16,64,512]{2,1,0:T(8,128)(2,1)}), bf16[16,64,512]{2,1,0:T(8,128)(2,1)S(1)}, u32[]{:S(2)}, u32[]{:S(2)}) async-start(bf16[16,64,512]{2,1,0:T(8,128)(2,1)} %bitcast.38), calls=%async_computation.2 | async-start | bytes 2097152 | tf_op jit(solution)/shard_map/all_to_all | solution.py:422
  86.7 0.4 collective-permute-start
  87.1 1.8 %collective-permute-done = bf16[4,128,512]{2,1,0:T(8,128)(2,1)S(1)} collective-permute-done((bf16[4,128,512]{2,1,0:T(8,128)(2,1)}, bf16[4,128,512]{2,1,0:T(8,128)(2,1)S(1)}, u32[]{:S(2)}, u32[]{:S(2)}) %collective-permute-start) | collective-permute-done | bytes 524320 | tf_op jit(solution)/shard_map/ppermute | solution.py:331
  88.9 0.8 copy-done.2
  89.7 1.0 copy-done.1
  90.8 1.0 copy-done.3
  91.8 0.8 add_and_cut.2
  92.6 1.9 %collective-permute-start.1 = (bf16[256,512]{1,0:T(8,128)(2,1)}, bf16[256,512]{1,0:T(8,128)(2,1)S(1)}, u32[]{:S(2)}, u32[]{:S(2)}) collective-permute-start(bf16[256,512]{1,0:T(8,128)(2,1)} %get-tuple-element.60), channel_id=1, source_target_pairs={{0,2},{1,3},{2,0},{3,1},{4,6},{5,7},{6,4},{7,5},{8,10},{9,11},{10,... | collective-permute-start | bytes 786440 | tf_op jit(solution)/shard_map/ppermute | solution.py:331
  94.4 10.9 %collective-permute-done.1.refs_1_ = bf16[256,512]{1,0:T(8,128)(2,1)S(1)} collective-permute-done((bf16[256,512]{1,0:T(8,128)(2,1)}, bf16[256,512]{1,0:T(8,128)(2,1)S(1)}, u32[]{:S(2)}, u32[]{:S(2)}) %collective-permute-start.1) | collective-permute-done | bytes 262176 | tf_op jit(solution)/shard_map/ppermute | solution.py:331
  105.4 0.7 add_and_cut.3
  106.1 3.3 %collective-permute-start.2 = (bf16[64,512]{1,0:T(8,128)(2,1)}, bf16[64,512]{1,0:T(8,128)(2,1)S(1)}, u32[]{:S(2)}, u32[]{:S(2)}) collective-permute-start(bf16[64,512]{1,0:T(8,128)(2,1)} %get-tuple-element.62), channel_id=1, source_target_pairs={{0,4},{1,5},{2,6},{3,7},{4,0},{5,1},{6,2},{7,3},{8,12},{9,13},{10,... | collective-permute-start | bytes 196616 | tf_op jit(solution)/shard_map/ppermute | solution.py:331
  109.3 0.6 collective-permute-start.3
  109.9 1.8 %collective-permute-start.4 = (bf16[64,512]{1,0:T(8,128)(2,1)}, bf16[64,512]{1,0:T(8,128)(2,1)S(1)}, u32[]{:S(2)}, u32[]{:S(2)}) collective-permute-start(bf16[64,512]{1,0:T(8,128)(2,1)} %get-tuple-element.64), channel_id=1, source_target_pairs={{0,12},{1,13},{2,14},{3,15},{4,8},{5,9},{6,10},{7,11},{8,4},{9,5},... | collective-permute-start | bytes 196616 | tf_op jit(solution)/shard_map/ppermute | solution.py:331
  111.7 1.3 mix_second_back.1
  113.0 5.0 %collective-permute-done.3 = bf16[64,512]{1,0:T(8,128)(2,1)S(1)} collective-permute-done((bf16[64,512]{1,0:T(8,128)(2,1)}, bf16[64,512]{1,0:T(8,128)(2,1)S(1)}, u32[]{:S(2)}, u32[]{:S(2)}) %collective-permute-start.3) | collective-permute-done | bytes 65568 | tf_op jit(solution)/shard_map/ppermute | solution.py:331
  118.0 1.6 %collective-permute-start.7 = (bf16[64,512]{1,0:T(8,128)(2,1)S(1)}, bf16[64,512]{1,0:T(8,128)(2,1)S(1)}, u32[]{:S(2)}, u32[]{:S(2)}) collective-permute-start(bf16[64,512]{1,0:T(8,128)(2,1)S(1)} %add_convert_fusion), channel_id=1, source_target_pairs={{0,12},{1,13},{2,14},{3,15},{4,8},{5,9},{6,10},{7,11},{8,4},{9,5},... | collective-permute-start | bytes 196616 | tf_op jit(solution)/shard_map/ppermute | solution.py:331
  119.6 1.4 collective-permute-start.6
  121.0 1.4 collective-permute-start.5
  122.5 4.4 %all-to-all-start.3 = ((bf16[16,64,512]{2,1,0:T(8,128)(2,1)}), bf16[16,64,512]{2,1,0:T(8,128)(2,1)}, u32[]{:S(2)}, u32[]{:S(2)}) async-start(bf16[16,64,512]{2,1,0:T(8,128)(2,1)} %mix_second_back.1), calls=%async_computation.3 | async-start | bytes 2097152 | tf_op jit(solution)/shard_map/all_to_all | solution.py:422
  127.0 1.8 %collective-permute-start.8 = (bf16[256,512]{1,0:T(8,128)(2,1)S(1)}, bf16[256,512]{1,0:T(8,128)(2,1)S(1)}, u32[]{:S(2)}, u32[]{:S(2)}) collective-permute-start(bf16[256,512]{1,0:T(8,128)(2,1)S(1)} %bitcast.39), channel_id=1, source_target_pairs={{0,2},{1,3},{2,0},{3,1},{4,6},{5,7},{6,4},{7,5},{8,10},{9,11},{10,... | collective-permute-start | bytes 786440 | tf_op jit(solution)/shard_map/ppermute | solution.py:331
  128.8 1.5 grad_second.1
  130.3 0.2 copy.12
  130.5 0.9 reshape.72
  131.4 12.4 %collective-permute-done.8 = bf16[256,512]{1,0:T(8,128)(2,1)S(1)} collective-permute-done((bf16[256,512]{1,0:T(8,128)(2,1)S(1)}, bf16[256,512]{1,0:T(8,128)(2,1)S(1)}, u32[]{:S(2)}, u32[]{:S(2)}) %collective-permute-start.8) | collective-permute-done | bytes 262176 | tf_op jit(solution)/shard_map/ppermute | solution.py:331
  144.0 1.9 %collective-permute-done.9 = bf16[512,512]{1,0:T(8,128)(2,1)S(1)} collective-permute-done((bf16[512,512]{1,0:T(8,128)(2,1)S(1)}, bf16[512,512]{1,0:T(8,128)(2,1)S(1)}, u32[]{:S(2)}, u32[]{:S(2)}) %collective-permute-start.9) | collective-permute-done | bytes 524320 | tf_op jit(solution)/shard_map/ppermute | solution.py:331
  146.1 1.9 %write_weights.1 = (f32[4,128,512]{2,1,0:T(8,128)}, f32[4,512,128]{2,1,0:T(8,128)}) custom-call(bf16[1024,512]{1,0:T(8,128)(2,1)S(1)} %pad_maximum_fusion.up_in.down_in, bf16[1024,512]{1,0:T(8,128)(2,1)S(1)} %pad_maximum_fusion.up_in.down_in), custom_call_target="tpu_custom_call" | custom-call | flops 262144 | bytes 3145728 | tf_op jit(solution)/shard_map/write_weights/pallas_call | solution.py:391
  148.0 1.8 %all-to-all-done.3 = bf16[16,64,512]{2,1,0:T(8,128)(2,1)} async-done(((bf16[16,64,512]{2,1,0:T(8,128)(2,1)}), bf16[16,64,512]{2,1,0:T(8,128)(2,1)}, u32[]{:S(2)}, u32[]{:S(2)}) %all-to-all-start.3) | async-done | bytes 1048608 | tf_op jit(solution)/shard_map/all_to_all | solution.py:422
  149.8 1.2 copy-done.15
  151.0 4.4 %finish.1 = (f32[1024,1024]{1,0:T(8,128)}, bf16[1024,512]{1,0:T(8,128)(2,1)}) custom-call(bf16[1024,1024]{1,0:T(8,128)(2,1)S(1)} %copy-done.5, bf16[1024,512]{1,0:T(8,128)(2,1)S(1)} %copy-done.8, bf16[1024,512]{1,0:T(8,128)(2,1)S(1)} %copy-done.15, bf16[1024,512]{1,0:T(8,128)(2,1)} %bitcast.11.d), custom_call_target="tpu_custom_call" | custom-call | flops 2147483648 | bytes 10485760 | tf_op jit(solution)/shard_map/finish/pallas_call | solution.py:305
  (39 shorter events, 0.8 us)
Async XLA Ops:
  4.6 7.5 %copy-start.16 = (bf16[64,16,16]{0,2,1:T(8,128)(2,1)S(1)}, bf16[64,16,16]{0,2,1:T(8,128)(2,1)}, u32[]{:S(2)}) copy-start(bf16[64,16,16]{0,2,1:T(8,128)(2,1)} %param.9) | copy-start | bytes 98308
  4.6 30.5 %all-to-all-start = ((bf16[16,64,512]{2,1,0:T(8,128)(2,1)}), bf16[16,64,512]{2,1,0:T(8,128)(2,1)S(1)}, u32[]{:S(2)}, u32[]{:S(2)}) async-start(bf16[16,64,512]{2,1,0:T(8,128)(2,1)} %bitcast.37), calls=%async_computation | async-start | bytes 2097152 | tf_op jit(solution)/shard_map/all_to_all | solution.py:422
  36.3 29.8 %all-to-all-start.1 = ((bf16[16,64,512]{2,1,0:T(8,128)(2,1)}), bf16[16,64,512]{2,1,0:T(8,128)(2,1)S(1)}, u32[]{:S(2)}, u32[]{:S(2)}) async-start(bf16[16,64,512]{2,1,0:T(8,128)(2,1)} %mix_second.1), calls=%async_computation.1 | async-start | bytes 2097152 | tf_op jit(solution)/shard_map/all_to_all | solution.py:422
  45.7 1.3 copy-start.4
  47.0 1.0 copy-start.6
  48.0 1.0 copy-start.9
  48.9 0.8 copy-start.12
  66.1 1.2 copy-start.7
  67.3 1.2 copy-start.10
  68.5 1.0 copy-start.13
  77.3 0.8 copy-start
  78.1 0.8 copy-start.11
  78.9 1.0 copy-start.14
  79.9 31.8 %all-to-all-start.2 = ((bf16[16,64,512]{2,1,0:T(8,128)(2,1)}), bf16[16,64,512]{2,1,0:T(8,128)(2,1)S(1)}, u32[]{:S(2)}, u32[]{:S(2)}) async-start(bf16[16,64,512]{2,1,0:T(8,128)(2,1)} %bitcast.38), calls=%async_computation.2 | async-start | bytes 2097152 | tf_op jit(solution)/shard_map/all_to_all | solution.py:422
  86.7 2.2 %collective-permute-start = (bf16[4,128,512]{2,1,0:T(8,128)(2,1)}, bf16[4,128,512]{2,1,0:T(8,128)(2,1)S(1)}, u32[]{:S(2)}, u32[]{:S(2)}) collective-permute-start(bf16[4,128,512]{2,1,0:T(8,128)(2,1)} %copy-done.11), channel_id=1, source_target_pairs={{0,1},{1,0},{2,3},{3,2},{4,5},{5,4},{6,7},{7,6},{8,9},{9,8},{10,11... | collective-permute-start | bytes 1572872 | tf_op jit(solution)/shard_map/ppermute | solution.py:331
  88.9 0.8 copy-start.2
  89.7 1.0 copy-start.1
  90.8 1.0 copy-start.3
  92.6 12.8 %collective-permute-start.1 = (bf16[256,512]{1,0:T(8,128)(2,1)}, bf16[256,512]{1,0:T(8,128)(2,1)S(1)}, u32[]{:S(2)}, u32[]{:S(2)}) collective-permute-start(bf16[256,512]{1,0:T(8,128)(2,1)} %get-tuple-element.60), channel_id=1, source_target_pairs={{0,2},{1,3},{2,0},{3,1},{4,6},{5,7},{6,4},{7,5},{8,10},{9,11},{10,... | collective-permute-start | bytes 786440 | tf_op jit(solution)/shard_map/ppermute | solution.py:331
  106.1 6.9 %collective-permute-start.2 = (bf16[64,512]{1,0:T(8,128)(2,1)}, bf16[64,512]{1,0:T(8,128)(2,1)S(1)}, u32[]{:S(2)}, u32[]{:S(2)}) collective-permute-start(bf16[64,512]{1,0:T(8,128)(2,1)} %get-tuple-element.62), channel_id=1, source_target_pairs={{0,4},{1,5},{2,6},{3,7},{4,0},{5,1},{6,2},{7,3},{8,12},{9,13},{10,... | collective-permute-start | bytes 196616 | tf_op jit(solution)/shard_map/ppermute | solution.py:331
  109.3 8.6 %collective-permute-start.3 = (bf16[64,512]{1,0:T(8,128)(2,1)}, bf16[64,512]{1,0:T(8,128)(2,1)S(1)}, u32[]{:S(2)}, u32[]{:S(2)}) collective-permute-start(bf16[64,512]{1,0:T(8,128)(2,1)} %get-tuple-element.63), channel_id=1, source_target_pairs={{0,8},{1,9},{2,10},{3,11},{4,12},{5,13},{6,14},{7,15},{8,0},{9,1},... | collective-permute-start | bytes 196616 | tf_op jit(solution)/shard_map/ppermute | solution.py:331
  109.9 8.0 %collective-permute-start.4 = (bf16[64,512]{1,0:T(8,128)(2,1)}, bf16[64,512]{1,0:T(8,128)(2,1)S(1)}, u32[]{:S(2)}, u32[]{:S(2)}) collective-permute-start(bf16[64,512]{1,0:T(8,128)(2,1)} %get-tuple-element.64), channel_id=1, source_target_pairs={{0,12},{1,13},{2,14},{3,15},{4,8},{5,9},{6,10},{7,11},{8,4},{9,5},... | collective-permute-start | bytes 196616 | tf_op jit(solution)/shard_map/ppermute | solution.py:331
  118.0 8.8 %collective-permute-start.7 = (bf16[64,512]{1,0:T(8,128)(2,1)S(1)}, bf16[64,512]{1,0:T(8,128)(2,1)S(1)}, u32[]{:S(2)}, u32[]{:S(2)}) collective-permute-start(bf16[64,512]{1,0:T(8,128)(2,1)S(1)} %add_convert_fusion), channel_id=1, source_target_pairs={{0,12},{1,13},{2,14},{3,15},{4,8},{5,9},{6,10},{7,11},{8,4},{9,5},... | collective-permute-start | bytes 196616 | tf_op jit(solution)/shard_map/ppermute | solution.py:331
  119.6 7.2 %collective-permute-start.6 = (bf16[64,512]{1,0:T(8,128)(2,1)S(1)}, bf16[64,512]{1,0:T(8,128)(2,1)S(1)}, u32[]{:S(2)}, u32[]{:S(2)}) collective-permute-start(bf16[64,512]{1,0:T(8,128)(2,1)S(1)} %add_convert_fusion), channel_id=1, source_target_pairs={{0,8},{1,9},{2,10},{3,11},{4,12},{5,13},{6,14},{7,15},{8,0},{9,1},... | collective-permute-start | bytes 196616 | tf_op jit(solution)/shard_map/ppermute | solution.py:331
  121.0 5.8 %collective-permute-start.5 = (bf16[64,512]{1,0:T(8,128)(2,1)S(1)}, bf16[64,512]{1,0:T(8,128)(2,1)S(1)}, u32[]{:S(2)}, u32[]{:S(2)}) collective-permute-start(bf16[64,512]{1,0:T(8,128)(2,1)S(1)} %add_convert_fusion), channel_id=1, source_target_pairs={{0,4},{1,5},{2,6},{3,7},{4,0},{5,1},{6,2},{7,3},{8,12},{9,13},{10,... | collective-permute-start | bytes 196616 | tf_op jit(solution)/shard_map/ppermute | solution.py:331
  122.5 27.3 %all-to-all-start.3 = ((bf16[16,64,512]{2,1,0:T(8,128)(2,1)}), bf16[16,64,512]{2,1,0:T(8,128)(2,1)}, u32[]{:S(2)}, u32[]{:S(2)}) async-start(bf16[16,64,512]{2,1,0:T(8,128)(2,1)} %mix_second_back.1), calls=%async_computation.3 | async-start | bytes 2097152 | tf_op jit(solution)/shard_map/all_to_all | solution.py:422
  127.0 16.9 %collective-permute-start.8 = (bf16[256,512]{1,0:T(8,128)(2,1)S(1)}, bf16[256,512]{1,0:T(8,128)(2,1)S(1)}, u32[]{:S(2)}, u32[]{:S(2)}) collective-permute-start(bf16[256,512]{1,0:T(8,128)(2,1)S(1)} %bitcast.39), channel_id=1, source_target_pairs={{0,2},{1,3},{2,0},{3,1},{4,6},{5,7},{6,4},{7,5},{8,10},{9,11},{10,... | collective-permute-start | bytes 786440 | tf_op jit(solution)/shard_map/ppermute | solution.py:331
  143.9 2.0 %collective-permute-start.9 = (bf16[512,512]{1,0:T(8,128)(2,1)S(1)}, bf16[512,512]{1,0:T(8,128)(2,1)S(1)}, u32[]{:S(2)}, u32[]{:S(2)}) collective-permute-start(bf16[512,512]{1,0:T(8,128)(2,1)S(1)} %pad_maximum_fusion.1), channel_id=1, source_target_pairs={{0,1},{1,0},{2,3},{3,2},{4,5},{5,4},{6,7},{7,6},{8,9},{9,8},{10,11... | collective-permute-start | bytes 1572872 | tf_op jit(solution)/shard_map/ppermute | solution.py:331
  146.0 3.8 %copy-start.5 = (bf16[1024,1024]{1,0:T(8,128)(2,1)S(1)}, bf16[1024,1024]{1,0:T(8,128)(2,1)}, u32[]{:S(2)}) copy-start(bf16[1024,1024]{1,0:T(8,128)(2,1)} %copy-done.4) | copy-start | bytes 6291460
  146.0 3.8 %copy-start.8 = (bf16[1024,512]{1,0:T(8,128)(2,1)S(1)}, bf16[1024,512]{1,0:T(8,128)(2,1)}, u32[]{:S(2)}) copy-start(bf16[1024,512]{1,0:T(8,128)(2,1)} %copy-done.6) | copy-start | bytes 3145732
  149.8 1.2 copy-start.15

commit v9 on v8

--- a/solution.py
+++ b/solution.py
@@ -58,10 +58,12 @@
         xs = row_copies(x_hbm, x_all, sems, 0, tiles)
         fs = row_copies(f_hbm, f_all, sems, tiles, tiles)
         us = row_copies(u_all, u_hbm, sems, 2 * tiles, tiles)
-        for c in xs + fs:
+        for c in xs + fs[:1]:
             c.start()
         for c in xs:
             c.wait()
+        for c in fs[1:]:
+            c.start()
         for t in range(tiles):
             fs[t].wait()
             at = slice(t * step, (t + 1) * step)
@@ -186,15 +188,33 @@
     step = min(256, rows)
     tiles = rows // step
 
-    def body(half_ref, x_ref, g_ref, v_ref, up_ref, down_ref, dv_hbm, r_ref, kept_ref, sent_ref, *tmp):
-        dv, w, sems = tmp
+    def body(half_ref, x_hbm, g_hbm, v_ref, up_hbm, down_hbm, *refs):
+        dv_hbm, r_hbm, kept_hbm, sent_hbm = refs[:4]
+        x_ref, g_ref, up_ref, down_ref, dv, r_ref, w, halves, sems = refs[4:]
+
+        def rows_copy(src, dst, kind, t):
+            at = pl.ds(t * step, step)
+            return pltpu.make_async_copy(src.at[at], dst.at[at], sems.at[kind * tiles + t])
+
+        def whole_copy(src, dst, number):
+            return pltpu.make_async_copy(src, dst, sems.at[4 * tiles + number])
+
+        fetch_up = whole_copy(up_hbm, up_ref, 0)
+        fetch_down = whole_copy(down_hbm, down_ref, 1)
+        rows_copy(x_hbm, x_ref, 0, 0).start()
+        fetch_up.start()
+        rows_copy(g_hbm, g_ref, 1, 0).start()
+        fetch_down.start()
+        for t in range(1, tiles):
+            rows_copy(x_hbm, x_ref, 0, t).start()
+            rows_copy(g_hbm, g_ref, 1, t).start()
         w[...] = jnp.zeros_like(w)
-
-        def send(t):
-            at = pl.ds(t * step, step)
-            return pltpu.make_async_copy(dv.at[at], dv_hbm.at[at], sems.at[t])
+        fetch_up.wait()
+        fetch_down.wait()
 
         def tile(t, carry):
+            rows_copy(x_hbm, x_ref, 0, t).wait()
+            rows_copy(g_hbm, g_ref, 1, t).wait()
             at = pl.ds(pl.multiple_of(t * step, step), step)
             x = x_ref[at, :].astype(F32)
             g = g_ref[at, :]
@@ -223,63 +243,52 @@
                 grads.append(dot(da, up_ref[b], 1, 1))
             dh = (g.astype(F32) + jnp.concatenate(grads, axis=1)).astype(BF).astype(F32)
             dv[at, :] = (dh * gate).astype(BF)
-            send(t).start()
+            rows_copy(dv, dv_hbm, 2, t).start()
             r_ref[at, :] = (dh * (1.0 + v * (sx + gate * (1.0 - sx)))).astype(BF)
+            rows_copy(r_ref, r_hbm, 3, t).start()
             return carry
 
         lax.fori_loop(0, tiles, tile, 0)
-        kept_ref[...] = w[half_ref[0]].astype(BF)
-        sent_ref[...] = w[1 - half_ref[0]].astype(BF)
+        halves[1] = w[1 - half_ref[0]].astype(BF)
+        send = whole_copy(halves.at[1], sent_hbm, 2)
+        send.start()
+        halves[0] = w[half_ref[0]].astype(BF)
+        keep = whole_copy(halves.at[0], kept_hbm, 3)
+        keep.start()
         for t in range(tiles):
-            send(t).wait()
+            rows_copy(dv, dv_hbm, 2, t).wait()
+            rows_copy(r_ref, r_hbm, 3, t).wait()
+        send.wait()
+        keep.wait()
 
     hidden = rows * groups * inner
     return pl.pallas_call(
         body,
-        in_specs=[SCALAR] + [VMEM] * 5,
-        out_specs=[ANY, VMEM, VMEM, VMEM],
+        in_specs=[SCALAR, ANY, ANY, VMEM, ANY, ANY],
+        out_specs=[ANY] * 4,
         out_shape=[
             pltpu.HBM((rows, channels), BF),
+            pltpu.HBM((rows, channels), BF),
+            pltpu.HBM(up_blocks.shape, BF),
+            pltpu.HBM(up_blocks.shape, BF),
+        ],
+        scratch_shapes=[
+            pltpu.VMEM((rows, channels), BF),
             pltpu.VMEM((rows, channels), BF),
             pltpu.VMEM(up_blocks.shape, BF),
-            pltpu.VMEM(up_blocks.shape, BF),
-        ],
-        scratch_shapes=[
+            pltpu.VMEM(down_blocks.shape, BF),
+            pltpu.VMEM((rows, channels), BF),
             pltpu.VMEM((rows, channels), BF),
             pltpu.VMEM((2, groups, width, inner), F32),
-            pltpu.SemaphoreType.DMA((tiles,)),
+            pltpu.VMEM((2, groups, width, inner), BF),
+            pltpu.SemaphoreType.DMA((4 * tiles + 4,)),
         ],
         compiler_params=params(0),
         cost_estimate=cost(
             10 * hidden * width, 10 * rows * channels + 8 * groups * width * inner, hidden
         ),
         name="middle",
-    )(half, *[in_vmem(a) for a in (blocked, incoming, mixed, up_blocks, down_blocks)])
-
-
-def bring(arrays, name):
-    number = len(arrays)
-
-    def body(*refs):
-        sems = refs[-1]
-        copies = [
-            pltpu.make_async_copy(refs[i], refs[number + i], sems.at[i]) for i in range(number)
-        ]
-        for c in copies:
-            c.start()
-        for c in copies:
-            c.wait()
-
-    return pl.pallas_call(
-        body,
-        in_specs=[ANY] * number,
-        out_specs=[pl.BlockSpec(memory_space=pltpu.VMEM)] * number,
-        out_shape=[pltpu.VMEM(a.shape, a.dtype) for a in arrays],
-        scratch_shapes=[pltpu.SemaphoreType.DMA((number,))],
-        compiler_params=pltpu.CompilerParams(vmem_limit_bytes=16 * 1024 * 1024),
-        cost_estimate=cost(0, sum(2 * a.size * a.dtype.itemsize for a in arrays)),
-        name=name,
-    )(*[in_hbm(a) for a in arrays])
+    )(half, in_hbm(blocked), in_hbm(incoming), in_vmem(mixed), in_hbm(up_blocks), in_hbm(down_blocks))
 
 
 def finish(factor, grad_first, blocked, gate_grad, scale):
@@ -287,15 +296,29 @@
     tiles = 4
     step = block // tiles
 
-    def body(f, x, r, d, one_hbm, out_hbm, one, out, sems):
-        ones = row_copies(one, one_hbm, sems, 0, tiles)
-        outs = row_copies(out, out_hbm, sems, tiles, tiles)
+    def body(f_hbm, d_hbm, x_hbm, r_hbm, one_hbm, out_hbm, f, d, x, r, one, out, sems):
+        ds = row_copies(d_hbm, d, sems, 0, tiles)
+        xs = row_copies(x_hbm, x, sems, tiles, tiles)
+        fs = row_copies(f_hbm, f, sems, 2 * tiles, tiles)
+        rs = row_copies(r_hbm, r, sems, 3 * tiles, tiles)
+        ones = row_copies(one, one_hbm, sems, 4 * tiles, tiles)
+        outs = row_copies(out, out_hbm, sems, 5 * tiles, tiles)
+        for c in xs + ds:
+            c.start()
+        for c in xs:
+            c.wait()
         for t in range(tiles):
             at = slice(t * step, (t + 1) * step)
+            ds[t].wait()
+            fs[t].start()
+            rs[t].start()
             one[at, :] = dot(d[at, :], x[...], 1, 1) * scale
             ones[t].start()
+        for c in fs:
+            c.wait()
         for t in range(tiles):
             at = slice(t * step, (t + 1) * step)
+            rs[t].wait()
             total = dot(f[:, at], d[...], 0, 0) + r[at, :].astype(F32)
             out[at, :] = total.astype(BF)
             outs[t].start()
@@ -304,18 +327,22 @@
 
     return pl.pallas_call(
         body,
-        in_specs=[VMEM] * 4,
+        in_specs=[ANY] * 4,
         out_specs=[ANY] * 2,
         out_shape=[pltpu.HBM((block, block), F32), pltpu.HBM((block, channels), BF)],
         scratch_shapes=[
+            pltpu.VMEM((block, block), BF),
+            pltpu.VMEM((block, channels), BF),
+            pltpu.VMEM((block, channels), BF),
+            pltpu.VMEM((block, channels), BF),
             pltpu.VMEM((block, block), F32),
             pltpu.VMEM((block, channels), BF),
-            pltpu.SemaphoreType.DMA((2 * tiles,)),
+            pltpu.SemaphoreType.DMA((6 * tiles,)),
         ],
         compiler_params=params(0),
         cost_estimate=cost(4 * block * block * channels, 6 * block * block + 8 * block * channels),
         name="finish",
-    )(*[in_vmem(a) for a in (factor, blocked, gate_grad, grad_first)])
+    )(in_hbm(factor), in_hbm(grad_first), in_hbm(blocked), in_hbm(gate_grad))
 
 
 def radices(count):
@@ -437,11 +464,8 @@
 
     half = (lax.axis_index("seq") % 2).astype(jnp.int32).reshape(1)
     firsts = exchange(mix_first(factor, tokens))
-    late = (tokens, cotangent, factor, up_blocks, down_blocks)
-    firsts, late = lax.optimization_barrier((firsts, late))
-    tokens_v, cotangent_v, factor_v, up_v, down_v = bring(late, "bring")
     mixed = exchange(second(firsts, False)).reshape(block, channels)
-    dv, gate_grad, kept, sent = middle(half, tokens_v, cotangent_v, mixed, up_v, down_v)
+    dv, gate_grad, kept, sent = middle(half, tokens, cotangent, mixed, up_blocks, down_blocks)
     grad_mixed = exchange(dv)
     back = second(grad_mixed, True)
     terms = [kept, swap(sent, count, 1, 1)]
@@ -457,7 +481,7 @@
     for step in reversed(steps):
         total = gather_step(total, count, *step, after=two if step == steps[1] else ())
     grad_up, grad_down = write_weights(total, up_blocks.shape, down_blocks.shape, scale)
-    one, grad_tokens = finish(factor_v, grad_first, tokens_v, gate_grad, scale)
+    one, grad_tokens = finish(factor, grad_first, tokens, gate_grad, scale)
     return (grad_tokens, one.reshape(1, block, block), two, grad_up, grad_down)
 
 

time: 157 us -> 156 us (level)
  local copies, waits for them, and re-layouts: 15.8 us -> 4.46 us
  waiting for transfers between devices: 71.9 us -> 78.9 us
  Pallas kernels: 26.6 us -> 29.7 us
    unnamed x34 -> x8, local copies, waits for them, and re-layouts: 14.2 us -> 2.88 us
    all_to_all x4, waiting for transfers between devices: 40 us -> 46.6 us  [exchange(): return lax.all_to_all(cut, 'seq', split_axis=0, concat_axis=0, tiled=True)]
    pallas_call x3 -> x2, Pallas kernels: 14.6 us -> 17.2 us  [the longest x1 9.56 us: middle(): pl.pallas_call(body, in_specs=[SCALAR, ANY, ANY, VMEM, ANY, ANY], out_spe...]
  transfers between devices with their start and end apart: 14 -> 14, of which waited for: 8 -> 9; matrix products, arithmetic and copies ran while one was open for 1% -> 1% of each run, Pallas kernels for 6% -> 4%
where the time goes in v9:
time: 156 us; the launch traced here: 154 us
  waiting for transfers between devices  78.9 us (51%)
  starting transfers between devices  39.6 us (25%)
  Pallas kernels  29.7 us (19%)
  local copies, waits for them, and re-layouts  4.46 us (3%)
    all_to_all x4, waiting for transfers between devices, exchange(): return lax.all_to_all(cut, 'seq', split_axis=0, concat_axis=0, tiled=True)  46.6 us
    ppermute x10, waiting for transfers between devices, swap(): lax.ppermute(values, 'seq', [(i, i ^ stride * s) for i in range(count)])  32.3 us
    all_to_all x4, starting transfers between devices, exchange(): return lax.all_to_all(cut, 'seq', split_axis=0, concat_axis=0, tiled=True)  25.6 us
    ppermute x10, starting transfers between devices, swap(): lax.ppermute(values, 'seq', [(i, i ^ stride * s) for i in range(count)])  14 us
    pallas_call x1, Pallas kernels, middle(): pl.pallas_call(body, in_specs=[SCALAR, ANY, ANY, VMEM, ANY, ANY], out_spe...  9.56 us
    pallas_call x1, Pallas kernels, finish(): pl.pallas_call(body, in_specs=[ANY] * 4, out_specs=[ANY] * 2, out_shape=[...  7.66 us
    pallas_call x1, Pallas kernels, mix_first(): pl.pallas_call(body, in_specs=[ANY, ANY], out_specs=ANY, out_shape=pltpu....  4.39 us
  transfers between devices with their start and end apart: 14, of which 9 were waited for; matrix products, arithmetic and copies ran while one was open for 1% of the time, Pallas kernels for 4%

profile of v9, /device:TPU:0, one launch (start us, length us, event | category | flops | bytes accessed | tf_op | source)
XLA Modules:
  0.0 153.7 jit_solution(14965877363374921552)
XLA Ops:
  0.6 4.4 %mix_first.1 = bf16[1024,512]{1,0:T(8,128)(2,1)} custom-call(bf16[1024,1024]{1,0:T(8,128)(2,1)} %bitcast.36, bf16[1024,512]{1,0:T(8,128)(2,1)} %x_hbm.5), custom_call_target="tpu_custom_call" | custom-call | flops 1073741824 | bytes 4194304 | tf_op jit(solution)/shard_map/mix_first/pallas_call | solution.py:75
  5.0 0.0 copy-start.3
  5.0 7.5 %all-to-all-start = ((bf16[16,64,512]{2,1,0:T(8,128)(2,1)}), bf16[16,64,512]{2,1,0:T(8,128)(2,1)S(1)}, u32[]{:S(2)}, u32[]{:S(2)}) async-start(bf16[16,64,512]{2,1,0:T(8,128)(2,1)} %bitcast.35), calls=%async_computation | async-start | bytes 2097152 | tf_op jit(solution)/shard_map/all_to_all | solution.py:449
  12.6 0.2 reshape.62
  12.7 0.2 copy.11
  12.9 0.7 spread_factor.1.m_ref
  13.6 21.9 %all-to-all-done.in_ref.u_ref = bf16[16,64,512]{2,1,0:T(8,128)(2,1)S(1)} async-done(((bf16[16,64,512]{2,1,0:T(8,128)(2,1)}), bf16[16,64,512]{2,1,0:T(8,128)(2,1)S(1)}, u32[]{:S(2)}, u32[]{:S(2)}) %all-to-all-start) | async-done | bytes 1048608 | tf_op jit(solution)/shard_map/all_to_all | solution.py:449
  35.5 1.2 mix_second.1
  36.7 6.9 %all-to-all-start.1 = ((bf16[16,64,512]{2,1,0:T(8,128)(2,1)}), bf16[16,64,512]{2,1,0:T(8,128)(2,1)S(1)}, u32[]{:S(2)}, u32[]{:S(2)}) async-start(bf16[16,64,512]{2,1,0:T(8,128)(2,1)} %mix_second.1), calls=%async_computation.1 | async-start | bytes 2097152 | tf_op jit(solution)/shard_map/all_to_all | solution.py:449
  43.6 22.9 %all-to-all-done.1 = bf16[16,64,512]{2,1,0:T(8,128)(2,1)S(1)} async-done(((bf16[16,64,512]{2,1,0:T(8,128)(2,1)}), bf16[16,64,512]{2,1,0:T(8,128)(2,1)S(1)}, u32[]{:S(2)}, u32[]{:S(2)}) %all-to-all-start.1) | async-done | bytes 1048608 | tf_op jit(solution)/shard_map/all_to_all | solution.py:449
  66.6 9.6 %middle.1 = (bf16[1024,512]{1,0:T(8,128)(2,1)}, bf16[1024,512]{1,0:T(8,128)(2,1)}, bf16[4,128,512]{2,1,0:T(8,128)(2,1)}, bf16[4,128,512]{2,1,0:T(8,128)(2,1)}) custom-call(s32[1]{0:T(128)} %bitcast.3.half_ref, bf16[1024,512]{1,0:T(8,128)(2,1)} %x_hbm.5, bf16[1024,512]{1,0:T(8,128)(2,1)} %g_hbm.1, bf16[1024,512]{1,0:T(8,128)(2,1)S(1)} %bitcast.32, ...), custom_call_target="tpu_custom_call" | custom-call | flops 2684354560 | bytes 7340032 | tf_op jit(solution)/shard_map/middle/pallas_call | solution.py:265
  76.1 6.9 %all-to-all-start.2 = ((bf16[16,64,512]{2,1,0:T(8,128)(2,1)}), bf16[16,64,512]{2,1,0:T(8,128)(2,1)S(1)}, u32[]{:S(2)}, u32[]{:S(2)}) async-start(bf16[16,64,512]{2,1,0:T(8,128)(2,1)} %bitcast.38), calls=%async_computation.2 | async-start | bytes 2097152 | tf_op jit(solution)/shard_map/all_to_all | solution.py:449
  83.0 0.4 collective-permute-start
  83.4 1.8 %collective-permute-done = bf16[4,128,512]{2,1,0:T(8,128)(2,1)S(1)} collective-permute-done((bf16[4,128,512]{2,1,0:T(8,128)(2,1)}, bf16[4,128,512]{2,1,0:T(8,128)(2,1)S(1)}, u32[]{:S(2)}, u32[]{:S(2)}) %collective-permute-start) | collective-permute-done | bytes 524320 | tf_op jit(solution)/shard_map/ppermute | solution.py:358
  85.2 0.8 copy-done.1
  86.0 1.0 copy-done
  87.0 1.0 copy-done.2
  88.1 0.8 add_and_cut.2
  88.8 1.9 %collective-permute-start.1 = (bf16[256,512]{1,0:T(8,128)(2,1)}, bf16[256,512]{1,0:T(8,128)(2,1)S(1)}, u32[]{:S(2)}, u32[]{:S(2)}) collective-permute-start(bf16[256,512]{1,0:T(8,128)(2,1)} %get-tuple-element.37), channel_id=1, source_target_pairs={{0,2},{1,3},{2,0},{3,1},{4,6},{5,7},{6,4},{7,5},{8,10},{9,11},{10,... | collective-permute-start | bytes 786440 | tf_op jit(solution)/shard_map/ppermute | solution.py:358
  90.7 10.9 %collective-permute-done.1.refs_1_ = bf16[256,512]{1,0:T(8,128)(2,1)S(1)} collective-permute-done((bf16[256,512]{1,0:T(8,128)(2,1)}, bf16[256,512]{1,0:T(8,128)(2,1)S(1)}, u32[]{:S(2)}, u32[]{:S(2)}) %collective-permute-start.1) | collective-permute-done | bytes 262176 | tf_op jit(solution)/shard_map/ppermute | solution.py:358
  101.6 0.7 add_and_cut.3
  102.3 3.3 %collective-permute-start.2 = (bf16[64,512]{1,0:T(8,128)(2,1)}, bf16[64,512]{1,0:T(8,128)(2,1)S(1)}, u32[]{:S(2)}, u32[]{:S(2)}) collective-permute-start(bf16[64,512]{1,0:T(8,128)(2,1)} %get-tuple-element.39), channel_id=1, source_target_pairs={{0,4},{1,5},{2,6},{3,7},{4,0},{5,1},{6,2},{7,3},{8,12},{9,13},{10,... | collective-permute-start | bytes 196616 | tf_op jit(solution)/shard_map/ppermute | solution.py:358
  105.6 0.6 collective-permute-start.3
  106.2 1.8 %collective-permute-start.4 = (bf16[64,512]{1,0:T(8,128)(2,1)}, bf16[64,512]{1,0:T(8,128)(2,1)S(1)}, u32[]{:S(2)}, u32[]{:S(2)}) collective-permute-start(bf16[64,512]{1,0:T(8,128)(2,1)} %get-tuple-element.41), channel_id=1, source_target_pairs={{0,12},{1,13},{2,14},{3,15},{4,8},{5,9},{6,10},{7,11},{8,4},{9,5},... | collective-permute-start | bytes 196616 | tf_op jit(solution)/shard_map/ppermute | solution.py:358
  108.0 0.0 all-to-all-done.2.in_ref.g_ref
  108.0 1.3 mix_second_back.1
  109.2 0.0 collective-permute-done.2
  109.2 5.0 %collective-permute-done.3 = bf16[64,512]{1,0:T(8,128)(2,1)S(1)} collective-permute-done((bf16[64,512]{1,0:T(8,128)(2,1)}, bf16[64,512]{1,0:T(8,128)(2,1)S(1)}, u32[]{:S(2)}, u32[]{:S(2)}) %collective-permute-start.3) | collective-permute-done | bytes 65568 | tf_op jit(solution)/shard_map/ppermute | solution.py:358
  114.2 0.0 collective-permute-done.4
  114.3 1.6 %collective-permute-start.5 = (bf16[64,512]{1,0:T(8,128)(2,1)S(1)}, bf16[64,512]{1,0:T(8,128)(2,1)S(1)}, u32[]{:S(2)}, u32[]{:S(2)}) collective-permute-start(bf16[64,512]{1,0:T(8,128)(2,1)S(1)} %add_convert_fusion), channel_id=1, source_target_pairs={{0,4},{1,5},{2,6},{3,7},{4,0},{5,1},{6,2},{7,3},{8,12},{9,13},{10,... | collective-permute-start | bytes 196616 | tf_op jit(solution)/shard_map/ppermute | solution.py:358
  115.8 0.6 collective-permute-start.6
  116.5 2.3 %collective-permute-start.7 = (bf16[64,512]{1,0:T(8,128)(2,1)S(1)}, bf16[64,512]{1,0:T(8,128)(2,1)S(1)}, u32[]{:S(2)}, u32[]{:S(2)}) collective-permute-start(bf16[64,512]{1,0:T(8,128)(2,1)S(1)} %add_convert_fusion), channel_id=1, source_target_pairs={{0,12},{1,13},{2,14},{3,15},{4,8},{5,9},{6,10},{7,11},{8,4},{9,5},... | collective-permute-start | bytes 196616 | tf_op jit(solution)/shard_map/ppermute | solution.py:358
  118.7 4.3 %all-to-all-start.3 = ((bf16[16,64,512]{2,1,0:T(8,128)(2,1)}), bf16[16,64,512]{2,1,0:T(8,128)(2,1)}, u32[]{:S(2)}, u32[]{:S(2)}) async-start(bf16[16,64,512]{2,1,0:T(8,128)(2,1)} %mix_second_back.1), calls=%async_computation.3 | async-start | bytes 2097152 | tf_op jit(solution)/shard_map/all_to_all | solution.py:449
  123.1 0.0 collective-permute-done.5
  123.1 0.3 collective-permute-done.6
  123.4 0.0 collective-permute-done.7
  123.5 1.5 %collective-permute-start.8 = (bf16[256,512]{1,0:T(8,128)(2,1)S(1)}, bf16[256,512]{1,0:T(8,128)(2,1)S(1)}, u32[]{:S(2)}, u32[]{:S(2)}) collective-permute-start(bf16[256,512]{1,0:T(8,128)(2,1)S(1)} %bitcast.39), channel_id=1, source_target_pairs={{0,2},{1,3},{2,0},{3,1},{4,6},{5,7},{6,4},{7,5},{8,10},{9,11},{10,... | collective-permute-start | bytes 786440 | tf_op jit(solution)/shard_map/ppermute | solution.py:358
  125.1 1.5 grad_second.1
  126.6 0.2 copy.12
  126.8 0.9 reshape.72
  127.7 12.4 %collective-permute-done.8 = bf16[256,512]{1,0:T(8,128)(2,1)S(1)} collective-permute-done((bf16[256,512]{1,0:T(8,128)(2,1)S(1)}, bf16[256,512]{1,0:T(8,128)(2,1)S(1)}, u32[]{:S(2)}, u32[]{:S(2)}) %collective-permute-start.8) | collective-permute-done | bytes 262176 | tf_op jit(solution)/shard_map/ppermute | solution.py:358
  140.2 0.1 collective-permute-start.9
  140.3 1.9 %collective-permute-done.9 = bf16[512,512]{1,0:T(8,128)(2,1)S(1)} collective-permute-done((bf16[512,512]{1,0:T(8,128)(2,1)S(1)}, bf16[512,512]{1,0:T(8,128)(2,1)S(1)}, u32[]{:S(2)}, u32[]{:S(2)}) %collective-permute-start.9) | collective-permute-done | bytes 524320 | tf_op jit(solution)/shard_map/ppermute | solution.py:358
  142.2 0.1 broadcast_select_fusion.1
  142.2 0.1 pad_maximum_fusion.up_in.down_in
  142.3 1.9 %write_weights.1 = (f32[4,128,512]{2,1,0:T(8,128)}, f32[4,512,128]{2,1,0:T(8,128)}) custom-call(bf16[1024,512]{1,0:T(8,128)(2,1)S(1)} %pad_maximum_fusion.up_in.down_in, bf16[1024,512]{1,0:T(8,128)(2,1)S(1)} %pad_maximum_fusion.up_in.down_in), custom_call_target="tpu_custom_call" | custom-call | flops 262144 | bytes 3145728 | tf_op jit(solution)/shard_map/write_weights/pallas_call | solution.py:418
  144.3 1.8 %all-to-all-done.3 = bf16[16,64,512]{2,1,0:T(8,128)(2,1)} async-done(((bf16[16,64,512]{2,1,0:T(8,128)(2,1)}), bf16[16,64,512]{2,1,0:T(8,128)(2,1)}, u32[]{:S(2)}, u32[]{:S(2)}) %all-to-all-start.3) | async-done | bytes 1048608 | tf_op jit(solution)/shard_map/all_to_all | solution.py:449
  146.0 7.7 %finish.1 = (f32[1024,1024]{1,0:T(8,128)}, bf16[1024,512]{1,0:T(8,128)(2,1)}) custom-call(bf16[1024,1024]{1,0:T(8,128)(2,1)} %bitcast.37, bf16[1024,512]{1,0:T(8,128)(2,1)} %bitcast.11.d_hbm, bf16[1024,512]{1,0:T(8,128)(2,1)} %x_hbm.5, bf16[1024,512]{1,0:T(8,128)(2,1)} %get-tuple-element.49.r_hbm), custom_call_target="tpu_custom_call" | custom-call | flops 2147483648 | bytes 10485760 | tf_op jit(solution)/shard_map/finish/pallas_call | solution.py:328
  (12 shorter events, 0.2 us)
Async XLA Ops:
  5.0 7.5 %copy-start.3 = (bf16[64,16,16]{0,2,1:T(8,128)(2,1)S(1)}, bf16[64,16,16]{0,2,1:T(8,128)(2,1)}, u32[]{:S(2)}) copy-start(bf16[64,16,16]{0,2,1:T(8,128)(2,1)} %param.9) | copy-start | bytes 98308
  5.0 30.5 %all-to-all-start = ((bf16[16,64,512]{2,1,0:T(8,128)(2,1)}), bf16[16,64,512]{2,1,0:T(8,128)(2,1)S(1)}, u32[]{:S(2)}, u32[]{:S(2)}) async-start(bf16[16,64,512]{2,1,0:T(8,128)(2,1)} %bitcast.35), calls=%async_computation | async-start | bytes 2097152 | tf_op jit(solution)/shard_map/all_to_all | solution.py:449
  36.7 29.8 %all-to-all-start.1 = ((bf16[16,64,512]{2,1,0:T(8,128)(2,1)}), bf16[16,64,512]{2,1,0:T(8,128)(2,1)S(1)}, u32[]{:S(2)}, u32[]{:S(2)}) async-start(bf16[16,64,512]{2,1,0:T(8,128)(2,1)} %mix_second.1), calls=%async_computation.1 | async-start | bytes 2097152 | tf_op jit(solution)/shard_map/all_to_all | solution.py:449
  76.1 31.8 %all-to-all-start.2 = ((bf16[16,64,512]{2,1,0:T(8,128)(2,1)}), bf16[16,64,512]{2,1,0:T(8,128)(2,1)S(1)}, u32[]{:S(2)}, u32[]{:S(2)}) async-start(bf16[16,64,512]{2,1,0:T(8,128)(2,1)} %bitcast.38), calls=%async_computation.2 | async-start | bytes 2097152 | tf_op jit(solution)/shard_map/all_to_all | solution.py:449
  83.0 2.2 %collective-permute-start = (bf16[4,128,512]{2,1,0:T(8,128)(2,1)}, bf16[4,128,512]{2,1,0:T(8,128)(2,1)S(1)}, u32[]{:S(2)}, u32[]{:S(2)}) collective-permute-start(bf16[4,128,512]{2,1,0:T(8,128)(2,1)} %get-tuple-element.35), channel_id=1, source_target_pairs={{0,1},{1,0},{2,3},{3,2},{4,5},{5,4},{6,7},{7,6},{8,9},{9,8},{10,11... | collective-permute-start | bytes 1572872 | tf_op jit(solution)/shard_map/ppermute | solution.py:358
  85.2 0.8 copy-start.1
  86.0 1.0 copy-start
  87.0 1.0 copy-start.2
  88.8 12.8 %collective-permute-start.1 = (bf16[256,512]{1,0:T(8,128)(2,1)}, bf16[256,512]{1,0:T(8,128)(2,1)S(1)}, u32[]{:S(2)}, u32[]{:S(2)}) collective-permute-start(bf16[256,512]{1,0:T(8,128)(2,1)} %get-tuple-element.37), channel_id=1, source_target_pairs={{0,2},{1,3},{2,0},{3,1},{4,6},{5,7},{6,4},{7,5},{8,10},{9,11},{10,... | collective-permute-start | bytes 786440 | tf_op jit(solution)/shard_map/ppermute | solution.py:358
  102.3 6.9 %collective-permute-start.2 = (bf16[64,512]{1,0:T(8,128)(2,1)}, bf16[64,512]{1,0:T(8,128)(2,1)S(1)}, u32[]{:S(2)}, u32[]{:S(2)}) collective-permute-start(bf16[64,512]{1,0:T(8,128)(2,1)} %get-tuple-element.39), channel_id=1, source_target_pairs={{0,4},{1,5},{2,6},{3,7},{4,0},{5,1},{6,2},{7,3},{8,12},{9,13},{10,... | collective-permute-start | bytes 196616 | tf_op jit(solution)/shard_map/ppermute | solution.py:358
  105.6 8.7 %collective-permute-start.3 = (bf16[64,512]{1,0:T(8,128)(2,1)}, bf16[64,512]{1,0:T(8,128)(2,1)S(1)}, u32[]{:S(2)}, u32[]{:S(2)}) collective-permute-start(bf16[64,512]{1,0:T(8,128)(2,1)} %get-tuple-element.40), channel_id=1, source_target_pairs={{0,8},{1,9},{2,10},{3,11},{4,12},{5,13},{6,14},{7,15},{8,0},{9,1},... | collective-permute-start | bytes 196616 | tf_op jit(solution)/shard_map/ppermute | solution.py:358
  106.2 8.1 %collective-permute-start.4 = (bf16[64,512]{1,0:T(8,128)(2,1)}, bf16[64,512]{1,0:T(8,128)(2,1)S(1)}, u32[]{:S(2)}, u32[]{:S(2)}) collective-permute-start(bf16[64,512]{1,0:T(8,128)(2,1)} %get-tuple-element.41), channel_id=1, source_target_pairs={{0,12},{1,13},{2,14},{3,15},{4,8},{5,9},{6,10},{7,11},{8,4},{9,5},... | collective-permute-start | bytes 196616 | tf_op jit(solution)/shard_map/ppermute | solution.py:358
  114.3 8.8 %collective-permute-start.5 = (bf16[64,512]{1,0:T(8,128)(2,1)S(1)}, bf16[64,512]{1,0:T(8,128)(2,1)S(1)}, u32[]{:S(2)}, u32[]{:S(2)}) collective-permute-start(bf16[64,512]{1,0:T(8,128)(2,1)S(1)} %add_convert_fusion), channel_id=1, source_target_pairs={{0,4},{1,5},{2,6},{3,7},{4,0},{5,1},{6,2},{7,3},{8,12},{9,13},{10,... | collective-permute-start | bytes 196616 | tf_op jit(solution)/shard_map/ppermute | solution.py:358
  115.8 7.6 %collective-permute-start.6 = (bf16[64,512]{1,0:T(8,128)(2,1)S(1)}, bf16[64,512]{1,0:T(8,128)(2,1)S(1)}, u32[]{:S(2)}, u32[]{:S(2)}) collective-permute-start(bf16[64,512]{1,0:T(8,128)(2,1)S(1)} %add_convert_fusion), channel_id=1, source_target_pairs={{0,8},{1,9},{2,10},{3,11},{4,12},{5,13},{6,14},{7,15},{8,0},{9,1},... | collective-permute-start | bytes 196616 | tf_op jit(solution)/shard_map/ppermute | solution.py:358
  116.5 6.9 %collective-permute-start.7 = (bf16[64,512]{1,0:T(8,128)(2,1)S(1)}, bf16[64,512]{1,0:T(8,128)(2,1)S(1)}, u32[]{:S(2)}, u32[]{:S(2)}) collective-permute-start(bf16[64,512]{1,0:T(8,128)(2,1)S(1)} %add_convert_fusion), channel_id=1, source_target_pairs={{0,12},{1,13},{2,14},{3,15},{4,8},{5,9},{6,10},{7,11},{8,4},{9,5},... | collective-permute-start | bytes 196616 | tf_op jit(solution)/shard_map/ppermute | solution.py:358
  118.7 27.3 %all-to-all-start.3 = ((bf16[16,64,512]{2,1,0:T(8,128)(2,1)}), bf16[16,64,512]{2,1,0:T(8,128)(2,1)}, u32[]{:S(2)}, u32[]{:S(2)}) async-start(bf16[16,64,512]{2,1,0:T(8,128)(2,1)} %mix_second_back.1), calls=%async_computation.3 | async-start | bytes 2097152 | tf_op jit(solution)/shard_map/all_to_all | solution.py:449
  123.5 16.6 %collective-permute-start.8 = (bf16[256,512]{1,0:T(8,128)(2,1)S(1)}, bf16[256,512]{1,0:T(8,128)(2,1)S(1)}, u32[]{:S(2)}, u32[]{:S(2)}) collective-permute-start(bf16[256,512]{1,0:T(8,128)(2,1)S(1)} %bitcast.39), channel_id=1, source_target_pairs={{0,2},{1,3},{2,0},{3,1},{4,6},{5,7},{6,4},{7,5},{8,10},{9,11},{10,... | collective-permute-start | bytes 786440 | tf_op jit(solution)/shard_map/ppermute | solution.py:358
  140.2 2.0 %collective-permute-start.9 = (bf16[512,512]{1,0:T(8,128)(2,1)S(1)}, bf16[512,512]{1,0:T(8,128)(2,1)S(1)}, u32[]{:S(2)}, u32[]{:S(2)}) collective-permute-start(bf16[512,512]{1,0:T(8,128)(2,1)S(1)} %pad_maximum_fusion.1), channel_id=1, source_target_pairs={{0,1},{1,0},{2,3},{3,2},{4,5},{5,4},{6,7},{7,6},{8,9},{9,8},{10,11... | collective-permute-start | bytes 1572872 | tf_op jit(solution)/shard_map/ppermute | solution.py:358

commit v10 on v9

--- a/solution.py
+++ b/solution.py
@@ -58,12 +58,10 @@
         xs = row_copies(x_hbm, x_all, sems, 0, tiles)
         fs = row_copies(f_hbm, f_all, sems, tiles, tiles)
         us = row_copies(u_all, u_hbm, sems, 2 * tiles, tiles)
-        for c in xs + fs[:1]:
+        for c in xs + fs:
             c.start()
         for c in xs:
             c.wait()
-        for c in fs[1:]:
-            c.start()
         for t in range(tiles):
             fs[t].wait()
             at = slice(t * step, (t + 1) * step)
@@ -226,19 +224,19 @@
             g_parts = [g[:, b * width : (b + 1) * width] for b in range(groups)]
             acts, slopes, back = [], [], []
             for b in range(groups):
-                a = dot(h_parts[b], up_ref[b], 1, 0)
+                a = dot(h_parts[b], up_ref[b], 1, 0).astype(BF)
                 s = sigmoid(a)
                 q = a * s
-                acts.append(q.astype(BF))
-                slopes.append(s + q * (1.0 - s))
-                back.append(dot(g_parts[b], down_ref[b], 1, 1))
+                acts.append(q)
+                slopes.append(s + q * (1 - s))
+                back.append(dot(g_parts[b], down_ref[b], 1, 1).astype(BF))
             grads = []
             for b in range(groups):
                 lanes = slice(b * sub, (b + 1) * sub)
                 perm = jnp.concatenate([acts[p][:, lanes] for p in range(groups)], axis=1)
                 w[1, b] += dot(g_parts[b], perm, 0, 0)
                 dq = jnp.concatenate([back[p][:, lanes] for p in range(groups)], axis=1)
-                da = (dq * slopes[b]).astype(BF)
+                da = dq * slopes[b]
                 w[0, b] += dot(h_parts[b], da, 0, 0)
                 grads.append(dot(da, up_ref[b], 1, 1))
             dh = (g.astype(F32) + jnp.concatenate(grads, axis=1)).astype(BF).astype(F32)
@@ -303,15 +301,13 @@
         rs = row_copies(r_hbm, r, sems, 3 * tiles, tiles)
         ones = row_copies(one, one_hbm, sems, 4 * tiles, tiles)
         outs = row_copies(out, out_hbm, sems, 5 * tiles, tiles)
-        for c in xs + ds:
+        for c in xs + ds + fs + rs:
             c.start()
         for c in xs:
             c.wait()
         for t in range(tiles):
             at = slice(t * step, (t + 1) * step)
             ds[t].wait()
-            fs[t].start()
-            rs[t].start()
             one[at, :] = dot(d[at, :], x[...], 1, 1) * scale
             ones[t].start()
         for c in fs:
@@ -362,30 +358,43 @@
     rows, columns = terms[0].shape
     share = rows // radix
 
+    number = len(terms)
+
+    number = len(terms)
+    shape = (radix, share, columns)
+
     def body(digit_ref, *refs):
-        ins, kept_ref, outs = refs[: len(terms)], refs[len(terms)], refs[len(terms) + 1 :]
-
-        def part(s):
-            at = pl.ds(pl.multiple_of((digit_ref[0] ^ s) * share, share), share)
-            total = ins[0][at, :].astype(F32)
-            for ref in ins[1:]:
-                total = total + ref[at, :].astype(F32)
-            return total
-
-        kept_ref[...] = part(0)
-        for s, ref in enumerate(outs):
-            ref[...] = part(s + 1).astype(BF)
-
-    return pl.pallas_call(
-        body,
-        in_specs=[SCALAR] + [VMEM] * len(terms),
-        out_specs=[VMEM] * radix,
-        out_shape=[jax.ShapeDtypeStruct((share, columns), F32)]
-        + [jax.ShapeDtypeStruct((share, columns), BF)] * (radix - 1),
-        compiler_params=pltpu.CompilerParams(vmem_limit_bytes=16 * 1024 * 1024),
+        ins, outs = refs[:number], refs[number : number + radix]
+        held, made, sems = refs[number + radix : -radix - 1], refs[-radix - 1 : -1], refs[-1]
+        copies = [pltpu.make_async_copy(ins[i], held[i], sems.at[i]) for i in range(number)]
+        for c in copies:
+            c.start()
+        for c in copies:
+            c.wait()
+        copies = []
+        for s, ref in enumerate(made):
+            total = held[0][digit_ref[0] ^ s].astype(F32)
+            for term in held[1:]:
+                total = total + term[digit_ref[0] ^ s].astype(F32)
+            ref[...] = total.astype(ref.dtype)
+            copies.append(pltpu.make_async_copy(ref, outs[s], sems.at[number + s]))
+            copies[-1].start()
+        for c in copies:
+            c.wait()
+
+    types = [F32] + [BF] * (radix - 1)
+    return pl.pallas_call(
+        body,
+        in_specs=[SCALAR] + [ANY] * number,
+        out_specs=[ANY] * radix,
+        out_shape=[pltpu.HBM((share, columns), t) for t in types],
+        scratch_shapes=[pltpu.VMEM(shape, t.dtype) for t in terms]
+        + [pltpu.VMEM((share, columns), t) for t in types]
+        + [pltpu.SemaphoreType.DMA((number + radix,))],
+        compiler_params=params(0),
         cost_estimate=cost(rows * columns, 8 * rows * columns),
         name="add_and_cut",
-    )(digit.reshape(1), *terms)
+    )(digit.reshape(1), *[t.reshape(shape) for t in terms])
 
 
 def scatter_step(terms, count, stride, radix):

time: 156 us -> 152 us (0.974)
  local copies, waits for them, and re-layouts: 4.46 us -> 2.64 us
  Pallas kernels: 29.7 us -> 27.9 us
    unnamed x8, local copies, waits for them, and re-layouts: 2.88 us -> 1.06 us
    pallas_call x1, Pallas kernels: 7.66 us -> 5.99 us  [finish(): pl.pallas_call(body, in_specs=[ANY] * 4, out_specs=[ANY] * 2, out_shape=[...]
  transfers between devices with their start and end apart: 14 -> 14, of which waited for: 9 -> 9; matrix products, arithmetic and copies ran while one was open for 1% -> 1% of each run, Pallas kernels for 4% -> 5%
where the time goes in v10:
time: 152 us; the launch traced here: 151 us
  waiting for transfers between devices  80.3 us (53%)
  starting transfers between devices  38.6 us (25%)
  Pallas kernels  27.9 us (18%)
  local copies, waits for them, and re-layouts  2.64 us (2%)
    all_to_all x4, waiting for transfers between devices, exchange(): return lax.all_to_all(cut, 'seq', split_axis=0, concat_axis=0, tiled=True)  46.6 us
    ppermute x10, waiting for transfers between devices, swap(): lax.ppermute(values, 'seq', [(i, i ^ stride * s) for i in range(count)])  33.8 us
    all_to_all x4, starting transfers between devices, exchange(): return lax.all_to_all(cut, 'seq', split_axis=0, concat_axis=0, tiled=True)  25.7 us
    ppermute x10, starting transfers between devices, swap(): lax.ppermute(values, 'seq', [(i, i ^ stride * s) for i in range(count)])  12.9 us
    pallas_call x1, Pallas kernels, middle(): pl.pallas_call(body, in_specs=[SCALAR, ANY, ANY, VMEM, ANY, ANY], out_spe...  8.52 us
    pallas_call x1, Pallas kernels, finish(): pl.pallas_call(body, in_specs=[ANY] * 4, out_specs=[ANY] * 2, out_shape=[...  5.99 us
    pallas_call x1, Pallas kernels, mix_first(): pl.pallas_call(body, in_specs=[ANY, ANY], out_specs=ANY, out_shape=pltpu....  3.92 us
  transfers between devices with their start and end apart: 14, of which 9 were waited for; matrix products, arithmetic and copies ran while one was open for 1% of the time, Pallas kernels for 5%

profile of v10, /device:TPU:0, one launch (start us, length us, event | category | flops | bytes accessed | tf_op | source)
XLA Modules:
  0.0 150.6 jit_solution(3702767098924186153)
XLA Ops:
  0.6 3.9 %mix_first.1 = bf16[1024,512]{1,0:T(8,128)(2,1)} custom-call(bf16[1024,1024]{1,0:T(8,128)(2,1)} %bitcast.39, bf16[1024,512]{1,0:T(8,128)(2,1)} %x_hbm.5), custom_call_target="tpu_custom_call" | custom-call | flops 1073741824 | bytes 4194304 | tf_op jit(solution)/shard_map/mix_first/pallas_call | solution.py:73
  4.6 0.0 copy-start.3
  4.6 7.5 %all-to-all-start = ((bf16[16,64,512]{2,1,0:T(8,128)(2,1)}), bf16[16,64,512]{2,1,0:T(8,128)(2,1)S(1)}, u32[]{:S(2)}, u32[]{:S(2)}) async-start(bf16[16,64,512]{2,1,0:T(8,128)(2,1)} %bitcast.38), calls=%async_computation | async-start | bytes 2097152 | tf_op jit(solution)/shard_map/all_to_all | solution.py:458
  12.1 0.2 reshape.62
  12.3 0.2 copy.11
  12.5 0.7 spread_factor.1.m_ref
  13.2 21.9 %all-to-all-done.in_ref.u_ref = bf16[16,64,512]{2,1,0:T(8,128)(2,1)S(1)} async-done(((bf16[16,64,512]{2,1,0:T(8,128)(2,1)}), bf16[16,64,512]{2,1,0:T(8,128)(2,1)S(1)}, u32[]{:S(2)}, u32[]{:S(2)}) %all-to-all-start) | async-done | bytes 1048608 | tf_op jit(solution)/shard_map/all_to_all | solution.py:458
  35.0 1.2 mix_second.1
  36.3 6.9 %all-to-all-start.1 = ((bf16[16,64,512]{2,1,0:T(8,128)(2,1)}), bf16[16,64,512]{2,1,0:T(8,128)(2,1)S(1)}, u32[]{:S(2)}, u32[]{:S(2)}) async-start(bf16[16,64,512]{2,1,0:T(8,128)(2,1)} %mix_second.1), calls=%async_computation.1 | async-start | bytes 2097152 | tf_op jit(solution)/shard_map/all_to_all | solution.py:458
  43.2 22.9 %all-to-all-done.1 = bf16[16,64,512]{2,1,0:T(8,128)(2,1)S(1)} async-done(((bf16[16,64,512]{2,1,0:T(8,128)(2,1)}), bf16[16,64,512]{2,1,0:T(8,128)(2,1)S(1)}, u32[]{:S(2)}, u32[]{:S(2)}) %all-to-all-start.1) | async-done | bytes 1048608 | tf_op jit(solution)/shard_map/all_to_all | solution.py:458
  66.1 8.5 %middle.1 = (bf16[1024,512]{1,0:T(8,128)(2,1)}, bf16[1024,512]{1,0:T(8,128)(2,1)}, bf16[4,128,512]{2,1,0:T(8,128)(2,1)}, bf16[4,128,512]{2,1,0:T(8,128)(2,1)}) custom-call(s32[1]{0:T(128)} %bitcast.3.half_ref, bf16[1024,512]{1,0:T(8,128)(2,1)} %x_hbm.5, bf16[1024,512]{1,0:T(8,128)(2,1)} %g_hbm.1, bf16[1024,512]{1,0:T(8,128)(2,1)S(1)} %bitcast.34, ...), custom_call_target="tpu_custom_call" | custom-call | flops 2684354560 | bytes 7340032 | tf_op jit(solution)/shard_map/middle/pallas_call | solution.py:263
  74.6 0.0 copy-start.1
  74.6 7.0 %all-to-all-start.2 = ((bf16[16,64,512]{2,1,0:T(8,128)(2,1)}), bf16[16,64,512]{2,1,0:T(8,128)(2,1)S(1)}, u32[]{:S(2)}, u32[]{:S(2)}) async-start(bf16[16,64,512]{2,1,0:T(8,128)(2,1)} %bitcast.41), calls=%async_computation.2 | async-start | bytes 2097152 | tf_op jit(solution)/shard_map/all_to_all | solution.py:458
  81.6 0.4 collective-permute-start
  82.0 1.9 %collective-permute-done = bf16[4,128,512]{2,1,0:T(8,128)(2,1)} collective-permute-done((bf16[4,128,512]{2,1,0:T(8,128)(2,1)}, bf16[4,128,512]{2,1,0:T(8,128)(2,1)}, u32[]{:S(2)}, u32[]{:S(2)}) %collective-permute-start) | collective-permute-done | bytes 524320 | tf_op jit(solution)/shard_map/ppermute | solution.py:354
  83.9 2.0 %add_and_cut.2 = (f32[256,512]{1,0:T(8,128)}, bf16[256,512]{1,0:T(8,128)(2,1)}) custom-call(s32[1]{0:T(128)} %bitcast.2.digit_ref, bf16[2,256,512]{2,1,0:T(8,128)(2,1)S(1)} %bitcast.36, bf16[2,256,512]{2,1,0:T(8,128)(2,1)} %bitcast.9.refs_1_), custom_call_target="tpu_custom_call" | custom-call | flops 262144 | bytes 2097152 | tf_op jit(solution)/shard_map/add_and_cut/pallas_call | solution.py:386
  86.0 1.9 %collective-permute-start.1 = (bf16[256,512]{1,0:T(8,128)(2,1)}, bf16[256,512]{1,0:T(8,128)(2,1)S(1)}, u32[]{:S(2)}, u32[]{:S(2)}) collective-permute-start(bf16[256,512]{1,0:T(8,128)(2,1)} %get-tuple-element.37), channel_id=1, source_target_pairs={{0,2},{1,3},{2,0},{3,1},{4,6},{5,7},{6,4},{7,5},{8,10},{9,11},{10,... | collective-permute-start | bytes 786440 | tf_op jit(solution)/shard_map/ppermute | solution.py:354
  87.9 12.0 %collective-permute-done.1 = bf16[256,512]{1,0:T(8,128)(2,1)S(1)} collective-permute-done((bf16[256,512]{1,0:T(8,128)(2,1)}, bf16[256,512]{1,0:T(8,128)(2,1)S(1)}, u32[]{:S(2)}, u32[]{:S(2)}) %collective-permute-start.1) | collective-permute-done | bytes 262176 | tf_op jit(solution)/shard_map/ppermute | solution.py:354
  99.9 1.0 copy-done
  100.9 0.8 add_and_cut.3
  101.8 0.0 copy-start.2
  101.8 0.8 collective-permute-start.2
  102.6 3.4 %collective-permute-start.3 = (bf16[64,512]{1,0:T(8,128)(2,1)}, bf16[64,512]{1,0:T(8,128)(2,1)S(1)}, u32[]{:S(2)}, u32[]{:S(2)}) collective-permute-start(bf16[64,512]{1,0:T(8,128)(2,1)} %get-tuple-element.40), channel_id=1, source_target_pairs={{0,8},{1,9},{2,10},{3,11},{4,12},{5,13},{6,14},{7,15},{8,0},{9,1},... | collective-permute-start | bytes 196616 | tf_op jit(solution)/shard_map/ppermute | solution.py:354
  106.0 0.2 collective-permute-start.4
  106.2 0.0 all-to-all-done.2.in_ref.g_ref
  106.2 1.3 mix_second_back.1
  107.5 0.0 collective-permute-done.2
  107.5 5.3 %collective-permute-done.3 = bf16[64,512]{1,0:T(8,128)(2,1)S(1)} collective-permute-done((bf16[64,512]{1,0:T(8,128)(2,1)}, bf16[64,512]{1,0:T(8,128)(2,1)S(1)}, u32[]{:S(2)}, u32[]{:S(2)}) %collective-permute-start.3) | collective-permute-done | bytes 65568 | tf_op jit(solution)/shard_map/ppermute | solution.py:354
  112.9 0.0 collective-permute-done.4
  112.9 1.6 %collective-permute-start.5 = (bf16[64,512]{1,0:T(8,128)(2,1)S(1)}, bf16[64,512]{1,0:T(8,128)(2,1)S(1)}, u32[]{:S(2)}, u32[]{:S(2)}) collective-permute-start(bf16[64,512]{1,0:T(8,128)(2,1)S(1)} %add_convert_fusion), channel_id=1, source_target_pairs={{0,4},{1,5},{2,6},{3,7},{4,0},{5,1},{6,2},{7,3},{8,12},{9,13},{10,... | collective-permute-start | bytes 196616 | tf_op jit(solution)/shard_map/ppermute | solution.py:354
  114.5 0.7 collective-permute-start.6
  115.1 2.2 %collective-permute-start.7 = (bf16[64,512]{1,0:T(8,128)(2,1)S(1)}, bf16[64,512]{1,0:T(8,128)(2,1)S(1)}, u32[]{:S(2)}, u32[]{:S(2)}) collective-permute-start(bf16[64,512]{1,0:T(8,128)(2,1)S(1)} %add_convert_fusion), channel_id=1, source_target_pairs={{0,12},{1,13},{2,14},{3,15},{4,8},{5,9},{6,10},{7,11},{8,4},{9,5},... | collective-permute-start | bytes 196616 | tf_op jit(solution)/shard_map/ppermute | solution.py:354
  117.4 4.3 %all-to-all-start.3 = ((bf16[16,64,512]{2,1,0:T(8,128)(2,1)}), bf16[16,64,512]{2,1,0:T(8,128)(2,1)}, u32[]{:S(2)}, u32[]{:S(2)}) async-start(bf16[16,64,512]{2,1,0:T(8,128)(2,1)} %mix_second_back.1), calls=%async_computation.3 | async-start | bytes 2097152 | tf_op jit(solution)/shard_map/all_to_all | solution.py:458
  121.7 0.0 collective-permute-done.5
  121.7 0.3 collective-permute-done.6
  122.0 0.0 collective-permute-done.7
  122.1 1.5 %collective-permute-start.8 = (bf16[256,512]{1,0:T(8,128)(2,1)S(1)}, bf16[256,512]{1,0:T(8,128)(2,1)S(1)}, u32[]{:S(2)}, u32[]{:S(2)}) collective-permute-start(bf16[256,512]{1,0:T(8,128)(2,1)S(1)} %bitcast.42), channel_id=1, source_target_pairs={{0,2},{1,3},{2,0},{3,1},{4,6},{5,7},{6,4},{7,5},{8,10},{9,11},{10,... | collective-permute-start | bytes 786440 | tf_op jit(solution)/shard_map/ppermute | solution.py:354
  123.7 1.5 grad_second.1
  125.2 0.2 copy.12
  125.4 0.9 reshape.72
  126.3 12.4 %collective-permute-done.8 = bf16[256,512]{1,0:T(8,128)(2,1)S(1)} collective-permute-done((bf16[256,512]{1,0:T(8,128)(2,1)S(1)}, bf16[256,512]{1,0:T(8,128)(2,1)S(1)}, u32[]{:S(2)}, u32[]{:S(2)}) %collective-permute-start.8) | collective-permute-done | bytes 262176 | tf_op jit(solution)/shard_map/ppermute | solution.py:354
  138.8 0.1 collective-permute-start.9
  138.9 1.9 %collective-permute-done.9 = bf16[512,512]{1,0:T(8,128)(2,1)S(1)} collective-permute-done((bf16[512,512]{1,0:T(8,128)(2,1)S(1)}, bf16[512,512]{1,0:T(8,128)(2,1)S(1)}, u32[]{:S(2)}, u32[]{:S(2)}) %collective-permute-start.9) | collective-permute-done | bytes 524320 | tf_op jit(solution)/shard_map/ppermute | solution.py:354
  140.8 0.1 broadcast_select_fusion.1
  140.8 0.1 pad_maximum_fusion.up_in.down_in
  140.9 1.9 %write_weights.1 = (f32[4,128,512]{2,1,0:T(8,128)}, f32[4,512,128]{2,1,0:T(8,128)}) custom-call(bf16[1024,512]{1,0:T(8,128)(2,1)S(1)} %pad_maximum_fusion.up_in.down_in, bf16[1024,512]{1,0:T(8,128)(2,1)S(1)} %pad_maximum_fusion.up_in.down_in), custom_call_target="tpu_custom_call" | custom-call | flops 262144 | bytes 3145728 | tf_op jit(solution)/shard_map/write_weights/pallas_call | solution.py:427
  142.9 1.8 %all-to-all-done.3 = bf16[16,64,512]{2,1,0:T(8,128)(2,1)} async-done(((bf16[16,64,512]{2,1,0:T(8,128)(2,1)}), bf16[16,64,512]{2,1,0:T(8,128)(2,1)}, u32[]{:S(2)}, u32[]{:S(2)}) %all-to-all-start.3) | async-done | bytes 1048608 | tf_op jit(solution)/shard_map/all_to_all | solution.py:458
  144.6 6.0 %finish.1 = (f32[1024,1024]{1,0:T(8,128)}, bf16[1024,512]{1,0:T(8,128)(2,1)}) custom-call(bf16[1024,1024]{1,0:T(8,128)(2,1)} %bitcast.40, bf16[1024,512]{1,0:T(8,128)(2,1)} %bitcast.13.d_hbm, bf16[1024,512]{1,0:T(8,128)(2,1)} %x_hbm.5, bf16[1024,512]{1,0:T(8,128)(2,1)} %get-tuple-element.49.r_hbm), custom_call_target="tpu_custom_call" | custom-call | flops 2147483648 | bytes 10485760 | tf_op jit(solution)/shard_map/finish/pallas_call | solution.py:324
  (12 shorter events, 0.2 us)
Async XLA Ops:
  4.6 7.5 %copy-start.3 = (bf16[64,16,16]{0,2,1:T(8,128)(2,1)S(1)}, bf16[64,16,16]{0,2,1:T(8,128)(2,1)}, u32[]{:S(2)}) copy-start(bf16[64,16,16]{0,2,1:T(8,128)(2,1)} %param.9) | copy-start | bytes 98308
  4.6 30.5 %all-to-all-start = ((bf16[16,64,512]{2,1,0:T(8,128)(2,1)}), bf16[16,64,512]{2,1,0:T(8,128)(2,1)S(1)}, u32[]{:S(2)}, u32[]{:S(2)}) async-start(bf16[16,64,512]{2,1,0:T(8,128)(2,1)} %bitcast.38), calls=%async_computation | async-start | bytes 2097152 | tf_op jit(solution)/shard_map/all_to_all | solution.py:458
  36.3 29.8 %all-to-all-start.1 = ((bf16[16,64,512]{2,1,0:T(8,128)(2,1)}), bf16[16,64,512]{2,1,0:T(8,128)(2,1)S(1)}, u32[]{:S(2)}, u32[]{:S(2)}) async-start(bf16[16,64,512]{2,1,0:T(8,128)(2,1)} %mix_second.1), calls=%async_computation.1 | async-start | bytes 2097152 | tf_op jit(solution)/shard_map/all_to_all | solution.py:458
  74.6 9.3 %copy-start.1 = (bf16[4,128,512]{2,1,0:T(8,128)(2,1)S(1)}, bf16[4,128,512]{2,1,0:T(8,128)(2,1)}, u32[]{:S(2)}) copy-start(bf16[4,128,512]{2,1,0:T(8,128)(2,1)} %get-tuple-element.34) | copy-start | bytes 1572868
  74.6 31.6 %all-to-all-start.2 = ((bf16[16,64,512]{2,1,0:T(8,128)(2,1)}), bf16[16,64,512]{2,1,0:T(8,128)(2,1)S(1)}, u32[]{:S(2)}, u32[]{:S(2)}) async-start(bf16[16,64,512]{2,1,0:T(8,128)(2,1)} %bitcast.41), calls=%async_computation.2 | async-start | bytes 2097152 | tf_op jit(solution)/shard_map/all_to_all | solution.py:458
  81.6 2.3 %collective-permute-start = (bf16[4,128,512]{2,1,0:T(8,128)(2,1)}, bf16[4,128,512]{2,1,0:T(8,128)(2,1)}, u32[]{:S(2)}, u32[]{:S(2)}) collective-permute-start(bf16[4,128,512]{2,1,0:T(8,128)(2,1)} %get-tuple-element.35), channel_id=1, source_target_pairs={{0,1},{1,0},{2,3},{3,2},{4,5},{5,4},{6,7},{7,6},{8,9},{9,8},{10,11... | collective-permute-start | bytes 1572872 | tf_op jit(solution)/shard_map/ppermute | solution.py:354
  86.0 13.9 %collective-permute-start.1 = (bf16[256,512]{1,0:T(8,128)(2,1)}, bf16[256,512]{1,0:T(8,128)(2,1)S(1)}, u32[]{:S(2)}, u32[]{:S(2)}) collective-permute-start(bf16[256,512]{1,0:T(8,128)(2,1)} %get-tuple-element.37), channel_id=1, source_target_pairs={{0,2},{1,3},{2,0},{3,1},{4,6},{5,7},{6,4},{7,5},{8,10},{9,11},{10,... | collective-permute-start | bytes 786440 | tf_op jit(solution)/shard_map/ppermute | solution.py:354
  99.9 1.0 copy-start
  101.8 11.1 %copy-start.2 = (f32[64,512]{1,0:T(8,128)S(1)}, f32[64,512]{1,0:T(8,128)}, u32[]{:S(2)}) copy-start(f32[64,512]{1,0:T(8,128)} %get-tuple-element.44) | copy-start | bytes 393220
  101.8 5.7 %collective-permute-start.2 = (bf16[64,512]{1,0:T(8,128)(2,1)}, bf16[64,512]{1,0:T(8,128)(2,1)S(1)}, u32[]{:S(2)}, u32[]{:S(2)}) collective-permute-start(bf16[64,512]{1,0:T(8,128)(2,1)} %get-tuple-element.39), channel_id=1, source_target_pairs={{0,4},{1,5},{2,6},{3,7},{4,0},{5,1},{6,2},{7,3},{8,12},{9,13},{10,... | collective-permute-start | bytes 196616 | tf_op jit(solution)/shard_map/ppermute | solution.py:354
  102.6 10.3 %collective-permute-start.3 = (bf16[64,512]{1,0:T(8,128)(2,1)}, bf16[64,512]{1,0:T(8,128)(2,1)S(1)}, u32[]{:S(2)}, u32[]{:S(2)}) collective-permute-start(bf16[64,512]{1,0:T(8,128)(2,1)} %get-tuple-element.40), channel_id=1, source_target_pairs={{0,8},{1,9},{2,10},{3,11},{4,12},{5,13},{6,14},{7,15},{8,0},{9,1},... | collective-permute-start | bytes 196616 | tf_op jit(solution)/shard_map/ppermute | solution.py:354
  106.0 6.9 %collective-permute-start.4 = (bf16[64,512]{1,0:T(8,128)(2,1)}, bf16[64,512]{1,0:T(8,128)(2,1)S(1)}, u32[]{:S(2)}, u32[]{:S(2)}) collective-permute-start(bf16[64,512]{1,0:T(8,128)(2,1)} %get-tuple-element.41), channel_id=1, source_target_pairs={{0,12},{1,13},{2,14},{3,15},{4,8},{5,9},{6,10},{7,11},{8,4},{9,5},... | collective-permute-start | bytes 196616 | tf_op jit(solution)/shard_map/ppermute | solution.py:354
  112.9 8.8 %collective-permute-start.5 = (bf16[64,512]{1,0:T(8,128)(2,1)S(1)}, bf16[64,512]{1,0:T(8,128)(2,1)S(1)}, u32[]{:S(2)}, u32[]{:S(2)}) collective-permute-start(bf16[64,512]{1,0:T(8,128)(2,1)S(1)} %add_convert_fusion), channel_id=1, source_target_pairs={{0,4},{1,5},{2,6},{3,7},{4,0},{5,1},{6,2},{7,3},{8,12},{9,13},{10,... | collective-permute-start | bytes 196616 | tf_op jit(solution)/shard_map/ppermute | solution.py:354
  114.5 7.6 %collective-permute-start.6 = (bf16[64,512]{1,0:T(8,128)(2,1)S(1)}, bf16[64,512]{1,0:T(8,128)(2,1)S(1)}, u32[]{:S(2)}, u32[]{:S(2)}) collective-permute-start(bf16[64,512]{1,0:T(8,128)(2,1)S(1)} %add_convert_fusion), channel_id=1, source_target_pairs={{0,8},{1,9},{2,10},{3,11},{4,12},{5,13},{6,14},{7,15},{8,0},{9,1},... | collective-permute-start | bytes 196616 | tf_op jit(solution)/shard_map/ppermute | solution.py:354
  115.1 6.9 %collective-permute-start.7 = (bf16[64,512]{1,0:T(8,128)(2,1)S(1)}, bf16[64,512]{1,0:T(8,128)(2,1)S(1)}, u32[]{:S(2)}, u32[]{:S(2)}) collective-permute-start(bf16[64,512]{1,0:T(8,128)(2,1)S(1)} %add_convert_fusion), channel_id=1, source_target_pairs={{0,12},{1,13},{2,14},{3,15},{4,8},{5,9},{6,10},{7,11},{8,4},{9,5},... | collective-permute-start | bytes 196616 | tf_op jit(solution)/shard_map/ppermute | solution.py:354
  117.4 27.3 %all-to-all-start.3 = ((bf16[16,64,512]{2,1,0:T(8,128)(2,1)}), bf16[16,64,512]{2,1,0:T(8,128)(2,1)}, u32[]{:S(2)}, u32[]{:S(2)}) async-start(bf16[16,64,512]{2,1,0:T(8,128)(2,1)} %mix_second_back.1), calls=%async_computation.3 | async-start | bytes 2097152 | tf_op jit(solution)/shard_map/all_to_all | solution.py:458
  122.1 16.6 %collective-permute-start.8 = (bf16[256,512]{1,0:T(8,128)(2,1)S(1)}, bf16[256,512]{1,0:T(8,128)(2,1)S(1)}, u32[]{:S(2)}, u32[]{:S(2)}) collective-permute-start(bf16[256,512]{1,0:T(8,128)(2,1)S(1)} %bitcast.42), channel_id=1, source_target_pairs={{0,2},{1,3},{2,0},{3,1},{4,6},{5,7},{6,4},{7,5},{8,10},{9,11},{10,... | collective-permute-start | bytes 786440 | tf_op jit(solution)/shard_map/ppermute | solution.py:354
  138.8 2.0 %collective-permute-start.9 = (bf16[512,512]{1,0:T(8,128)(2,1)S(1)}, bf16[512,512]{1,0:T(8,128)(2,1)S(1)}, u32[]{:S(2)}, u32[]{:S(2)}) collective-permute-start(bf16[512,512]{1,0:T(8,128)(2,1)S(1)} %pad_maximum_fusion.1), channel_id=1, source_target_pairs={{0,1},{1,0},{2,3},{3,2},{4,5},{5,4},{6,7},{7,6},{8,9},{9,8},{10,11... | collective-permute-start | bytes 1572872 | tf_op jit(solution)/shard_map/ppermute | solution.py:354

commit v11 on v10

--- a/solution.py
+++ b/solution.py
@@ -183,7 +183,7 @@
     groups, width, inner = up_blocks.shape
     sub = inner // groups
     rows, channels = blocked.shape
-    step = min(256, rows)
+    step = min(512, rows)
     tiles = rows // step
 
     def body(half_ref, x_hbm, g_hbm, v_ref, up_hbm, down_hbm, *refs):
@@ -207,8 +207,6 @@
             rows_copy(x_hbm, x_ref, 0, t).start()
             rows_copy(g_hbm, g_ref, 1, t).start()
         w[...] = jnp.zeros_like(w)
-        fetch_up.wait()
-        fetch_down.wait()
 
         def tile(t, carry):
             rows_copy(x_hbm, x_ref, 0, t).wait()
@@ -222,6 +220,12 @@
             h = (x + v * gate).astype(BF)
             h_parts = [h[:, b * width : (b + 1) * width] for b in range(groups)]
             g_parts = [g[:, b * width : (b + 1) * width] for b in range(groups)]
+
+            @pl.when(t == 0)
+            def _():
+                fetch_up.wait()
+                fetch_down.wait()
+
             acts, slopes, back = [], [], []
             for b in range(groups):
                 a = dot(h_parts[b], up_ref[b], 1, 0).astype(BF)
@@ -289,29 +293,48 @@
     )(half, in_hbm(blocked), in_hbm(incoming), in_vmem(mixed), in_hbm(up_blocks), in_hbm(down_blocks))
 
 
+def bring(arrays, name):
+    number = len(arrays)
+
+    def body(*refs):
+        sems = refs[-1]
+        copies = [
+            pltpu.make_async_copy(refs[i], refs[number + i], sems.at[i]) for i in range(number)
+        ]
+        for c in copies:
+            c.start()
+        for c in copies:
+            c.wait()
+
+    return pl.pallas_call(
+        body,
+        in_specs=[ANY] * number,
+        out_specs=[pl.BlockSpec(memory_space=pltpu.VMEM)] * number,
+        out_shape=[pltpu.VMEM(a.shape, a.dtype) for a in arrays],
+        scratch_shapes=[pltpu.SemaphoreType.DMA((number,))],
+        compiler_params=pltpu.CompilerParams(vmem_limit_bytes=16 * 1024 * 1024),
+        cost_estimate=cost(0, sum(2 * a.size * a.dtype.itemsize for a in arrays)),
+        name=name,
+    )(*[in_hbm(a) for a in arrays])
+
+
 def finish(factor, grad_first, blocked, gate_grad, scale):
     block, channels = blocked.shape
     tiles = 4
     step = block // tiles
 
-    def body(f_hbm, d_hbm, x_hbm, r_hbm, one_hbm, out_hbm, f, d, x, r, one, out, sems):
+    def body(f, x, d_hbm, r_hbm, one_hbm, out_hbm, d, r, one, out, sems):
         ds = row_copies(d_hbm, d, sems, 0, tiles)
-        xs = row_copies(x_hbm, x, sems, tiles, tiles)
-        fs = row_copies(f_hbm, f, sems, 2 * tiles, tiles)
-        rs = row_copies(r_hbm, r, sems, 3 * tiles, tiles)
-        ones = row_copies(one, one_hbm, sems, 4 * tiles, tiles)
-        outs = row_copies(out, out_hbm, sems, 5 * tiles, tiles)
-        for c in xs + ds + fs + rs:
+        rs = row_copies(r_hbm, r, sems, tiles, tiles)
+        ones = row_copies(one, one_hbm, sems, 2 * tiles, tiles)
+        outs = row_copies(out, out_hbm, sems, 3 * tiles, tiles)
+        for c in ds + rs:
             c.start()
-        for c in xs:
-            c.wait()
         for t in range(tiles):
             at = slice(t * step, (t + 1) * step)
             ds[t].wait()
             one[at, :] = dot(d[at, :], x[...], 1, 1) * scale
             ones[t].start()
-        for c in fs:
-            c.wait()
         for t in range(tiles):
             at = slice(t * step, (t + 1) * step)
             rs[t].wait()
@@ -323,22 +346,20 @@
 
     return pl.pallas_call(
         body,
-        in_specs=[ANY] * 4,
+        in_specs=[VMEM, VMEM, ANY, ANY],
         out_specs=[ANY] * 2,
         out_shape=[pltpu.HBM((block, block), F32), pltpu.HBM((block, channels), BF)],
         scratch_shapes=[
-            pltpu.VMEM((block, block), BF),
-            pltpu.VMEM((block, channels), BF),
             pltpu.VMEM((block, channels), BF),
             pltpu.VMEM((block, channels), BF),
             pltpu.VMEM((block, block), F32),
             pltpu.VMEM((block, channels), BF),
-            pltpu.SemaphoreType.DMA((6 * tiles,)),
+            pltpu.SemaphoreType.DMA((4 * tiles,)),
         ],
         compiler_params=params(0),
         cost_estimate=cost(4 * block * block * channels, 6 * block * block + 8 * block * channels),
         name="finish",
-    )(in_hbm(factor), in_hbm(grad_first), in_hbm(blocked), in_hbm(gate_grad))
+    )(in_vmem(factor), in_vmem(blocked), in_hbm(grad_first), in_hbm(gate_grad))
 
 
 def radices(count):
@@ -490,6 +511,9 @@
     for step in reversed(steps):
         total = gather_step(total, count, *step, after=two if step == steps[1] else ())
     grad_up, grad_down = write_weights(total, up_blocks.shape, down_blocks.shape, scale)
+    late = (factor, tokens)
+    late, grad_up, grad_down = lax.optimization_barrier((late, grad_up, grad_down))
+    factor, tokens = bring(late, "bring")
     one, grad_tokens = finish(factor, grad_first, tokens, gate_grad, scale)
     return (grad_tokens, one.reshape(1, block, block), two, grad_up, grad_down)
 

time: 152 us -> 153 us (level)
  Pallas kernels: 27.9 us -> 30.4 us
  waiting for transfers between devices: 80.3 us -> 78.3 us
    all_to_all x4, waiting for transfers between devices: 46.6 us -> 44.8 us  [exchange(): return lax.all_to_all(cut, 'seq', split_axis=0, concat_axis=0, tiled=True)]
    pallas_call x1 -> x2, Pallas kernels: 5.99 us -> 7.48 us  [the longest x1 5.6 us: finish(): pl.pallas_call(body, in_specs=[VMEM, VMEM, ANY, ANY], out_specs=[ANY] * 2...]
  transfers between devices with their start and end apart: 14 -> 14, of which waited for: 9 -> 7; matrix products, arithmetic and copies ran while one was open for 1% -> 1% of each run, Pallas kernels for 5% -> 7%
where the time goes in v11:
time: 153 us; the launch traced here: 151 us
  waiting for transfers between devices  78.3 us (51%)
  starting transfers between devices  38.9 us (25%)
  Pallas kernels  30.4 us (20%)
  local copies, waits for them, and re-layouts  2.64 us (2%)
    all_to_all x4, waiting for transfers between devices, exchange(): return lax.all_to_all(cut, 'seq', split_axis=0, concat_axis=0, tiled=True)  44.8 us
    ppermute x10, waiting for transfers between devices, swap(): lax.ppermute(values, 'seq', [(i, i ^ stride * s) for i in range(count)])  33.5 us
    all_to_all x4, starting transfers between devices, exchange(): return lax.all_to_all(cut, 'seq', split_axis=0, concat_axis=0, tiled=True)  25.9 us
    ppermute x10, starting transfers between devices, swap(): lax.ppermute(values, 'seq', [(i, i ^ stride * s) for i in range(count)])  12.9 us
    pallas_call x1, Pallas kernels, middle(): pl.pallas_call(body, in_specs=[SCALAR, ANY, ANY, VMEM, ANY, ANY], out_spe...  9.46 us
    pallas_call x1, Pallas kernels, finish(): pl.pallas_call(body, in_specs=[VMEM, VMEM, ANY, ANY], out_specs=[ANY] * 2...  5.6 us
    pallas_call x1, Pallas kernels, mix_first(): pl.pallas_call(body, in_specs=[ANY, ANY], out_specs=ANY, out_shape=pltpu....  3.92 us
  transfers between devices with their start and end apart: 14, of which 7 were waited for; matrix products, arithmetic and copies ran while one was open for 1% of the time, Pallas kernels for 7%

profile of v11, /device:TPU:0, one launch (start us, length us, event | category | flops | bytes accessed | tf_op | source)
XLA Modules:
  0.0 151.5 jit_solution(7938842118906599183)
XLA Ops:
  0.6 3.9 %mix_first.1 = bf16[1024,512]{1,0:T(8,128)(2,1)} custom-call(bf16[1024,1024]{1,0:T(8,128)(2,1)} %bitcast.38, bf16[1024,512]{1,0:T(8,128)(2,1)} %refs_1_), custom_call_target="tpu_custom_call" | custom-call | flops 1073741824 | bytes 4194304 | tf_op jit(solution)/shard_map/mix_first/pallas_call | solution.py:73
  4.6 0.0 copy-start.3
  4.6 7.5 %all-to-all-start = ((bf16[16,64,512]{2,1,0:T(8,128)(2,1)}), bf16[16,64,512]{2,1,0:T(8,128)(2,1)S(1)}, u32[]{:S(2)}, u32[]{:S(2)}) async-start(bf16[16,64,512]{2,1,0:T(8,128)(2,1)} %bitcast.40), calls=%async_computation | async-start | bytes 2097152 | tf_op jit(solution)/shard_map/all_to_all | solution.py:479
  12.1 0.2 reshape.62
  12.2 0.2 copy.11
  12.5 0.7 spread_factor.1.m_ref
  13.2 21.9 %all-to-all-done.in_ref.u_ref = bf16[16,64,512]{2,1,0:T(8,128)(2,1)S(1)} async-done(((bf16[16,64,512]{2,1,0:T(8,128)(2,1)}), bf16[16,64,512]{2,1,0:T(8,128)(2,1)S(1)}, u32[]{:S(2)}, u32[]{:S(2)}) %all-to-all-start) | async-done | bytes 1048608 | tf_op jit(solution)/shard_map/all_to_all | solution.py:479
  35.0 1.2 mix_second.1
  36.3 6.9 %all-to-all-start.1 = ((bf16[16,64,512]{2,1,0:T(8,128)(2,1)}), bf16[16,64,512]{2,1,0:T(8,128)(2,1)S(1)}, u32[]{:S(2)}, u32[]{:S(2)}) async-start(bf16[16,64,512]{2,1,0:T(8,128)(2,1)} %mix_second.1), calls=%async_computation.1 | async-start | bytes 2097152 | tf_op jit(solution)/shard_map/all_to_all | solution.py:479
  43.2 22.9 %all-to-all-done.1 = bf16[16,64,512]{2,1,0:T(8,128)(2,1)S(1)} async-done(((bf16[16,64,512]{2,1,0:T(8,128)(2,1)}), bf16[16,64,512]{2,1,0:T(8,128)(2,1)S(1)}, u32[]{:S(2)}, u32[]{:S(2)}) %all-to-all-start.1) | async-done | bytes 1048608 | tf_op jit(solution)/shard_map/all_to_all | solution.py:479
  66.1 9.5 %middle.1 = (bf16[1024,512]{1,0:T(8,128)(2,1)}, bf16[1024,512]{1,0:T(8,128)(2,1)}, bf16[4,128,512]{2,1,0:T(8,128)(2,1)}, bf16[4,128,512]{2,1,0:T(8,128)(2,1)}) custom-call(s32[1]{0:T(128)} %bitcast.3.half_ref, bf16[1024,512]{1,0:T(8,128)(2,1)} %refs_1_, bf16[1024,512]{1,0:T(8,128)(2,1)} %g_hbm.1, bf16[1024,512]{1,0:T(8,128)(2,1)S(1)} %bitcast.34, ...), custom_call_target="tpu_custom_call" | custom-call | flops 2684354560 | bytes 7340032 | tf_op jit(solution)/shard_map/middle/pallas_call | solution.py:267
  75.6 0.0 copy-start.1
  75.6 7.0 %all-to-all-start.2 = ((bf16[16,64,512]{2,1,0:T(8,128)(2,1)}), bf16[16,64,512]{2,1,0:T(8,128)(2,1)S(1)}, u32[]{:S(2)}, u32[]{:S(2)}) async-start(bf16[16,64,512]{2,1,0:T(8,128)(2,1)} %bitcast.41), calls=%async_computation.2 | async-start | bytes 2097152 | tf_op jit(solution)/shard_map/all_to_all | solution.py:479
  82.6 0.4 collective-permute-start
  83.0 1.9 %collective-permute-done = bf16[4,128,512]{2,1,0:T(8,128)(2,1)} collective-permute-done((bf16[4,128,512]{2,1,0:T(8,128)(2,1)}, bf16[4,128,512]{2,1,0:T(8,128)(2,1)}, u32[]{:S(2)}, u32[]{:S(2)}) %collective-permute-start) | collective-permute-done | bytes 524320 | tf_op jit(solution)/shard_map/ppermute | solution.py:375
  84.9 2.0 %add_and_cut.2 = (f32[256,512]{1,0:T(8,128)}, bf16[256,512]{1,0:T(8,128)(2,1)}) custom-call(s32[1]{0:T(128)} %bitcast.2.digit_ref, bf16[2,256,512]{2,1,0:T(8,128)(2,1)S(1)} %bitcast.36, bf16[2,256,512]{2,1,0:T(8,128)(2,1)} %bitcast.9.refs_1_), custom_call_target="tpu_custom_call" | custom-call | flops 262144 | bytes 2097152 | tf_op jit(solution)/shard_map/add_and_cut/pallas_call | solution.py:407
  87.0 1.9 %collective-permute-start.1 = (bf16[256,512]{1,0:T(8,128)(2,1)}, bf16[256,512]{1,0:T(8,128)(2,1)S(1)}, u32[]{:S(2)}, u32[]{:S(2)}) collective-permute-start(bf16[256,512]{1,0:T(8,128)(2,1)} %get-tuple-element.43), channel_id=1, source_target_pairs={{0,2},{1,3},{2,0},{3,1},{4,6},{5,7},{6,4},{7,5},{8,10},{9,11},{10,... | collective-permute-start | bytes 786440 | tf_op jit(solution)/shard_map/ppermute | solution.py:375
  88.9 12.0 %collective-permute-done.1 = bf16[256,512]{1,0:T(8,128)(2,1)S(1)} collective-permute-done((bf16[256,512]{1,0:T(8,128)(2,1)}, bf16[256,512]{1,0:T(8,128)(2,1)S(1)}, u32[]{:S(2)}, u32[]{:S(2)}) %collective-permute-start.1) | collective-permute-done | bytes 262176 | tf_op jit(solution)/shard_map/ppermute | solution.py:375
  100.9 1.0 copy-done
  101.9 0.8 add_and_cut.3
  102.7 0.0 copy-start.2
  102.7 0.8 collective-permute-start.2
  103.6 3.4 %collective-permute-start.3 = (bf16[64,512]{1,0:T(8,128)(2,1)}, bf16[64,512]{1,0:T(8,128)(2,1)S(1)}, u32[]{:S(2)}, u32[]{:S(2)}) collective-permute-start(bf16[64,512]{1,0:T(8,128)(2,1)} %get-tuple-element.46), channel_id=1, source_target_pairs={{0,8},{1,9},{2,10},{3,11},{4,12},{5,13},{6,14},{7,15},{8,0},{9,1},... | collective-permute-start | bytes 196616 | tf_op jit(solution)/shard_map/ppermute | solution.py:375
  107.0 0.2 collective-permute-start.4
  107.2 0.0 all-to-all-done.2.in_ref.g_ref
  107.2 1.3 mix_second_back.1
  108.5 0.0 collective-permute-done.2
  108.5 5.4 %collective-permute-done.3 = bf16[64,512]{1,0:T(8,128)(2,1)S(1)} collective-permute-done((bf16[64,512]{1,0:T(8,128)(2,1)}, bf16[64,512]{1,0:T(8,128)(2,1)S(1)}, u32[]{:S(2)}, u32[]{:S(2)}) %collective-permute-start.3) | collective-permute-done | bytes 65568 | tf_op jit(solution)/shard_map/ppermute | solution.py:375
  113.8 0.0 collective-permute-done.4
  113.9 1.6 %collective-permute-start.7 = (bf16[64,512]{1,0:T(8,128)(2,1)S(1)}, bf16[64,512]{1,0:T(8,128)(2,1)S(1)}, u32[]{:S(2)}, u32[]{:S(2)}) collective-permute-start(bf16[64,512]{1,0:T(8,128)(2,1)S(1)} %add_convert_fusion), channel_id=1, source_target_pairs={{0,12},{1,13},{2,14},{3,15},{4,8},{5,9},{6,10},{7,11},{8,4},{9,5},... | collective-permute-start | bytes 196616 | tf_op jit(solution)/shard_map/ppermute | solution.py:375
  115.5 1.4 collective-permute-start.6
  116.9 1.4 collective-permute-start.5
  118.3 4.5 %all-to-all-start.3 = ((bf16[16,64,512]{2,1,0:T(8,128)(2,1)}), bf16[16,64,512]{2,1,0:T(8,128)(2,1)}, u32[]{:S(2)}, u32[]{:S(2)}) async-start(bf16[16,64,512]{2,1,0:T(8,128)(2,1)} %mix_second_back.1), calls=%async_computation.3 | async-start | bytes 2097152 | tf_op jit(solution)/shard_map/all_to_all | solution.py:479
  122.9 0.0 collective-permute-done.7
  122.9 0.0 collective-permute-done.5
  123.0 1.6 %collective-permute-start.8 = (bf16[256,512]{1,0:T(8,128)(2,1)S(1)}, bf16[256,512]{1,0:T(8,128)(2,1)S(1)}, u32[]{:S(2)}, u32[]{:S(2)}) collective-permute-start(bf16[256,512]{1,0:T(8,128)(2,1)S(1)} %bitcast.42), channel_id=1, source_target_pairs={{0,2},{1,3},{2,0},{3,1},{4,6},{5,7},{6,4},{7,5},{8,10},{9,11},{10,... | collective-permute-start | bytes 786440 | tf_op jit(solution)/shard_map/ppermute | solution.py:375
  124.6 1.5 grad_second.1
  126.1 0.2 copy.12
  126.4 0.9 reshape.71
  127.3 12.4 %collective-permute-done.8 = bf16[256,512]{1,0:T(8,128)(2,1)S(1)} collective-permute-done((bf16[256,512]{1,0:T(8,128)(2,1)S(1)}, bf16[256,512]{1,0:T(8,128)(2,1)S(1)}, u32[]{:S(2)}, u32[]{:S(2)}) %collective-permute-start.8) | collective-permute-done | bytes 262176 | tf_op jit(solution)/shard_map/ppermute | solution.py:375
  139.8 0.1 collective-permute-start.9
  139.8 1.9 %collective-permute-done.9 = bf16[512,512]{1,0:T(8,128)(2,1)S(1)} collective-permute-done((bf16[512,512]{1,0:T(8,128)(2,1)S(1)}, bf16[512,512]{1,0:T(8,128)(2,1)S(1)}, u32[]{:S(2)}, u32[]{:S(2)}) %collective-permute-start.9) | collective-permute-done | bytes 524320 | tf_op jit(solution)/shard_map/ppermute | solution.py:375
  141.7 0.1 broadcast_select_fusion.1
  141.8 0.1 pad_maximum_fusion.up_in.down_in
  141.9 1.9 %write_weights.1 = (f32[4,128,512]{2,1,0:T(8,128)}, f32[4,512,128]{2,1,0:T(8,128)}) custom-call(bf16[1024,512]{1,0:T(8,128)(2,1)S(1)} %pad_maximum_fusion.up_in.down_in, bf16[1024,512]{1,0:T(8,128)(2,1)S(1)} %pad_maximum_fusion.up_in.down_in), custom_call_target="tpu_custom_call" | custom-call | flops 262144 | bytes 3145728 | tf_op jit(solution)/shard_map/write_weights/pallas_call | solution.py:448
  143.8 1.9 %bring.1 = (bf16[1024,1024]{1,0:T(8,128)(2,1)S(1)}, bf16[1024,512]{1,0:T(8,128)(2,1)S(1)}) custom-call(bf16[1024,1024]{1,0:T(8,128)(2,1)} %bitcast.39, bf16[1024,512]{1,0:T(8,128)(2,1)} %refs_1_), custom_call_target="tpu_custom_call" | custom-call | bytes 6291456 | tf_op jit(solution)/shard_map/bring/pallas_call | solution.py:309
  145.7 0.0 all-to-all-done.3
  145.7 5.6 %finish.1 = (f32[1024,1024]{1,0:T(8,128)}, bf16[1024,512]{1,0:T(8,128)(2,1)}) custom-call(bf16[1024,1024]{1,0:T(8,128)(2,1)S(1)} %get-tuple-element.67.f, bf16[1024,512]{1,0:T(8,128)(2,1)S(1)} %get-tuple-element.68.x, bf16[1024,512]{1,0:T(8,128)(2,1)} %bitcast.20.d_hbm, bf16[1024,512]{1,0:T(8,128)(2,1)} %get-tuple-element.70.r_hbm), custom_call_target="tpu_custom_call" | custom-call | flops 2147483648 | bytes 10485760 | tf_op jit(solution)/shard_map/finish/pallas_call | solution.py:347
  (13 shorter events, 0.2 us)
Async XLA Ops:
  4.6 7.5 %copy-start.3 = (bf16[64,16,16]{0,2,1:T(8,128)(2,1)S(1)}, bf16[64,16,16]{0,2,1:T(8,128)(2,1)}, u32[]{:S(2)}) copy-start(bf16[64,16,16]{0,2,1:T(8,128)(2,1)} %param.9) | copy-start | bytes 98308
  4.6 30.4 %all-to-all-start = ((bf16[16,64,512]{2,1,0:T(8,128)(2,1)}), bf16[16,64,512]{2,1,0:T(8,128)(2,1)S(1)}, u32[]{:S(2)}, u32[]{:S(2)}) async-start(bf16[16,64,512]{2,1,0:T(8,128)(2,1)} %bitcast.40), calls=%async_computation | async-start | bytes 2097152 | tf_op jit(solution)/shard_map/all_to_all | solution.py:479
  36.3 29.8 %all-to-all-start.1 = ((bf16[16,64,512]{2,1,0:T(8,128)(2,1)}), bf16[16,64,512]{2,1,0:T(8,128)(2,1)S(1)}, u32[]{:S(2)}, u32[]{:S(2)}) async-start(bf16[16,64,512]{2,1,0:T(8,128)(2,1)} %mix_second.1), calls=%async_computation.1 | async-start | bytes 2097152 | tf_op jit(solution)/shard_map/all_to_all | solution.py:479
  75.6 9.4 %copy-start.1 = (bf16[4,128,512]{2,1,0:T(8,128)(2,1)S(1)}, bf16[4,128,512]{2,1,0:T(8,128)(2,1)}, u32[]{:S(2)}) copy-start(bf16[4,128,512]{2,1,0:T(8,128)(2,1)} %get-tuple-element.40) | copy-start | bytes 1572868
  75.6 31.6 %all-to-all-start.2 = ((bf16[16,64,512]{2,1,0:T(8,128)(2,1)}), bf16[16,64,512]{2,1,0:T(8,128)(2,1)S(1)}, u32[]{:S(2)}, u32[]{:S(2)}) async-start(bf16[16,64,512]{2,1,0:T(8,128)(2,1)} %bitcast.41), calls=%async_computation.2 | async-start | bytes 2097152 | tf_op jit(solution)/shard_map/all_to_all | solution.py:479
  82.6 2.3 %collective-permute-start = (bf16[4,128,512]{2,1,0:T(8,128)(2,1)}, bf16[4,128,512]{2,1,0:T(8,128)(2,1)}, u32[]{:S(2)}, u32[]{:S(2)}) collective-permute-start(bf16[4,128,512]{2,1,0:T(8,128)(2,1)} %get-tuple-element.41), channel_id=1, source_target_pairs={{0,1},{1,0},{2,3},{3,2},{4,5},{5,4},{6,7},{7,6},{8,9},{9,8},{10,11... | collective-permute-start | bytes 1572872 | tf_op jit(solution)/shard_map/ppermute | solution.py:375
  87.0 13.9 %collective-permute-start.1 = (bf16[256,512]{1,0:T(8,128)(2,1)}, bf16[256,512]{1,0:T(8,128)(2,1)S(1)}, u32[]{:S(2)}, u32[]{:S(2)}) collective-permute-start(bf16[256,512]{1,0:T(8,128)(2,1)} %get-tuple-element.43), channel_id=1, source_target_pairs={{0,2},{1,3},{2,0},{3,1},{4,6},{5,7},{6,4},{7,5},{8,10},{9,11},{10,... | collective-permute-start | bytes 786440 | tf_op jit(solution)/shard_map/ppermute | solution.py:375
  100.8 1.0 copy-start
  102.7 11.1 %copy-start.2 = (f32[64,512]{1,0:T(8,128)S(1)}, f32[64,512]{1,0:T(8,128)}, u32[]{:S(2)}) copy-start(f32[64,512]{1,0:T(8,128)} %get-tuple-element.50) | copy-start | bytes 393220
  102.7 5.7 %collective-permute-start.2 = (bf16[64,512]{1,0:T(8,128)(2,1)}, bf16[64,512]{1,0:T(8,128)(2,1)S(1)}, u32[]{:S(2)}, u32[]{:S(2)}) collective-permute-start(bf16[64,512]{1,0:T(8,128)(2,1)} %get-tuple-element.45), channel_id=1, source_target_pairs={{0,4},{1,5},{2,6},{3,7},{4,0},{5,1},{6,2},{7,3},{8,12},{9,13},{10,... | collective-permute-start | bytes 196616 | tf_op jit(solution)/shard_map/ppermute | solution.py:375
  103.6 10.3 %collective-permute-start.3 = (bf16[64,512]{1,0:T(8,128)(2,1)}, bf16[64,512]{1,0:T(8,128)(2,1)S(1)}, u32[]{:S(2)}, u32[]{:S(2)}) collective-permute-start(bf16[64,512]{1,0:T(8,128)(2,1)} %get-tuple-element.46), channel_id=1, source_target_pairs={{0,8},{1,9},{2,10},{3,11},{4,12},{5,13},{6,14},{7,15},{8,0},{9,1},... | collective-permute-start | bytes 196616 | tf_op jit(solution)/shard_map/ppermute | solution.py:375
  107.0 6.9 %collective-permute-start.4 = (bf16[64,512]{1,0:T(8,128)(2,1)}, bf16[64,512]{1,0:T(8,128)(2,1)S(1)}, u32[]{:S(2)}, u32[]{:S(2)}) collective-permute-start(bf16[64,512]{1,0:T(8,128)(2,1)} %get-tuple-element.47), channel_id=1, source_target_pairs={{0,12},{1,13},{2,14},{3,15},{4,8},{5,9},{6,10},{7,11},{8,4},{9,5},... | collective-permute-start | bytes 196616 | tf_op jit(solution)/shard_map/ppermute | solution.py:375
  113.9 9.0 %collective-permute-start.7 = (bf16[64,512]{1,0:T(8,128)(2,1)S(1)}, bf16[64,512]{1,0:T(8,128)(2,1)S(1)}, u32[]{:S(2)}, u32[]{:S(2)}) collective-permute-start(bf16[64,512]{1,0:T(8,128)(2,1)S(1)} %add_convert_fusion), channel_id=1, source_target_pairs={{0,12},{1,13},{2,14},{3,15},{4,8},{5,9},{6,10},{7,11},{8,4},{9,5},... | collective-permute-start | bytes 196616 | tf_op jit(solution)/shard_map/ppermute | solution.py:375
  115.5 7.3 %collective-permute-start.6 = (bf16[64,512]{1,0:T(8,128)(2,1)S(1)}, bf16[64,512]{1,0:T(8,128)(2,1)S(1)}, u32[]{:S(2)}, u32[]{:S(2)}) collective-permute-start(bf16[64,512]{1,0:T(8,128)(2,1)S(1)} %add_convert_fusion), channel_id=1, source_target_pairs={{0,8},{1,9},{2,10},{3,11},{4,12},{5,13},{6,14},{7,15},{8,0},{9,1},... | collective-permute-start | bytes 196616 | tf_op jit(solution)/shard_map/ppermute | solution.py:375
  116.9 6.0 %collective-permute-start.5 = (bf16[64,512]{1,0:T(8,128)(2,1)S(1)}, bf16[64,512]{1,0:T(8,128)(2,1)S(1)}, u32[]{:S(2)}, u32[]{:S(2)}) collective-permute-start(bf16[64,512]{1,0:T(8,128)(2,1)S(1)} %add_convert_fusion), channel_id=1, source_target_pairs={{0,4},{1,5},{2,6},{3,7},{4,0},{5,1},{6,2},{7,3},{8,12},{9,13},{10,... | collective-permute-start | bytes 196616 | tf_op jit(solution)/shard_map/ppermute | solution.py:375
  118.3 27.4 %all-to-all-start.3 = ((bf16[16,64,512]{2,1,0:T(8,128)(2,1)}), bf16[16,64,512]{2,1,0:T(8,128)(2,1)}, u32[]{:S(2)}, u32[]{:S(2)}) async-start(bf16[16,64,512]{2,1,0:T(8,128)(2,1)} %mix_second_back.1), calls=%async_computation.3 | async-start | bytes 2097152 | tf_op jit(solution)/shard_map/all_to_all | solution.py:479
  123.0 16.7 %collective-permute-start.8 = (bf16[256,512]{1,0:T(8,128)(2,1)S(1)}, bf16[256,512]{1,0:T(8,128)(2,1)S(1)}, u32[]{:S(2)}, u32[]{:S(2)}) collective-permute-start(bf16[256,512]{1,0:T(8,128)(2,1)S(1)} %bitcast.42), channel_id=1, source_target_pairs={{0,2},{1,3},{2,0},{3,1},{4,6},{5,7},{6,4},{7,5},{8,10},{9,11},{10,... | collective-permute-start | bytes 786440 | tf_op jit(solution)/shard_map/ppermute | solution.py:375
  139.8 2.0 %collective-permute-start.9 = (bf16[512,512]{1,0:T(8,128)(2,1)S(1)}, bf16[512,512]{1,0:T(8,128)(2,1)S(1)}, u32[]{:S(2)}, u32[]{:S(2)}) collective-permute-start(bf16[512,512]{1,0:T(8,128)(2,1)S(1)} %pad_maximum_fusion.1), channel_id=1, source_target_pairs={{0,1},{1,0},{2,3},{3,2},{4,5},{5,4},{6,7},{7,6},{8,9},{9,8},{10,11... | collective-permute-start | bytes 1572872 | tf_op jit(solution)/shard_map/ppermute | solution.py:375

commit v12 on v10

--- a/solution.py
+++ b/solution.py
@@ -179,16 +179,56 @@
     return out.reshape(groups, n, 16, n).transpose(0, 2, 1, 3).reshape(here, n, n)
 
 
-def middle(half, blocked, incoming, mixed, up_blocks, down_blocks):
+def turn(factor, incoming, up_blocks, down_blocks):
+    block = factor.shape[0]
+    rows, channels = incoming.shape
+    groups, width, inner = up_blocks.shape
+
+    def body(f_ref, g_ref, up_ref, down_ref, f_out, g_out, up_out, down_out):
+        f_out[...] = f_ref[...].T
+        g_out[...] = g_ref[...].T
+        up_out[0] = up_ref[0].T
+        down_out[0] = down_ref[0].T
+
+    step, part = rows // groups, block // groups
+    return pl.pallas_call(
+        body,
+        grid=(groups,),
+        in_specs=[
+            pl.BlockSpec((block, part), lambda i: (0, i)),
+            pl.BlockSpec((step, channels), lambda i: (i, 0)),
+            pl.BlockSpec((1, width, inner), lambda i: (i, 0, 0)),
+            pl.BlockSpec((1, inner, width), lambda i: (i, 0, 0)),
+        ],
+        out_specs=[
+            pl.BlockSpec((part, block), lambda i: (i, 0)),
+            pl.BlockSpec((channels, step), lambda i: (0, i)),
+            pl.BlockSpec((1, inner, width), lambda i: (i, 0, 0)),
+            pl.BlockSpec((1, width, inner), lambda i: (i, 0, 0)),
+        ],
+        out_shape=[
+            pltpu.HBM((block, block), BF),
+            pltpu.HBM((channels, rows), BF),
+            pltpu.HBM((groups, inner, width), BF),
+            pltpu.HBM((groups, width, inner), BF),
+        ],
+        compiler_params=params(),
+        cost_estimate=cost(0, 4 * (block * block + rows * channels)),
+        name="turn",
+    )(in_hbm(factor), in_hbm(incoming), in_hbm(up_blocks), in_hbm(down_blocks))
+
+
+def middle(half, blocked, incoming, mixed, up_blocks, turned):
     groups, width, inner = up_blocks.shape
     sub = inner // groups
     rows, channels = blocked.shape
     step = min(256, rows)
     tiles = rows // step
-
-    def body(half_ref, x_hbm, g_hbm, v_ref, up_hbm, down_hbm, *refs):
+    incoming_t, up_t, down_t = turned
+
+    def body(half_ref, x_hbm, g_hbm, gt_hbm, v_ref, up_hbm, upt_hbm, downt_hbm, *refs):
         dv_hbm, r_hbm, kept_hbm, sent_hbm = refs[:4]
-        x_ref, g_ref, up_ref, down_ref, dv, r_ref, w, halves, sems = refs[4:]
+        x_ref, g_ref, gt_ref, up_ref, upt_ref, downt_ref, dv, r_ref, w, halves, sems = refs[4:]
 
         def rows_copy(src, dst, kind, t):
             at = pl.ds(t * step, step)
@@ -198,60 +238,65 @@
             return pltpu.make_async_copy(src, dst, sems.at[4 * tiles + number])
 
         fetch_up = whole_copy(up_hbm, up_ref, 0)
-        fetch_down = whole_copy(down_hbm, down_ref, 1)
+        fetch_downt = whole_copy(downt_hbm, downt_ref, 1)
+        fetch_upt = whole_copy(upt_hbm, upt_ref, 2)
+        fetch_gt = whole_copy(gt_hbm, gt_ref, 3)
         rows_copy(x_hbm, x_ref, 0, 0).start()
         fetch_up.start()
         rows_copy(g_hbm, g_ref, 1, 0).start()
-        fetch_down.start()
+        fetch_downt.start()
+        fetch_gt.start()
+        fetch_upt.start()
         for t in range(1, tiles):
             rows_copy(x_hbm, x_ref, 0, t).start()
             rows_copy(g_hbm, g_ref, 1, t).start()
         w[...] = jnp.zeros_like(w)
-        fetch_up.wait()
-        fetch_down.wait()
-
-        def tile(t, carry):
+        for t in range(tiles):
+            at = slice(t * step, (t + 1) * step)
             rows_copy(x_hbm, x_ref, 0, t).wait()
-            rows_copy(g_hbm, g_ref, 1, t).wait()
-            at = pl.ds(pl.multiple_of(t * step, step), step)
             x = x_ref[at, :].astype(F32)
-            g = g_ref[at, :]
             v = v_ref[at, :].astype(F32)
             sx = sigmoid(x)
             gate = x * sx
             h = (x + v * gate).astype(BF)
-            h_parts = [h[:, b * width : (b + 1) * width] for b in range(groups)]
-            g_parts = [g[:, b * width : (b + 1) * width] for b in range(groups)]
+            ht = h.T
+            rows_copy(g_hbm, g_ref, 1, t).wait()
+            if t == 0:
+                fetch_up.wait()
+                fetch_downt.wait()
             acts, slopes, back = [], [], []
             for b in range(groups):
-                a = dot(h_parts[b], up_ref[b], 1, 0).astype(BF)
+                part = slice(b * width, (b + 1) * width)
+                a = dot(h[:, part], up_ref[b], 1, 0).astype(BF)
                 s = sigmoid(a)
                 q = a * s
                 acts.append(q)
                 slopes.append(s + q * (1 - s))
-                back.append(dot(g_parts[b], down_ref[b], 1, 1).astype(BF))
+                back.append(dot(g_ref[at, part], downt_ref[b], 1, 0).astype(BF))
+            if t == 0:
+                fetch_gt.wait()
+                fetch_upt.wait()
             grads = []
             for b in range(groups):
+                part = slice(b * width, (b + 1) * width)
                 lanes = slice(b * sub, (b + 1) * sub)
                 perm = jnp.concatenate([acts[p][:, lanes] for p in range(groups)], axis=1)
-                w[1, b] += dot(g_parts[b], perm, 0, 0)
+                w[1, b] += dot(gt_ref[part, at], perm, 1, 0)
                 dq = jnp.concatenate([back[p][:, lanes] for p in range(groups)], axis=1)
                 da = dq * slopes[b]
-                w[0, b] += dot(h_parts[b], da, 0, 0)
-                grads.append(dot(da, up_ref[b], 1, 1))
-            dh = (g.astype(F32) + jnp.concatenate(grads, axis=1)).astype(BF).astype(F32)
+                w[0, b] += dot(ht[part, :], da, 1, 0)
+                grads.append(dot(da, upt_ref[b], 1, 0))
+            g = g_ref[at, :].astype(F32)
+            dh = (g + jnp.concatenate(grads, axis=1)).astype(BF).astype(F32)
             dv[at, :] = (dh * gate).astype(BF)
             rows_copy(dv, dv_hbm, 2, t).start()
             r_ref[at, :] = (dh * (1.0 + v * (sx + gate * (1.0 - sx)))).astype(BF)
             rows_copy(r_ref, r_hbm, 3, t).start()
-            return carry
-
-        lax.fori_loop(0, tiles, tile, 0)
         halves[1] = w[1 - half_ref[0]].astype(BF)
-        send = whole_copy(halves.at[1], sent_hbm, 2)
+        send = whole_copy(halves.at[1], sent_hbm, 4)
         send.start()
         halves[0] = w[half_ref[0]].astype(BF)
-        keep = whole_copy(halves.at[0], kept_hbm, 3)
+        keep = whole_copy(halves.at[0], kept_hbm, 5)
         keep.start()
         for t in range(tiles):
             rows_copy(dv, dv_hbm, 2, t).wait()
@@ -262,7 +307,7 @@
     hidden = rows * groups * inner
     return pl.pallas_call(
         body,
-        in_specs=[SCALAR, ANY, ANY, VMEM, ANY, ANY],
+        in_specs=[SCALAR, ANY, ANY, ANY, VMEM, ANY, ANY, ANY],
         out_specs=[ANY] * 4,
         out_shape=[
             pltpu.HBM((rows, channels), BF),
@@ -273,23 +318,34 @@
         scratch_shapes=[
             pltpu.VMEM((rows, channels), BF),
             pltpu.VMEM((rows, channels), BF),
+            pltpu.VMEM(incoming_t.shape, BF),
             pltpu.VMEM(up_blocks.shape, BF),
-            pltpu.VMEM(down_blocks.shape, BF),
+            pltpu.VMEM(up_t.shape, BF),
+            pltpu.VMEM(down_t.shape, BF),
             pltpu.VMEM((rows, channels), BF),
             pltpu.VMEM((rows, channels), BF),
             pltpu.VMEM((2, groups, width, inner), F32),
             pltpu.VMEM((2, groups, width, inner), BF),
-            pltpu.SemaphoreType.DMA((4 * tiles + 4,)),
+            pltpu.SemaphoreType.DMA((4 * tiles + 6,)),
         ],
         compiler_params=params(0),
         cost_estimate=cost(
             10 * hidden * width, 10 * rows * channels + 8 * groups * width * inner, hidden
         ),
         name="middle",
-    )(half, in_hbm(blocked), in_hbm(incoming), in_vmem(mixed), in_hbm(up_blocks), in_hbm(down_blocks))
-
-
-def finish(factor, grad_first, blocked, gate_grad, scale):
+    )(
+        half,
+        in_hbm(blocked),
+        in_hbm(incoming),
+        in_hbm(incoming_t),
+        in_vmem(mixed),
+        in_hbm(up_blocks),
+        in_hbm(up_t),
+        in_hbm(down_t),
+    )
+
+
+def finish(factor_t, grad_first, blocked, gate_grad, scale):
     block, channels = blocked.shape
     tiles = 4
     step = block // tiles
@@ -310,12 +366,11 @@
             ds[t].wait()
             one[at, :] = dot(d[at, :], x[...], 1, 1) * scale
             ones[t].start()
-        for c in fs:
-            c.wait()
         for t in range(tiles):
             at = slice(t * step, (t + 1) * step)
+            fs[t].wait()
             rs[t].wait()
-            total = dot(f[:, at], d[...], 0, 0) + r[at, :].astype(F32)
+            total = dot(f[at, :], d[...], 1, 0) + r[at, :].astype(F32)
             out[at, :] = total.astype(BF)
             outs[t].start()
         for c in ones + outs:
@@ -338,7 +393,7 @@
         compiler_params=params(0),
         cost_estimate=cost(4 * block * block * channels, 6 * block * block + 8 * block * channels),
         name="finish",
-    )(in_hbm(factor), in_hbm(grad_first), in_hbm(blocked), in_hbm(gate_grad))
+    )(in_hbm(factor_t), in_hbm(grad_first), in_hbm(blocked), in_hbm(gate_grad))
 
 
 def radices(count):
@@ -474,7 +529,10 @@
     half = (lax.axis_index("seq") % 2).astype(jnp.int32).reshape(1)
     firsts = exchange(mix_first(factor, tokens))
     mixed = exchange(second(firsts, False)).reshape(block, channels)
-    dv, gate_grad, kept, sent = middle(half, tokens, cotangent, mixed, up_blocks, down_blocks)
+    late = (factor, cotangent, up_blocks, down_blocks)
+    firsts, late = lax.optimization_barrier((firsts, late))
+    factor_t, *turned = turn(*late)
+    dv, gate_grad, kept, sent = middle(half, tokens, cotangent, mixed, up_blocks, turned)
     grad_mixed = exchange(dv)
     back = second(grad_mixed, True)
     terms = [kept, swap(sent, count, 1, 1)]
@@ -490,7 +548,7 @@
     for step in reversed(steps):
         total = gather_step(total, count, *step, after=two if step == steps[1] else ())
     grad_up, grad_down = write_weights(total, up_blocks.shape, down_blocks.shape, scale)
-    one, grad_tokens = finish(factor, grad_first, tokens, gate_grad, scale)
+    one, grad_tokens = finish(factor_t, grad_first, tokens, gate_grad, scale)
     return (grad_tokens, one.reshape(1, block, block), two, grad_up, grad_down)
 
 

time: 152 us -> 153 us (level)
  Pallas kernels: 27.9 us -> 33.4 us
  waiting for transfers between devices: 80.3 us -> 75.2 us
    pallas_call x1 -> x2, Pallas kernels: 8.52 us -> 14.2 us  [the longest x1 9.2 us: middle(): pl.pallas_call(body, in_specs=[SCALAR, ANY, ANY, ANY, VMEM, ANY, ANY, ANY...]
    all_to_all x4, waiting for transfers between devices: 46.6 us -> 41.6 us  [exchange(): return lax.all_to_all(cut, 'seq', split_axis=0, concat_axis=0, tiled=True)]
  transfers between devices with their start and end apart: 14 -> 14, of which waited for: 9 -> 9; matrix products, arithmetic and copies ran while one was open for 1% -> 1% of each run, Pallas kernels for 5% -> 9%
where the time goes in v12:
time: 153 us; the launch traced here: 151 us
  waiting for transfers between devices  75.2 us (49%)
  starting transfers between devices  38.8 us (25%)
  Pallas kernels  33.4 us (22%)
  local copies, waits for them, and re-layouts  2.63 us (2%)
    all_to_all x4, waiting for transfers between devices, exchange(): return lax.all_to_all(cut, 'seq', split_axis=0, concat_axis=0, tiled=True)  41.6 us
    ppermute x10, waiting for transfers between devices, swap(): lax.ppermute(values, 'seq', [(i, i ^ stride * s) for i in range(count)])  33.6 us
    all_to_all x4, starting transfers between devices, exchange(): return lax.all_to_all(cut, 'seq', split_axis=0, concat_axis=0, tiled=True)  25.9 us
    ppermute x10, starting transfers between devices, swap(): lax.ppermute(values, 'seq', [(i, i ^ stride * s) for i in range(count)])  12.9 us
    pallas_call x1, Pallas kernels, middle(): pl.pallas_call(body, in_specs=[SCALAR, ANY, ANY, ANY, VMEM, ANY, ANY, ANY...  9.2 us
    pallas_call x1, Pallas kernels, finish(): pl.pallas_call(body, in_specs=[ANY] * 4, out_specs=[ANY] * 2, out_shape=[...  5.83 us
    pallas_call x1, Pallas kernels, turn(): pl.pallas_call(body, grid=(groups,), in_specs=[pl.BlockSpec((block, part)...  4.98 us
    pallas_call x1, Pallas kernels, mix_first(): pl.pallas_call(body, in_specs=[ANY, ANY], out_specs=ANY, out_shape=pltpu....  3.92 us
  transfers between devices with their start and end apart: 14, of which 9 were waited for; matrix products, arithmetic and copies ran while one was open for 1% of the time, Pallas kernels for 9%

profile of v12, /device:TPU:0, one launch (start us, length us, event | category | flops | bytes accessed | tf_op | source)
XLA Modules:
  0.0 151.3 jit_solution(551779422408426538)
XLA Ops:
  0.6 3.9 %mix_first.1 = bf16[1024,512]{1,0:T(8,128)(2,1)} custom-call(bf16[1024,1024]{1,0:T(8,128)(2,1)} %bitcast.38, bf16[1024,512]{1,0:T(8,128)(2,1)} %x_hbm.5), custom_call_target="tpu_custom_call" | custom-call | flops 1073741824 | bytes 4194304 | tf_op jit(solution)/shard_map/mix_first/pallas_call | solution.py:73
  4.6 0.0 copy-start.3
  4.6 7.5 %all-to-all-start = ((bf16[16,64,512]{2,1,0:T(8,128)(2,1)}), bf16[16,64,512]{2,1,0:T(8,128)(2,1)S(1)}, u32[]{:S(2)}, u32[]{:S(2)}) async-start(bf16[16,64,512]{2,1,0:T(8,128)(2,1)} %bitcast.40), calls=%async_computation | async-start | bytes 2097152 | tf_op jit(solution)/shard_map/all_to_all | solution.py:513
  12.1 0.2 reshape.63
  12.2 0.2 copy.11
  12.5 0.7 spread_factor.1.m_ref
  13.2 21.9 %all-to-all-done.in_ref.u_ref = bf16[16,64,512]{2,1,0:T(8,128)(2,1)S(1)} async-done(((bf16[16,64,512]{2,1,0:T(8,128)(2,1)}), bf16[16,64,512]{2,1,0:T(8,128)(2,1)S(1)}, u32[]{:S(2)}, u32[]{:S(2)}) %all-to-all-start) | async-done | bytes 1048608 | tf_op jit(solution)/shard_map/all_to_all | solution.py:513
  35.0 1.2 mix_second.1
  36.3 6.9 %all-to-all-start.1 = ((bf16[16,64,512]{2,1,0:T(8,128)(2,1)}), bf16[16,64,512]{2,1,0:T(8,128)(2,1)S(1)}, u32[]{:S(2)}, u32[]{:S(2)}) async-start(bf16[16,64,512]{2,1,0:T(8,128)(2,1)} %mix_second.1), calls=%async_computation.1 | async-start | bytes 2097152 | tf_op jit(solution)/shard_map/all_to_all | solution.py:513
  43.2 5.0 %turn.1 = (bf16[1024,1024]{1,0:T(8,128)(2,1)}, bf16[512,1024]{1,0:T(8,128)(2,1)}, bf16[4,512,128]{2,1,0:T(8,128)(2,1)}, bf16[4,128,512]{2,1,0:T(8,128)(2,1)}) custom-call(bf16[1024,1024]{1,0:T(8,128)(2,1)} %bitcast.39, bf16[1024,512]{1,0:T(8,128)(2,1)} %g_hbm.1, bf16[4,128,512]{2,1,0:T(8,128)(2,1)} %up_hbm.1, bf16[4,512,128]{2,1,0:T(8,128)(2,1)} %down_ref), custom_call_target="tpu_custom_call" | custom-call | bytes 6291456 | tf_op jit(solution)/shard_map/turn/pallas_call | solution.py:194
  48.1 17.9 %all-to-all-done.1 = bf16[16,64,512]{2,1,0:T(8,128)(2,1)S(1)} async-done(((bf16[16,64,512]{2,1,0:T(8,128)(2,1)}), bf16[16,64,512]{2,1,0:T(8,128)(2,1)S(1)}, u32[]{:S(2)}, u32[]{:S(2)}) %all-to-all-start.1) | async-done | bytes 1048608 | tf_op jit(solution)/shard_map/all_to_all | solution.py:513
  66.1 9.2 %middle.1 = (bf16[1024,512]{1,0:T(8,128)(2,1)}, bf16[1024,512]{1,0:T(8,128)(2,1)}, bf16[4,128,512]{2,1,0:T(8,128)(2,1)}, bf16[4,128,512]{2,1,0:T(8,128)(2,1)}) custom-call(s32[1]{0:T(128)} %bitcast.4.half_ref, bf16[1024,512]{1,0:T(8,128)(2,1)} %x_hbm.5, bf16[1024,512]{1,0:T(8,128)(2,1)} %g_hbm.1, bf16[512,1024]{1,0:T(8,128)(2,1)} %get-tuple-element.48.gt_hbm, ...), custom_call_target="tpu_custom_call" | custom-call | flops 2684354560 | bytes 7340032 | tf_op jit(solution)/shard_map/middle/pallas_call | solution.py:308
  75.3 7.0 %all-to-all-start.2 = ((bf16[16,64,512]{2,1,0:T(8,128)(2,1)}), bf16[16,64,512]{2,1,0:T(8,128)(2,1)S(1)}, u32[]{:S(2)}, u32[]{:S(2)}) async-start(bf16[16,64,512]{2,1,0:T(8,128)(2,1)} %bitcast.41), calls=%async_computation.2 | async-start | bytes 2097152 | tf_op jit(solution)/shard_map/all_to_all | solution.py:513
  82.3 0.4 collective-permute-start
  82.7 1.9 %collective-permute-done = bf16[4,128,512]{2,1,0:T(8,128)(2,1)} collective-permute-done((bf16[4,128,512]{2,1,0:T(8,128)(2,1)}, bf16[4,128,512]{2,1,0:T(8,128)(2,1)}, u32[]{:S(2)}, u32[]{:S(2)}) %collective-permute-start) | collective-permute-done | bytes 524320 | tf_op jit(solution)/shard_map/ppermute | solution.py:409
  84.6 2.0 %add_and_cut.2 = (f32[256,512]{1,0:T(8,128)}, bf16[256,512]{1,0:T(8,128)(2,1)}) custom-call(s32[1]{0:T(128)} %bitcast.3.digit_ref, bf16[2,256,512]{2,1,0:T(8,128)(2,1)S(1)} %bitcast.36, bf16[2,256,512]{2,1,0:T(8,128)(2,1)} %bitcast.9.refs_1_), custom_call_target="tpu_custom_call" | custom-call | flops 262144 | bytes 2097152 | tf_op jit(solution)/shard_map/add_and_cut/pallas_call | solution.py:441
  86.7 1.9 %collective-permute-start.1 = (bf16[256,512]{1,0:T(8,128)(2,1)}, bf16[256,512]{1,0:T(8,128)(2,1)S(1)}, u32[]{:S(2)}, u32[]{:S(2)}) collective-permute-start(bf16[256,512]{1,0:T(8,128)(2,1)} %get-tuple-element.54), channel_id=1, source_target_pairs={{0,2},{1,3},{2,0},{3,1},{4,6},{5,7},{6,4},{7,5},{8,10},{9,11},{10,... | collective-permute-start | bytes 786440 | tf_op jit(solution)/shard_map/ppermute | solution.py:409
  88.6 12.0 %collective-permute-done.1 = bf16[256,512]{1,0:T(8,128)(2,1)S(1)} collective-permute-done((bf16[256,512]{1,0:T(8,128)(2,1)}, bf16[256,512]{1,0:T(8,128)(2,1)S(1)}, u32[]{:S(2)}, u32[]{:S(2)}) %collective-permute-start.1) | collective-permute-done | bytes 262176 | tf_op jit(solution)/shard_map/ppermute | solution.py:409
  100.6 1.0 copy-done
  101.6 0.8 add_and_cut.3
  102.4 0.0 copy-start.2
  102.5 0.8 collective-permute-start.2
  103.3 3.4 %collective-permute-start.3 = (bf16[64,512]{1,0:T(8,128)(2,1)}, bf16[64,512]{1,0:T(8,128)(2,1)S(1)}, u32[]{:S(2)}, u32[]{:S(2)}) collective-permute-start(bf16[64,512]{1,0:T(8,128)(2,1)} %get-tuple-element.57), channel_id=1, source_target_pairs={{0,8},{1,9},{2,10},{3,11},{4,12},{5,13},{6,14},{7,15},{8,0},{9,1},... | collective-permute-start | bytes 196616 | tf_op jit(solution)/shard_map/ppermute | solution.py:409
  106.7 0.2 collective-permute-start.4
  106.9 0.0 all-to-all-done.2.in_ref.g_ref
  106.9 1.3 mix_second_back.1
  108.2 0.0 collective-permute-done.2
  108.2 5.4 %collective-permute-done.3 = bf16[64,512]{1,0:T(8,128)(2,1)S(1)} collective-permute-done((bf16[64,512]{1,0:T(8,128)(2,1)}, bf16[64,512]{1,0:T(8,128)(2,1)S(1)}, u32[]{:S(2)}, u32[]{:S(2)}) %collective-permute-start.3) | collective-permute-done | bytes 65568 | tf_op jit(solution)/shard_map/ppermute | solution.py:409
  113.5 0.0 collective-permute-done.4
  113.6 1.6 %collective-permute-start.5 = (bf16[64,512]{1,0:T(8,128)(2,1)S(1)}, bf16[64,512]{1,0:T(8,128)(2,1)S(1)}, u32[]{:S(2)}, u32[]{:S(2)}) collective-permute-start(bf16[64,512]{1,0:T(8,128)(2,1)S(1)} %add_convert_fusion), channel_id=1, source_target_pairs={{0,4},{1,5},{2,6},{3,7},{4,0},{5,1},{6,2},{7,3},{8,12},{9,13},{10,... | collective-permute-start | bytes 196616 | tf_op jit(solution)/shard_map/ppermute | solution.py:409
  115.1 0.6 collective-permute-start.6
  115.8 2.2 %collective-permute-start.7 = (bf16[64,512]{1,0:T(8,128)(2,1)S(1)}, bf16[64,512]{1,0:T(8,128)(2,1)S(1)}, u32[]{:S(2)}, u32[]{:S(2)}) collective-permute-start(bf16[64,512]{1,0:T(8,128)(2,1)S(1)} %add_convert_fusion), channel_id=1, source_target_pairs={{0,12},{1,13},{2,14},{3,15},{4,8},{5,9},{6,10},{7,11},{8,4},{9,5},... | collective-permute-start | bytes 196616 | tf_op jit(solution)/shard_map/ppermute | solution.py:409
  118.0 4.5 %all-to-all-start.3 = ((bf16[16,64,512]{2,1,0:T(8,128)(2,1)}), bf16[16,64,512]{2,1,0:T(8,128)(2,1)}, u32[]{:S(2)}, u32[]{:S(2)}) async-start(bf16[16,64,512]{2,1,0:T(8,128)(2,1)} %mix_second_back.1), calls=%async_computation.3 | async-start | bytes 2097152 | tf_op jit(solution)/shard_map/all_to_all | solution.py:513
  122.6 0.0 collective-permute-done.5
  122.6 0.1 collective-permute-done.6
  122.7 0.0 collective-permute-done.7
  122.8 1.5 %collective-permute-start.8 = (bf16[256,512]{1,0:T(8,128)(2,1)S(1)}, bf16[256,512]{1,0:T(8,128)(2,1)S(1)}, u32[]{:S(2)}, u32[]{:S(2)}) collective-permute-start(bf16[256,512]{1,0:T(8,128)(2,1)S(1)} %bitcast.42), channel_id=1, source_target_pairs={{0,2},{1,3},{2,0},{3,1},{4,6},{5,7},{6,4},{7,5},{8,10},{9,11},{10,... | collective-permute-start | bytes 786440 | tf_op jit(solution)/shard_map/ppermute | solution.py:409
  124.4 1.5 grad_second.1
  125.9 0.2 copy.12
  126.1 0.9 reshape.72
  127.0 12.4 %collective-permute-done.8 = bf16[256,512]{1,0:T(8,128)(2,1)S(1)} collective-permute-done((bf16[256,512]{1,0:T(8,128)(2,1)S(1)}, bf16[256,512]{1,0:T(8,128)(2,1)S(1)}, u32[]{:S(2)}, u32[]{:S(2)}) %collective-permute-start.8) | collective-permute-done | bytes 262176 | tf_op jit(solution)/shard_map/ppermute | solution.py:409
  139.5 0.1 collective-permute-start.9
  139.6 1.9 %collective-permute-done.9 = bf16[512,512]{1,0:T(8,128)(2,1)S(1)} collective-permute-done((bf16[512,512]{1,0:T(8,128)(2,1)S(1)}, bf16[512,512]{1,0:T(8,128)(2,1)S(1)}, u32[]{:S(2)}, u32[]{:S(2)}) %collective-permute-start.9) | collective-permute-done | bytes 524320 | tf_op jit(solution)/shard_map/ppermute | solution.py:409
  141.4 0.1 broadcast_select_fusion.1
  141.5 0.1 pad_maximum_fusion.up_in.down_in
  141.6 1.9 %write_weights.1 = (f32[4,128,512]{2,1,0:T(8,128)}, f32[4,512,128]{2,1,0:T(8,128)}) custom-call(bf16[1024,512]{1,0:T(8,128)(2,1)S(1)} %pad_maximum_fusion.up_in.down_in, bf16[1024,512]{1,0:T(8,128)(2,1)S(1)} %pad_maximum_fusion.up_in.down_in), custom_call_target="tpu_custom_call" | custom-call | flops 262144 | bytes 3145728 | tf_op jit(solution)/shard_map/write_weights/pallas_call | solution.py:482
  143.5 1.8 %all-to-all-done.3 = bf16[16,64,512]{2,1,0:T(8,128)(2,1)} async-done(((bf16[16,64,512]{2,1,0:T(8,128)(2,1)}), bf16[16,64,512]{2,1,0:T(8,128)(2,1)}, u32[]{:S(2)}, u32[]{:S(2)}) %all-to-all-start.3) | async-done | bytes 1048608 | tf_op jit(solution)/shard_map/all_to_all | solution.py:513
  145.3 5.8 %finish.1 = (f32[1024,1024]{1,0:T(8,128)}, bf16[1024,512]{1,0:T(8,128)(2,1)}) custom-call(bf16[1024,1024]{1,0:T(8,128)(2,1)} %get-tuple-element.47.f_hbm, bf16[1024,512]{1,0:T(8,128)(2,1)} %bitcast.13.d_hbm, bf16[1024,512]{1,0:T(8,128)(2,1)} %x_hbm.5, bf16[1024,512]{1,0:T(8,128)(2,1)} %get-tuple-element.66.r_hbm), custom_call_target="tpu_custom_call" | custom-call | flops 2147483648 | bytes 10485760 | tf_op jit(solution)/shard_map/finish/pallas_call | solution.py:379
  (13 shorter events, 0.2 us)
Async XLA Ops:
  4.6 7.5 %copy-start.3 = (bf16[64,16,16]{0,2,1:T(8,128)(2,1)S(1)}, bf16[64,16,16]{0,2,1:T(8,128)(2,1)}, u32[]{:S(2)}) copy-start(bf16[64,16,16]{0,2,1:T(8,128)(2,1)} %param.9) | copy-start | bytes 98308
  4.6 30.4 %all-to-all-start = ((bf16[16,64,512]{2,1,0:T(8,128)(2,1)}), bf16[16,64,512]{2,1,0:T(8,128)(2,1)S(1)}, u32[]{:S(2)}, u32[]{:S(2)}) async-start(bf16[16,64,512]{2,1,0:T(8,128)(2,1)} %bitcast.40), calls=%async_computation | async-start | bytes 2097152 | tf_op jit(solution)/shard_map/all_to_all | solution.py:513
  36.3 29.8 %all-to-all-start.1 = ((bf16[16,64,512]{2,1,0:T(8,128)(2,1)}), bf16[16,64,512]{2,1,0:T(8,128)(2,1)S(1)}, u32[]{:S(2)}, u32[]{:S(2)}) async-start(bf16[16,64,512]{2,1,0:T(8,128)(2,1)} %mix_second.1), calls=%async_computation.1 | async-start | bytes 2097152 | tf_op jit(solution)/shard_map/all_to_all | solution.py:513
  75.3 9.3 %copy-start.1 = (bf16[4,128,512]{2,1,0:T(8,128)(2,1)S(1)}, bf16[4,128,512]{2,1,0:T(8,128)(2,1)}, u32[]{:S(2)}) copy-start(bf16[4,128,512]{2,1,0:T(8,128)(2,1)} %get-tuple-element.51) | copy-start | bytes 1572868
  75.3 31.6 %all-to-all-start.2 = ((bf16[16,64,512]{2,1,0:T(8,128)(2,1)}), bf16[16,64,512]{2,1,0:T(8,128)(2,1)S(1)}, u32[]{:S(2)}, u32[]{:S(2)}) async-start(bf16[16,64,512]{2,1,0:T(8,128)(2,1)} %bitcast.41), calls=%async_computation.2 | async-start | bytes 2097152 | tf_op jit(solution)/shard_map/all_to_all | solution.py:513
  82.3 2.3 %collective-permute-start = (bf16[4,128,512]{2,1,0:T(8,128)(2,1)}, bf16[4,128,512]{2,1,0:T(8,128)(2,1)}, u32[]{:S(2)}, u32[]{:S(2)}) collective-permute-start(bf16[4,128,512]{2,1,0:T(8,128)(2,1)} %get-tuple-element.52), channel_id=1, source_target_pairs={{0,1},{1,0},{2,3},{3,2},{4,5},{5,4},{6,7},{7,6},{8,9},{9,8},{10,11... | collective-permute-start | bytes 1572872 | tf_op jit(solution)/shard_map/ppermute | solution.py:409
  86.7 13.9 %collective-permute-start.1 = (bf16[256,512]{1,0:T(8,128)(2,1)}, bf16[256,512]{1,0:T(8,128)(2,1)S(1)}, u32[]{:S(2)}, u32[]{:S(2)}) collective-permute-start(bf16[256,512]{1,0:T(8,128)(2,1)} %get-tuple-element.54), channel_id=1, source_target_pairs={{0,2},{1,3},{2,0},{3,1},{4,6},{5,7},{6,4},{7,5},{8,10},{9,11},{10,... | collective-permute-start | bytes 786440 | tf_op jit(solution)/shard_map/ppermute | solution.py:409
  100.6 1.0 copy-start
  102.4 11.1 %copy-start.2 = (f32[64,512]{1,0:T(8,128)S(1)}, f32[64,512]{1,0:T(8,128)}, u32[]{:S(2)}) copy-start(f32[64,512]{1,0:T(8,128)} %get-tuple-element.61) | copy-start | bytes 393220
  102.5 5.7 %collective-permute-start.2 = (bf16[64,512]{1,0:T(8,128)(2,1)}, bf16[64,512]{1,0:T(8,128)(2,1)S(1)}, u32[]{:S(2)}, u32[]{:S(2)}) collective-permute-start(bf16[64,512]{1,0:T(8,128)(2,1)} %get-tuple-element.56), channel_id=1, source_target_pairs={{0,4},{1,5},{2,6},{3,7},{4,0},{5,1},{6,2},{7,3},{8,12},{9,13},{10,... | collective-permute-start | bytes 196616 | tf_op jit(solution)/shard_map/ppermute | solution.py:409
  103.3 10.3 %collective-permute-start.3 = (bf16[64,512]{1,0:T(8,128)(2,1)}, bf16[64,512]{1,0:T(8,128)(2,1)S(1)}, u32[]{:S(2)}, u32[]{:S(2)}) collective-permute-start(bf16[64,512]{1,0:T(8,128)(2,1)} %get-tuple-element.57), channel_id=1, source_target_pairs={{0,8},{1,9},{2,10},{3,11},{4,12},{5,13},{6,14},{7,15},{8,0},{9,1},... | collective-permute-start | bytes 196616 | tf_op jit(solution)/shard_map/ppermute | solution.py:409
  106.7 6.9 %collective-permute-start.4 = (bf16[64,512]{1,0:T(8,128)(2,1)}, bf16[64,512]{1,0:T(8,128)(2,1)S(1)}, u32[]{:S(2)}, u32[]{:S(2)}) collective-permute-start(bf16[64,512]{1,0:T(8,128)(2,1)} %get-tuple-element.58), channel_id=1, source_target_pairs={{0,12},{1,13},{2,14},{3,15},{4,8},{5,9},{6,10},{7,11},{8,4},{9,5},... | collective-permute-start | bytes 196616 | tf_op jit(solution)/shard_map/ppermute | solution.py:409
  113.6 9.0 %collective-permute-start.5 = (bf16[64,512]{1,0:T(8,128)(2,1)S(1)}, bf16[64,512]{1,0:T(8,128)(2,1)S(1)}, u32[]{:S(2)}, u32[]{:S(2)}) collective-permute-start(bf16[64,512]{1,0:T(8,128)(2,1)S(1)} %add_convert_fusion), channel_id=1, source_target_pairs={{0,4},{1,5},{2,6},{3,7},{4,0},{5,1},{6,2},{7,3},{8,12},{9,13},{10,... | collective-permute-start | bytes 196616 | tf_op jit(solution)/shard_map/ppermute | solution.py:409
  115.1 7.6 %collective-permute-start.6 = (bf16[64,512]{1,0:T(8,128)(2,1)S(1)}, bf16[64,512]{1,0:T(8,128)(2,1)S(1)}, u32[]{:S(2)}, u32[]{:S(2)}) collective-permute-start(bf16[64,512]{1,0:T(8,128)(2,1)S(1)} %add_convert_fusion), channel_id=1, source_target_pairs={{0,8},{1,9},{2,10},{3,11},{4,12},{5,13},{6,14},{7,15},{8,0},{9,1},... | collective-permute-start | bytes 196616 | tf_op jit(solution)/shard_map/ppermute | solution.py:409
  115.8 6.9 %collective-permute-start.7 = (bf16[64,512]{1,0:T(8,128)(2,1)S(1)}, bf16[64,512]{1,0:T(8,128)(2,1)S(1)}, u32[]{:S(2)}, u32[]{:S(2)}) collective-permute-start(bf16[64,512]{1,0:T(8,128)(2,1)S(1)} %add_convert_fusion), channel_id=1, source_target_pairs={{0,12},{1,13},{2,14},{3,15},{4,8},{5,9},{6,10},{7,11},{8,4},{9,5},... | collective-permute-start | bytes 196616 | tf_op jit(solution)/shard_map/ppermute | solution.py:409
  118.0 27.3 %all-to-all-start.3 = ((bf16[16,64,512]{2,1,0:T(8,128)(2,1)}), bf16[16,64,512]{2,1,0:T(8,128)(2,1)}, u32[]{:S(2)}, u32[]{:S(2)}) async-start(bf16[16,64,512]{2,1,0:T(8,128)(2,1)} %mix_second_back.1), calls=%async_computation.3 | async-start | bytes 2097152 | tf_op jit(solution)/shard_map/all_to_all | solution.py:513
  122.8 16.6 %collective-permute-start.8 = (bf16[256,512]{1,0:T(8,128)(2,1)S(1)}, bf16[256,512]{1,0:T(8,128)(2,1)S(1)}, u32[]{:S(2)}, u32[]{:S(2)}) collective-permute-start(bf16[256,512]{1,0:T(8,128)(2,1)S(1)} %bitcast.42), channel_id=1, source_target_pairs={{0,2},{1,3},{2,0},{3,1},{4,6},{5,7},{6,4},{7,5},{8,10},{9,11},{10,... | collective-permute-start | bytes 786440 | tf_op jit(solution)/shard_map/ppermute | solution.py:409
  139.5 2.0 %collective-permute-start.9 = (bf16[512,512]{1,0:T(8,128)(2,1)S(1)}, bf16[512,512]{1,0:T(8,128)(2,1)S(1)}, u32[]{:S(2)}, u32[]{:S(2)}) collective-permute-start(bf16[512,512]{1,0:T(8,128)(2,1)S(1)} %pad_maximum_fusion.1), channel_id=1, source_target_pairs={{0,1},{1,0},{2,3},{3,2},{4,5},{5,4},{6,7},{7,6},{8,9},{9,8},{10,11... | collective-permute-start | bytes 1572872 | tf_op jit(solution)/shard_map/ppermute | solution.py:409

commit v13 on v10

--- a/solution.py
+++ b/solution.py
@@ -51,7 +51,7 @@
 
 def mix_first(factor, blocked):
     block, channels = factor.shape[0], blocked.shape[1]
-    tiles = 4
+    tiles = 2
     step = block // tiles
 
     def body(f_hbm, x_hbm, u_hbm, f_all, x_all, u_all, sems):
@@ -299,25 +299,26 @@
         xs = row_copies(x_hbm, x, sems, tiles, tiles)
         fs = row_copies(f_hbm, f, sems, 2 * tiles, tiles)
         rs = row_copies(r_hbm, r, sems, 3 * tiles, tiles)
-        ones = row_copies(one, one_hbm, sems, 4 * tiles, tiles)
-        outs = row_copies(out, out_hbm, sems, 5 * tiles, tiles)
-        for c in xs + ds + fs + rs:
+        outs = row_copies(out, out_hbm, sems, 4 * tiles, 1)
+        ones = []
+        for c in ds + xs + fs + rs:
             c.start()
-        for c in xs:
+        for c in ds:
             c.wait()
         for t in range(tiles):
             at = slice(t * step, (t + 1) * step)
-            ds[t].wait()
-            one[at, :] = dot(d[at, :], x[...], 1, 1) * scale
+            xs[t].wait()
+            one[t] = dot(d[...], x[at, :], 1, 1) * scale
+            ones.append(
+                pltpu.make_async_copy(
+                    one.at[t], one_hbm.at[:, pl.ds(t * step, step)], sems.at[4 * tiles + 1 + t]
+                )
+            )
             ones[t].start()
-        for c in fs:
-            c.wait()
-        for t in range(tiles):
-            at = slice(t * step, (t + 1) * step)
-            rs[t].wait()
-            total = dot(f[:, at], d[...], 0, 0) + r[at, :].astype(F32)
-            out[at, :] = total.astype(BF)
-            outs[t].start()
+        for c in fs + rs:
+            c.wait()
+        out[...] = (dot(f[...], d[...], 0, 0) + r[...].astype(F32)).astype(BF)
+        outs[0].start()
         for c in ones + outs:
             c.wait()
 
@@ -331,9 +332,9 @@
             pltpu.VMEM((block, channels), BF),
             pltpu.VMEM((block, channels), BF),
             pltpu.VMEM((block, channels), BF),
-            pltpu.VMEM((block, block), F32),
+            pltpu.VMEM((tiles, block, step), F32),
             pltpu.VMEM((block, channels), BF),
-            pltpu.SemaphoreType.DMA((6 * tiles,)),
+            pltpu.SemaphoreType.DMA((5 * tiles + 1,)),
         ],
         compiler_params=params(0),
         cost_estimate=cost(4 * block * block * channels, 6 * block * block + 8 * block * channels),

time: 152 us -> 153 us (level)
  no operation moved by 1% of the time
where the time goes in v13:
time: 153 us; the launch traced here: 151 us
  waiting for transfers between devices  80.4 us (53%)
  starting transfers between devices  38.6 us (25%)
  Pallas kernels  28.4 us (19%)
  local copies, waits for them, and re-layouts  2.64 us (2%)
    all_to_all x4, waiting for transfers between devices, exchange(): return lax.all_to_all(cut, 'seq', split_axis=0, concat_axis=0, tiled=True)  46.6 us
    ppermute x10, waiting for transfers between devices, swap(): lax.ppermute(values, 'seq', [(i, i ^ stride * s) for i in range(count)])  33.8 us
    all_to_all x4, starting transfers between devices, exchange(): return lax.all_to_all(cut, 'seq', split_axis=0, concat_axis=0, tiled=True)  25.7 us
    ppermute x10, starting transfers between devices, swap(): lax.ppermute(values, 'seq', [(i, i ^ stride * s) for i in range(count)])  12.9 us
    pallas_call x1, Pallas kernels, middle(): pl.pallas_call(body, in_specs=[SCALAR, ANY, ANY, VMEM, ANY, ANY], out_spe...  8.52 us
    pallas_call x1, Pallas kernels, finish(): pl.pallas_call(body, in_specs=[ANY] * 4, out_specs=[ANY] * 2, out_shape=[...  6.61 us
    pallas_call x1, Pallas kernels, mix_first(): pl.pallas_call(body, in_specs=[ANY, ANY], out_specs=ANY, out_shape=pltpu....  3.81 us
  transfers between devices with their start and end apart: 14, of which 9 were waited for; matrix products, arithmetic and copies ran while one was open for 1% of the time, Pallas kernels for 5%

profile of v13, /device:TPU:0, one launch (start us, length us, event | category | flops | bytes accessed | tf_op | source)
XLA Modules:
  0.0 151.2 jit_solution(1087967755362954552)
XLA Ops:
  0.6 3.8 %mix_first.1 = bf16[1024,512]{1,0:T(8,128)(2,1)} custom-call(bf16[1024,1024]{1,0:T(8,128)(2,1)} %bitcast.39, bf16[1024,512]{1,0:T(8,128)(2,1)} %x_hbm.5), custom_call_target="tpu_custom_call" | custom-call | flops 1073741824 | bytes 4194304 | tf_op jit(solution)/shard_map/mix_first/pallas_call | solution.py:73
  4.5 0.0 copy-start.3
  4.5 7.5 %all-to-all-start = ((bf16[16,64,512]{2,1,0:T(8,128)(2,1)}), bf16[16,64,512]{2,1,0:T(8,128)(2,1)S(1)}, u32[]{:S(2)}, u32[]{:S(2)}) async-start(bf16[16,64,512]{2,1,0:T(8,128)(2,1)} %bitcast.38), calls=%async_computation | async-start | bytes 2097152 | tf_op jit(solution)/shard_map/all_to_all | solution.py:459
  12.0 0.2 reshape.62
  12.1 0.2 copy.11
  12.4 0.7 spread_factor.1.m_ref
  13.1 21.9 %all-to-all-done.in_ref.u_ref = bf16[16,64,512]{2,1,0:T(8,128)(2,1)S(1)} async-done(((bf16[16,64,512]{2,1,0:T(8,128)(2,1)}), bf16[16,64,512]{2,1,0:T(8,128)(2,1)S(1)}, u32[]{:S(2)}, u32[]{:S(2)}) %all-to-all-start) | async-done | bytes 1048608 | tf_op jit(solution)/shard_map/all_to_all | solution.py:459
  34.9 1.2 mix_second.1
  36.1 6.9 %all-to-all-start.1 = ((bf16[16,64,512]{2,1,0:T(8,128)(2,1)}), bf16[16,64,512]{2,1,0:T(8,128)(2,1)S(1)}, u32[]{:S(2)}, u32[]{:S(2)}) async-start(bf16[16,64,512]{2,1,0:T(8,128)(2,1)} %mix_second.1), calls=%async_computation.1 | async-start | bytes 2097152 | tf_op jit(solution)/shard_map/all_to_all | solution.py:459
  43.0 22.9 %all-to-all-done.1 = bf16[16,64,512]{2,1,0:T(8,128)(2,1)S(1)} async-done(((bf16[16,64,512]{2,1,0:T(8,128)(2,1)}), bf16[16,64,512]{2,1,0:T(8,128)(2,1)S(1)}, u32[]{:S(2)}, u32[]{:S(2)}) %all-to-all-start.1) | async-done | bytes 1048608 | tf_op jit(solution)/shard_map/all_to_all | solution.py:459
  66.0 8.5 %middle.1 = (bf16[1024,512]{1,0:T(8,128)(2,1)}, bf16[1024,512]{1,0:T(8,128)(2,1)}, bf16[4,128,512]{2,1,0:T(8,128)(2,1)}, bf16[4,128,512]{2,1,0:T(8,128)(2,1)}) custom-call(s32[1]{0:T(128)} %bitcast.3.half_ref, bf16[1024,512]{1,0:T(8,128)(2,1)} %x_hbm.5, bf16[1024,512]{1,0:T(8,128)(2,1)} %g_hbm.1, bf16[1024,512]{1,0:T(8,128)(2,1)S(1)} %bitcast.34, ...), custom_call_target="tpu_custom_call" | custom-call | flops 2684354560 | bytes 7340032 | tf_op jit(solution)/shard_map/middle/pallas_call | solution.py:263
  74.5 0.0 copy-start.1
  74.5 7.0 %all-to-all-start.2 = ((bf16[16,64,512]{2,1,0:T(8,128)(2,1)}), bf16[16,64,512]{2,1,0:T(8,128)(2,1)S(1)}, u32[]{:S(2)}, u32[]{:S(2)}) async-start(bf16[16,64,512]{2,1,0:T(8,128)(2,1)} %bitcast.41), calls=%async_computation.2 | async-start | bytes 2097152 | tf_op jit(solution)/shard_map/all_to_all | solution.py:459
  81.5 0.4 collective-permute-start
  82.0 1.9 %collective-permute-done = bf16[4,128,512]{2,1,0:T(8,128)(2,1)} collective-permute-done((bf16[4,128,512]{2,1,0:T(8,128)(2,1)}, bf16[4,128,512]{2,1,0:T(8,128)(2,1)}, u32[]{:S(2)}, u32[]{:S(2)}) %collective-permute-start) | collective-permute-done | bytes 524320 | tf_op jit(solution)/shard_map/ppermute | solution.py:355
  83.9 2.0 %add_and_cut.2 = (f32[256,512]{1,0:T(8,128)}, bf16[256,512]{1,0:T(8,128)(2,1)}) custom-call(s32[1]{0:T(128)} %bitcast.2.digit_ref, bf16[2,256,512]{2,1,0:T(8,128)(2,1)S(1)} %bitcast.36, bf16[2,256,512]{2,1,0:T(8,128)(2,1)} %bitcast.9.refs_1_), custom_call_target="tpu_custom_call" | custom-call | flops 262144 | bytes 2097152 | tf_op jit(solution)/shard_map/add_and_cut/pallas_call | solution.py:387
  85.9 1.9 %collective-permute-start.1 = (bf16[256,512]{1,0:T(8,128)(2,1)}, bf16[256,512]{1,0:T(8,128)(2,1)S(1)}, u32[]{:S(2)}, u32[]{:S(2)}) collective-permute-start(bf16[256,512]{1,0:T(8,128)(2,1)} %get-tuple-element.37), channel_id=1, source_target_pairs={{0,2},{1,3},{2,0},{3,1},{4,6},{5,7},{6,4},{7,5},{8,10},{9,11},{10,... | collective-permute-start | bytes 786440 | tf_op jit(solution)/shard_map/ppermute | solution.py:355
  87.8 12.0 %collective-permute-done.1 = bf16[256,512]{1,0:T(8,128)(2,1)S(1)} collective-permute-done((bf16[256,512]{1,0:T(8,128)(2,1)}, bf16[256,512]{1,0:T(8,128)(2,1)S(1)}, u32[]{:S(2)}, u32[]{:S(2)}) %collective-permute-start.1) | collective-permute-done | bytes 262176 | tf_op jit(solution)/shard_map/ppermute | solution.py:355
  99.8 1.0 copy-done
  100.8 0.8 add_and_cut.3
  101.7 0.0 copy-start.2
  101.7 0.8 collective-permute-start.2
  102.5 3.4 %collective-permute-start.3 = (bf16[64,512]{1,0:T(8,128)(2,1)}, bf16[64,512]{1,0:T(8,128)(2,1)S(1)}, u32[]{:S(2)}, u32[]{:S(2)}) collective-permute-start(bf16[64,512]{1,0:T(8,128)(2,1)} %get-tuple-element.40), channel_id=1, source_target_pairs={{0,8},{1,9},{2,10},{3,11},{4,12},{5,13},{6,14},{7,15},{8,0},{9,1},... | collective-permute-start | bytes 196616 | tf_op jit(solution)/shard_map/ppermute | solution.py:355
  105.9 0.2 collective-permute-start.4
  106.2 0.0 all-to-all-done.2.in_ref.g_ref
  106.2 1.3 mix_second_back.1
  107.4 0.0 collective-permute-done.2
  107.4 5.4 %collective-permute-done.3 = bf16[64,512]{1,0:T(8,128)(2,1)S(1)} collective-permute-done((bf16[64,512]{1,0:T(8,128)(2,1)}, bf16[64,512]{1,0:T(8,128)(2,1)S(1)}, u32[]{:S(2)}, u32[]{:S(2)}) %collective-permute-start.3) | collective-permute-done | bytes 65568 | tf_op jit(solution)/shard_map/ppermute | solution.py:355
  112.8 0.0 collective-permute-done.4
  112.8 1.6 %collective-permute-start.5 = (bf16[64,512]{1,0:T(8,128)(2,1)S(1)}, bf16[64,512]{1,0:T(8,128)(2,1)S(1)}, u32[]{:S(2)}, u32[]{:S(2)}) collective-permute-start(bf16[64,512]{1,0:T(8,128)(2,1)S(1)} %add_convert_fusion), channel_id=1, source_target_pairs={{0,4},{1,5},{2,6},{3,7},{4,0},{5,1},{6,2},{7,3},{8,12},{9,13},{10,... | collective-permute-start | bytes 196616 | tf_op jit(solution)/shard_map/ppermute | solution.py:355
  114.4 0.7 collective-permute-start.6
  115.0 2.2 %collective-permute-start.7 = (bf16[64,512]{1,0:T(8,128)(2,1)S(1)}, bf16[64,512]{1,0:T(8,128)(2,1)S(1)}, u32[]{:S(2)}, u32[]{:S(2)}) collective-permute-start(bf16[64,512]{1,0:T(8,128)(2,1)S(1)} %add_convert_fusion), channel_id=1, source_target_pairs={{0,12},{1,13},{2,14},{3,15},{4,8},{5,9},{6,10},{7,11},{8,4},{9,5},... | collective-permute-start | bytes 196616 | tf_op jit(solution)/shard_map/ppermute | solution.py:355
  117.3 4.3 %all-to-all-start.3 = ((bf16[16,64,512]{2,1,0:T(8,128)(2,1)}), bf16[16,64,512]{2,1,0:T(8,128)(2,1)}, u32[]{:S(2)}, u32[]{:S(2)}) async-start(bf16[16,64,512]{2,1,0:T(8,128)(2,1)} %mix_second_back.1), calls=%async_computation.3 | async-start | bytes 2097152 | tf_op jit(solution)/shard_map/all_to_all | solution.py:459
  121.6 0.0 collective-permute-done.5
  121.6 0.3 collective-permute-done.6
  121.9 0.0 collective-permute-done.7
  122.0 1.5 %collective-permute-start.8 = (bf16[256,512]{1,0:T(8,128)(2,1)S(1)}, bf16[256,512]{1,0:T(8,128)(2,1)S(1)}, u32[]{:S(2)}, u32[]{:S(2)}) collective-permute-start(bf16[256,512]{1,0:T(8,128)(2,1)S(1)} %bitcast.42), channel_id=1, source_target_pairs={{0,2},{1,3},{2,0},{3,1},{4,6},{5,7},{6,4},{7,5},{8,10},{9,11},{10,... | collective-permute-start | bytes 786440 | tf_op jit(solution)/shard_map/ppermute | solution.py:355
  123.6 1.5 grad_second.1
  125.1 0.2 copy.12
  125.3 0.9 reshape.72
  126.3 12.4 %collective-permute-done.8 = bf16[256,512]{1,0:T(8,128)(2,1)S(1)} collective-permute-done((bf16[256,512]{1,0:T(8,128)(2,1)S(1)}, bf16[256,512]{1,0:T(8,128)(2,1)S(1)}, u32[]{:S(2)}, u32[]{:S(2)}) %collective-permute-start.8) | collective-permute-done | bytes 262176 | tf_op jit(solution)/shard_map/ppermute | solution.py:355
  138.7 0.1 collective-permute-start.9
  138.8 1.9 %collective-permute-done.9 = bf16[512,512]{1,0:T(8,128)(2,1)S(1)} collective-permute-done((bf16[512,512]{1,0:T(8,128)(2,1)S(1)}, bf16[512,512]{1,0:T(8,128)(2,1)S(1)}, u32[]{:S(2)}, u32[]{:S(2)}) %collective-permute-start.9) | collective-permute-done | bytes 524320 | tf_op jit(solution)/shard_map/ppermute | solution.py:355
  140.7 0.1 broadcast_select_fusion.1
  140.8 0.1 pad_maximum_fusion.up_in.down_in
  140.8 1.9 %write_weights.1 = (f32[4,128,512]{2,1,0:T(8,128)}, f32[4,512,128]{2,1,0:T(8,128)}) custom-call(bf16[1024,512]{1,0:T(8,128)(2,1)S(1)} %pad_maximum_fusion.up_in.down_in, bf16[1024,512]{1,0:T(8,128)(2,1)S(1)} %pad_maximum_fusion.up_in.down_in), custom_call_target="tpu_custom_call" | custom-call | flops 262144 | bytes 3145728 | tf_op jit(solution)/shard_map/write_weights/pallas_call | solution.py:428
  142.8 1.8 %all-to-all-done.3 = bf16[16,64,512]{2,1,0:T(8,128)(2,1)} async-done(((bf16[16,64,512]{2,1,0:T(8,128)(2,1)}), bf16[16,64,512]{2,1,0:T(8,128)(2,1)}, u32[]{:S(2)}, u32[]{:S(2)}) %all-to-all-start.3) | async-done | bytes 1048608 | tf_op jit(solution)/shard_map/all_to_all | solution.py:459
  144.6 6.6 %finish.1 = (f32[1024,1024]{1,0:T(8,128)}, bf16[1024,512]{1,0:T(8,128)(2,1)}) custom-call(bf16[1024,1024]{1,0:T(8,128)(2,1)} %bitcast.40, bf16[1024,512]{1,0:T(8,128)(2,1)} %bitcast.13.d_hbm, bf16[1024,512]{1,0:T(8,128)(2,1)} %x_hbm.5, bf16[1024,512]{1,0:T(8,128)(2,1)} %get-tuple-element.49.r_hbm), custom_call_target="tpu_custom_call" | custom-call | flops 2147483648 | bytes 10485760 | tf_op jit(solution)/shard_map/finish/pallas_call | solution.py:325
  (12 shorter events, 0.2 us)
Async XLA Ops:
  4.5 7.5 %copy-start.3 = (bf16[64,16,16]{0,2,1:T(8,128)(2,1)S(1)}, bf16[64,16,16]{0,2,1:T(8,128)(2,1)}, u32[]{:S(2)}) copy-start(bf16[64,16,16]{0,2,1:T(8,128)(2,1)} %param.9) | copy-start | bytes 98308
  4.5 30.4 %all-to-all-start = ((bf16[16,64,512]{2,1,0:T(8,128)(2,1)}), bf16[16,64,512]{2,1,0:T(8,128)(2,1)S(1)}, u32[]{:S(2)}, u32[]{:S(2)}) async-start(bf16[16,64,512]{2,1,0:T(8,128)(2,1)} %bitcast.38), calls=%async_computation | async-start | bytes 2097152 | tf_op jit(solution)/shard_map/all_to_all | solution.py:459
  36.1 29.8 %all-to-all-start.1 = ((bf16[16,64,512]{2,1,0:T(8,128)(2,1)}), bf16[16,64,512]{2,1,0:T(8,128)(2,1)S(1)}, u32[]{:S(2)}, u32[]{:S(2)}) async-start(bf16[16,64,512]{2,1,0:T(8,128)(2,1)} %mix_second.1), calls=%async_computation.1 | async-start | bytes 2097152 | tf_op jit(solution)/shard_map/all_to_all | solution.py:459
  74.5 9.4 %copy-start.1 = (bf16[4,128,512]{2,1,0:T(8,128)(2,1)S(1)}, bf16[4,128,512]{2,1,0:T(8,128)(2,1)}, u32[]{:S(2)}) copy-start(bf16[4,128,512]{2,1,0:T(8,128)(2,1)} %get-tuple-element.34) | copy-start | bytes 1572868
  74.5 31.6 %all-to-all-start.2 = ((bf16[16,64,512]{2,1,0:T(8,128)(2,1)}), bf16[16,64,512]{2,1,0:T(8,128)(2,1)S(1)}, u32[]{:S(2)}, u32[]{:S(2)}) async-start(bf16[16,64,512]{2,1,0:T(8,128)(2,1)} %bitcast.41), calls=%async_computation.2 | async-start | bytes 2097152 | tf_op jit(solution)/shard_map/all_to_all | solution.py:459
  81.5 2.3 %collective-permute-start = (bf16[4,128,512]{2,1,0:T(8,128)(2,1)}, bf16[4,128,512]{2,1,0:T(8,128)(2,1)}, u32[]{:S(2)}, u32[]{:S(2)}) collective-permute-start(bf16[4,128,512]{2,1,0:T(8,128)(2,1)} %get-tuple-element.35), channel_id=1, source_target_pairs={{0,1},{1,0},{2,3},{3,2},{4,5},{5,4},{6,7},{7,6},{8,9},{9,8},{10,11... | collective-permute-start | bytes 1572872 | tf_op jit(solution)/shard_map/ppermute | solution.py:355
  85.9 13.9 %collective-permute-start.1 = (bf16[256,512]{1,0:T(8,128)(2,1)}, bf16[256,512]{1,0:T(8,128)(2,1)S(1)}, u32[]{:S(2)}, u32[]{:S(2)}) collective-permute-start(bf16[256,512]{1,0:T(8,128)(2,1)} %get-tuple-element.37), channel_id=1, source_target_pairs={{0,2},{1,3},{2,0},{3,1},{4,6},{5,7},{6,4},{7,5},{8,10},{9,11},{10,... | collective-permute-start | bytes 786440 | tf_op jit(solution)/shard_map/ppermute | solution.py:355
  99.8 1.0 copy-start
  101.7 11.1 %copy-start.2 = (f32[64,512]{1,0:T(8,128)S(1)}, f32[64,512]{1,0:T(8,128)}, u32[]{:S(2)}) copy-start(f32[64,512]{1,0:T(8,128)} %get-tuple-element.44) | copy-start | bytes 393220
  101.7 5.7 %collective-permute-start.2 = (bf16[64,512]{1,0:T(8,128)(2,1)}, bf16[64,512]{1,0:T(8,128)(2,1)S(1)}, u32[]{:S(2)}, u32[]{:S(2)}) collective-permute-start(bf16[64,512]{1,0:T(8,128)(2,1)} %get-tuple-element.39), channel_id=1, source_target_pairs={{0,4},{1,5},{2,6},{3,7},{4,0},{5,1},{6,2},{7,3},{8,12},{9,13},{10,... | collective-permute-start | bytes 196616 | tf_op jit(solution)/shard_map/ppermute | solution.py:355
  102.5 10.3 %collective-permute-start.3 = (bf16[64,512]{1,0:T(8,128)(2,1)}, bf16[64,512]{1,0:T(8,128)(2,1)S(1)}, u32[]{:S(2)}, u32[]{:S(2)}) collective-permute-start(bf16[64,512]{1,0:T(8,128)(2,1)} %get-tuple-element.40), channel_id=1, source_target_pairs={{0,8},{1,9},{2,10},{3,11},{4,12},{5,13},{6,14},{7,15},{8,0},{9,1},... | collective-permute-start | bytes 196616 | tf_op jit(solution)/shard_map/ppermute | solution.py:355
  105.9 6.9 %collective-permute-start.4 = (bf16[64,512]{1,0:T(8,128)(2,1)}, bf16[64,512]{1,0:T(8,128)(2,1)S(1)}, u32[]{:S(2)}, u32[]{:S(2)}) collective-permute-start(bf16[64,512]{1,0:T(8,128)(2,1)} %get-tuple-element.41), channel_id=1, source_target_pairs={{0,12},{1,13},{2,14},{3,15},{4,8},{5,9},{6,10},{7,11},{8,4},{9,5},... | collective-permute-start | bytes 196616 | tf_op jit(solution)/shard_map/ppermute | solution.py:355
  112.8 8.8 %collective-permute-start.5 = (bf16[64,512]{1,0:T(8,128)(2,1)S(1)}, bf16[64,512]{1,0:T(8,128)(2,1)S(1)}, u32[]{:S(2)}, u32[]{:S(2)}) collective-permute-start(bf16[64,512]{1,0:T(8,128)(2,1)S(1)} %add_convert_fusion), channel_id=1, source_target_pairs={{0,4},{1,5},{2,6},{3,7},{4,0},{5,1},{6,2},{7,3},{8,12},{9,13},{10,... | collective-permute-start | bytes 196616 | tf_op jit(solution)/shard_map/ppermute | solution.py:355
  114.4 7.6 %collective-permute-start.6 = (bf16[64,512]{1,0:T(8,128)(2,1)S(1)}, bf16[64,512]{1,0:T(8,128)(2,1)S(1)}, u32[]{:S(2)}, u32[]{:S(2)}) collective-permute-start(bf16[64,512]{1,0:T(8,128)(2,1)S(1)} %add_convert_fusion), channel_id=1, source_target_pairs={{0,8},{1,9},{2,10},{3,11},{4,12},{5,13},{6,14},{7,15},{8,0},{9,1},... | collective-permute-start | bytes 196616 | tf_op jit(solution)/shard_map/ppermute | solution.py:355
  115.0 6.9 %collective-permute-start.7 = (bf16[64,512]{1,0:T(8,128)(2,1)S(1)}, bf16[64,512]{1,0:T(8,128)(2,1)S(1)}, u32[]{:S(2)}, u32[]{:S(2)}) collective-permute-start(bf16[64,512]{1,0:T(8,128)(2,1)S(1)} %add_convert_fusion), channel_id=1, source_target_pairs={{0,12},{1,13},{2,14},{3,15},{4,8},{5,9},{6,10},{7,11},{8,4},{9,5},... | collective-permute-start | bytes 196616 | tf_op jit(solution)/shard_map/ppermute | solution.py:355
  117.3 27.3 %all-to-all-start.3 = ((bf16[16,64,512]{2,1,0:T(8,128)(2,1)}), bf16[16,64,512]{2,1,0:T(8,128)(2,1)}, u32[]{:S(2)}, u32[]{:S(2)}) async-start(bf16[16,64,512]{2,1,0:T(8,128)(2,1)} %mix_second_back.1), calls=%async_computation.3 | async-start | bytes 2097152 | tf_op jit(solution)/shard_map/all_to_all | solution.py:459
  122.0 16.6 %collective-permute-start.8 = (bf16[256,512]{1,0:T(8,128)(2,1)S(1)}, bf16[256,512]{1,0:T(8,128)(2,1)S(1)}, u32[]{:S(2)}, u32[]{:S(2)}) collective-permute-start(bf16[256,512]{1,0:T(8,128)(2,1)S(1)} %bitcast.42), channel_id=1, source_target_pairs={{0,2},{1,3},{2,0},{3,1},{4,6},{5,7},{6,4},{7,5},{8,10},{9,11},{10,... | collective-permute-start | bytes 786440 | tf_op jit(solution)/shard_map/ppermute | solution.py:355
  138.7 2.0 %collective-permute-start.9 = (bf16[512,512]{1,0:T(8,128)(2,1)S(1)}, bf16[512,512]{1,0:T(8,128)(2,1)S(1)}, u32[]{:S(2)}, u32[]{:S(2)}) collective-permute-start(bf16[512,512]{1,0:T(8,128)(2,1)S(1)} %pad_maximum_fusion.1), channel_id=1, source_target_pairs={{0,1},{1,0},{2,3},{3,2},{4,5},{5,4},{6,7},{7,6},{8,9},{9,8},{10,11... | collective-permute-start | bytes 1572872 | tf_op jit(solution)/shard_map/ppermute | solution.py:355

commit v14 on v10

--- a/solution.py
+++ b/solution.py
@@ -403,9 +403,11 @@
     return [kept] + [swap(a, count, stride, s + 1) for s, a in enumerate(send)]
 
 
-def gather_step(share, count, stride, radix, after=()):
+def gather_step(share, count, stride, radix, before=(), after=()):
     digit = (lax.axis_index("seq") // stride) % radix
-    got = [share] + [swap(share, count, stride, s) for s in range(1, radix)]
+    near, before = lax.optimization_barrier((share, before))
+    far = [swap(share, count, stride, s) for s in range(2, radix)]
+    got = [share, swap(near, count, stride, 1)] + far
     got, after = lax.optimization_barrier((got, after))
     if radix == 2:
         low = jnp.where(digit == 0, got[0], got[1])
@@ -417,20 +419,20 @@
     return whole.reshape(radix * share.shape[0], share.shape[1])
 
 
-def write_weights(total, up_shape, down_shape, scale):
+def write_weights(half, mine, other, up_shape, down_shape, scale):
     groups, width, inner = up_shape
 
-    def body(up_in, down_in, up_ref, down_ref):
-        up_ref[0] = up_in[...].astype(F32) * scale
-        down_ref[0] = (down_in[...].astype(F32) * scale).T
-
+    def body(half_ref, mine_ref, other_ref, up_ref, down_ref):
+        first = half_ref[0] == 0
+        a, b = mine_ref[...].astype(F32) * scale, other_ref[...].astype(F32) * scale
+        up_ref[0] = jnp.where(first, a, b)
+        down_ref[0] = jnp.where(first, b, a).T
+
+    block = pl.BlockSpec((width, inner), lambda b: (b, 0))
     return pl.pallas_call(
         body,
         grid=(groups,),
-        in_specs=[
-            pl.BlockSpec((width, inner), lambda b: (b, 0)),
-            pl.BlockSpec((width, inner), lambda b: (groups + b, 0)),
-        ],
+        in_specs=[SCALAR, block, block],
         out_specs=[
             pl.BlockSpec((1, width, inner), lambda b: (b, 0, 0)),
             pl.BlockSpec((1, inner, width), lambda b: (b, 0, 0)),
@@ -442,7 +444,7 @@
         compiler_params=params(),
         cost_estimate=cost(groups * width * inner, 12 * groups * width * inner),
         name="write_weights",
-    )(total, total)
+    )(half, mine, other)
 
 
 def on_device(tokens, cotangent, factor_one, factor_two, up_blocks, down_blocks):
@@ -487,9 +489,13 @@
     back, total = lax.optimization_barrier((back, total))
     grad_first = exchange(back).reshape(block, channels)
     two = second_grad(grad_mixed, firsts)
-    for step in reversed(steps):
-        total = gather_step(total, count, *step, after=two if step == steps[1] else ())
-    grad_up, grad_down = write_weights(total, up_blocks.shape, down_blocks.shape, scale)
+    for step in reversed(steps[1:]):
+        last = step == steps[-1]
+        total = gather_step(
+            total, count, *step, before=two if last else (), after=() if last else two
+        )
+    other = swap(total, count, 1, 1)
+    grad_up, grad_down = write_weights(half, total, other, up_blocks.shape, down_blocks.shape, scale)
     one, grad_tokens = finish(factor, grad_first, tokens, gate_grad, scale)
     return (grad_tokens, one.reshape(1, block, block), two, grad_up, grad_down)
 

time: 152 us -> 156 us (1.026)
  waiting for transfers between devices: 80.3 us -> 83.3 us
  local copies, waits for them, and re-layouts: 2.64 us -> 4.61 us
    ppermute x10, waiting for transfers between devices: 33.8 us -> 36.6 us  [swap(): lax.ppermute(values, 'seq', [(i, i ^ stride * s) for i in range(count)])]
    unnamed x8, local copies, waits for them, and re-layouts: 1.06 us -> 3.03 us
  transfers between devices with their start and end apart: 14 -> 14, of which waited for: 9 -> 9; matrix products, arithmetic and copies ran while one was open for 1% -> 0% of each run, Pallas kernels for 5% -> 4%
where the time goes in v14:
time: 156 us; the launch traced here: 154 us
  waiting for transfers between devices  83.3 us (53%)
  starting transfers between devices  37.7 us (24%)
  Pallas kernels  26.8 us (17%)
  local copies, waits for them, and re-layouts  4.61 us (3%)
    all_to_all x4, waiting for transfers between devices, exchange(): return lax.all_to_all(cut, 'seq', split_axis=0, concat_axis=0, tiled=True)  46.6 us
    ppermute x10, waiting for transfers between devices, swap(): lax.ppermute(values, 'seq', [(i, i ^ stride * s) for i in range(count)])  36.6 us
    all_to_all x4, starting transfers between devices, exchange(): return lax.all_to_all(cut, 'seq', split_axis=0, concat_axis=0, tiled=True)  24.9 us
    ppermute x10, starting transfers between devices, swap(): lax.ppermute(values, 'seq', [(i, i ^ stride * s) for i in range(count)])  12.8 us
    pallas_call x1, Pallas kernels, middle(): pl.pallas_call(body, in_specs=[SCALAR, ANY, ANY, VMEM, ANY, ANY], out_spe...  8.51 us
    pallas_call x1, Pallas kernels, finish(): pl.pallas_call(body, in_specs=[ANY] * 4, out_specs=[ANY] * 2, out_shape=[...  5.99 us
    pallas_call x1, Pallas kernels, mix_first(): pl.pallas_call(body, in_specs=[ANY, ANY], out_specs=ANY, out_shape=pltpu....  3.95 us
  transfers between devices with their start and end apart: 14, of which 9 were waited for; matrix products, arithmetic and copies ran while one was open for 0% of the time, Pallas kernels for 4%

profile of v14, /device:TPU:0, one launch (start us, length us, event | category | flops | bytes accessed | tf_op | source)
XLA Modules:
  0.0 154.3 jit_solution(17016425607119233626)
XLA Ops:
  0.6 0.0 copy-start.3
  0.6 4.0 %mix_first.1 = bf16[1024,512]{1,0:T(8,128)(2,1)} custom-call(bf16[1024,1024]{1,0:T(8,128)(2,1)} %bitcast.40, bf16[1024,512]{1,0:T(8,128)(2,1)} %x_hbm.5), custom_call_target="tpu_custom_call" | custom-call | flops 1073741824 | bytes 4194304 | tf_op jit(solution)/shard_map/mix_first/pallas_call | solution.py:73
  4.6 7.4 %all-to-all-start = ((bf16[16,64,512]{2,1,0:T(8,128)(2,1)}), bf16[16,64,512]{2,1,0:T(8,128)(2,1)S(1)}, u32[]{:S(2)}, u32[]{:S(2)}) async-start(bf16[16,64,512]{2,1,0:T(8,128)(2,1)} %bitcast.39), calls=%async_computation | async-start | bytes 2097152 | tf_op jit(solution)/shard_map/all_to_all | solution.py:460
  12.0 0.0 copy-done.3
  12.0 0.2 reshape.62
  12.1 0.2 copy.11
  12.4 0.7 spread_factor.1.m_ref
  13.1 21.9 %all-to-all-done.in_ref.u_ref = bf16[16,64,512]{2,1,0:T(8,128)(2,1)S(1)} async-done(((bf16[16,64,512]{2,1,0:T(8,128)(2,1)}), bf16[16,64,512]{2,1,0:T(8,128)(2,1)S(1)}, u32[]{:S(2)}, u32[]{:S(2)}) %all-to-all-start) | async-done | bytes 1048608 | tf_op jit(solution)/shard_map/all_to_all | solution.py:460
  34.9 1.2 mix_second.1
  36.2 6.9 %all-to-all-start.1 = ((bf16[16,64,512]{2,1,0:T(8,128)(2,1)}), bf16[16,64,512]{2,1,0:T(8,128)(2,1)S(1)}, u32[]{:S(2)}, u32[]{:S(2)}) async-start(bf16[16,64,512]{2,1,0:T(8,128)(2,1)} %mix_second.1), calls=%async_computation.1 | async-start | bytes 2097152 | tf_op jit(solution)/shard_map/all_to_all | solution.py:460
  43.1 22.9 %all-to-all-done.1 = bf16[16,64,512]{2,1,0:T(8,128)(2,1)S(1)} async-done(((bf16[16,64,512]{2,1,0:T(8,128)(2,1)}), bf16[16,64,512]{2,1,0:T(8,128)(2,1)S(1)}, u32[]{:S(2)}, u32[]{:S(2)}) %all-to-all-start.1) | async-done | bytes 1048608 | tf_op jit(solution)/shard_map/all_to_all | solution.py:460
  66.0 8.5 %middle.1 = (bf16[1024,512]{1,0:T(8,128)(2,1)}, bf16[1024,512]{1,0:T(8,128)(2,1)}, bf16[4,128,512]{2,1,0:T(8,128)(2,1)}, bf16[4,128,512]{2,1,0:T(8,128)(2,1)}) custom-call(s32[1]{0:T(128)} %bitcast.3.half_ref, bf16[1024,512]{1,0:T(8,128)(2,1)} %x_hbm.5, bf16[1024,512]{1,0:T(8,128)(2,1)} %g_hbm.1, bf16[1024,512]{1,0:T(8,128)(2,1)S(1)} %bitcast.34, ...), custom_call_target="tpu_custom_call" | custom-call | flops 2684354560 | bytes 7340032 | tf_op jit(solution)/shard_map/middle/pallas_call | solution.py:263
  74.5 6.9 %all-to-all-start.2 = ((bf16[16,64,512]{2,1,0:T(8,128)(2,1)}), bf16[16,64,512]{2,1,0:T(8,128)(2,1)S(1)}, u32[]{:S(2)}, u32[]{:S(2)}) async-start(bf16[16,64,512]{2,1,0:T(8,128)(2,1)} %bitcast.42), calls=%async_computation.2 | async-start | bytes 2097152 | tf_op jit(solution)/shard_map/all_to_all | solution.py:460
  81.4 0.4 collective-permute-start
  81.8 1.8 %collective-permute-done = bf16[4,128,512]{2,1,0:T(8,128)(2,1)S(1)} collective-permute-done((bf16[4,128,512]{2,1,0:T(8,128)(2,1)}, bf16[4,128,512]{2,1,0:T(8,128)(2,1)S(1)}, u32[]{:S(2)}, u32[]{:S(2)}) %collective-permute-start) | collective-permute-done | bytes 524320 | tf_op jit(solution)/shard_map/ppermute | solution.py:354
  83.6 1.0 copy-done.1
  84.6 1.0 add_and_cut.2
  85.7 1.9 %collective-permute-start.1 = (bf16[256,512]{1,0:T(8,128)(2,1)}, bf16[256,512]{1,0:T(8,128)(2,1)S(1)}, u32[]{:S(2)}, u32[]{:S(2)}) collective-permute-start(bf16[256,512]{1,0:T(8,128)(2,1)} %get-tuple-element.36), channel_id=1, source_target_pairs={{0,2},{1,3},{2,0},{3,1},{4,6},{5,7},{6,4},{7,5},{8,10},{9,11},{10,... | collective-permute-start | bytes 786440 | tf_op jit(solution)/shard_map/ppermute | solution.py:354
  87.6 12.0 %collective-permute-done.1 = bf16[256,512]{1,0:T(8,128)(2,1)S(1)} collective-permute-done((bf16[256,512]{1,0:T(8,128)(2,1)}, bf16[256,512]{1,0:T(8,128)(2,1)S(1)}, u32[]{:S(2)}, u32[]{:S(2)}) %collective-permute-start.1) | collective-permute-done | bytes 262176 | tf_op jit(solution)/shard_map/ppermute | solution.py:354
  99.6 1.0 copy-done
  100.7 0.8 add_and_cut.3
  101.5 0.8 collective-permute-start.2
  102.3 3.5 %collective-permute-start.3 = (bf16[64,512]{1,0:T(8,128)(2,1)}, bf16[64,512]{1,0:T(8,128)(2,1)S(1)}, u32[]{:S(2)}, u32[]{:S(2)}) collective-permute-start(bf16[64,512]{1,0:T(8,128)(2,1)} %get-tuple-element.39), channel_id=1, source_target_pairs={{0,8},{1,9},{2,10},{3,11},{4,12},{5,13},{6,14},{7,15},{8,0},{9,1},... | collective-permute-start | bytes 196616 | tf_op jit(solution)/shard_map/ppermute | solution.py:354
  105.7 0.2 collective-permute-start.4
  105.9 0.0 all-to-all-done.2.in_ref.g_ref
  106.0 1.3 mix_second_back.1
  107.2 0.0 collective-permute-done.2
  107.2 5.4 %collective-permute-done.3 = bf16[64,512]{1,0:T(8,128)(2,1)S(1)} collective-permute-done((bf16[64,512]{1,0:T(8,128)(2,1)}, bf16[64,512]{1,0:T(8,128)(2,1)S(1)}, u32[]{:S(2)}, u32[]{:S(2)}) %collective-permute-start.3) | collective-permute-done | bytes 65568 | tf_op jit(solution)/shard_map/ppermute | solution.py:354
  112.6 0.0 collective-permute-done.4
  112.6 0.9 add_convert_fusion
  113.6 1.5 grad_second.1
  115.1 0.2 copy.12
  115.3 0.9 reshape.72
  116.2 1.5 collective-permute-start.5
  117.7 0.6 collective-permute-start.6
  118.4 2.3 %collective-permute-start.7 = (bf16[64,512]{1,0:T(8,128)(2,1)S(1)}, bf16[64,512]{1,0:T(8,128)(2,1)S(1)}, u32[]{:S(2)}, u32[]{:S(2)}) collective-permute-start(bf16[64,512]{1,0:T(8,128)(2,1)S(1)} %add_convert_fusion), channel_id=1, source_target_pairs={{0,12},{1,13},{2,14},{3,15},{4,8},{5,9},{6,10},{7,11},{8,4},{9,5},... | collective-permute-start | bytes 196616 | tf_op jit(solution)/shard_map/ppermute | solution.py:354
  120.6 3.8 %all-to-all-start.3 = ((bf16[16,64,512]{2,1,0:T(8,128)(2,1)}), bf16[16,64,512]{2,1,0:T(8,128)(2,1)S(1)}, u32[]{:S(2)}, u32[]{:S(2)}) async-start(bf16[16,64,512]{2,1,0:T(8,128)(2,1)} %mix_second_back.1), calls=%async_computation.3 | async-start | bytes 2097152 | tf_op jit(solution)/shard_map/all_to_all | solution.py:460
  124.4 0.0 collective-permute-done.5
  124.4 0.8 collective-permute-done.6
  125.2 0.0 collective-permute-done.7
  125.3 1.6 %collective-permute-start.8 = (bf16[256,512]{1,0:T(8,128)(2,1)S(1)}, bf16[256,512]{1,0:T(8,128)(2,1)S(1)}, u32[]{:S(2)}, u32[]{:S(2)}) collective-permute-start(bf16[256,512]{1,0:T(8,128)(2,1)S(1)} %bitcast.44), channel_id=1, source_target_pairs={{0,2},{1,3},{2,0},{3,1},{4,6},{5,7},{6,4},{7,5},{8,10},{9,11},{10,... | collective-permute-start | bytes 786440 | tf_op jit(solution)/shard_map/ppermute | solution.py:354
  126.9 14.7 %collective-permute-done.8 = bf16[256,512]{1,0:T(8,128)(2,1)S(1)} collective-permute-done((bf16[256,512]{1,0:T(8,128)(2,1)S(1)}, bf16[256,512]{1,0:T(8,128)(2,1)S(1)}, u32[]{:S(2)}, u32[]{:S(2)}) %collective-permute-start.8) | collective-permute-done | bytes 262176 | tf_op jit(solution)/shard_map/ppermute | solution.py:354
  141.6 0.1 collective-permute-start.9
  141.7 1.9 %collective-permute-done.9.other_ref = bf16[512,512]{1,0:T(8,128)(2,1)S(1)} collective-permute-done((bf16[512,512]{1,0:T(8,128)(2,1)S(1)}, bf16[512,512]{1,0:T(8,128)(2,1)S(1)}, u32[]{:S(2)}, u32[]{:S(2)}) %collective-permute-start.9) | collective-permute-done | bytes 524320 | tf_op jit(solution)/shard_map/ppermute | solution.py:354
  143.6 1.9 %write_weights.1 = (f32[4,128,512]{2,1,0:T(8,128)}, f32[4,512,128]{2,1,0:T(8,128)}) custom-call(s32[1]{0:T(128)} %bitcast.3.half_ref, bf16[512,512]{1,0:T(8,128)(2,1)S(1)} %pad_maximum_fusion.mine_ref, bf16[512,512]{1,0:T(8,128)(2,1)S(1)} %collective-permute-done.9.other_ref), custom_call_target="tpu_custom_call" | custom-call | flops 262144 | bytes 3145728 | tf_op jit(solution)/shard_map/write_weights/pallas_call | solution.py:432
  145.5 1.9 %all-to-all-done.3 = bf16[16,64,512]{2,1,0:T(8,128)(2,1)S(1)} async-done(((bf16[16,64,512]{2,1,0:T(8,128)(2,1)}), bf16[16,64,512]{2,1,0:T(8,128)(2,1)S(1)}, u32[]{:S(2)}, u32[]{:S(2)}) %all-to-all-start.3) | async-done | bytes 1048608 | tf_op jit(solution)/shard_map/all_to_all | solution.py:460
  147.3 0.9 copy-done.2
  148.3 6.0 %finish.1 = (f32[1024,1024]{1,0:T(8,128)}, bf16[1024,512]{1,0:T(8,128)(2,1)}) custom-call(bf16[1024,1024]{1,0:T(8,128)(2,1)} %bitcast.41, bf16[1024,512]{1,0:T(8,128)(2,1)} %bitcast.43, bf16[1024,512]{1,0:T(8,128)(2,1)} %x_hbm.5, bf16[1024,512]{1,0:T(8,128)(2,1)} %get-tuple-element.48.r_hbm), custom_call_target="tpu_custom_call" | custom-call | flops 2147483648 | bytes 10485760 | tf_op jit(solution)/shard_map/finish/pallas_call | solution.py:324
  (10 shorter events, 0.1 us)
Async XLA Ops:
  0.6 11.3 %copy-start.3 = (bf16[64,16,16]{0,2,1:T(8,128)(2,1)S(1)}, bf16[64,16,16]{0,2,1:T(8,128)(2,1)}, u32[]{:S(2)}) copy-start(bf16[64,16,16]{0,2,1:T(8,128)(2,1)} %param.9) | copy-start | bytes 98308
  4.6 30.3 %all-to-all-start = ((bf16[16,64,512]{2,1,0:T(8,128)(2,1)}), bf16[16,64,512]{2,1,0:T(8,128)(2,1)S(1)}, u32[]{:S(2)}, u32[]{:S(2)}) async-start(bf16[16,64,512]{2,1,0:T(8,128)(2,1)} %bitcast.39), calls=%async_computation | async-start | bytes 2097152 | tf_op jit(solution)/shard_map/all_to_all | solution.py:460
  36.2 29.8 %all-to-all-start.1 = ((bf16[16,64,512]{2,1,0:T(8,128)(2,1)}), bf16[16,64,512]{2,1,0:T(8,128)(2,1)S(1)}, u32[]{:S(2)}, u32[]{:S(2)}) async-start(bf16[16,64,512]{2,1,0:T(8,128)(2,1)} %mix_second.1), calls=%async_computation.1 | async-start | bytes 2097152 | tf_op jit(solution)/shard_map/all_to_all | solution.py:460
  74.5 31.5 %all-to-all-start.2 = ((bf16[16,64,512]{2,1,0:T(8,128)(2,1)}), bf16[16,64,512]{2,1,0:T(8,128)(2,1)S(1)}, u32[]{:S(2)}, u32[]{:S(2)}) async-start(bf16[16,64,512]{2,1,0:T(8,128)(2,1)} %bitcast.42), calls=%async_computation.2 | async-start | bytes 2097152 | tf_op jit(solution)/shard_map/all_to_all | solution.py:460
  81.4 2.2 %collective-permute-start = (bf16[4,128,512]{2,1,0:T(8,128)(2,1)}, bf16[4,128,512]{2,1,0:T(8,128)(2,1)S(1)}, u32[]{:S(2)}, u32[]{:S(2)}) collective-permute-start(bf16[4,128,512]{2,1,0:T(8,128)(2,1)} %get-tuple-element.34), channel_id=1, source_target_pairs={{0,1},{1,0},{2,3},{3,2},{4,5},{5,4},{6,7},{7,6},{8,9},{9,8},{10,11... | collective-permute-start | bytes 1572872 | tf_op jit(solution)/shard_map/ppermute | solution.py:354
  83.6 1.0 copy-start.1
  85.7 14.0 %collective-permute-start.1 = (bf16[256,512]{1,0:T(8,128)(2,1)}, bf16[256,512]{1,0:T(8,128)(2,1)S(1)}, u32[]{:S(2)}, u32[]{:S(2)}) collective-permute-start(bf16[256,512]{1,0:T(8,128)(2,1)} %get-tuple-element.36), channel_id=1, source_target_pairs={{0,2},{1,3},{2,0},{3,1},{4,6},{5,7},{6,4},{7,5},{8,10},{9,11},{10,... | collective-permute-start | bytes 786440 | tf_op jit(solution)/shard_map/ppermute | solution.py:354
  99.6 1.0 copy-start
  101.5 5.7 %collective-permute-start.2 = (bf16[64,512]{1,0:T(8,128)(2,1)}, bf16[64,512]{1,0:T(8,128)(2,1)S(1)}, u32[]{:S(2)}, u32[]{:S(2)}) collective-permute-start(bf16[64,512]{1,0:T(8,128)(2,1)} %get-tuple-element.38), channel_id=1, source_target_pairs={{0,4},{1,5},{2,6},{3,7},{4,0},{5,1},{6,2},{7,3},{8,12},{9,13},{10,... | collective-permute-start | bytes 196616 | tf_op jit(solution)/shard_map/ppermute | solution.py:354
  102.3 10.4 %collective-permute-start.3 = (bf16[64,512]{1,0:T(8,128)(2,1)}, bf16[64,512]{1,0:T(8,128)(2,1)S(1)}, u32[]{:S(2)}, u32[]{:S(2)}) collective-permute-start(bf16[64,512]{1,0:T(8,128)(2,1)} %get-tuple-element.39), channel_id=1, source_target_pairs={{0,8},{1,9},{2,10},{3,11},{4,12},{5,13},{6,14},{7,15},{8,0},{9,1},... | collective-permute-start | bytes 196616 | tf_op jit(solution)/shard_map/ppermute | solution.py:354
  105.7 6.9 %collective-permute-start.4 = (bf16[64,512]{1,0:T(8,128)(2,1)}, bf16[64,512]{1,0:T(8,128)(2,1)S(1)}, u32[]{:S(2)}, u32[]{:S(2)}) collective-permute-start(bf16[64,512]{1,0:T(8,128)(2,1)} %get-tuple-element.40), channel_id=1, source_target_pairs={{0,12},{1,13},{2,14},{3,15},{4,8},{5,9},{6,10},{7,11},{8,4},{9,5},... | collective-permute-start | bytes 196616 | tf_op jit(solution)/shard_map/ppermute | solution.py:354
  116.2 8.2 %collective-permute-start.5 = (bf16[64,512]{1,0:T(8,128)(2,1)S(1)}, bf16[64,512]{1,0:T(8,128)(2,1)S(1)}, u32[]{:S(2)}, u32[]{:S(2)}) collective-permute-start(bf16[64,512]{1,0:T(8,128)(2,1)S(1)} %add_convert_fusion), channel_id=1, source_target_pairs={{0,4},{1,5},{2,6},{3,7},{4,0},{5,1},{6,2},{7,3},{8,12},{9,13},{10,... | collective-permute-start | bytes 196616 | tf_op jit(solution)/shard_map/ppermute | solution.py:354
  117.7 7.5 %collective-permute-start.6 = (bf16[64,512]{1,0:T(8,128)(2,1)S(1)}, bf16[64,512]{1,0:T(8,128)(2,1)S(1)}, u32[]{:S(2)}, u32[]{:S(2)}) collective-permute-start(bf16[64,512]{1,0:T(8,128)(2,1)S(1)} %add_convert_fusion), channel_id=1, source_target_pairs={{0,8},{1,9},{2,10},{3,11},{4,12},{5,13},{6,14},{7,15},{8,0},{9,1},... | collective-permute-start | bytes 196616 | tf_op jit(solution)/shard_map/ppermute | solution.py:354
  118.4 6.8 %collective-permute-start.7 = (bf16[64,512]{1,0:T(8,128)(2,1)S(1)}, bf16[64,512]{1,0:T(8,128)(2,1)S(1)}, u32[]{:S(2)}, u32[]{:S(2)}) collective-permute-start(bf16[64,512]{1,0:T(8,128)(2,1)S(1)} %add_convert_fusion), channel_id=1, source_target_pairs={{0,12},{1,13},{2,14},{3,15},{4,8},{5,9},{6,10},{7,11},{8,4},{9,5},... | collective-permute-start | bytes 196616 | tf_op jit(solution)/shard_map/ppermute | solution.py:354
  120.6 26.7 %all-to-all-start.3 = ((bf16[16,64,512]{2,1,0:T(8,128)(2,1)}), bf16[16,64,512]{2,1,0:T(8,128)(2,1)S(1)}, u32[]{:S(2)}, u32[]{:S(2)}) async-start(bf16[16,64,512]{2,1,0:T(8,128)(2,1)} %mix_second_back.1), calls=%async_computation.3 | async-start | bytes 2097152 | tf_op jit(solution)/shard_map/all_to_all | solution.py:460
  125.3 16.2 %collective-permute-start.8 = (bf16[256,512]{1,0:T(8,128)(2,1)S(1)}, bf16[256,512]{1,0:T(8,128)(2,1)S(1)}, u32[]{:S(2)}, u32[]{:S(2)}) collective-permute-start(bf16[256,512]{1,0:T(8,128)(2,1)S(1)} %bitcast.44), channel_id=1, source_target_pairs={{0,2},{1,3},{2,0},{3,1},{4,6},{5,7},{6,4},{7,5},{8,10},{9,11},{10,... | collective-permute-start | bytes 786440 | tf_op jit(solution)/shard_map/ppermute | solution.py:354
  141.6 2.0 %collective-permute-start.9 = (bf16[512,512]{1,0:T(8,128)(2,1)S(1)}, bf16[512,512]{1,0:T(8,128)(2,1)S(1)}, u32[]{:S(2)}, u32[]{:S(2)}) collective-permute-start(bf16[512,512]{1,0:T(8,128)(2,1)S(1)} %pad_maximum_fusion.mine_ref), channel_id=1, source_target_pairs={{0,1},{1,0},{2,3},{3,2},{4,5},{5,4},{6,7},{7,6},{8,9},{9,8},{10,11... | collective-permute-start | bytes 1572872 | tf_op jit(solution)/shard_map/ppermute | solution.py:354
  147.3 0.9 copy-start.2

commit v15 on v10

--- a/solution.py
+++ b/solution.py
@@ -413,7 +413,9 @@
         return jnp.concatenate([low, high], axis=0)
     whole = jnp.zeros((radix,) + share.shape, share.dtype)
     for s in range(radix):
-        whole = lax.dynamic_update_index_in_dim(whole, got[s], digit ^ s, 0)
+        owner = digit ^ s
+        place = 2 * (owner % 2) + owner // 2
+        whole = lax.dynamic_update_index_in_dim(whole, got[s], place, 0)
     return whole.reshape(radix * share.shape[0], share.shape[1])
 
 
@@ -480,8 +482,10 @@
     terms = [kept, swap(sent, count, 1, 1)]
     terms = [t.reshape(-1, t.shape[-1]) for t in terms]
     steps = radices(count)
-    for step in steps[1:]:
-        terms = scatter_step(terms, count, *step)
+    for stride, radix in steps[1:]:
+        terms = scatter_step(terms, count, stride, 2)
+        if radix == 4:
+            terms = scatter_step(terms, count, 2 * stride, 2)
     terms, back = lax.optimization_barrier((terms, back))
     total = sum(t.astype(F32) for t in terms).astype(BF)
     back, total = lax.optimization_barrier((back, total))

time: 152 us -> 157 us (1.033)
  waiting for transfers between devices: 80.3 us -> 82.7 us
    ppermute x10 -> x9, waiting for transfers between devices: 33.8 us -> 36.2 us  [swap(): lax.ppermute(values, 'seq', [(i, i ^ stride * s) for i in range(count)])]
    pallas_call x2 -> x3, Pallas kernels: 2.87 us -> 3.8 us  [add_and_cut(): pl.pallas_call(body, in_specs=[SCALAR] + [ANY] * number, out_specs=[ANY]...]
    ppermute x10 -> x9, starting transfers between devices: 12.9 us -> 12.2 us  [swap(): lax.ppermute(values, 'seq', [(i, i ^ stride * s) for i in range(count)])]
  transfers between devices with their start and end apart: 14 -> 13, of which waited for: 9 -> 10; matrix products, arithmetic and copies ran while one was open for 1% -> 1% of each run, Pallas kernels for 5% -> 6%
where the time goes in v15:
time: 157 us; the launch traced here: 155 us
  waiting for transfers between devices  82.7 us (53%)
  starting transfers between devices  38.9 us (25%)
  Pallas kernels  28.9 us (18%)
  local copies, waits for them, and re-layouts  3.59 us (2%)
    all_to_all x4, waiting for transfers between devices, exchange(): return lax.all_to_all(cut, 'seq', split_axis=0, concat_axis=0, tiled=True)  46.5 us
    ppermute x9, waiting for transfers between devices, swap(): lax.ppermute(values, 'seq', [(i, i ^ stride * s) for i in range(count)])  36.2 us
    all_to_all x4, starting transfers between devices, exchange(): return lax.all_to_all(cut, 'seq', split_axis=0, concat_axis=0, tiled=True)  26.6 us
    ppermute x9, starting transfers between devices, swap(): lax.ppermute(values, 'seq', [(i, i ^ stride * s) for i in range(count)])  12.2 us
    pallas_call x1, Pallas kernels, middle(): pl.pallas_call(body, in_specs=[SCALAR, ANY, ANY, VMEM, ANY, ANY], out_spe...  8.52 us
    pallas_call x1, Pallas kernels, finish(): pl.pallas_call(body, in_specs=[ANY] * 4, out_specs=[ANY] * 2, out_shape=[...  5.99 us
    pallas_call x1, Pallas kernels, mix_first(): pl.pallas_call(body, in_specs=[ANY, ANY], out_specs=ANY, out_shape=pltpu....  3.92 us
    pallas_call x3, Pallas kernels, add_and_cut(): pl.pallas_call(body, in_specs=[SCALAR] + [ANY] * number, out_specs=[ANY]...  3.8 us
  transfers between devices with their start and end apart: 13, of which 10 were waited for; matrix products, arithmetic and copies ran while one was open for 1% of the time, Pallas kernels for 6%

profile of v15, /device:TPU:0, one launch (start us, length us, event | category | flops | bytes accessed | tf_op | source)
XLA Modules:
  0.0 155.1 jit_solution(10999500468271851578)
XLA Ops:
  0.6 3.9 %mix_first.1 = bf16[1024,512]{1,0:T(8,128)(2,1)} custom-call(bf16[1024,1024]{1,0:T(8,128)(2,1)} %bitcast.44, bf16[1024,512]{1,0:T(8,128)(2,1)} %x_hbm.5), custom_call_target="tpu_custom_call" | custom-call | flops 1073741824 | bytes 4194304 | tf_op jit(solution)/shard_map/mix_first/pallas_call | solution.py:73
  4.6 0.0 copy-start.4
  4.6 7.5 %all-to-all-start = ((bf16[16,64,512]{2,1,0:T(8,128)(2,1)}), bf16[16,64,512]{2,1,0:T(8,128)(2,1)S(1)}, u32[]{:S(2)}, u32[]{:S(2)}) async-start(bf16[16,64,512]{2,1,0:T(8,128)(2,1)} %bitcast.43), calls=%async_computation | async-start | bytes 2097152 | tf_op jit(solution)/shard_map/all_to_all | solution.py:460
  12.1 0.2 reshape.72
  12.3 0.2 copy.11
  12.5 0.7 spread_factor.1.m_ref
  13.2 21.9 %all-to-all-done.in_ref.u_ref = bf16[16,64,512]{2,1,0:T(8,128)(2,1)S(1)} async-done(((bf16[16,64,512]{2,1,0:T(8,128)(2,1)}), bf16[16,64,512]{2,1,0:T(8,128)(2,1)S(1)}, u32[]{:S(2)}, u32[]{:S(2)}) %all-to-all-start) | async-done | bytes 1048608 | tf_op jit(solution)/shard_map/all_to_all | solution.py:460
  35.0 1.2 mix_second.1
  36.3 6.9 %all-to-all-start.1 = ((bf16[16,64,512]{2,1,0:T(8,128)(2,1)}), bf16[16,64,512]{2,1,0:T(8,128)(2,1)S(1)}, u32[]{:S(2)}, u32[]{:S(2)}) async-start(bf16[16,64,512]{2,1,0:T(8,128)(2,1)} %mix_second.1), calls=%async_computation.1 | async-start | bytes 2097152 | tf_op jit(solution)/shard_map/all_to_all | solution.py:460
  43.2 22.9 %all-to-all-done.1 = bf16[16,64,512]{2,1,0:T(8,128)(2,1)S(1)} async-done(((bf16[16,64,512]{2,1,0:T(8,128)(2,1)}), bf16[16,64,512]{2,1,0:T(8,128)(2,1)S(1)}, u32[]{:S(2)}, u32[]{:S(2)}) %all-to-all-start.1) | async-done | bytes 1048608 | tf_op jit(solution)/shard_map/all_to_all | solution.py:460
  66.1 8.5 %middle.1 = (bf16[1024,512]{1,0:T(8,128)(2,1)}, bf16[1024,512]{1,0:T(8,128)(2,1)}, bf16[4,128,512]{2,1,0:T(8,128)(2,1)}, bf16[4,128,512]{2,1,0:T(8,128)(2,1)}) custom-call(s32[1]{0:T(128)} %bitcast.4.half_ref, bf16[1024,512]{1,0:T(8,128)(2,1)} %x_hbm.5, bf16[1024,512]{1,0:T(8,128)(2,1)} %g_hbm.1, bf16[1024,512]{1,0:T(8,128)(2,1)S(1)} %bitcast.37, ...), custom_call_target="tpu_custom_call" | custom-call | flops 2684354560 | bytes 7340032 | tf_op jit(solution)/shard_map/middle/pallas_call | solution.py:263
  74.6 0.0 copy-start.1
  74.6 7.0 %all-to-all-start.2 = ((bf16[16,64,512]{2,1,0:T(8,128)(2,1)}), bf16[16,64,512]{2,1,0:T(8,128)(2,1)S(1)}, u32[]{:S(2)}, u32[]{:S(2)}) async-start(bf16[16,64,512]{2,1,0:T(8,128)(2,1)} %bitcast.46), calls=%async_computation.2 | async-start | bytes 2097152 | tf_op jit(solution)/shard_map/all_to_all | solution.py:460
  81.6 0.4 collective-permute-start
  82.0 1.9 %collective-permute-done = bf16[4,128,512]{2,1,0:T(8,128)(2,1)} collective-permute-done((bf16[4,128,512]{2,1,0:T(8,128)(2,1)}, bf16[4,128,512]{2,1,0:T(8,128)(2,1)}, u32[]{:S(2)}, u32[]{:S(2)}) %collective-permute-start) | collective-permute-done | bytes 524320 | tf_op jit(solution)/shard_map/ppermute | solution.py:354
  83.9 2.0 %add_and_cut.3 = (f32[256,512]{1,0:T(8,128)}, bf16[256,512]{1,0:T(8,128)(2,1)}) custom-call(s32[1]{0:T(128)} %bitcast.3.digit_ref, bf16[2,256,512]{2,1,0:T(8,128)(2,1)S(1)} %bitcast.39, bf16[2,256,512]{2,1,0:T(8,128)(2,1)} %bitcast.10.refs_1_), custom_call_target="tpu_custom_call" | custom-call | flops 262144 | bytes 2097152 | tf_op jit(solution)/shard_map/add_and_cut/pallas_call | solution.py:386
  86.0 1.9 %collective-permute-start.1 = (bf16[256,512]{1,0:T(8,128)(2,1)}, bf16[256,512]{1,0:T(8,128)(2,1)S(1)}, u32[]{:S(2)}, u32[]{:S(2)}) collective-permute-start(bf16[256,512]{1,0:T(8,128)(2,1)} %get-tuple-element.35), channel_id=1, source_target_pairs={{0,2},{1,3},{2,0},{3,1},{4,6},{5,7},{6,4},{7,5},{8,10},{9,11},{10,... | collective-permute-start | bytes 786440 | tf_op jit(solution)/shard_map/ppermute | solution.py:354
  87.9 12.0 %collective-permute-done.1 = bf16[256,512]{1,0:T(8,128)(2,1)S(1)} collective-permute-done((bf16[256,512]{1,0:T(8,128)(2,1)}, bf16[256,512]{1,0:T(8,128)(2,1)S(1)}, u32[]{:S(2)}, u32[]{:S(2)}) %collective-permute-start.1) | collective-permute-done | bytes 262176 | tf_op jit(solution)/shard_map/ppermute | solution.py:354
  99.9 1.0 copy-done
  100.9 0.9 add_and_cut.4
  101.8 0.8 collective-permute-start.2
  102.6 5.6 %collective-permute-done.2 = bf16[128,512]{1,0:T(8,128)(2,1)S(1)} collective-permute-done((bf16[128,512]{1,0:T(8,128)(2,1)}, bf16[128,512]{1,0:T(8,128)(2,1)S(1)}, u32[]{:S(2)}, u32[]{:S(2)}) %collective-permute-start.2) | collective-permute-done | bytes 131104 | tf_op jit(solution)/shard_map/ppermute | solution.py:354
  108.2 0.9 copy-done.2
  109.1 0.9 add_and_cut.5
  110.0 0.0 copy-start.3
  110.0 2.5 %collective-permute-start.3 = (bf16[64,512]{1,0:T(8,128)(2,1)}, bf16[64,512]{1,0:T(8,128)(2,1)S(1)}, u32[]{:S(2)}, u32[]{:S(2)}) collective-permute-start(bf16[64,512]{1,0:T(8,128)(2,1)} %get-tuple-element.39), channel_id=1, source_target_pairs={{0,8},{1,9},{2,10},{3,11},{4,12},{5,13},{6,14},{7,15},{8,0},{9,1},... | collective-permute-start | bytes 196616 | tf_op jit(solution)/shard_map/ppermute | solution.py:354
  112.6 0.0 all-to-all-done.2.in_ref.g_ref
  112.6 1.3 mix_second_back.1
  113.8 1.7 %collective-permute-done.3 = bf16[64,512]{1,0:T(8,128)(2,1)S(1)} collective-permute-done((bf16[64,512]{1,0:T(8,128)(2,1)}, bf16[64,512]{1,0:T(8,128)(2,1)S(1)}, u32[]{:S(2)}, u32[]{:S(2)}) %collective-permute-start.3) | collective-permute-done | bytes 65568 | tf_op jit(solution)/shard_map/ppermute | solution.py:354
  115.5 2.1 %collective-permute-start.4 = (bf16[64,512]{1,0:T(8,128)(2,1)S(1)}, bf16[64,512]{1,0:T(8,128)(2,1)S(1)}, u32[]{:S(2)}, u32[]{:S(2)}) collective-permute-start(bf16[64,512]{1,0:T(8,128)(2,1)S(1)} %add_convert_fusion), channel_id=1, source_target_pairs={{0,4},{1,5},{2,6},{3,7},{4,0},{5,1},{6,2},{7,3},{8,12},{9,13},{10,... | collective-permute-start | bytes 196616 | tf_op jit(solution)/shard_map/ppermute | solution.py:354
  117.6 3.3 %collective-permute-start.5 = (bf16[64,512]{1,0:T(8,128)(2,1)S(1)}, bf16[64,512]{1,0:T(8,128)(2,1)S(1)}, u32[]{:S(2)}, u32[]{:S(2)}) collective-permute-start(bf16[64,512]{1,0:T(8,128)(2,1)S(1)} %add_convert_fusion), channel_id=1, source_target_pairs={{0,8},{1,9},{2,10},{3,11},{4,12},{5,13},{6,14},{7,15},{8,0},{9,1},... | collective-permute-start | bytes 196616 | tf_op jit(solution)/shard_map/ppermute | solution.py:354
  120.9 0.0 collective-permute-start.6
  120.9 5.3 %all-to-all-start.3 = ((bf16[16,64,512]{2,1,0:T(8,128)(2,1)}), bf16[16,64,512]{2,1,0:T(8,128)(2,1)}, u32[]{:S(2)}, u32[]{:S(2)}) async-start(bf16[16,64,512]{2,1,0:T(8,128)(2,1)} %mix_second_back.1), calls=%async_computation.3 | async-start | bytes 2097152 | tf_op jit(solution)/shard_map/all_to_all | solution.py:460
  126.1 0.0 collective-permute-done.4
  126.1 0.0 collective-permute-done.5
  126.1 0.8 collective-permute-done.6
  127.0 1.2 collective-permute-start.7
  128.2 1.5 grad_second.1
  129.7 0.2 copy.12
  129.9 0.9 reshape.84
  130.9 12.4 %collective-permute-done.7 = bf16[256,512]{1,0:T(8,128)(2,1)S(1)} collective-permute-done((bf16[256,512]{1,0:T(8,128)(2,1)S(1)}, bf16[256,512]{1,0:T(8,128)(2,1)S(1)}, u32[]{:S(2)}, u32[]{:S(2)}) %collective-permute-start.7) | collective-permute-done | bytes 262176 | tf_op jit(solution)/shard_map/ppermute | solution.py:354
  143.3 0.1 collective-permute-start.8
  143.4 1.9 %collective-permute-done.8 = bf16[512,512]{1,0:T(8,128)(2,1)S(1)} collective-permute-done((bf16[512,512]{1,0:T(8,128)(2,1)S(1)}, bf16[512,512]{1,0:T(8,128)(2,1)S(1)}, u32[]{:S(2)}, u32[]{:S(2)}) %collective-permute-start.8) | collective-permute-done | bytes 524320 | tf_op jit(solution)/shard_map/ppermute | solution.py:354
  145.3 0.1 broadcast_select_fusion.1
  145.4 0.1 pad_maximum_fusion.up_in.down_in
  145.5 1.9 %write_weights.1 = (f32[4,128,512]{2,1,0:T(8,128)}, f32[4,512,128]{2,1,0:T(8,128)}) custom-call(bf16[1024,512]{1,0:T(8,128)(2,1)S(1)} %pad_maximum_fusion.up_in.down_in, bf16[1024,512]{1,0:T(8,128)(2,1)S(1)} %pad_maximum_fusion.up_in.down_in), custom_call_target="tpu_custom_call" | custom-call | flops 262144 | bytes 3145728 | tf_op jit(solution)/shard_map/write_weights/pallas_call | solution.py:429
  147.4 1.7 %all-to-all-done.3 = bf16[16,64,512]{2,1,0:T(8,128)(2,1)} async-done(((bf16[16,64,512]{2,1,0:T(8,128)(2,1)}), bf16[16,64,512]{2,1,0:T(8,128)(2,1)}, u32[]{:S(2)}, u32[]{:S(2)}) %all-to-all-start.3) | async-done | bytes 1048608 | tf_op jit(solution)/shard_map/all_to_all | solution.py:460
  149.1 6.0 %finish.1 = (f32[1024,1024]{1,0:T(8,128)}, bf16[1024,512]{1,0:T(8,128)(2,1)}) custom-call(bf16[1024,1024]{1,0:T(8,128)(2,1)} %bitcast.45, bf16[1024,512]{1,0:T(8,128)(2,1)} %bitcast.16.d_hbm, bf16[1024,512]{1,0:T(8,128)(2,1)} %x_hbm.5, bf16[1024,512]{1,0:T(8,128)(2,1)} %get-tuple-element.45.r_hbm), custom_call_target="tpu_custom_call" | custom-call | flops 2147483648 | bytes 10485760 | tf_op jit(solution)/shard_map/finish/pallas_call | solution.py:324
  (13 shorter events, 0.2 us)
Async XLA Ops:
  4.6 7.5 %copy-start.4 = (bf16[64,16,16]{0,2,1:T(8,128)(2,1)S(1)}, bf16[64,16,16]{0,2,1:T(8,128)(2,1)}, u32[]{:S(2)}) copy-start(bf16[64,16,16]{0,2,1:T(8,128)(2,1)} %param.9) | copy-start | bytes 98308
  4.6 30.5 %all-to-all-start = ((bf16[16,64,512]{2,1,0:T(8,128)(2,1)}), bf16[16,64,512]{2,1,0:T(8,128)(2,1)S(1)}, u32[]{:S(2)}, u32[]{:S(2)}) async-start(bf16[16,64,512]{2,1,0:T(8,128)(2,1)} %bitcast.43), calls=%async_computation | async-start | bytes 2097152 | tf_op jit(solution)/shard_map/all_to_all | solution.py:460
  36.3 29.8 %all-to-all-start.1 = ((bf16[16,64,512]{2,1,0:T(8,128)(2,1)}), bf16[16,64,512]{2,1,0:T(8,128)(2,1)S(1)}, u32[]{:S(2)}, u32[]{:S(2)}) async-start(bf16[16,64,512]{2,1,0:T(8,128)(2,1)} %mix_second.1), calls=%async_computation.1 | async-start | bytes 2097152 | tf_op jit(solution)/shard_map/all_to_all | solution.py:460
  74.6 9.3 %copy-start.1 = (bf16[4,128,512]{2,1,0:T(8,128)(2,1)S(1)}, bf16[4,128,512]{2,1,0:T(8,128)(2,1)}, u32[]{:S(2)}) copy-start(bf16[4,128,512]{2,1,0:T(8,128)(2,1)} %get-tuple-element.32) | copy-start | bytes 1572868
  74.6 37.9 %all-to-all-start.2 = ((bf16[16,64,512]{2,1,0:T(8,128)(2,1)}), bf16[16,64,512]{2,1,0:T(8,128)(2,1)S(1)}, u32[]{:S(2)}, u32[]{:S(2)}) async-start(bf16[16,64,512]{2,1,0:T(8,128)(2,1)} %bitcast.46), calls=%async_computation.2 | async-start | bytes 2097152 | tf_op jit(solution)/shard_map/all_to_all | solution.py:460
  81.6 2.3 %collective-permute-start = (bf16[4,128,512]{2,1,0:T(8,128)(2,1)}, bf16[4,128,512]{2,1,0:T(8,128)(2,1)}, u32[]{:S(2)}, u32[]{:S(2)}) collective-permute-start(bf16[4,128,512]{2,1,0:T(8,128)(2,1)} %get-tuple-element.33), channel_id=1, source_target_pairs={{0,1},{1,0},{2,3},{3,2},{4,5},{5,4},{6,7},{7,6},{8,9},{9,8},{10,11... | collective-permute-start | bytes 1572872 | tf_op jit(solution)/shard_map/ppermute | solution.py:354
  86.0 13.9 %collective-permute-start.1 = (bf16[256,512]{1,0:T(8,128)(2,1)}, bf16[256,512]{1,0:T(8,128)(2,1)S(1)}, u32[]{:S(2)}, u32[]{:S(2)}) collective-permute-start(bf16[256,512]{1,0:T(8,128)(2,1)} %get-tuple-element.35), channel_id=1, source_target_pairs={{0,2},{1,3},{2,0},{3,1},{4,6},{5,7},{6,4},{7,5},{8,10},{9,11},{10,... | collective-permute-start | bytes 786440 | tf_op jit(solution)/shard_map/ppermute | solution.py:354
  99.9 1.0 copy-start
  101.8 6.4 %collective-permute-start.2 = (bf16[128,512]{1,0:T(8,128)(2,1)}, bf16[128,512]{1,0:T(8,128)(2,1)S(1)}, u32[]{:S(2)}, u32[]{:S(2)}) collective-permute-start(bf16[128,512]{1,0:T(8,128)(2,1)} %get-tuple-element.37), channel_id=1, source_target_pairs={{0,4},{1,5},{2,6},{3,7},{4,0},{5,1},{6,2},{7,3},{8,12},{9,13},{10,... | collective-permute-start | bytes 393224 | tf_op jit(solution)/shard_map/ppermute | solution.py:354
  108.2 1.0 copy-start.2
  110.0 5.5 %copy-start.3 = (f32[64,512]{1,0:T(8,128)S(1)}, f32[64,512]{1,0:T(8,128)}, u32[]{:S(2)}) copy-start(f32[64,512]{1,0:T(8,128)} %get-tuple-element.42) | copy-start | bytes 393220
  110.0 5.5 %collective-permute-start.3 = (bf16[64,512]{1,0:T(8,128)(2,1)}, bf16[64,512]{1,0:T(8,128)(2,1)S(1)}, u32[]{:S(2)}, u32[]{:S(2)}) collective-permute-start(bf16[64,512]{1,0:T(8,128)(2,1)} %get-tuple-element.39), channel_id=1, source_target_pairs={{0,8},{1,9},{2,10},{3,11},{4,12},{5,13},{6,14},{7,15},{8,0},{9,1},... | collective-permute-start | bytes 196616 | tf_op jit(solution)/shard_map/ppermute | solution.py:354
  115.5 10.6 %collective-permute-start.4 = (bf16[64,512]{1,0:T(8,128)(2,1)S(1)}, bf16[64,512]{1,0:T(8,128)(2,1)S(1)}, u32[]{:S(2)}, u32[]{:S(2)}) collective-permute-start(bf16[64,512]{1,0:T(8,128)(2,1)S(1)} %add_convert_fusion), channel_id=1, source_target_pairs={{0,4},{1,5},{2,6},{3,7},{4,0},{5,1},{6,2},{7,3},{8,12},{9,13},{10,... | collective-permute-start | bytes 196616 | tf_op jit(solution)/shard_map/ppermute | solution.py:354
  117.6 8.6 %collective-permute-start.5 = (bf16[64,512]{1,0:T(8,128)(2,1)S(1)}, bf16[64,512]{1,0:T(8,128)(2,1)S(1)}, u32[]{:S(2)}, u32[]{:S(2)}) collective-permute-start(bf16[64,512]{1,0:T(8,128)(2,1)S(1)} %add_convert_fusion), channel_id=1, source_target_pairs={{0,8},{1,9},{2,10},{3,11},{4,12},{5,13},{6,14},{7,15},{8,0},{9,1},... | collective-permute-start | bytes 196616 | tf_op jit(solution)/shard_map/ppermute | solution.py:354
  120.9 6.1 %collective-permute-start.6 = (bf16[64,512]{1,0:T(8,128)(2,1)S(1)}, bf16[64,512]{1,0:T(8,128)(2,1)S(1)}, u32[]{:S(2)}, u32[]{:S(2)}) collective-permute-start(bf16[64,512]{1,0:T(8,128)(2,1)S(1)} %add_convert_fusion), channel_id=1, source_target_pairs={{0,12},{1,13},{2,14},{3,15},{4,8},{5,9},{6,10},{7,11},{8,4},{9,5},... | collective-permute-start | bytes 196616 | tf_op jit(solution)/shard_map/ppermute | solution.py:354
  120.9 28.3 %all-to-all-start.3 = ((bf16[16,64,512]{2,1,0:T(8,128)(2,1)}), bf16[16,64,512]{2,1,0:T(8,128)(2,1)}, u32[]{:S(2)}, u32[]{:S(2)}) async-start(bf16[16,64,512]{2,1,0:T(8,128)(2,1)} %mix_second_back.1), calls=%async_computation.3 | async-start | bytes 2097152 | tf_op jit(solution)/shard_map/all_to_all | solution.py:460
  127.0 16.2 %collective-permute-start.7 = (bf16[256,512]{1,0:T(8,128)(2,1)S(1)}, bf16[256,512]{1,0:T(8,128)(2,1)S(1)}, u32[]{:S(2)}, u32[]{:S(2)}) collective-permute-start(bf16[256,512]{1,0:T(8,128)(2,1)S(1)} %bitcast.47), channel_id=1, source_target_pairs={{0,2},{1,3},{2,0},{3,1},{4,6},{5,7},{6,4},{7,5},{8,10},{9,11},{10,... | collective-permute-start | bytes 786440 | tf_op jit(solution)/shard_map/ppermute | solution.py:354
  143.3 2.0 %collective-permute-start.8 = (bf16[512,512]{1,0:T(8,128)(2,1)S(1)}, bf16[512,512]{1,0:T(8,128)(2,1)S(1)}, u32[]{:S(2)}, u32[]{:S(2)}) collective-permute-start(bf16[512,512]{1,0:T(8,128)(2,1)S(1)} %pad_maximum_fusion.1), channel_id=1, source_target_pairs={{0,1},{1,0},{2,3},{3,2},{4,5},{5,4},{6,7},{7,6},{8,9},{9,8},{10,11... | collective-permute-start | bytes 1572872 | tf_op jit(solution)/shard_map/ppermute | solution.py:354

commit v16 on v10

--- a/solution.py
+++ b/solution.py
@@ -179,36 +179,63 @@
     return out.reshape(groups, n, 16, n).transpose(0, 2, 1, 3).reshape(here, n, n)
 
 
-def middle(half, blocked, incoming, mixed, up_blocks, down_blocks):
+def pull_back(incoming, down_blocks):
+    rows, channels = incoming.shape
+    groups, inner, width = down_blocks.shape
+    sub = inner // groups
+    step = min(256, rows)
+
+    def body(g_ref, down_ref, out_ref):
+        for p in range(groups):
+            back = dot(g_ref[:, p * width : (p + 1) * width], down_ref[p], 1, 1).astype(BF)
+            for b in range(groups):
+                at = b * inner + p * sub
+                out_ref[:, at : at + sub] = back[:, b * sub : (b + 1) * sub]
+
+    return pl.pallas_call(
+        body,
+        grid=(rows // step,),
+        in_specs=[
+            pl.BlockSpec((step, channels), lambda i: (i, 0)),
+            pl.BlockSpec(down_blocks.shape, lambda i: (0, 0, 0)),
+        ],
+        out_specs=pl.BlockSpec((step, groups * inner), lambda i: (i, 0)),
+        out_shape=pltpu.HBM((rows, groups * inner), BF),
+        compiler_params=params(),
+        cost_estimate=cost(2 * rows * groups * inner * width, 2 * rows * groups * inner),
+        name="pull_back",
+    )(in_hbm(incoming), in_hbm(down_blocks))
+
+
+def middle(half, blocked, incoming, mixed, up_blocks, pulled):
     groups, width, inner = up_blocks.shape
     sub = inner // groups
     rows, channels = blocked.shape
     step = min(256, rows)
     tiles = rows // step
 
-    def body(half_ref, x_hbm, g_hbm, v_ref, up_hbm, down_hbm, *refs):
+    def body(half_ref, x_hbm, g_hbm, v_ref, up_hbm, dq_hbm, *refs):
         dv_hbm, r_hbm, kept_hbm, sent_hbm = refs[:4]
-        x_ref, g_ref, up_ref, down_ref, dv, r_ref, w, halves, sems = refs[4:]
+        x_ref, g_ref, up_ref, dq_ref, dv, r_ref, w, halves, sems = refs[4:]
 
         def rows_copy(src, dst, kind, t):
             at = pl.ds(t * step, step)
             return pltpu.make_async_copy(src.at[at], dst.at[at], sems.at[kind * tiles + t])
 
         def whole_copy(src, dst, number):
-            return pltpu.make_async_copy(src, dst, sems.at[4 * tiles + number])
+            return pltpu.make_async_copy(src, dst, sems.at[5 * tiles + number])
 
         fetch_up = whole_copy(up_hbm, up_ref, 0)
-        fetch_down = whole_copy(down_hbm, down_ref, 1)
         rows_copy(x_hbm, x_ref, 0, 0).start()
         fetch_up.start()
         rows_copy(g_hbm, g_ref, 1, 0).start()
-        fetch_down.start()
+        rows_copy(dq_hbm, dq_ref, 4, 0).start()
         for t in range(1, tiles):
             rows_copy(x_hbm, x_ref, 0, t).start()
             rows_copy(g_hbm, g_ref, 1, t).start()
+            rows_copy(dq_hbm, dq_ref, 4, t).start()
         w[...] = jnp.zeros_like(w)
         fetch_up.wait()
-        fetch_down.wait()
 
         def tile(t, carry):
             rows_copy(x_hbm, x_ref, 0, t).wait()
@@ -222,20 +249,20 @@
             h = (x + v * gate).astype(BF)
             h_parts = [h[:, b * width : (b + 1) * width] for b in range(groups)]
             g_parts = [g[:, b * width : (b + 1) * width] for b in range(groups)]
-            acts, slopes, back = [], [], []
+            acts, slopes = [], []
             for b in range(groups):
                 a = dot(h_parts[b], up_ref[b], 1, 0).astype(BF)
                 s = sigmoid(a)
                 q = a * s
                 acts.append(q)
                 slopes.append(s + q * (1 - s))
-                back.append(dot(g_parts[b], down_ref[b], 1, 1).astype(BF))
+            rows_copy(dq_hbm, dq_ref, 4, t).wait()
             grads = []
             for b in range(groups):
                 lanes = slice(b * sub, (b + 1) * sub)
                 perm = jnp.concatenate([acts[p][:, lanes] for p in range(groups)], axis=1)
                 w[1, b] += dot(g_parts[b], perm, 0, 0)
-                dq = jnp.concatenate([back[p][:, lanes] for p in range(groups)], axis=1)
+                dq = dq_ref[at, b * inner : (b + 1) * inner]
                 da = dq * slopes[b]
                 w[0, b] += dot(h_parts[b], da, 0, 0)
                 grads.append(dot(da, up_ref[b], 1, 1))
@@ -274,19 +301,19 @@
             pltpu.VMEM((rows, channels), BF),
             pltpu.VMEM((rows, channels), BF),
             pltpu.VMEM(up_blocks.shape, BF),
-            pltpu.VMEM(down_blocks.shape, BF),
+            pltpu.VMEM(pulled.shape, BF),
             pltpu.VMEM((rows, channels), BF),
             pltpu.VMEM((rows, channels), BF),
             pltpu.VMEM((2, groups, width, inner), F32),
             pltpu.VMEM((2, groups, width, inner), BF),
-            pltpu.SemaphoreType.DMA((4 * tiles + 4,)),
+            pltpu.SemaphoreType.DMA((5 * tiles + 4,)),
         ],
         compiler_params=params(0),
         cost_estimate=cost(
             10 * hidden * width, 10 * rows * channels + 8 * groups * width * inner, hidden
         ),
         name="middle",
-    )(half, in_hbm(blocked), in_hbm(incoming), in_vmem(mixed), in_hbm(up_blocks), in_hbm(down_blocks))
+    )(half, in_hbm(blocked), in_hbm(incoming), in_vmem(mixed), in_hbm(up_blocks), in_hbm(pulled))
 
 
 def finish(factor, grad_first, blocked, gate_grad, scale):
@@ -301,7 +328,7 @@
         rs = row_copies(r_hbm, r, sems, 3 * tiles, tiles)
         ones = row_copies(one, one_hbm, sems, 4 * tiles, tiles)
         outs = row_copies(out, out_hbm, sems, 5 * tiles, tiles)
-        for c in xs + ds + fs + rs:
+        for c in ds + xs + fs + rs:
             c.start()
         for c in xs:
             c.wait()
@@ -474,7 +501,10 @@
     half = (lax.axis_index("seq") % 2).astype(jnp.int32).reshape(1)
     firsts = exchange(mix_first(factor, tokens))
     mixed = exchange(second(firsts, False)).reshape(block, channels)
-    dv, gate_grad, kept, sent = middle(half, tokens, cotangent, mixed, up_blocks, down_blocks)
+    late = (cotangent, down_blocks)
+    firsts, late = lax.optimization_barrier((firsts, late))
+    pulled = pull_back(*late)
+    dv, gate_grad, kept, sent = middle(half, tokens, cotangent, mixed, up_blocks, pulled)
     grad_mixed = exchange(dv)
     back = second(grad_mixed, True)
     terms = [kept, swap(sent, count, 1, 1)]

time: 152 us -> 152 us (level)
  Pallas kernels: 27.9 us -> 32.8 us
  waiting for transfers between devices: 80.3 us -> 75.4 us
    all_to_all x4, waiting for transfers between devices: 46.6 us -> 41.6 us  [exchange(): return lax.all_to_all(cut, 'seq', split_axis=0, concat_axis=0, tiled=True)]
    pallas_call x0 -> x1, Pallas kernels: none -> 4.92 us  [pull_back(): pl.pallas_call(body, grid=(rows // step,), in_specs=[pl.BlockSpec((step,...]
  transfers between devices with their start and end apart: 14 -> 14, of which waited for: 9 -> 9; matrix products, arithmetic and copies ran while one was open for 1% -> 1% of each run, Pallas kernels for 5% -> 9%
where the time goes in v16:
time: 152 us; the launch traced here: 151 us
  waiting for transfers between devices  75.4 us (50%)
  starting transfers between devices  38.6 us (25%)
  Pallas kernels  32.8 us (22%)
  local copies, waits for them, and re-layouts  2.64 us (2%)
    all_to_all x4, waiting for transfers between devices, exchange(): return lax.all_to_all(cut, 'seq', split_axis=0, concat_axis=0, tiled=True)  41.6 us
    ppermute x10, waiting for transfers between devices, swap(): lax.ppermute(values, 'seq', [(i, i ^ stride * s) for i in range(count)])  33.8 us
    all_to_all x4, starting transfers between devices, exchange(): return lax.all_to_all(cut, 'seq', split_axis=0, concat_axis=0, tiled=True)  25.7 us
    ppermute x10, starting transfers between devices, swap(): lax.ppermute(values, 'seq', [(i, i ^ stride * s) for i in range(count)])  12.9 us
    pallas_call x1, Pallas kernels, middle(): pl.pallas_call(body, in_specs=[SCALAR, ANY, ANY, VMEM, ANY, ANY], out_spe...  8.26 us
    pallas_call x1, Pallas kernels, finish(): pl.pallas_call(body, in_specs=[ANY] * 4, out_specs=[ANY] * 2, out_shape=[...  6.22 us
    pallas_call x1, Pallas kernels, pull_back(): pl.pallas_call(body, grid=(rows // step,), in_specs=[pl.BlockSpec((step,...  4.92 us
    pallas_call x1, Pallas kernels, mix_first(): pl.pallas_call(body, in_specs=[ANY, ANY], out_specs=ANY, out_shape=pltpu....  3.92 us
  transfers between devices with their start and end apart: 14, of which 9 were waited for; matrix products, arithmetic and copies ran while one was open for 1% of the time, Pallas kernels for 9%

profile of v16, /device:TPU:0, one launch (start us, length us, event | category | flops | bytes accessed | tf_op | source)
XLA Modules:
  0.0 150.6 jit_solution(3786903399529946291)
XLA Ops:
  0.6 3.9 %mix_first.1 = bf16[1024,512]{1,0:T(8,128)(2,1)} custom-call(bf16[1024,1024]{1,0:T(8,128)(2,1)} %bitcast.39, bf16[1024,512]{1,0:T(8,128)(2,1)} %x_hbm.5), custom_call_target="tpu_custom_call" | custom-call | flops 1073741824 | bytes 4194304 | tf_op jit(solution)/shard_map/mix_first/pallas_call | solution.py:73
  4.6 0.0 copy-start.3
  4.6 7.5 %all-to-all-start = ((bf16[16,64,512]{2,1,0:T(8,128)(2,1)}), bf16[16,64,512]{2,1,0:T(8,128)(2,1)S(1)}, u32[]{:S(2)}, u32[]{:S(2)}) async-start(bf16[16,64,512]{2,1,0:T(8,128)(2,1)} %bitcast.38), calls=%async_computation | async-start | bytes 2097152 | tf_op jit(solution)/shard_map/all_to_all | solution.py:485
  12.1 0.2 reshape.62
  12.3 0.2 copy.11
  12.5 0.7 spread_factor.1.m_ref
  13.2 21.9 %all-to-all-done.in_ref.u_ref = bf16[16,64,512]{2,1,0:T(8,128)(2,1)S(1)} async-done(((bf16[16,64,512]{2,1,0:T(8,128)(2,1)}), bf16[16,64,512]{2,1,0:T(8,128)(2,1)S(1)}, u32[]{:S(2)}, u32[]{:S(2)}) %all-to-all-start) | async-done | bytes 1048608 | tf_op jit(solution)/shard_map/all_to_all | solution.py:485
  35.0 1.2 mix_second.1
  36.3 6.9 %all-to-all-start.1 = ((bf16[16,64,512]{2,1,0:T(8,128)(2,1)}), bf16[16,64,512]{2,1,0:T(8,128)(2,1)S(1)}, u32[]{:S(2)}, u32[]{:S(2)}) async-start(bf16[16,64,512]{2,1,0:T(8,128)(2,1)} %mix_second.1), calls=%async_computation.1 | async-start | bytes 2097152 | tf_op jit(solution)/shard_map/all_to_all | solution.py:485
  43.2 4.9 %pull_back.1.dq_hbm = bf16[1024,2048]{1,0:T(8,128)(2,1)} custom-call(bf16[1024,512]{1,0:T(8,128)(2,1)} %g_hbm.1, bf16[4,512,128]{2,1,0:T(8,128)(2,1)} %down_ref), custom_call_target="tpu_custom_call" | custom-call | flops 536870912 | bytes 4194304 | tf_op jit(solution)/shard_map/pull_back/pallas_call | solution.py:195
  48.1 18.0 %all-to-all-done.1 = bf16[16,64,512]{2,1,0:T(8,128)(2,1)S(1)} async-done(((bf16[16,64,512]{2,1,0:T(8,128)(2,1)}), bf16[16,64,512]{2,1,0:T(8,128)(2,1)S(1)}, u32[]{:S(2)}, u32[]{:S(2)}) %all-to-all-start.1) | async-done | bytes 1048608 | tf_op jit(solution)/shard_map/all_to_all | solution.py:485
  66.1 8.3 %middle.1 = (bf16[1024,512]{1,0:T(8,128)(2,1)}, bf16[1024,512]{1,0:T(8,128)(2,1)}, bf16[4,128,512]{2,1,0:T(8,128)(2,1)}, bf16[4,128,512]{2,1,0:T(8,128)(2,1)}) custom-call(s32[1]{0:T(128)} %bitcast.3.half_ref, bf16[1024,512]{1,0:T(8,128)(2,1)} %x_hbm.5, bf16[1024,512]{1,0:T(8,128)(2,1)} %g_hbm.1, bf16[1024,512]{1,0:T(8,128)(2,1)S(1)} %bitcast.34, ...), custom_call_target="tpu_custom_call" | custom-call | flops 2684354560 | bytes 7340032 | tf_op jit(solution)/shard_map/middle/pallas_call | solution.py:290
  74.4 0.0 copy-start.1
  74.4 7.0 %all-to-all-start.2 = ((bf16[16,64,512]{2,1,0:T(8,128)(2,1)}), bf16[16,64,512]{2,1,0:T(8,128)(2,1)S(1)}, u32[]{:S(2)}, u32[]{:S(2)}) async-start(bf16[16,64,512]{2,1,0:T(8,128)(2,1)} %bitcast.41), calls=%async_computation.2 | async-start | bytes 2097152 | tf_op jit(solution)/shard_map/all_to_all | solution.py:485
  81.4 0.4 collective-permute-start
  81.8 1.9 %collective-permute-done = bf16[4,128,512]{2,1,0:T(8,128)(2,1)} collective-permute-done((bf16[4,128,512]{2,1,0:T(8,128)(2,1)}, bf16[4,128,512]{2,1,0:T(8,128)(2,1)}, u32[]{:S(2)}, u32[]{:S(2)}) %collective-permute-start) | collective-permute-done | bytes 524320 | tf_op jit(solution)/shard_map/ppermute | solution.py:381
  83.7 2.0 %add_and_cut.2 = (f32[256,512]{1,0:T(8,128)}, bf16[256,512]{1,0:T(8,128)(2,1)}) custom-call(s32[1]{0:T(128)} %bitcast.2.digit_ref, bf16[2,256,512]{2,1,0:T(8,128)(2,1)S(1)} %bitcast.36, bf16[2,256,512]{2,1,0:T(8,128)(2,1)} %bitcast.9.refs_1_), custom_call_target="tpu_custom_call" | custom-call | flops 262144 | bytes 2097152 | tf_op jit(solution)/shard_map/add_and_cut/pallas_call | solution.py:413
  85.7 1.9 %collective-permute-start.1 = (bf16[256,512]{1,0:T(8,128)(2,1)}, bf16[256,512]{1,0:T(8,128)(2,1)S(1)}, u32[]{:S(2)}, u32[]{:S(2)}) collective-permute-start(bf16[256,512]{1,0:T(8,128)(2,1)} %get-tuple-element.42), channel_id=1, source_target_pairs={{0,2},{1,3},{2,0},{3,1},{4,6},{5,7},{6,4},{7,5},{8,10},{9,11},{10,... | collective-permute-start | bytes 786440 | tf_op jit(solution)/shard_map/ppermute | solution.py:381
  87.7 12.0 %collective-permute-done.1 = bf16[256,512]{1,0:T(8,128)(2,1)S(1)} collective-permute-done((bf16[256,512]{1,0:T(8,128)(2,1)}, bf16[256,512]{1,0:T(8,128)(2,1)S(1)}, u32[]{:S(2)}, u32[]{:S(2)}) %collective-permute-start.1) | collective-permute-done | bytes 262176 | tf_op jit(solution)/shard_map/ppermute | solution.py:381
  99.6 1.0 copy-done
  100.7 0.8 add_and_cut.3
  101.5 0.0 copy-start.2
  101.5 0.8 collective-permute-start.2
  102.3 3.4 %collective-permute-start.3 = (bf16[64,512]{1,0:T(8,128)(2,1)}, bf16[64,512]{1,0:T(8,128)(2,1)S(1)}, u32[]{:S(2)}, u32[]{:S(2)}) collective-permute-start(bf16[64,512]{1,0:T(8,128)(2,1)} %get-tuple-element.45), channel_id=1, source_target_pairs={{0,8},{1,9},{2,10},{3,11},{4,12},{5,13},{6,14},{7,15},{8,0},{9,1},... | collective-permute-start | bytes 196616 | tf_op jit(solution)/shard_map/ppermute | solution.py:381
  105.8 0.2 collective-permute-start.4
  106.0 0.0 all-to-all-done.2.in_ref.g_ref
  106.0 1.3 mix_second_back.1
  107.3 0.0 collective-permute-done.2
  107.3 5.3 %collective-permute-done.3 = bf16[64,512]{1,0:T(8,128)(2,1)S(1)} collective-permute-done((bf16[64,512]{1,0:T(8,128)(2,1)}, bf16[64,512]{1,0:T(8,128)(2,1)S(1)}, u32[]{:S(2)}, u32[]{:S(2)}) %collective-permute-start.3) | collective-permute-done | bytes 65568 | tf_op jit(solution)/shard_map/ppermute | solution.py:381
  112.6 0.0 collective-permute-done.4
  112.7 1.6 %collective-permute-start.5 = (bf16[64,512]{1,0:T(8,128)(2,1)S(1)}, bf16[64,512]{1,0:T(8,128)(2,1)S(1)}, u32[]{:S(2)}, u32[]{:S(2)}) collective-permute-start(bf16[64,512]{1,0:T(8,128)(2,1)S(1)} %add_convert_fusion), channel_id=1, source_target_pairs={{0,4},{1,5},{2,6},{3,7},{4,0},{5,1},{6,2},{7,3},{8,12},{9,13},{10,... | collective-permute-start | bytes 196616 | tf_op jit(solution)/shard_map/ppermute | solution.py:381
  114.2 0.7 collective-permute-start.6
  114.9 2.2 %collective-permute-start.7 = (bf16[64,512]{1,0:T(8,128)(2,1)S(1)}, bf16[64,512]{1,0:T(8,128)(2,1)S(1)}, u32[]{:S(2)}, u32[]{:S(2)}) collective-permute-start(bf16[64,512]{1,0:T(8,128)(2,1)S(1)} %add_convert_fusion), channel_id=1, source_target_pairs={{0,12},{1,13},{2,14},{3,15},{4,8},{5,9},{6,10},{7,11},{8,4},{9,5},... | collective-permute-start | bytes 196616 | tf_op jit(solution)/shard_map/ppermute | solution.py:381
  117.1 4.3 %all-to-all-start.3 = ((bf16[16,64,512]{2,1,0:T(8,128)(2,1)}), bf16[16,64,512]{2,1,0:T(8,128)(2,1)}, u32[]{:S(2)}, u32[]{:S(2)}) async-start(bf16[16,64,512]{2,1,0:T(8,128)(2,1)} %mix_second_back.1), calls=%async_computation.3 | async-start | bytes 2097152 | tf_op jit(solution)/shard_map/all_to_all | solution.py:485
  121.5 0.0 collective-permute-done.5
  121.5 0.3 collective-permute-done.6
  121.9 1.5 %collective-permute-start.8 = (bf16[256,512]{1,0:T(8,128)(2,1)S(1)}, bf16[256,512]{1,0:T(8,128)(2,1)S(1)}, u32[]{:S(2)}, u32[]{:S(2)}) collective-permute-start(bf16[256,512]{1,0:T(8,128)(2,1)S(1)} %bitcast.42), channel_id=1, source_target_pairs={{0,2},{1,3},{2,0},{3,1},{4,6},{5,7},{6,4},{7,5},{8,10},{9,11},{10,... | collective-permute-start | bytes 786440 | tf_op jit(solution)/shard_map/ppermute | solution.py:381
  123.4 1.5 %grad_second.1 = f32[4,256,16]{2,1,0:T(8,128)S(1)} custom-call(bf16[16,64,512]{2,1,0:T(8,128)(2,1)S(1)} %all-to-all-done.2.in_ref.g_ref, bf16[16,64,512]{2,1,0:T(8,128)(2,1)S(1)} %all-to-all-done.in_ref.u_ref), custom_call_target="tpu_custom_call" | custom-call | flops 268435456 | bytes 2097152 | tf_op jit(solution)/shard_map/grad_second/pallas_call | solution.py:170
  124.9 0.2 copy.12
  125.2 0.9 reshape.72
  126.1 12.4 %collective-permute-done.8 = bf16[256,512]{1,0:T(8,128)(2,1)S(1)} collective-permute-done((bf16[256,512]{1,0:T(8,128)(2,1)S(1)}, bf16[256,512]{1,0:T(8,128)(2,1)S(1)}, u32[]{:S(2)}, u32[]{:S(2)}) %collective-permute-start.8) | collective-permute-done | bytes 262176 | tf_op jit(solution)/shard_map/ppermute | solution.py:381
  138.6 0.1 collective-permute-start.9
  138.6 1.9 %collective-permute-done.9 = bf16[512,512]{1,0:T(8,128)(2,1)S(1)} collective-permute-done((bf16[512,512]{1,0:T(8,128)(2,1)S(1)}, bf16[512,512]{1,0:T(8,128)(2,1)S(1)}, u32[]{:S(2)}, u32[]{:S(2)}) %collective-permute-start.9) | collective-permute-done | bytes 524320 | tf_op jit(solution)/shard_map/ppermute | solution.py:381
  140.5 0.1 broadcast_select_fusion.1
  140.6 0.1 pad_maximum_fusion.up_in.down_in
  140.7 1.9 %write_weights.1 = (f32[4,128,512]{2,1,0:T(8,128)}, f32[4,512,128]{2,1,0:T(8,128)}) custom-call(bf16[1024,512]{1,0:T(8,128)(2,1)S(1)} %pad_maximum_fusion.up_in.down_in, bf16[1024,512]{1,0:T(8,128)(2,1)S(1)} %pad_maximum_fusion.up_in.down_in), custom_call_target="tpu_custom_call" | custom-call | flops 262144 | bytes 3145728 | tf_op jit(solution)/shard_map/write_weights/pallas_call | solution.py:454
  142.6 1.8 %all-to-all-done.3 = bf16[16,64,512]{2,1,0:T(8,128)(2,1)} async-done(((bf16[16,64,512]{2,1,0:T(8,128)(2,1)}), bf16[16,64,512]{2,1,0:T(8,128)(2,1)}, u32[]{:S(2)}, u32[]{:S(2)}) %all-to-all-start.3) | async-done | bytes 1048608 | tf_op jit(solution)/shard_map/all_to_all | solution.py:485
  144.4 6.2 %finish.1 = (f32[1024,1024]{1,0:T(8,128)}, bf16[1024,512]{1,0:T(8,128)(2,1)}) custom-call(bf16[1024,1024]{1,0:T(8,128)(2,1)} %bitcast.40, bf16[1024,512]{1,0:T(8,128)(2,1)} %bitcast.13.d_hbm, bf16[1024,512]{1,0:T(8,128)(2,1)} %x_hbm.5, bf16[1024,512]{1,0:T(8,128)(2,1)} %get-tuple-element.54.r_hbm), custom_call_target="tpu_custom_call" | custom-call | flops 2147483648 | bytes 10485760 | tf_op jit(solution)/shard_map/finish/pallas_call | solution.py:351
  (13 shorter events, 0.2 us)
Async XLA Ops:
  4.6 7.5 %copy-start.3 = (bf16[64,16,16]{0,2,1:T(8,128)(2,1)S(1)}, bf16[64,16,16]{0,2,1:T(8,128)(2,1)}, u32[]{:S(2)}) copy-start(bf16[64,16,16]{0,2,1:T(8,128)(2,1)} %param.9) | copy-start | bytes 98308
  4.6 30.5 %all-to-all-start = ((bf16[16,64,512]{2,1,0:T(8,128)(2,1)}), bf16[16,64,512]{2,1,0:T(8,128)(2,1)S(1)}, u32[]{:S(2)}, u32[]{:S(2)}) async-start(bf16[16,64,512]{2,1,0:T(8,128)(2,1)} %bitcast.38), calls=%async_computation | async-start | bytes 2097152 | tf_op jit(solution)/shard_map/all_to_all | solution.py:485
  36.3 29.8 %all-to-all-start.1 = ((bf16[16,64,512]{2,1,0:T(8,128)(2,1)}), bf16[16,64,512]{2,1,0:T(8,128)(2,1)S(1)}, u32[]{:S(2)}, u32[]{:S(2)}) async-start(bf16[16,64,512]{2,1,0:T(8,128)(2,1)} %mix_second.1), calls=%async_computation.1 | async-start | bytes 2097152 | tf_op jit(solution)/shard_map/all_to_all | solution.py:485
  74.4 9.3 %copy-start.1 = (bf16[4,128,512]{2,1,0:T(8,128)(2,1)S(1)}, bf16[4,128,512]{2,1,0:T(8,128)(2,1)}, u32[]{:S(2)}) copy-start(bf16[4,128,512]{2,1,0:T(8,128)(2,1)} %get-tuple-element.39) | copy-start | bytes 1572868
  74.4 31.6 %all-to-all-start.2 = ((bf16[16,64,512]{2,1,0:T(8,128)(2,1)}), bf16[16,64,512]{2,1,0:T(8,128)(2,1)S(1)}, u32[]{:S(2)}, u32[]{:S(2)}) async-start(bf16[16,64,512]{2,1,0:T(8,128)(2,1)} %bitcast.41), calls=%async_computation.2 | async-start | bytes 2097152 | tf_op jit(solution)/shard_map/all_to_all | solution.py:485
  81.4 2.3 %collective-permute-start = (bf16[4,128,512]{2,1,0:T(8,128)(2,1)}, bf16[4,128,512]{2,1,0:T(8,128)(2,1)}, u32[]{:S(2)}, u32[]{:S(2)}) collective-permute-start(bf16[4,128,512]{2,1,0:T(8,128)(2,1)} %get-tuple-element.40), channel_id=1, source_target_pairs={{0,1},{1,0},{2,3},{3,2},{4,5},{5,4},{6,7},{7,6},{8,9},{9,8},{10,11... | collective-permute-start | bytes 1572872 | tf_op jit(solution)/shard_map/ppermute | solution.py:381
  85.7 13.9 %collective-permute-start.1 = (bf16[256,512]{1,0:T(8,128)(2,1)}, bf16[256,512]{1,0:T(8,128)(2,1)S(1)}, u32[]{:S(2)}, u32[]{:S(2)}) collective-permute-start(bf16[256,512]{1,0:T(8,128)(2,1)} %get-tuple-element.42), channel_id=1, source_target_pairs={{0,2},{1,3},{2,0},{3,1},{4,6},{5,7},{6,4},{7,5},{8,10},{9,11},{10,... | collective-permute-start | bytes 786440 | tf_op jit(solution)/shard_map/ppermute | solution.py:381
  99.6 1.0 copy-start
  101.5 11.1 %copy-start.2 = (f32[64,512]{1,0:T(8,128)S(1)}, f32[64,512]{1,0:T(8,128)}, u32[]{:S(2)}) copy-start(f32[64,512]{1,0:T(8,128)} %get-tuple-element.49) | copy-start | bytes 393220
  101.5 5.7 %collective-permute-start.2 = (bf16[64,512]{1,0:T(8,128)(2,1)}, bf16[64,512]{1,0:T(8,128)(2,1)S(1)}, u32[]{:S(2)}, u32[]{:S(2)}) collective-permute-start(bf16[64,512]{1,0:T(8,128)(2,1)} %get-tuple-element.44), channel_id=1, source_target_pairs={{0,4},{1,5},{2,6},{3,7},{4,0},{5,1},{6,2},{7,3},{8,12},{9,13},{10,... | collective-permute-start | bytes 196616 | tf_op jit(solution)/shard_map/ppermute | solution.py:381
  102.3 10.3 %collective-permute-start.3 = (bf16[64,512]{1,0:T(8,128)(2,1)}, bf16[64,512]{1,0:T(8,128)(2,1)S(1)}, u32[]{:S(2)}, u32[]{:S(2)}) collective-permute-start(bf16[64,512]{1,0:T(8,128)(2,1)} %get-tuple-element.45), channel_id=1, source_target_pairs={{0,8},{1,9},{2,10},{3,11},{4,12},{5,13},{6,14},{7,15},{8,0},{9,1},... | collective-permute-start | bytes 196616 | tf_op jit(solution)/shard_map/ppermute | solution.py:381
  105.8 6.9 %collective-permute-start.4 = (bf16[64,512]{1,0:T(8,128)(2,1)}, bf16[64,512]{1,0:T(8,128)(2,1)S(1)}, u32[]{:S(2)}, u32[]{:S(2)}) collective-permute-start(bf16[64,512]{1,0:T(8,128)(2,1)} %get-tuple-element.46), channel_id=1, source_target_pairs={{0,12},{1,13},{2,14},{3,15},{4,8},{5,9},{6,10},{7,11},{8,4},{9,5},... | collective-permute-start | bytes 196616 | tf_op jit(solution)/shard_map/ppermute | solution.py:381
  112.7 8.8 %collective-permute-start.5 = (bf16[64,512]{1,0:T(8,128)(2,1)S(1)}, bf16[64,512]{1,0:T(8,128)(2,1)S(1)}, u32[]{:S(2)}, u32[]{:S(2)}) collective-permute-start(bf16[64,512]{1,0:T(8,128)(2,1)S(1)} %add_convert_fusion), channel_id=1, source_target_pairs={{0,4},{1,5},{2,6},{3,7},{4,0},{5,1},{6,2},{7,3},{8,12},{9,13},{10,... | collective-permute-start | bytes 196616 | tf_op jit(solution)/shard_map/ppermute | solution.py:381
  114.2 7.6 %collective-permute-start.6 = (bf16[64,512]{1,0:T(8,128)(2,1)S(1)}, bf16[64,512]{1,0:T(8,128)(2,1)S(1)}, u32[]{:S(2)}, u32[]{:S(2)}) collective-permute-start(bf16[64,512]{1,0:T(8,128)(2,1)S(1)} %add_convert_fusion), channel_id=1, source_target_pairs={{0,8},{1,9},{2,10},{3,11},{4,12},{5,13},{6,14},{7,15},{8,0},{9,1},... | collective-permute-start | bytes 196616 | tf_op jit(solution)/shard_map/ppermute | solution.py:381
  114.9 6.9 %collective-permute-start.7 = (bf16[64,512]{1,0:T(8,128)(2,1)S(1)}, bf16[64,512]{1,0:T(8,128)(2,1)S(1)}, u32[]{:S(2)}, u32[]{:S(2)}) collective-permute-start(bf16[64,512]{1,0:T(8,128)(2,1)S(1)} %add_convert_fusion), channel_id=1, source_target_pairs={{0,12},{1,13},{2,14},{3,15},{4,8},{5,9},{6,10},{7,11},{8,4},{9,5},... | collective-permute-start | bytes 196616 | tf_op jit(solution)/shard_map/ppermute | solution.py:381
  117.1 27.3 %all-to-all-start.3 = ((bf16[16,64,512]{2,1,0:T(8,128)(2,1)}), bf16[16,64,512]{2,1,0:T(8,128)(2,1)}, u32[]{:S(2)}, u32[]{:S(2)}) async-start(bf16[16,64,512]{2,1,0:T(8,128)(2,1)} %mix_second_back.1), calls=%async_computation.3 | async-start | bytes 2097152 | tf_op jit(solution)/shard_map/all_to_all | solution.py:485
  121.9 16.6 %collective-permute-start.8 = (bf16[256,512]{1,0:T(8,128)(2,1)S(1)}, bf16[256,512]{1,0:T(8,128)(2,1)S(1)}, u32[]{:S(2)}, u32[]{:S(2)}) collective-permute-start(bf16[256,512]{1,0:T(8,128)(2,1)S(1)} %bitcast.42), channel_id=1, source_target_pairs={{0,2},{1,3},{2,0},{3,1},{4,6},{5,7},{6,4},{7,5},{8,10},{9,11},{10,... | collective-permute-start | bytes 786440 | tf_op jit(solution)/shard_map/ppermute | solution.py:381
  138.6 2.0 %collective-permute-start.9 = (bf16[512,512]{1,0:T(8,128)(2,1)S(1)}, bf16[512,512]{1,0:T(8,128)(2,1)S(1)}, u32[]{:S(2)}, u32[]{:S(2)}) collective-permute-start(bf16[512,512]{1,0:T(8,128)(2,1)S(1)} %pad_maximum_fusion.1), channel_id=1, source_target_pairs={{0,1},{1,0},{2,3},{3,2},{4,5},{5,4},{6,7},{7,6},{8,9},{9,8},{10,11... | collective-permute-start | bytes 1572872 | tf_op jit(solution)/shard_map/ppermute | solution.py:381

commit v17 on v16

--- a/solution.py
+++ b/solution.py
@@ -316,29 +316,48 @@
     )(half, in_hbm(blocked), in_hbm(incoming), in_vmem(mixed), in_hbm(up_blocks), in_hbm(pulled))
 
 
+def bring(arrays, name):
+    number = len(arrays)
+
+    def body(*refs):
+        sems = refs[-1]
+        copies = [
+            pltpu.make_async_copy(refs[i], refs[number + i], sems.at[i]) for i in range(number)
+        ]
+        for c in copies:
+            c.start()
+        for c in copies:
+            c.wait()
+
+    return pl.pallas_call(
+        body,
+        in_specs=[ANY] * number,
+        out_specs=[pl.BlockSpec(memory_space=pltpu.VMEM)] * number,
+        out_shape=[pltpu.VMEM(a.shape, a.dtype) for a in arrays],
+        scratch_shapes=[pltpu.SemaphoreType.DMA((number,))],
+        compiler_params=pltpu.CompilerParams(vmem_limit_bytes=16 * 1024 * 1024),
+        cost_estimate=cost(0, sum(2 * a.size * a.dtype.itemsize for a in arrays)),
+        name=name,
+    )(*[in_hbm(a) for a in arrays])
+
+
 def finish(factor, grad_first, blocked, gate_grad, scale):
     block, channels = blocked.shape
     tiles = 4
     step = block // tiles
 
-    def body(f_hbm, d_hbm, x_hbm, r_hbm, one_hbm, out_hbm, f, d, x, r, one, out, sems):
+    def body(f, x, d_hbm, r_hbm, one_hbm, out_hbm, d, r, one, out, sems):
         ds = row_copies(d_hbm, d, sems, 0, tiles)
-        xs = row_copies(x_hbm, x, sems, tiles, tiles)
-        fs = row_copies(f_hbm, f, sems, 2 * tiles, tiles)
-        rs = row_copies(r_hbm, r, sems, 3 * tiles, tiles)
-        ones = row_copies(one, one_hbm, sems, 4 * tiles, tiles)
-        outs = row_copies(out, out_hbm, sems, 5 * tiles, tiles)
-        for c in ds + xs + fs + rs:
+        rs = row_copies(r_hbm, r, sems, tiles, tiles)
+        ones = row_copies(one, one_hbm, sems, 2 * tiles, tiles)
+        outs = row_copies(out, out_hbm, sems, 3 * tiles, tiles)
+        for c in ds + rs:
             c.start()
-        for c in xs:
-            c.wait()
         for t in range(tiles):
             at = slice(t * step, (t + 1) * step)
             ds[t].wait()
             one[at, :] = dot(d[at, :], x[...], 1, 1) * scale
             ones[t].start()
-        for c in fs:
-            c.wait()
         for t in range(tiles):
             at = slice(t * step, (t + 1) * step)
             rs[t].wait()
@@ -350,22 +369,20 @@
 
     return pl.pallas_call(
         body,
-        in_specs=[ANY] * 4,
+        in_specs=[VMEM, VMEM, ANY, ANY],
         out_specs=[ANY] * 2,
         out_shape=[pltpu.HBM((block, block), F32), pltpu.HBM((block, channels), BF)],
         scratch_shapes=[
-            pltpu.VMEM((block, block), BF),
-            pltpu.VMEM((block, channels), BF),
             pltpu.VMEM((block, channels), BF),
             pltpu.VMEM((block, channels), BF),
             pltpu.VMEM((block, block), F32),
             pltpu.VMEM((block, channels), BF),
-            pltpu.SemaphoreType.DMA((6 * tiles,)),
+            pltpu.SemaphoreType.DMA((4 * tiles,)),
         ],
         compiler_params=params(0),
         cost_estimate=cost(4 * block * block * channels, 6 * block * block + 8 * block * channels),
         name="finish",
-    )(in_hbm(factor), in_hbm(grad_first), in_hbm(blocked), in_hbm(gate_grad))
+    )(in_vmem(factor), in_vmem(blocked), in_hbm(grad_first), in_hbm(gate_grad))
 
 
 def radices(count):
@@ -520,6 +537,9 @@
     for step in reversed(steps):
         total = gather_step(total, count, *step, after=two if step == steps[1] else ())
     grad_up, grad_down = write_weights(total, up_blocks.shape, down_blocks.shape, scale)
+    late = (factor, tokens)
+    late, grad_up, grad_down = lax.optimization_barrier((late, grad_up, grad_down))
+    factor, tokens = bring(late, "bring")
     one, grad_tokens = finish(factor, grad_first, tokens, gate_grad, scale)
     return (grad_tokens, one.reshape(1, block, block), two, grad_up, grad_down)
 

time: 152 us -> 152 us (level)
  waiting for transfers between devices: 75.4 us -> 73.4 us
    all_to_all x4, waiting for transfers between devices: 41.6 us -> 39.9 us  [exchange(): return lax.all_to_all(cut, 'seq', split_axis=0, concat_axis=0, tiled=True)]
    pallas_call x1 -> x2, Pallas kernels: 6.22 us -> 7.48 us  [the longest x1 5.61 us: finish(): pl.pallas_call(body, in_specs=[VMEM, VMEM, ANY, ANY], out_specs=[ANY] * 2...]
  transfers between devices with their start and end apart: 14 -> 14, of which waited for: 9 -> 7; matrix products, arithmetic and copies ran while one was open for 1% -> 1% of each run, Pallas kernels for 9% -> 10%
where the time goes in v17:
time: 152 us; the launch traced here: 150 us
  waiting for transfers between devices  73.4 us (48%)
  starting transfers between devices  38.8 us (26%)
  Pallas kernels  34.1 us (22%)
  local copies, waits for them, and re-layouts  2.64 us (2%)
    all_to_all x4, waiting for transfers between devices, exchange(): return lax.all_to_all(cut, 'seq', split_axis=0, concat_axis=0, tiled=True)  39.9 us
    ppermute x10, waiting for transfers between devices, swap(): lax.ppermute(values, 'seq', [(i, i ^ stride * s) for i in range(count)])  33.5 us
    all_to_all x4, starting transfers between devices, exchange(): return lax.all_to_all(cut, 'seq', split_axis=0, concat_axis=0, tiled=True)  25.7 us
    ppermute x10, starting transfers between devices, swap(): lax.ppermute(values, 'seq', [(i, i ^ stride * s) for i in range(count)])  13.1 us
    pallas_call x1, Pallas kernels, middle(): pl.pallas_call(body, in_specs=[SCALAR, ANY, ANY, VMEM, ANY, ANY], out_spe...  8.26 us
    pallas_call x1, Pallas kernels, finish(): pl.pallas_call(body, in_specs=[VMEM, VMEM, ANY, ANY], out_specs=[ANY] * 2...  5.61 us
    pallas_call x1, Pallas kernels, pull_back(): pl.pallas_call(body, grid=(rows // step,), in_specs=[pl.BlockSpec((step,...  4.92 us
    pallas_call x1, Pallas kernels, mix_first(): pl.pallas_call(body, in_specs=[ANY, ANY], out_specs=ANY, out_shape=pltpu....  3.92 us
  transfers between devices with their start and end apart: 14, of which 7 were waited for; matrix products, arithmetic and copies ran while one was open for 1% of the time, Pallas kernels for 10%

profile of v17, /device:TPU:0, one launch (start us, length us, event | category | flops | bytes accessed | tf_op | source)
XLA Modules:
  0.0 150.1 jit_solution(8628737229763267685)
XLA Ops:
  0.6 3.9 %mix_first.1 = bf16[1024,512]{1,0:T(8,128)(2,1)} custom-call(bf16[1024,1024]{1,0:T(8,128)(2,1)} %bitcast.38, bf16[1024,512]{1,0:T(8,128)(2,1)} %refs_1_), custom_call_target="tpu_custom_call" | custom-call | flops 1073741824 | bytes 4194304 | tf_op jit(solution)/shard_map/mix_first/pallas_call | solution.py:73
  4.6 0.0 copy-start.3
  4.6 7.5 %all-to-all-start = ((bf16[16,64,512]{2,1,0:T(8,128)(2,1)}), bf16[16,64,512]{2,1,0:T(8,128)(2,1)S(1)}, u32[]{:S(2)}, u32[]{:S(2)}) async-start(bf16[16,64,512]{2,1,0:T(8,128)(2,1)} %bitcast.40), calls=%async_computation | async-start | bytes 2097152 | tf_op jit(solution)/shard_map/all_to_all | solution.py:502
  12.1 0.2 reshape.62
  12.3 0.2 copy.11
  12.5 0.7 spread_factor.1.m_ref
  13.2 21.9 %all-to-all-done.in_ref.u_ref = bf16[16,64,512]{2,1,0:T(8,128)(2,1)S(1)} async-done(((bf16[16,64,512]{2,1,0:T(8,128)(2,1)}), bf16[16,64,512]{2,1,0:T(8,128)(2,1)S(1)}, u32[]{:S(2)}, u32[]{:S(2)}) %all-to-all-start) | async-done | bytes 1048608 | tf_op jit(solution)/shard_map/all_to_all | solution.py:502
  35.0 1.2 mix_second.1
  36.3 6.9 %all-to-all-start.1 = ((bf16[16,64,512]{2,1,0:T(8,128)(2,1)}), bf16[16,64,512]{2,1,0:T(8,128)(2,1)S(1)}, u32[]{:S(2)}, u32[]{:S(2)}) async-start(bf16[16,64,512]{2,1,0:T(8,128)(2,1)} %mix_second.1), calls=%async_computation.1 | async-start | bytes 2097152 | tf_op jit(solution)/shard_map/all_to_all | solution.py:502
  43.2 4.9 %pull_back.1.dq_hbm = bf16[1024,2048]{1,0:T(8,128)(2,1)} custom-call(bf16[1024,512]{1,0:T(8,128)(2,1)} %g_hbm.1, bf16[4,512,128]{2,1,0:T(8,128)(2,1)} %down_ref), custom_call_target="tpu_custom_call" | custom-call | flops 536870912 | bytes 4194304 | tf_op jit(solution)/shard_map/pull_back/pallas_call | solution.py:195
  48.1 18.0 %all-to-all-done.1 = bf16[16,64,512]{2,1,0:T(8,128)(2,1)S(1)} async-done(((bf16[16,64,512]{2,1,0:T(8,128)(2,1)}), bf16[16,64,512]{2,1,0:T(8,128)(2,1)S(1)}, u32[]{:S(2)}, u32[]{:S(2)}) %all-to-all-start.1) | async-done | bytes 1048608 | tf_op jit(solution)/shard_map/all_to_all | solution.py:502
  66.1 8.3 %middle.1 = (bf16[1024,512]{1,0:T(8,128)(2,1)}, bf16[1024,512]{1,0:T(8,128)(2,1)}, bf16[4,128,512]{2,1,0:T(8,128)(2,1)}, bf16[4,128,512]{2,1,0:T(8,128)(2,1)}) custom-call(s32[1]{0:T(128)} %bitcast.3.half_ref, bf16[1024,512]{1,0:T(8,128)(2,1)} %refs_1_, bf16[1024,512]{1,0:T(8,128)(2,1)} %g_hbm.1, bf16[1024,512]{1,0:T(8,128)(2,1)S(1)} %bitcast.34, ...), custom_call_target="tpu_custom_call" | custom-call | flops 2684354560 | bytes 7340032 | tf_op jit(solution)/shard_map/middle/pallas_call | solution.py:290
  74.4 0.0 copy-start.1
  74.4 7.0 %all-to-all-start.2 = ((bf16[16,64,512]{2,1,0:T(8,128)(2,1)}), bf16[16,64,512]{2,1,0:T(8,128)(2,1)S(1)}, u32[]{:S(2)}, u32[]{:S(2)}) async-start(bf16[16,64,512]{2,1,0:T(8,128)(2,1)} %bitcast.41), calls=%async_computation.2 | async-start | bytes 2097152 | tf_op jit(solution)/shard_map/all_to_all | solution.py:502
  81.4 0.4 collective-permute-start
  81.8 1.9 %collective-permute-done = bf16[4,128,512]{2,1,0:T(8,128)(2,1)} collective-permute-done((bf16[4,128,512]{2,1,0:T(8,128)(2,1)}, bf16[4,128,512]{2,1,0:T(8,128)(2,1)}, u32[]{:S(2)}, u32[]{:S(2)}) %collective-permute-start) | collective-permute-done | bytes 524320 | tf_op jit(solution)/shard_map/ppermute | solution.py:398
  83.7 2.0 %add_and_cut.2 = (f32[256,512]{1,0:T(8,128)}, bf16[256,512]{1,0:T(8,128)(2,1)}) custom-call(s32[1]{0:T(128)} %bitcast.2.digit_ref, bf16[2,256,512]{2,1,0:T(8,128)(2,1)S(1)} %bitcast.36, bf16[2,256,512]{2,1,0:T(8,128)(2,1)} %bitcast.9.refs_1_), custom_call_target="tpu_custom_call" | custom-call | flops 262144 | bytes 2097152 | tf_op jit(solution)/shard_map/add_and_cut/pallas_call | solution.py:430
  85.7 1.9 %collective-permute-start.1 = (bf16[256,512]{1,0:T(8,128)(2,1)}, bf16[256,512]{1,0:T(8,128)(2,1)S(1)}, u32[]{:S(2)}, u32[]{:S(2)}) collective-permute-start(bf16[256,512]{1,0:T(8,128)(2,1)} %get-tuple-element.48), channel_id=1, source_target_pairs={{0,2},{1,3},{2,0},{3,1},{4,6},{5,7},{6,4},{7,5},{8,10},{9,11},{10,... | collective-permute-start | bytes 786440 | tf_op jit(solution)/shard_map/ppermute | solution.py:398
  87.7 12.0 %collective-permute-done.1 = bf16[256,512]{1,0:T(8,128)(2,1)S(1)} collective-permute-done((bf16[256,512]{1,0:T(8,128)(2,1)}, bf16[256,512]{1,0:T(8,128)(2,1)S(1)}, u32[]{:S(2)}, u32[]{:S(2)}) %collective-permute-start.1) | collective-permute-done | bytes 262176 | tf_op jit(solution)/shard_map/ppermute | solution.py:398
  99.6 1.0 copy-done
  100.7 0.8 add_and_cut.3
  101.5 0.0 copy-start.2
  101.5 0.8 collective-permute-start.2
  102.3 3.4 %collective-permute-start.3 = (bf16[64,512]{1,0:T(8,128)(2,1)}, bf16[64,512]{1,0:T(8,128)(2,1)S(1)}, u32[]{:S(2)}, u32[]{:S(2)}) collective-permute-start(bf16[64,512]{1,0:T(8,128)(2,1)} %get-tuple-element.51), channel_id=1, source_target_pairs={{0,8},{1,9},{2,10},{3,11},{4,12},{5,13},{6,14},{7,15},{8,0},{9,1},... | collective-permute-start | bytes 196616 | tf_op jit(solution)/shard_map/ppermute | solution.py:398
  105.7 0.2 collective-permute-start.4
  106.0 0.0 all-to-all-done.2.in_ref.g_ref
  106.0 1.3 mix_second_back.1
  107.2 0.0 collective-permute-done.2
  107.3 5.4 %collective-permute-done.3 = bf16[64,512]{1,0:T(8,128)(2,1)S(1)} collective-permute-done((bf16[64,512]{1,0:T(8,128)(2,1)}, bf16[64,512]{1,0:T(8,128)(2,1)S(1)}, u32[]{:S(2)}, u32[]{:S(2)}) %collective-permute-start.3) | collective-permute-done | bytes 65568 | tf_op jit(solution)/shard_map/ppermute | solution.py:398
  112.6 0.0 collective-permute-done.4
  112.7 1.6 %collective-permute-start.7 = (bf16[64,512]{1,0:T(8,128)(2,1)S(1)}, bf16[64,512]{1,0:T(8,128)(2,1)S(1)}, u32[]{:S(2)}, u32[]{:S(2)}) collective-permute-start(bf16[64,512]{1,0:T(8,128)(2,1)S(1)} %add_convert_fusion), channel_id=1, source_target_pairs={{0,12},{1,13},{2,14},{3,15},{4,8},{5,9},{6,10},{7,11},{8,4},{9,5},... | collective-permute-start | bytes 196616 | tf_op jit(solution)/shard_map/ppermute | solution.py:398
  114.3 1.4 collective-permute-start.6
  115.7 1.4 collective-permute-start.5
  117.1 4.3 %all-to-all-start.3 = ((bf16[16,64,512]{2,1,0:T(8,128)(2,1)}), bf16[16,64,512]{2,1,0:T(8,128)(2,1)}, u32[]{:S(2)}, u32[]{:S(2)}) async-start(bf16[16,64,512]{2,1,0:T(8,128)(2,1)} %mix_second_back.1), calls=%async_computation.3 | async-start | bytes 2097152 | tf_op jit(solution)/shard_map/all_to_all | solution.py:502
  121.5 0.0 collective-permute-done.7
  121.5 0.0 collective-permute-done.5
  121.6 1.8 %collective-permute-start.8 = (bf16[256,512]{1,0:T(8,128)(2,1)S(1)}, bf16[256,512]{1,0:T(8,128)(2,1)S(1)}, u32[]{:S(2)}, u32[]{:S(2)}) collective-permute-start(bf16[256,512]{1,0:T(8,128)(2,1)S(1)} %bitcast.42), channel_id=1, source_target_pairs={{0,2},{1,3},{2,0},{3,1},{4,6},{5,7},{6,4},{7,5},{8,10},{9,11},{10,... | collective-permute-start | bytes 786440 | tf_op jit(solution)/shard_map/ppermute | solution.py:398
  123.4 1.5 %grad_second.1 = f32[4,256,16]{2,1,0:T(8,128)S(1)} custom-call(bf16[16,64,512]{2,1,0:T(8,128)(2,1)S(1)} %all-to-all-done.2.in_ref.g_ref, bf16[16,64,512]{2,1,0:T(8,128)(2,1)S(1)} %all-to-all-done.in_ref.u_ref), custom_call_target="tpu_custom_call" | custom-call | flops 268435456 | bytes 2097152 | tf_op jit(solution)/shard_map/grad_second/pallas_call | solution.py:170
  124.9 0.2 copy.12
  125.2 0.9 reshape.71
  126.1 12.4 %collective-permute-done.8 = bf16[256,512]{1,0:T(8,128)(2,1)S(1)} collective-permute-done((bf16[256,512]{1,0:T(8,128)(2,1)S(1)}, bf16[256,512]{1,0:T(8,128)(2,1)S(1)}, u32[]{:S(2)}, u32[]{:S(2)}) %collective-permute-start.8) | collective-permute-done | bytes 262176 | tf_op jit(solution)/shard_map/ppermute | solution.py:398
  138.5 0.1 collective-permute-start.9
  138.6 1.9 %collective-permute-done.9 = bf16[512,512]{1,0:T(8,128)(2,1)S(1)} collective-permute-done((bf16[512,512]{1,0:T(8,128)(2,1)S(1)}, bf16[512,512]{1,0:T(8,128)(2,1)S(1)}, u32[]{:S(2)}, u32[]{:S(2)}) %collective-permute-start.9) | collective-permute-done | bytes 524320 | tf_op jit(solution)/shard_map/ppermute | solution.py:398
  140.5 0.1 broadcast_select_fusion.1
  140.6 0.1 pad_maximum_fusion.up_in.down_in
  140.7 1.9 %write_weights.1 = (f32[4,128,512]{2,1,0:T(8,128)}, f32[4,512,128]{2,1,0:T(8,128)}) custom-call(bf16[1024,512]{1,0:T(8,128)(2,1)S(1)} %pad_maximum_fusion.up_in.down_in, bf16[1024,512]{1,0:T(8,128)(2,1)S(1)} %pad_maximum_fusion.up_in.down_in), custom_call_target="tpu_custom_call" | custom-call | flops 262144 | bytes 3145728 | tf_op jit(solution)/shard_map/write_weights/pallas_call | solution.py:471
  142.6 1.9 %bring.1 = (bf16[1024,1024]{1,0:T(8,128)(2,1)S(1)}, bf16[1024,512]{1,0:T(8,128)(2,1)S(1)}) custom-call(bf16[1024,1024]{1,0:T(8,128)(2,1)} %bitcast.39, bf16[1024,512]{1,0:T(8,128)(2,1)} %refs_1_), custom_call_target="tpu_custom_call" | custom-call | bytes 6291456 | tf_op jit(solution)/shard_map/bring/pallas_call | solution.py:332
  144.5 5.6 %finish.1 = (f32[1024,1024]{1,0:T(8,128)}, bf16[1024,512]{1,0:T(8,128)(2,1)}) custom-call(bf16[1024,1024]{1,0:T(8,128)(2,1)S(1)} %get-tuple-element.73.f, bf16[1024,512]{1,0:T(8,128)(2,1)S(1)} %get-tuple-element.74.x, bf16[1024,512]{1,0:T(8,128)(2,1)} %bitcast.20.d_hbm, bf16[1024,512]{1,0:T(8,128)(2,1)} %get-tuple-element.76.r_hbm), custom_call_target="tpu_custom_call" | custom-call | flops 2147483648 | bytes 10485760 | tf_op jit(solution)/shard_map/finish/pallas_call | solution.py:370
  (14 shorter events, 0.2 us)
Async XLA Ops:
  4.6 7.5 %copy-start.3 = (bf16[64,16,16]{0,2,1:T(8,128)(2,1)S(1)}, bf16[64,16,16]{0,2,1:T(8,128)(2,1)}, u32[]{:S(2)}) copy-start(bf16[64,16,16]{0,2,1:T(8,128)(2,1)} %param.9) | copy-start | bytes 98308
  4.6 30.5 %all-to-all-start = ((bf16[16,64,512]{2,1,0:T(8,128)(2,1)}), bf16[16,64,512]{2,1,0:T(8,128)(2,1)S(1)}, u32[]{:S(2)}, u32[]{:S(2)}) async-start(bf16[16,64,512]{2,1,0:T(8,128)(2,1)} %bitcast.40), calls=%async_computation | async-start | bytes 2097152 | tf_op jit(solution)/shard_map/all_to_all | solution.py:502
  36.3 29.8 %all-to-all-start.1 = ((bf16[16,64,512]{2,1,0:T(8,128)(2,1)}), bf16[16,64,512]{2,1,0:T(8,128)(2,1)S(1)}, u32[]{:S(2)}, u32[]{:S(2)}) async-start(bf16[16,64,512]{2,1,0:T(8,128)(2,1)} %mix_second.1), calls=%async_computation.1 | async-start | bytes 2097152 | tf_op jit(solution)/shard_map/all_to_all | solution.py:502
  74.4 9.3 %copy-start.1 = (bf16[4,128,512]{2,1,0:T(8,128)(2,1)S(1)}, bf16[4,128,512]{2,1,0:T(8,128)(2,1)}, u32[]{:S(2)}) copy-start(bf16[4,128,512]{2,1,0:T(8,128)(2,1)} %get-tuple-element.45) | copy-start | bytes 1572868
  74.4 31.6 %all-to-all-start.2 = ((bf16[16,64,512]{2,1,0:T(8,128)(2,1)}), bf16[16,64,512]{2,1,0:T(8,128)(2,1)S(1)}, u32[]{:S(2)}, u32[]{:S(2)}) async-start(bf16[16,64,512]{2,1,0:T(8,128)(2,1)} %bitcast.41), calls=%async_computation.2 | async-start | bytes 2097152 | tf_op jit(solution)/shard_map/all_to_all | solution.py:502
  81.4 2.3 %collective-permute-start = (bf16[4,128,512]{2,1,0:T(8,128)(2,1)}, bf16[4,128,512]{2,1,0:T(8,128)(2,1)}, u32[]{:S(2)}, u32[]{:S(2)}) collective-permute-start(bf16[4,128,512]{2,1,0:T(8,128)(2,1)} %get-tuple-element.46), channel_id=1, source_target_pairs={{0,1},{1,0},{2,3},{3,2},{4,5},{5,4},{6,7},{7,6},{8,9},{9,8},{10,11... | collective-permute-start | bytes 1572872 | tf_op jit(solution)/shard_map/ppermute | solution.py:398
  85.7 13.9 %collective-permute-start.1 = (bf16[256,512]{1,0:T(8,128)(2,1)}, bf16[256,512]{1,0:T(8,128)(2,1)S(1)}, u32[]{:S(2)}, u32[]{:S(2)}) collective-permute-start(bf16[256,512]{1,0:T(8,128)(2,1)} %get-tuple-element.48), channel_id=1, source_target_pairs={{0,2},{1,3},{2,0},{3,1},{4,6},{5,7},{6,4},{7,5},{8,10},{9,11},{10,... | collective-permute-start | bytes 786440 | tf_op jit(solution)/shard_map/ppermute | solution.py:398
  99.6 1.0 copy-start
  101.5 11.1 %copy-start.2 = (f32[64,512]{1,0:T(8,128)S(1)}, f32[64,512]{1,0:T(8,128)}, u32[]{:S(2)}) copy-start(f32[64,512]{1,0:T(8,128)} %get-tuple-element.55) | copy-start | bytes 393220
  101.5 5.7 %collective-permute-start.2 = (bf16[64,512]{1,0:T(8,128)(2,1)}, bf16[64,512]{1,0:T(8,128)(2,1)S(1)}, u32[]{:S(2)}, u32[]{:S(2)}) collective-permute-start(bf16[64,512]{1,0:T(8,128)(2,1)} %get-tuple-element.50), channel_id=1, source_target_pairs={{0,4},{1,5},{2,6},{3,7},{4,0},{5,1},{6,2},{7,3},{8,12},{9,13},{10,... | collective-permute-start | bytes 196616 | tf_op jit(solution)/shard_map/ppermute | solution.py:398
  102.3 10.3 %collective-permute-start.3 = (bf16[64,512]{1,0:T(8,128)(2,1)}, bf16[64,512]{1,0:T(8,128)(2,1)S(1)}, u32[]{:S(2)}, u32[]{:S(2)}) collective-permute-start(bf16[64,512]{1,0:T(8,128)(2,1)} %get-tuple-element.51), channel_id=1, source_target_pairs={{0,8},{1,9},{2,10},{3,11},{4,12},{5,13},{6,14},{7,15},{8,0},{9,1},... | collective-permute-start | bytes 196616 | tf_op jit(solution)/shard_map/ppermute | solution.py:398
  105.7 6.9 %collective-permute-start.4 = (bf16[64,512]{1,0:T(8,128)(2,1)}, bf16[64,512]{1,0:T(8,128)(2,1)S(1)}, u32[]{:S(2)}, u32[]{:S(2)}) collective-permute-start(bf16[64,512]{1,0:T(8,128)(2,1)} %get-tuple-element.52), channel_id=1, source_target_pairs={{0,12},{1,13},{2,14},{3,15},{4,8},{5,9},{6,10},{7,11},{8,4},{9,5},... | collective-permute-start | bytes 196616 | tf_op jit(solution)/shard_map/ppermute | solution.py:398
  112.7 8.8 %collective-permute-start.7 = (bf16[64,512]{1,0:T(8,128)(2,1)S(1)}, bf16[64,512]{1,0:T(8,128)(2,1)S(1)}, u32[]{:S(2)}, u32[]{:S(2)}) collective-permute-start(bf16[64,512]{1,0:T(8,128)(2,1)S(1)} %add_convert_fusion), channel_id=1, source_target_pairs={{0,12},{1,13},{2,14},{3,15},{4,8},{5,9},{6,10},{7,11},{8,4},{9,5},... | collective-permute-start | bytes 196616 | tf_op jit(solution)/shard_map/ppermute | solution.py:398
  114.3 7.2 %collective-permute-start.6 = (bf16[64,512]{1,0:T(8,128)(2,1)S(1)}, bf16[64,512]{1,0:T(8,128)(2,1)S(1)}, u32[]{:S(2)}, u32[]{:S(2)}) collective-permute-start(bf16[64,512]{1,0:T(8,128)(2,1)S(1)} %add_convert_fusion), channel_id=1, source_target_pairs={{0,8},{1,9},{2,10},{3,11},{4,12},{5,13},{6,14},{7,15},{8,0},{9,1},... | collective-permute-start | bytes 196616 | tf_op jit(solution)/shard_map/ppermute | solution.py:398
  115.7 5.8 %collective-permute-start.5 = (bf16[64,512]{1,0:T(8,128)(2,1)S(1)}, bf16[64,512]{1,0:T(8,128)(2,1)S(1)}, u32[]{:S(2)}, u32[]{:S(2)}) collective-permute-start(bf16[64,512]{1,0:T(8,128)(2,1)S(1)} %add_convert_fusion), channel_id=1, source_target_pairs={{0,4},{1,5},{2,6},{3,7},{4,0},{5,1},{6,2},{7,3},{8,12},{9,13},{10,... | collective-permute-start | bytes 196616 | tf_op jit(solution)/shard_map/ppermute | solution.py:398
  117.1 27.4 %all-to-all-start.3 = ((bf16[16,64,512]{2,1,0:T(8,128)(2,1)}), bf16[16,64,512]{2,1,0:T(8,128)(2,1)}, u32[]{:S(2)}, u32[]{:S(2)}) async-start(bf16[16,64,512]{2,1,0:T(8,128)(2,1)} %mix_second_back.1), calls=%async_computation.3 | async-start | bytes 2097152 | tf_op jit(solution)/shard_map/all_to_all | solution.py:502
  121.6 16.9 %collective-permute-start.8 = (bf16[256,512]{1,0:T(8,128)(2,1)S(1)}, bf16[256,512]{1,0:T(8,128)(2,1)S(1)}, u32[]{:S(2)}, u32[]{:S(2)}) collective-permute-start(bf16[256,512]{1,0:T(8,128)(2,1)S(1)} %bitcast.42), channel_id=1, source_target_pairs={{0,2},{1,3},{2,0},{3,1},{4,6},{5,7},{6,4},{7,5},{8,10},{9,11},{10,... | collective-permute-start | bytes 786440 | tf_op jit(solution)/shard_map/ppermute | solution.py:398
  138.5 2.0 %collective-permute-start.9 = (bf16[512,512]{1,0:T(8,128)(2,1)S(1)}, bf16[512,512]{1,0:T(8,128)(2,1)S(1)}, u32[]{:S(2)}, u32[]{:S(2)}) collective-permute-start(bf16[512,512]{1,0:T(8,128)(2,1)S(1)} %pad_maximum_fusion.1), channel_id=1, source_target_pairs={{0,1},{1,0},{2,3},{3,2},{4,5},{5,4},{6,7},{7,6},{8,9},{9,8},{10,11... | collective-permute-start | bytes 1572872 | tf_op jit(solution)/shard_map/ppermute | solution.py:398
